TPU v7x, 32 devices: a whole 2x2x4 slice. The times are simulated.
32 devices in a mesh: dp: 4 (over y, x), pack: 8 (over z, core).
Axes of the slice: x: 2, y: 2, z: 4, core: 2. Of those that a mesh axis runs over, the one named last changes fastest.
Arguments:
- hidden_in: bfloat16 [64, 4096], P('dp', 'pack'), may hold values from -6 to 6
- attn_gain: float32 [4096], P('pack'), may hold values from 0.25 to 1.75
- w_query: bfloat16 [4096, 4096], P(None, 'pack'), may hold values from -0.09375 to 0.09375
- query_gain: float32 [128], replicated, may hold values from 0.25 to 1.75
- cached_keys: bfloat16 [10240, 1024], P(('dp', 'pack')), may hold values from -200 to 200
- cached_values: bfloat16 [10240, 1024], P(('dp', 'pack')), may hold values from -9 to 9
- w_out: bfloat16 [4096, 4096], P('pack'), may hold values from -0.09375 to 0.09375
- final_gain: float32 [4096], P('pack'), may hold values from 0.25 to 1.75
- lengths: int32 [4, 16], P('dp'), may hold values from 16 to 304, as said below
- pack_order: int32 [4, 16], P('dp'), may hold values from 0 to 15, each once within a row
- partner: int32 [64], replicated, may hold values from 0 to 63, as said below
Outputs:
- pooled: bfloat16 [64, 4096], P('dp', 'pack')
- loss_rows: float32 [64], P(('dp', 'pack'))
- grad_hidden: bfloat16 [64, 4096], P('dp', 'pack')
Inputs may be any that keep to these rules, and one draw needn't show every extreme that they name: Statements 2k and 2k+1 of a group have lengths that sum to 320, so a group's lengths sum to 320 * 8. `pack_order`: each row is a permutation of the group's statement indices. `partner`: no statement is its own positive.
All inputs are finite; a program needn't handle non-finite values.
Results may differ from a plain program's by a relative error of at most 0.019.
Values may be sent and summed in bfloat16 or wider, within the bound.
No kernel may reach another device: no remote copies, remote signals or barrier semaphores. Data moves between devices by JAX's collectives and lax.ppermute only.
A program may use at most 128 MiB of HBM per device.

v0:
```python
import jax
import jax.numpy as jnp
from jax import lax
from jax.sharding import PartitionSpec as P

EPSILON = 1e-06
SOFTMAX_WARMTH = 0.05
ROPE_BASE = 1000000.0
MASKED_LOGIT = -1e30


def merged(array, axis, combine):
    everything = jax.tree.map(
        lambda part, kind: lax.all_gather(part.astype(kind), axis),
        array,
        (jnp.bfloat16, jnp.bfloat16, jnp.bfloat16),
    )

    def take(k):
        return jax.tree.map(lambda part, own: part[k].astype(own.dtype), everything, array)

    return lax.fori_loop(
        1, lax.axis_size(axis), lambda k, so_far: combine(so_far, take(k)), take(0)
    )


def rotate_heads(queries, position):
    head_dim = queries.shape[-1]
    half_dim = head_dim // 2
    frequency = jnp.power(
        jnp.float32(ROPE_BASE), -jnp.arange(half_dim).astype(jnp.float32) * 2.0 / head_dim
    )
    angles = position[:, None] * frequency[None, :]
    cosine = jnp.concatenate([jnp.cos(angles), jnp.cos(angles)], axis=1)[:, None, :]
    sine_part = jnp.concatenate([jnp.sin(angles), jnp.sin(angles)], axis=1)[:, None, :]
    turned = jnp.concatenate([-queries[..., half_dim:], queries[..., :half_dim]], axis=-1)
    return queries * cosine + turned * sine_part


def token_owner(lengths_row, order_row, first_token, token_count):
    stmt_count = order_row.shape[0]
    picked = order_row[:, None] == jnp.arange(stmt_count, dtype=jnp.int32)[None, :]
    packed_len = jnp.sum(jnp.where(picked, lengths_row[None, :], 0), axis=1)
    range_end = jnp.cumsum(packed_len)
    token_index = first_token + jnp.arange(token_count, dtype=jnp.int32)
    slot_index = jnp.sum((token_index[:, None] >= range_end[None, :]).astype(jnp.int32), axis=1)
    return jnp.take(order_row, slot_index)


def block_attention(all_queries, cached_keys, cached_values, token_owners, score_scale):
    stmt_count, head_count, head_dim = all_queries.shape
    kv_heads = cached_keys.shape[1] // head_dim
    group_size = head_count // kv_heads
    grouped = all_queries.reshape(stmt_count, kv_heads, group_size, head_dim)
    key_heads = cached_keys.reshape(-1, kv_heads, head_dim)
    value_heads = cached_values.reshape(-1, kv_heads, head_dim)
    scores = (
        jnp.einsum("skgd,tkd->skgt", grouped, key_heads, preferred_element_type=jnp.float32)
        * score_scale
    )
    token_mask = (token_owners[None, :] == jnp.arange(stmt_count, dtype=jnp.int32)[:, None])[
        :, None, None, :
    ]
    block_max = jnp.max(jnp.where(token_mask, scores, MASKED_LOGIT), axis=3)
    softmax_weights = jnp.where(token_mask, jnp.exp(scores - block_max[..., None]), 0.0)
    block_sum = jnp.sum(softmax_weights, axis=3)
    numerators = jnp.einsum(
        "skgt,tkd->skgd",
        softmax_weights.astype(jnp.bfloat16),
        value_heads,
        preferred_element_type=jnp.float32,
    )
    return (
        block_max.reshape(stmt_count, head_count),
        block_sum.reshape(stmt_count, head_count),
        numerators.reshape(stmt_count, head_count, head_dim),
    )


def masked_logits(unscaled_logits, row_positions, column_ids):
    return jnp.where(
        column_ids[None, :] == row_positions[:, None],
        MASKED_LOGIT,
        unscaled_logits / SOFTMAX_WARMTH,
    )


def log_total(similarity_logits):
    highest = jnp.max(similarity_logits, axis=1)
    return highest + jnp.log(jnp.sum(jnp.exp(similarity_logits - highest[:, None]), axis=1))


def pair_weights(similarity_logits, row_lse, all_lse, row_positions, column_ids, partner):
    partner_rows = jnp.take(partner, row_positions)
    own_partner = (column_ids[None, :] == partner_rows[:, None]).astype(jnp.float32)
    other_partner = (partner[None, :] == row_positions[:, None]).astype(jnp.float32)
    return (
        jnp.exp(similarity_logits - row_lse[:, None])
        + jnp.exp(similarity_logits - all_lse[None, :])
        - own_partner
        - other_partner
    )


def partner_pick(similarity_logits, row_positions, column_ids, partner):
    partner_rows = jnp.take(partner, row_positions)
    return jnp.sum(
        jnp.where(column_ids[None, :] == partner_rows[:, None], similarity_logits, 0.0), axis=1
    )


def local(
    hidden_in,
    attn_gain,
    w_query,
    query_gain,
    cached_keys,
    cached_values,
    w_out,
    final_gain,
    lengths,
    pack_order,
    partner,
):
    pack_size = lax.axis_size("pack")
    pack_index = lax.axis_index("pack")
    group_index = lax.axis_index("dp")
    stmt_count, feature_count = hidden_in.shape
    model_width = feature_count * pack_size
    head_dim = query_gain.shape[0]
    local_heads = w_query.shape[1] // head_dim
    token_count = cached_keys.shape[0]
    total_stmts = partner.shape[0]
    inputs32 = hidden_in.astype(jnp.float32)
    input_squares = lax.psum(jnp.sum(inputs32 * inputs32, axis=1), "pack")
    input_rms = lax.rsqrt(input_squares / model_width + EPSILON)
    normed = (inputs32 * input_rms[:, None] * attn_gain[None, :]).astype(jnp.bfloat16)
    projected = jnp.dot(
        lax.all_gather(normed, "pack", axis=1, tiled=True),
        w_query,
        preferred_element_type=jnp.float32,
    )
    queries = projected.reshape(stmt_count, local_heads, head_dim)
    queries = (
        queries
        * lax.rsqrt(jnp.mean(queries * queries, axis=2, keepdims=True) + EPSILON)
        * query_gain
    )
    lengths_row = lengths[0]
    order_row = pack_order[0]
    queries = rotate_heads(queries, (lengths_row - 1).astype(jnp.float32)).astype(jnp.bfloat16)
    all_queries = lax.all_gather(queries, "pack", axis=1, tiled=True)
    token_owners = token_owner(lengths_row, order_row, pack_index * token_count, token_count)
    block_max, block_sum, numerators = block_attention(
        all_queries, cached_keys, cached_values, token_owners, head_dim ** (-0.5)
    )

    def join_parts(first_part, second_part):
        highest = jnp.maximum(first_part[0], second_part[0])
        first_scale = jnp.exp(first_part[0] - highest)
        second_scale = jnp.exp(second_part[0] - highest)
        return (
            highest,
            first_part[1] * first_scale + second_part[1] * second_scale,
            first_part[2] * first_scale[..., None] + second_part[2] * second_scale[..., None],
        )

    highest, denominator, summed = merged((block_max, block_sum, numerators), "pack", join_parts)
    attended = (summed / denominator[..., None]).astype(jnp.bfloat16)
    own_heads = lax.dynamic_slice_in_dim(attended, pack_index * local_heads, local_heads, 1)
    partial_out = jnp.dot(
        own_heads.reshape(stmt_count, local_heads * head_dim),
        w_out,
        preferred_element_type=jnp.float32,
    )
    attn_out = lax.psum_scatter(
        partial_out.astype(jnp.bfloat16), "pack", scatter_dimension=1, tiled=True
    ).astype(jnp.float32)
    hidden = inputs32 + attn_out
    hidden_squares = lax.psum(jnp.sum(hidden * hidden, axis=1), "pack")
    hidden_rms = jnp.sqrt(hidden_squares / model_width + EPSILON)
    pooled = (hidden / hidden_rms[:, None] * final_gain[None, :]).astype(jnp.bfloat16)
    pooled32 = pooled.astype(jnp.float32)
    pooled_squares = lax.psum(jnp.sum(pooled32 * pooled32, axis=1), "pack")
    pooled_norm = jnp.sqrt(pooled_squares)
    premise_vectors = (pooled32 / pooled_norm[:, None]).astype(jnp.bfloat16)
    partial_logits = lax.dot_general(
        premise_vectors,
        lax.all_gather(premise_vectors, "dp", axis=0, tiled=True),
        (((1,), (1,)), ((), ())),
        preferred_element_type=jnp.float32,
    )
    column_ids = jnp.arange(total_stmts, dtype=jnp.int32)
    row_base = group_index * stmt_count
    summed_logits = lax.psum(partial_logits.astype(jnp.bfloat16), "pack").astype(jnp.float32)
    row_positions = row_base + jnp.arange(stmt_count, dtype=jnp.int32)
    similarity_logits = masked_logits(summed_logits, row_positions, column_ids)
    group_lse = log_total(similarity_logits)
    own_count = stmt_count // pack_size
    loss_group = group_lse - partner_pick(similarity_logits, row_positions, column_ids, partner)
    loss_rows = lax.dynamic_slice_in_dim(loss_group, pack_index * own_count, own_count, 0)
    all_lse = lax.all_gather(group_lse, "dp", axis=0, tiled=True)
    all_weights = pair_weights(
        similarity_logits, group_lse, all_lse, row_positions, column_ids, partner
    ).astype(jnp.bfloat16)
    gathered_rows = jnp.dot(
        all_weights,
        lax.all_gather(premise_vectors, "dp", axis=0, tiled=True),
        preferred_element_type=jnp.float32,
    )
    embedding_gradient = gathered_rows / SOFTMAX_WARMTH
    embed32 = premise_vectors.astype(jnp.float32)
    inner_sum = lax.psum(jnp.sum(embed32 * embedding_gradient, axis=1), "pack")
    grad_pooled = (embedding_gradient - embed32 * inner_sum[:, None]) / pooled_norm[:, None]
    grad_hidden = (
        model_width**0.5 * final_gain[None, :] * grad_pooled / hidden_rms[:, None]
    ).astype(jnp.bfloat16)
    return (pooled, loss_rows, grad_hidden)


def solution(mesh):
    in_specs = (
        P("dp", "pack"),
        P("pack"),
        P(None, "pack"),
        P(),
        P(("dp", "pack"), None),
        P(("dp", "pack"), None),
        P("pack", None),
        P("pack"),
        P("dp", None),
        P("dp", None),
        P(),
    )
    out_specs = (P("dp", "pack"), P(("dp", "pack")), P("dp", "pack"))
    return jax.shard_map(local, mesh=mesh, in_specs=in_specs, out_specs=out_specs, check_vma=False)
```

profile of v0, /device:TPU:0, one launch (start us, length us, event | category | flops | bytes accessed | tf_op | source)
XLA Modules:
  0.0 228.0 jit_solution(6592832983714965298)
XLA Ops:
  7.3 2.0 fusion.46
  9.2 0.7 add_convert_fusion
  9.9 0.9 select_reduce_fusion.2
  10.9 0.1 reduce
  11.1 4.4 %fusion.40 = (s32[320]{0:T(512)S(1)}, s32[320,1]{0,1:T(1,128)S(1)}) fusion(s32[]{:T(128)} %bitcast.16, s32[]{:T(128)} %bitcast.17, s32[]{:T(128)} %bitcast.18, s32[]{:T(128)} %bitcast.19, s32[]{:T(128)} %bitcast.20, s32[]{:T(128)} %bitcast.22, s32[]{:T(128)} %bitcast.21, s32[320]{0:T(512)S(1)} %convert_reduce_fusion), kind=kLoop, calls=%fused_computation.106 | loop fusion | flops 4800 | bytes 3868 | tf_op jit(solution)/shard_map/jit(_take)/gather | solution.py:47
  15.6 5.6 %select_select_fusion = s32[320]{0:T(512)S(1)} fusion(pred[320]{0:T(512)(128)(4,1)S(1)} %get-tuple-element.200, pred[320]{0:T(512)(128)(4,1)S(1)} %get-tuple-element.199, pred[320]{0:T(512)(128)(4,1)S(1)} %get-tuple-element.198, pred[320]{0:T(512)(128)(4,1)S(1)} %get-tuple-element.197, pred[320]{0:T(512)(128)(4,1)S(1)} %get-tuple-element.196, ...), kind=kLoop, calls=%fused_computation.102 | loop fusion | flops 5120 | bytes 6756 | tf_op jit(solution)/shard_map/jit(_take)/select_n | solution.py:47
  21.2 0.8 fusion.20
  22.1 18.1 %psum.35 = f32[16]{0:T(128)S(1)} all-reduce(f32[16]{0:T(128)S(1)} %fusion.20), channel_id=1, replica_groups=mesh['dp'=4,'pack'=8] {'pack'}, use_global_device_ids=true, to_apply=%region_4.5 | all-reduce | flops 16 | bytes 128 | tf_op jit(solution)/shard_map/psum | solution.py:135
  40.1 0.8 fusion.22
  40.9 13.9 %all_gather.25 = bf16[16,4096]{1,0:T(8,128)(2,1)S(1)} all-gather(bf16[16,512]{1,0:T(8,128)(2,1)S(1)} %fusion.22), channel_id=1, replica_groups=mesh['dp'=4,'pack'=8] {'pack'}, dimensions={1}, use_global_device_ids=true | all-gather | bytes 147456 | tf_op jit(solution)/shard_map/all_gather | solution.py:139
  54.9 2.8 %fusion.47 = f32[16,512]{1,0:T(8,128)S(1)} fusion(bf16[16,4096]{1,0:T(8,128)(2,1)S(1)} %all_gather.25, bf16[4096,512]{1,0:T(8,128)(2,1)} %param.17), kind=kOutput, calls=%fused_computation.120 | convolution fusion | flops 67108864 | bytes 4358144 | tf_op jit(solution)/shard_map/dot_general | solution.py:138
  58.1 0.1 multiply_cosine_fusion
  58.4 14.0 %all_gather.26 = bf16[16,32,128]{2,0,1:T(8,128)(2,1)S(1)} all-gather(bf16[16,4,128]{2,0,1:T(8,128)(2,1)S(1)} %fusion.25), channel_id=1, replica_groups=mesh['dp'=4,'pack'=8] {'pack'}, dimensions={1}, use_global_device_ids=true | all-gather | bytes 147456 | tf_op jit(solution)/shard_map/all_gather | solution.py:152
  72.4 0.1 copy.67
  72.5 0.1 copy.68
  72.6 0.4 select_reduce_fusion
  73.1 0.4 convolution_convert_fusion.1
  73.5 0.7 copy.59
  74.3 0.3 fusion.7
  74.7 0.7 gather_fusion
  75.4 14.0 %all_gather.27 = bf16[8,16,32]{2,1,0:T(8,128)(2,1)S(1)} all-gather(bf16[1,16,32]{2,1,0:T(8,128)(2,1)S(1)} %copy.56), channel_id=1, replica_groups=mesh['dp'=4,'pack'=8] {'pack'}, dimensions={0}, use_global_device_ids=true | all-gather | bytes 9216 | tf_op jit(solution)/shard_map/all_gather | solution.py:14
  89.4 14.0 %all_gather.28 = bf16[8,16,32]{2,1,0:T(8,128)(2,1)S(1)} all-gather(bf16[1,16,32]{2,1,0:T(8,128)(2,1)S(1)} %copy.57), channel_id=1, replica_groups=mesh['dp'=4,'pack'=8] {'pack'}, dimensions={0}, use_global_device_ids=true | all-gather | bytes 9216 | tf_op jit(solution)/shard_map/all_gather | solution.py:14
  103.4 0.9 fusion.12
  104.4 8.6 %while.19 = (s32[]{:T(128)}, f32[16,32]{1,0:T(8,128)S(1)}, f32[16,32]{1,0:T(8,128)S(1)}, f32[16,32,128]{2,1,0:T(8,128)S(1)}, bf16[8,16,32]{2,1,0:T(8,128)(2,1)S(...) while((s32[]{:T(128)}, f32[16,32]{1,0:T(8,128)S(1)}, ...), condition=%wide.region_9.10_spmd, body=%wide.region_8.9_spmd.sunk | while | flops 266245 | bytes 673943 | solution.py:22
  104.4 1.2 fusion.60
  105.7 1.2 fusion.60
  106.9 1.2 fusion.60
  108.1 1.2 fusion.60
  109.3 1.2 fusion.60
  110.6 1.2 fusion.60
  111.8 1.2 fusion.60
  113.2 3.5 %convolution_convert_fusion = bf16[16,4096]{1,0:T(8,128)(2,1)} fusion(bf16[512,4096]{1,0:T(8,128)(2,1)} %param.21, bf16[2,8,4,128]{3,2,1,0:T(4,128)(2,1)S(1)} %bitcast.97), kind=kOutput, calls=%fused_computation.9 | convolution fusion | flops 67174400 | bytes 4341760 | tf_op jit(solution)/shard_map/dot_general | solution.py:171
  116.7 0.6 dynamic-slice
  118.0 27.2 %reduce-scatter.2.cloned.1.call-done = bf16[16,512]{1,0:T(8,128)(2,1)} async-done(((bf16[16,4096]{1,0:T(8,128)(2,1)}), bf16[16,512]{1,0:T(8,128)(2,1)}) %reduce-scatter.2.cloned.1.call-update) | async-done | bytes 16400 | tf_op jit(solution)/shard_map/reduce_scatter | solution.py:176
  145.2 0.8 multiply_reduce_fusion
  146.1 13.7 %psum.36 = f32[16]{0:T(128)S(1)} all-reduce(f32[16]{0:T(128)S(1)} %multiply_reduce_fusion), channel_id=1, replica_groups=mesh['dp'=4,'pack'=8] {'pack'}, use_global_device_ids=true, to_apply=%region_12.13 | all-reduce | flops 16 | bytes 128 | tf_op jit(solution)/shard_map/psum | solution.py:180
  159.8 0.9 fusion.13
  160.7 13.6 %psum.37 = f32[16]{0:T(128)S(1)} all-reduce(f32[16]{0:T(128)S(1)} %get-tuple-element.221), channel_id=1, replica_groups=mesh['dp'=4,'pack'=8] {'pack'}, use_global_device_ids=true, to_apply=%region_14.15 | all-reduce | flops 16 | bytes 128 | tf_op jit(solution)/shard_map/psum | solution.py:184
  174.4 8.5 %all_gather.30 = bf16[64,512]{1,0:T(8,128)(2,1)S(1)} all-gather(bf16[16,512]{1,0:T(8,128)(2,1)S(1)} %fusion.14), channel_id=1, replica_groups=mesh['dp'=4,'pack'=8] {'dp'}, dimensions={0}, use_global_device_ids=true | all-gather | bytes 81920 | tf_op jit(solution)/shard_map/all_gather | solution.py:189
  182.8 0.1 convolution_convert_fusion.2
  183.0 13.6 %psum.38 = bf16[16,64]{1,0:T(8,128)(2,1)S(1)} all-reduce(bf16[16,64]{1,0:T(8,128)(2,1)S(1)} %convolution_convert_fusion.2), channel_id=1, replica_groups=mesh['dp'=4,'pack'=8] {'pack'}, use_global_device_ids=true, to_apply=%region_15.16 | all-reduce | flops 1024 | bytes 4096 | tf_op jit(solution)/shard_map/psum | solution.py:195
  196.6 0.2 fusion.30
  196.7 0.2 select_reduce_fusion.1
  197.1 8.9 %all-reduce = f32[64]{0:T(128)S(1)} all-reduce(f32[64]{0:T(128)S(1)} %get-tuple-element.219), channel_id=1, replica_groups=mesh['dp'=4,'pack'=8] {'dp'}, use_global_device_ids=true, to_apply=%add | all-reduce | flops 64 | bytes 512
  206.0 0.3 fusion.15
  206.3 13.6 %psum.39 = f32[16]{0:T(128)S(1)} all-reduce(f32[16]{0:T(128)S(1)} %get-tuple-element.247), channel_id=1, replica_groups=mesh['dp'=4,'pack'=8] {'pack'}, use_global_device_ids=true, to_apply=%region_20.22 | all-reduce | flops 16 | bytes 128 | tf_op jit(solution)/shard_map/psum | solution.py:213
  219.9 0.6 dynamic_slice.37
  220.4 0.7 fusion.27
  (61 shorter events, 1.7 us)
Async XLA Ops:
  7.2 50.8 %copy-start.6 = (f32[128]{0:T(128)S(1)}, f32[128]{0:T(128)}, u32[]{:S(2)}) copy-start(f32[128]{0:T(128)} %param.18) | copy-start | bytes 1540
  7.2 65.2 %copy-start.1 = (bf16[320,1024]{1,0:T(8,128)(2,1)S(1)}, bf16[320,1024]{1,0:T(8,128)(2,1)}, u32[]{:S(2)}) copy-start(bf16[320,1024]{1,0:T(8,128)(2,1)} %param.19) | copy-start | bytes 1966084
  7.2 65.3 %copy-start.2 = (bf16[320,1024]{1,0:T(8,128)(2,1)S(1)}, bf16[320,1024]{1,0:T(8,128)(2,1)}, u32[]{:S(2)}) copy-start(bf16[320,1024]{1,0:T(8,128)(2,1)} %param.20) | copy-start | bytes 1966084
  7.2 96.2 %all-gather.2.cloned.1.call-start = ((), (), s32[]{:S(2)}) async-start(), calls=%async_computation.1 | async-start | bytes 1179648 | tf_op jit(solution)/shard_map/all_gather | solution.py:14
  57.7 17.0 %copy-start = (s32[64]{0:T(128)S(1)}, s32[64]{0:T(128)}, u32[]{:S(2)}) copy-start(s32[64]{0:T(128)} %param.25) | copy-start | bytes 772
  74.2 71.1 %reduce-scatter.2.cloned.1.call-start = ((), (), s32[]{:S(2)}) async-start(), calls=%async_computation.2 | async-start | bytes 147456 | tf_op jit(solution)/shard_map/reduce_scatter | solution.py:176
  104.4 12.4 %copy-start.7 = (u32[32]{0:T(128)S(1)}, u32[32]{0:T(128)}, u32[]{:S(2)}) copy-start(u32[32]{0:T(128)} %constant.138) | copy-start | bytes 388
  104.4 13.6 %copy-start.5 = (f32[512]{0:T(512)S(1)}, f32[512]{0:T(512)}, u32[]{:S(2)}) copy-start(f32[512]{0:T(512)} %param.22) | copy-start | bytes 6148
  104.4 40.8 %copy-start.3 = (bf16[16,512]{1,0:T(8,128)(2,1)S(1)}, bf16[16,512]{1,0:T(8,128)(2,1)}, u32[]{:S(2)}) copy-start(bf16[16,512]{1,0:T(8,128)(2,1)} %param.15) | copy-start | bytes 49156
  160.7 60.5 %copy-start.4 = (bf16[16,512]{1,0:T(8,128)(2,1)}, bf16[16,512]{1,0:T(8,128)(2,1)S(1)}, u32[]{:S(2)}) copy-start(bf16[16,512]{1,0:T(8,128)(2,1)S(1)} %get-tuple-element.222) | copy-start | bytes 49156
Sparse Core Ops, SparseCore 0:
  74.3 20.3 all-gather.1
  116.8 28.3 reduce-scatter.1
where the time goes:
time: 229 us; the launch traced here: 228 us
  blocking collectives  146 us (64%)
  waiting for transfers between devices  27.3 us (12%)
  other arithmetic  26.8 us (12%)
  between operations  15 us (7%)
  matrix products  7.55 us (3%)
  local copies, waits for them, and re-layouts  5.17 us (2%)
    all_gather x2, blocking collectives, merged(): lax.all_gather(part.astype(kind), axis)  28 us
    reduce_scatter x1, waiting for transfers between devices, local(): lax.psum_scatter(partial_out.astype(jnp.bfloat16), 'pack', scatter_dimens...  27.2 us
    psum x1, blocking collectives, local(): input_squares = lax.psum(jnp.sum(inputs32 * inputs32, axis=1), 'pack')  18.1 us
    all_gather x1, blocking collectives, local(): all_queries = lax.all_gather(queries, 'pack', axis=1, tiled=True)  14 us
    all_gather x1, blocking collectives, local(): lax.all_gather(normed, 'pack', axis=1, tiled=True)  13.9 us
    psum x1, blocking collectives, local(): hidden_squares = lax.psum(jnp.sum(hidden * hidden, axis=1), 'pack')  13.7 us
    psum x1, blocking collectives, local(): lax.psum(partial_logits.astype(jnp.bfloat16), 'pack').astype(jnp.float32)  13.6 us
    psum x1, blocking collectives, local(): pooled_squares = lax.psum(jnp.sum(pooled32 * pooled32, axis=1), 'pack')  13.6 us
  transfers between devices with their start and end apart: 2, of which 1 were waited for; matrix products, arithmetic and copies ran while one was open for 1% of the time, Pallas kernels for 0%

commit v1 on v0

v1 whole, which is shorter than its diff:
```python
import numpy as np
import jax
import jax.numpy as jnp
from jax import lax
from jax.sharding import PartitionSpec as P

EPSILON = 1e-06
SOFTMAX_WARMTH = 0.05
ROPE_BASE = 1000000.0
MASKED_LOGIT = -1e30


def gather_blocks(block, axis):
    size = lax.axis_size(axis)
    return lax.all_to_all(jnp.broadcast_to(block[None], (size,) + block.shape), axis, 0, 0)


def split_float(value, pieces):
    out = []
    for _ in range(pieces):
        piece = lax.reduce_precision(value, 8, 7)
        out.append(piece.astype(jnp.bfloat16))
        value = value - piece
    return out


def cosine_and_sine(angles):
    turns = jnp.round(angles * np.float32(2.0 / np.pi))
    rest = angles - turns * np.float32(1.5703125)
    rest = rest - turns * np.float32(4.837512969970703125e-4)
    rest = rest - turns * np.float32(7.549789948768648e-8)
    square = rest * rest
    sine = rest + rest * square * (
        np.float32(-1.6666654611e-1)
        + square * (np.float32(8.3321608736e-3) + square * np.float32(-1.9515295891e-4))
    )
    cosine = (
        1.0
        - 0.5 * square
        + square
        * square
        * (
            np.float32(4.166664568298827e-2)
            + square
            * (np.float32(-1.388731625493765e-3) + square * np.float32(2.443315711809948e-5))
        )
    )
    quarter = turns.astype(jnp.int32) & 3
    swap = (quarter & 1) == 1
    cos_out = jnp.where(swap, sine, cosine)
    sin_out = jnp.where(swap, cosine, sine)
    cos_out = jnp.where((quarter == 1) | (quarter == 2), -cos_out, cos_out)
    sin_out = jnp.where(quarter >= 2, -sin_out, sin_out)
    return cos_out, sin_out


def rotate_heads(queries, position):
    head_dim = queries.shape[-1]
    half_dim = head_dim // 2
    frequency = (ROPE_BASE ** (-np.arange(half_dim) * 2.0 / head_dim)).astype(np.float32)
    cosine, sine = cosine_and_sine(position[:, None] * frequency[None, :])
    cosine = jnp.concatenate([cosine, cosine], axis=1)[:, None, :]
    sine = jnp.concatenate([-sine, sine], axis=1)[:, None, :]
    turned = jnp.concatenate([queries[..., half_dim:], queries[..., :half_dim]], axis=-1)
    return queries * cosine + turned * sine


def statement_ranges(lengths_row, order_row):
    stmt_count = order_row.shape[0]
    index = jnp.arange(stmt_count, dtype=jnp.int32)
    slot = jnp.sum(jnp.where(order_row[None, :] == index[:, None], index[None, :], 0), axis=1)
    start = jnp.sum(jnp.where(slot[None, :] < slot[:, None], lengths_row[None, :], 0), axis=1)
    return start, start + lengths_row


def block_attention(all_queries, cached_keys, cached_values, token_mask, score_scale):
    stmt_count, head_count, head_dim = all_queries.shape
    kv_heads = cached_keys.shape[1] // head_dim
    group_size = head_count // kv_heads
    grouped = all_queries.reshape(stmt_count, kv_heads, group_size, head_dim)
    key_heads = cached_keys.reshape(-1, kv_heads, head_dim)
    value_heads = cached_values.reshape(-1, kv_heads, head_dim)
    scores = (
        jnp.einsum("skgd,tkd->skgt", grouped, key_heads, preferred_element_type=jnp.float32)
        * score_scale
    )
    token_mask = token_mask[:, None, None, :]
    block_max = jnp.max(jnp.where(token_mask, scores, MASKED_LOGIT), axis=3)
    softmax_weights = jnp.where(token_mask, jnp.exp(scores - block_max[..., None]), 0.0)
    block_sum = jnp.sum(softmax_weights, axis=3)
    numerators = jnp.einsum(
        "skgt,tkd->skgd",
        softmax_weights.astype(jnp.bfloat16),
        value_heads,
        preferred_element_type=jnp.float32,
    )
    return (
        block_max.reshape(stmt_count, head_count),
        block_sum.reshape(stmt_count, head_count),
        numerators.reshape(stmt_count, head_count, head_dim),
    )


def local(
    hidden_in,
    attn_gain,
    w_query,
    query_gain,
    cached_keys,
    cached_values,
    w_out,
    final_gain,
    lengths,
    pack_order,
    partner,
):
    pack_size = lax.axis_size("pack")
    pack_index = lax.axis_index("pack")
    group_index = lax.axis_index("dp")
    stmt_count, feature_count = hidden_in.shape
    model_width = feature_count * pack_size
    head_dim = query_gain.shape[0]
    local_heads = w_query.shape[1] // head_dim
    token_count = cached_keys.shape[0]
    total_stmts = partner.shape[0]
    lengths_row = lengths[0]
    order_row = pack_order[0]
    inputs32 = hidden_in.astype(jnp.float32)

    scaled = (inputs32 * attn_gain[None, :]).astype(jnp.bfloat16)
    squares = split_float(jnp.sum(inputs32 * inputs32, axis=1), 3)
    extra = jnp.stack(squares + [jnp.zeros_like(squares[0])] * 125, axis=1)
    arrived = gather_blocks(jnp.concatenate([scaled, extra], axis=1), "pack")
    input_squares = jnp.sum(arrived[:, :, feature_count : feature_count + 3].astype(jnp.float32), axis=(0, 2))
    input_rms = lax.rsqrt(input_squares / model_width + EPSILON)
    features = jnp.moveaxis(arrived[:, :, :feature_count], 0, 1).reshape(stmt_count, model_width)
    projected = jnp.dot(features, w_query, preferred_element_type=jnp.float32)
    queries = (projected * input_rms[:, None]).reshape(stmt_count, local_heads, head_dim)
    queries = (
        queries
        * lax.rsqrt(jnp.mean(queries * queries, axis=2, keepdims=True) + EPSILON)
        * query_gain
    )
    queries = rotate_heads(queries, (lengths_row - 1).astype(jnp.float32)).astype(jnp.bfloat16)
    all_queries = jnp.moveaxis(gather_blocks(queries, "pack"), 0, 1).reshape(
        stmt_count, pack_size * local_heads, head_dim
    )
    start, end = statement_ranges(lengths_row, order_row)
    tokens = pack_index * token_count + jnp.arange(token_count, dtype=jnp.int32)
    token_mask = (tokens[None, :] >= start[:, None]) & (tokens[None, :] < end[:, None])
    block_max, block_sum, numerators = block_attention(
        all_queries, cached_keys, cached_values, token_mask, head_dim ** (-0.5)
    )

    def by_owner(part):
        return jnp.moveaxis(part.reshape((stmt_count, pack_size, -1)), 1, 0)

    message = jnp.concatenate(
        [by_owner(numerators.astype(jnp.bfloat16))]
        + [by_owner(piece) for piece in split_float(block_max, 3) + split_float(block_sum, 2)],
        axis=2,
    )
    message = lax.all_to_all(message, "pack", 0, 0)
    width = local_heads * head_dim
    stats = message[:, :, width:].astype(jnp.float32).reshape(pack_size, stmt_count, 5, local_heads)
    maxima = stats[:, :, 0] + stats[:, :, 1] + stats[:, :, 2]
    factor = jnp.exp(maxima - jnp.max(maxima, axis=0, keepdims=True))
    denominator = jnp.sum((stats[:, :, 3] + stats[:, :, 4]) * factor, axis=0)
    numerators = message[:, :, :width].astype(jnp.float32).reshape(pack_size, stmt_count, local_heads, head_dim)
    summed = jnp.sum(numerators * factor[..., None], axis=0)
    attended = (summed / denominator[..., None]).astype(jnp.bfloat16)
    partial_out = jnp.dot(
        attended.reshape(stmt_count, width), w_out, preferred_element_type=jnp.float32
    )
    partial_out = jnp.moveaxis(
        partial_out.astype(jnp.bfloat16).reshape(stmt_count, pack_size, feature_count), 1, 0
    )
    partial_out = lax.all_to_all(partial_out, "pack", 0, 0)
    hidden = inputs32 + jnp.sum(partial_out.astype(jnp.float32), axis=0)
    scaled_out = hidden * final_gain[None, :]
    vectors = lax.all_gather(scaled_out.astype(jnp.bfloat16), "dp", axis=0, tiled=True)
    gram = lax.dot_general(
        vectors, vectors, (((1,), (1,)), ((), ())), preferred_element_type=jnp.float32
    )
    own_squares = jnp.sum(hidden * hidden, axis=1)
    extra = jnp.zeros((total_stmts,), jnp.float32).at[:stmt_count].set(own_squares)
    gram = jnp.concatenate([gram, extra[:, None]], axis=1)
    if total_stmts <= 128:
        gram = jnp.sum(gather_blocks(gram, "pack"), axis=0)
    else:
        gram = lax.psum(gram, "pack")
    hidden_rms = jnp.sqrt(gram[:stmt_count, total_stmts] / model_width + EPSILON)
    gram = gram[:, :total_stmts]
    column_ids = jnp.arange(total_stmts, dtype=jnp.int32)
    diagonal = column_ids[:, None] == column_ids[None, :]
    norms_row = lax.rsqrt(jnp.sum(jnp.where(diagonal, gram, 0.0), axis=0))
    norms_column = lax.rsqrt(jnp.sum(jnp.where(diagonal, gram, 0.0), axis=1))
    cosines = gram * norms_column[:, None] * norms_row[None, :]
    logits = jnp.where(diagonal, MASKED_LOGIT, cosines / SOFTMAX_WARMTH)
    highest = jnp.max(logits, axis=1)
    all_lse = highest + jnp.log(jnp.sum(jnp.exp(logits - highest[:, None]), axis=1))
    is_partner = column_ids[None, :] == partner[:, None]
    all_loss = all_lse - jnp.sum(jnp.where(is_partner, logits, 0.0), axis=1)
    own_count = stmt_count // pack_size
    row_base = group_index * stmt_count
    loss_rows = lax.dynamic_slice_in_dim(all_loss, row_base + pack_index * own_count, own_count, 0)
    weights = (
        jnp.exp(logits - all_lse[:, None])
        + jnp.exp(logits - all_lse[None, :])
        - is_partner.astype(jnp.float32)
        - is_partner.T.astype(jnp.float32)
    ).astype(jnp.bfloat16)
    own_weights = lax.dynamic_slice_in_dim(weights, row_base, stmt_count, 0)
    own_cosines = lax.dynamic_slice_in_dim(cosines, row_base, stmt_count, 0)
    own_norm = lax.dynamic_slice_in_dim(norms_column, row_base, stmt_count, 0)
    inner = jnp.sum(own_weights.astype(jnp.float32) * own_cosines, axis=1)
    own_norm = own_norm[:, None]
    embeddings = (vectors.astype(jnp.float32) * norms_column[:, None]).astype(jnp.bfloat16)
    gradient = jnp.dot(own_weights, embeddings, preferred_element_type=jnp.float32)
    scale = model_width**0.5 / SOFTMAX_WARMTH
    pooled = (scaled_out / hidden_rms[:, None]).astype(jnp.bfloat16)
    grad_hidden = (
        scale * final_gain[None, :] * (gradient - scaled_out * own_norm * inner[:, None]) * own_norm
    ).astype(jnp.bfloat16)
    return (pooled, loss_rows, grad_hidden)


def solution(mesh):
    in_specs = (
        P("dp", "pack"),
        P("pack"),
        P(None, "pack"),
        P(),
        P(("dp", "pack"), None),
        P(("dp", "pack"), None),
        P("pack", None),
        P("pack"),
        P("dp", None),
        P("dp", None),
        P(),
    )
    out_specs = (P("dp", "pack"), P(("dp", "pack")), P("dp", "pack"))
    return jax.shard_map(local, mesh=mesh, in_specs=in_specs, out_specs=out_specs, check_vma=False)
```

time: 229 us -> 82 us (0.36)
  blocking collectives: 146 us -> 27.4 us
  other arithmetic: 26.8 us -> 6.91 us
  between operations: 15 us -> 1.02 us
  starting transfers between devices: 0.08 us -> 13.1 us
  waiting for transfers between devices: 27.3 us -> 20 us
    psum x5 -> x0, blocking collectives: 72.5 us -> none  [the longest x1 18.1 us: local(): input_squares = lax.psum(jnp.sum(inputs32 * inputs32, axis=1), 'pack')]
    all_gather x5 -> x1, blocking collectives: 64.4 us -> 8.24 us  [local(): lax.all_gather(scaled_out.astype(jnp.bfloat16), 'dp', axis=0, tiled=True)]
    reduce_scatter x1 -> x0, waiting for transfers between devices: 27.2 us -> none  [local(): lax.psum_scatter(partial_out.astype(jnp.bfloat16), 'pack', scatter_dimens...]
    all_to_all x0 -> x3, waiting for transfers between devices: none -> 20 us  [gather_blocks(): lax.all_to_all(jnp.broadcast_to(block[None], (size,) + block.shape), axis...]
    all_to_all x0 -> x2, blocking collectives: none -> 19.2 us  [the longest x1 9.67 us: local(): message = lax.all_to_all(message, 'pack', 0, 0)]
    all_to_all x0 -> x3, starting transfers between devices: none -> 13.1 us  [gather_blocks(): lax.all_to_all(jnp.broadcast_to(block[None], (size,) + block.shape), axis...]
    unnamed x1 -> x0, blocking collectives: 8.9 us -> none
    add x15 -> x2, other arithmetic: 8.37 us -> 0.67 us  [the longest x1 0.66 us: statement_ranges(): return (start, start + lengths_row)]
  transfers between devices with their start and end apart: 2 -> 3, of which waited for: 1 -> 3; matrix products, arithmetic and copies ran while one was open for 1% -> 4% of each run, Pallas kernels for 0% -> 0%
where the time goes in v1:
time: 82 us; the launch traced here: 81.4 us
  blocking collectives  27.4 us (33%)
  waiting for transfers between devices  20 us (24%)
  starting transfers between devices  13.1 us (16%)
  matrix products  7.4 us (9%)
  other arithmetic  6.91 us (8%)
  local copies, waits for them, and re-layouts  5.44 us (7%)
  between operations  1.02 us (1%)
    all_to_all x3, waiting for transfers between devices, gather_blocks(): lax.all_to_all(jnp.broadcast_to(block[None], (size,) + block.shape), axis...  20 us
    all_to_all x3, starting transfers between devices, gather_blocks(): lax.all_to_all(jnp.broadcast_to(block[None], (size,) + block.shape), axis...  13.1 us
    all_to_all x1, blocking collectives, local(): message = lax.all_to_all(message, 'pack', 0, 0)  9.67 us
    all_to_all x1, blocking collectives, local(): partial_out = lax.all_to_all(partial_out, 'pack', 0, 0)  9.53 us
    all_gather x1, blocking collectives, local(): lax.all_gather(scaled_out.astype(jnp.bfloat16), 'dp', axis=0, tiled=True)  8.24 us
    dot_general x1, matrix products, local(): jnp.dot(attended.reshape(stmt_count, width), w_out, preferred_element_typ...  2.85 us
    dot_general x1, matrix products, local(): projected = jnp.dot(features, w_query, preferred_element_type=jnp.float32)  2.8 us
    broadcast_in_dim x3, local copies, waits for them, and re-layouts, gather_blocks(): jnp.broadcast_to(block[None], (size,) + block.shape)  2.05 us
  transfers between devices with their start and end apart: 3, of which 3 were waited for; matrix products, arithmetic and copies ran while one was open for 4% of the time, Pallas kernels for 0%

profile of v1, /device:TPU:0, one launch (start us, length us, event | category | flops | bytes accessed | tf_op | source)
XLA Modules:
  0.0 81.4 jit_solution(12778353909013810919)
XLA Ops:
  0.7 0.9 %fusion.16 = (f32[16]{0:T(128)S(1)}, bf16[16,512]{1,0:T(8,128)(2,1)S(1)}) fusion(bf16[16,512]{1,0:T(8,128)(2,1)} %param.14, f32[512]{0:T(512)} %param.15), kind=kLoop, calls=%fused_computation.32 | loop fusion | flops 40944 | bytes 34880 | tf_op jit(solution)/shard_map/reduce_sum | solution.py:131
  1.6 0.1 copy.92
  2.0 0.1 concatenate.44
  2.1 0.7 broadcast_in_dim.61
  2.7 6.3 %all-to-all-start = ((bf16[8,16,640]{2,1,0:T(8,128)(2,1)}), bf16[8,16,640]{2,1,0:T(8,128)(2,1)S(1)}, u32[]{:S(2)}, u32[]{:S(2)}) async-start(bf16[8,16,640]{2,1,0:T(8,128)(2,1)} %broadcast_in_dim.61), calls=%async_computation | async-start | bytes 327680 | tf_op jit(solution)/shard_map/all_to_all | solution.py:15
  9.1 0.8 select_reduce_fusion.3
  9.8 0.8 %select_reduce_fusion.2 = s32[16]{0:T(128)S(1)} fusion(s32[16]{0:T(128)} %bitcast.91, s32[16]{0:T(128)S(1)} %select_reduce_fusion.3), kind=kLoop, calls=%fused_computation.116 | loop fusion | flops 752 | bytes 192 | tf_op jit(solution)/shard_map/reduce_sum | solution.py:72
  10.7 0.7 bitcast_add_fusion
  11.3 0.7 negate_select_fusion.1
  12.1 4.1 %all-to-all-done = bf16[8,16,640]{2,1,0:T(8,128)(2,1)S(1)} async-done(((bf16[8,16,640]{2,1,0:T(8,128)(2,1)}), bf16[8,16,640]{2,1,0:T(8,128)(2,1)S(1)}, u32[]{:S(2)}, u32[]{:S(2)}) %all-to-all-start) | async-done | bytes 163872 | tf_op jit(solution)/shard_map/all_to_all | solution.py:15
  16.3 0.1 convert_reduce_fusion.1
  16.4 2.8 %convolution_multiply_fusion.1 = f32[16,512]{1,0:T(8,128)S(1)} fusion(bf16[16,4096]{1,0:T(8,128)(2,1)S(1)} %bitcast.85, bf16[4096,512]{1,0:T(8,128)(2,1)} %param.16, f32[16]{0:T(128)S(1)} %add_rsqrt_fusion.1), kind=kOutput, calls=%fused_computation.8 | convolution fusion | flops 67117056 | bytes 4358208 | tf_op jit(solution)/shard_map/dot_general | solution.py:137
  19.6 0.1 fusion.19
  19.7 0.7 broadcast_in_dim.62
  20.4 3.4 %all-to-all-start.1 = ((bf16[8,16,4,128]{3,1,2,0:T(8,128)(2,1)}), bf16[8,16,4,128]{3,1,2,0:T(8,128)(2,1)S(1)}, u32[]{:S(2)}, u32[]{:S(2)}) async-start(bf16[8,16,4,128]{3,1,2,0:T(8,128)(2,1)} %broadcast_in_dim.62), calls=%async_computation.1 | async-start | bytes 262144 | tf_op jit(solution)/shard_map/all_to_all | solution.py:15
  23.8 0.1 copy.122
  23.9 0.1 copy.123
  24.1 6.4 %all-to-all-done.1 = bf16[8,16,4,128]{3,1,2,0:T(8,128)(2,1)S(1)} async-done(((bf16[8,16,4,128]{3,1,2,0:T(8,128)(2,1)}), bf16[8,16,4,128]{3,1,2,0:T(8,128)(2,1)S(1)}, u32[]{:S(2)}, u32[]{:S(2)}) %all-to-all-start.1) | async-done | bytes 131104 | tf_op jit(solution)/shard_map/all_to_all | solution.py:15
  30.5 0.4 select_reduce_fusion
  30.9 0.3 fusion.7
  31.2 0.1 copy.105
  31.4 0.1 copy.106
  31.5 0.4 fusion.1
  32.0 0.1 copy.102
  32.2 0.1 copy.103
  32.3 0.1 copy.104
  32.5 0.1 concatenate.48
  32.7 9.7 %all_to_all.25 = bf16[8,16,532]{2,1,0:T(8,128)(2,1)S(1)} all-to-all(bf16[8,16,532]{2,1,0:T(8,128)(2,1)S(1)} %copy.107), channel_id=1, replica_groups=mesh['dp'=4,'pack'=8] {'pack'}, dimensions={0} | all-to-all | bytes 272384 | tf_op jit(solution)/shard_map/all_to_all | solution.py:163
  42.3 0.1 copy.119
  42.6 0.1 copy.109
  42.7 0.2 mul.298
  42.9 0.1 mul.299
  43.2 2.9 %convolution_convert_fusion = bf16[16,4096]{1,0:T(8,128)(2,1)S(1)} fusion(bf16[512,4096]{1,0:T(8,128)(2,1)} %param.20, f32[16,512]{1,0:T(8,128)S(1)} %multiply_reduce_fusion, f32[2,8,4,128]{3,2,1,0:T(4,128)S(1)} %bitcast.89), kind=kOutput, calls=%fused_computation | convolution fusion | flops 67190784 | bytes 4390912 | tf_op jit(solution)/shard_map/dot_general | solution.py:172
  46.1 9.5 %all_to_all.26 = bf16[8,16,512]{2,1,0:T(8,128)(2,1)S(1)} all-to-all(bf16[8,16,512]{2,1,0:T(8,128)(2,1)S(1)} %bitcast.87), channel_id=1, replica_groups=mesh['dp'=4,'pack'=8] {'pack'}, dimensions={0} | all-to-all | bytes 262144 | tf_op jit(solution)/shard_map/all_to_all | solution.py:178
  55.6 0.1 multiply_convert_fusion.2
  55.8 8.2 %all_gather.3 = bf16[64,512]{1,0:T(8,128)(2,1)S(1)} all-gather(bf16[16,512]{1,0:T(8,128)(2,1)S(1)} %get-tuple-element.27), channel_id=1, replica_groups=mesh['dp'=4,'pack'=8] {'dp'}, dimensions={0}, use_global_device_ids=true | all-gather | bytes 81920 | tf_op jit(solution)/shard_map/all_gather | solution.py:181
  64.0 0.1 fusion.67
  64.3 0.7 broadcast_in_dim.66
  65.0 3.4 %all-to-all-start.4 = ((f32[8,64,65]{2,1,0:T(8,128)}), f32[8,64,65]{2,1,0:T(8,128)S(1)}, u32[]{:S(2)}, u32[]{:S(2)}) async-start(f32[8,64,65]{2,1,0:T(8,128)} %broadcast_in_dim.66), calls=%async_computation.4 | async-start | bytes 524288 | tf_op jit(solution)/shard_map/all_to_all | solution.py:15
  68.6 9.6 %all-to-all-done.4 = f32[8,64,65]{2,1,0:T(8,128)S(1)} async-done(((f32[8,64,65]{2,1,0:T(8,128)}), f32[8,64,65]{2,1,0:T(8,128)S(1)}, u32[]{:S(2)}, u32[]{:S(2)}) %all-to-all-start.4) | async-done | bytes 133152 | tf_op jit(solution)/shard_map/all_to_all | solution.py:15
  78.1 0.1 fusion.22
  78.3 0.2 fusion.56
  78.5 0.2 select_reduce_fusion.1
  78.7 0.2 exponential_reduce_fusion
  79.1 0.7 divide_convert_fusion
  79.8 0.6 dynamic_slice.12
  80.4 0.2 multiply_reduce_fusion.3
  80.5 0.8 %fusion.4 = bf16[16,512]{1,0:T(8,128)(2,1)} fusion(bf16[16,64]{1,0:T(8,128)(2,1)S(1)} %get-tuple-element.20, bf16[64,512]{1,0:T(8,128)(2,1)S(1)} %all_gather.3, f32[64]{0:T(128)S(1)} %rsqrt.31, f32[16]{0:T(128)S(1)} %get-tuple-element.19, f32[16]{0:T(128)S(1)} %dynamic_slice.14, f32[512]{0:T(512)S(1)} %broadcast_multiply_fusion, f32[512]{0:T(512)S(1)} %copy-done.3, ...), kind=kOutput, calls=%fused_computation.9 | convolution fusion | flops 1220608 | bytes 137600 | tf_op jit(solution)/shard_map/dot_general | solution.py:219
  (57 shorter events, 1.7 us)
Async XLA Ops:
  0.6 18.8 %copy-start.5 = (f32[128]{0:T(128)S(1)}, f32[128]{0:T(128)}, u32[]{:S(2)}) copy-start(f32[128]{0:T(128)} %param.17) | copy-start | bytes 1540
  0.6 23.1 %copy-start = (bf16[320,1024]{1,0:T(8,128)(2,1)S(1)}, bf16[320,1024]{1,0:T(8,128)(2,1)}, u32[]{:S(2)}) copy-start(bf16[320,1024]{1,0:T(8,128)(2,1)} %param.18) | copy-start | bytes 1966084
  0.7 23.2 %copy-start.1 = (bf16[320,1024]{1,0:T(8,128)(2,1)S(1)}, bf16[320,1024]{1,0:T(8,128)(2,1)}, u32[]{:S(2)}) copy-start(bf16[320,1024]{1,0:T(8,128)(2,1)} %param.19) | copy-start | bytes 1966084
  2.7 13.5 %all-to-all-start = ((bf16[8,16,640]{2,1,0:T(8,128)(2,1)}), bf16[8,16,640]{2,1,0:T(8,128)(2,1)S(1)}, u32[]{:S(2)}, u32[]{:S(2)}) async-start(bf16[8,16,640]{2,1,0:T(8,128)(2,1)} %broadcast_in_dim.61), calls=%async_computation | async-start | bytes 327680 | tf_op jit(solution)/shard_map/all_to_all | solution.py:15
  20.4 10.1 %all-to-all-start.1 = ((bf16[8,16,4,128]{3,1,2,0:T(8,128)(2,1)}), bf16[8,16,4,128]{3,1,2,0:T(8,128)(2,1)S(1)}, u32[]{:S(2)}, u32[]{:S(2)}) async-start(bf16[8,16,4,128]{3,1,2,0:T(8,128)(2,1)} %broadcast_in_dim.62), calls=%async_computation.1 | async-start | bytes 262144 | tf_op jit(solution)/shard_map/all_to_all | solution.py:15
  31.9 23.7 %copy-start.2 = (bf16[16,512]{1,0:T(8,128)(2,1)S(1)}, bf16[16,512]{1,0:T(8,128)(2,1)}, u32[]{:S(2)}) copy-start(bf16[16,512]{1,0:T(8,128)(2,1)} %param.14) | copy-start | bytes 49156
  31.9 23.7 %copy-start.3 = (f32[512]{0:T(512)S(1)}, f32[512]{0:T(512)}, u32[]{:S(2)}) copy-start(f32[512]{0:T(512)} %param.21) | copy-start | bytes 6148
  32.6 35.8 %copy-start.4 = (s32[64]{0:T(128)S(1)}, s32[64]{0:T(128)}, u32[]{:S(2)}) copy-start(s32[64]{0:T(128)} %param.24) | copy-start | bytes 772
  65.0 13.1 %all-to-all-start.4 = ((f32[8,64,65]{2,1,0:T(8,128)}), f32[8,64,65]{2,1,0:T(8,128)S(1)}, u32[]{:S(2)}, u32[]{:S(2)}) async-start(f32[8,64,65]{2,1,0:T(8,128)} %broadcast_in_dim.66), calls=%async_computation.4 | async-start | bytes 524288 | tf_op jit(solution)/shard_map/all_to_all | solution.py:15

commit v2 on v1

--- a/solution.py
+++ b/solution.py
@@ -2,6 +2,8 @@
 import jax
 import jax.numpy as jnp
 from jax import lax
+from jax.experimental import pallas as pl
+from jax.experimental.pallas import tpu as pltpu
 from jax.sharding import PartitionSpec as P
 
 EPSILON = 1e-06
@@ -99,6 +101,522 @@
         block_sum.reshape(stmt_count, head_count),
         numerators.reshape(stmt_count, head_count, head_dim),
     )
+
+
+def flip(array, axis, offset):
+    size = lax.axis_size(axis)
+    return lax.ppermute(array, axis, [(i, i ^ offset) for i in range(size)])
+
+
+def in_vmem(body, outputs, *operands, limit=8, flops=1_000_000):
+    whole = pl.BlockSpec(memory_space=pltpu.VMEM)
+    moved = sum(operand.size * operand.dtype.itemsize for operand in operands)
+    return pl.pallas_call(
+        body,
+        out_shape=outputs,
+        in_specs=[whole] * len(operands),
+        out_specs=jax.tree.map(lambda _: whole, outputs),
+        compiler_params=pltpu.CompilerParams(vmem_limit_bytes=limit << 20),
+        cost_estimate=pl.CostEstimate(flops=flops, bytes_accessed=moved, transcendentals=0),
+    )(*operands)
+
+
+def shaped(shape, kind):
+    return jax.ShapeDtypeStruct(shape, kind)
+
+
+def lane_pieces(values, width=128):
+    rows = values[0].shape[0]
+    lane = lax.broadcasted_iota(jnp.int32, (rows, width), 1)
+    out = jnp.zeros((rows, width), jnp.float32)
+    for place, value in enumerate(values):
+        rest = value
+        for part in range(3):
+            piece = rest.astype(jnp.bfloat16).astype(jnp.float32)
+            out = jnp.where(lane == 3 * place + part, piece, out)
+            rest = rest - piece
+    return out.astype(jnp.bfloat16)
+
+
+def lane_sum(block, place):
+    lane = lax.broadcasted_iota(jnp.int32, block.shape, 1)
+    own = (lane >= 3 * place) & (lane < 3 * place + 3)
+    return jnp.sum(jnp.where(own, block, 0.0), axis=1, keepdims=True)
+
+
+def prepare_inputs(hidden_ref, gain_ref, message_ref):
+    inputs = hidden_ref[...].astype(jnp.float32)
+    width = inputs.shape[1]
+    message_ref[:, :width] = (inputs * gain_ref[...]).astype(jnp.bfloat16)
+    message_ref[:, width:] = lane_pieces([jnp.sum(inputs * inputs, axis=1, keepdims=True)])
+
+
+def positions_and_ranges(frequency_ref, lengths_ref, order_ref, rope_ref, range_ref):
+    count = lengths_ref.shape[1]
+    half = frequency_ref.shape[1] // 2
+    row = lax.broadcasted_iota(jnp.int32, (count, count), 0)
+    column = lax.broadcasted_iota(jnp.int32, (count, count), 1)
+    lengths = jnp.broadcast_to(lengths_ref[...], (count, count)).astype(jnp.float32)
+    length = jnp.sum(jnp.where(row == column, lengths, 0.0), axis=1, keepdims=True)
+    order = jnp.broadcast_to(order_ref[...], (count, count))
+    placed = order == row
+    slot = jnp.sum(jnp.where(placed, column, 0).astype(jnp.float32), axis=1, keepdims=True)
+    packed = jnp.sum(jnp.where(placed, length, 0.0), axis=0, keepdims=True)
+    earlier = column.astype(jnp.float32) < slot
+    start = jnp.sum(jnp.where(earlier, packed, 0.0), axis=1, keepdims=True)
+    range_ref[:, :128] = jnp.broadcast_to(start, (count, 128))
+    range_ref[:, 128:] = jnp.broadcast_to(start + length, (count, 128))
+    cosine, sine = cosine_and_sine((length - 1.0) * frequency_ref[...])
+    lane = lax.broadcasted_iota(jnp.int32, cosine.shape, 1)
+    rope_ref[:, : 2 * half] = cosine
+    rope_ref[:, 2 * half :] = jnp.where(lane < half, -sine, sine)
+
+
+def send_heads(key_ref, value_ref, out_ref, semaphore):
+    me = lax.axis_index("pack")
+    heads = out_ref.shape[1] // 256
+    copies = []
+    for i in range(heads):
+        column = pl.multiple_of((me ^ 1 ^ (2 * i)) * 128, 128)
+        for place, source in enumerate((key_ref, value_ref)):
+            copies.append(
+                pltpu.make_async_copy(
+                    source.at[:, pl.ds(column, 128)],
+                    out_ref.at[:, pl.ds((place * heads + i) * 128, 128)],
+                    semaphore.at[place * heads + i],
+                )
+            )
+    for copy in copies:
+        copy.start()
+    for copy in copies:
+        copy.wait()
+
+
+def project_blocks(offsets, blocks, weight_ref, width):
+    me = lax.axis_index("pack")
+    total = None
+    for offset, block in zip(offsets, blocks):
+        rows = pl.ds(pl.multiple_of((me ^ offset) * width, width), width)
+        part = jnp.dot(
+            block[:, :width].astype(jnp.bfloat16),
+            weight_ref[rows, :],
+            preferred_element_type=jnp.float32,
+        )
+        total = part if total is None else total + part
+    return total
+
+
+def join_blocks(*refs):
+    out_ref = refs[-1]
+    for i, ref in enumerate(refs[:-1]):
+        out_ref[i] = ref[...]
+
+
+def first_half(blocks_ref, weight_ref, total_ref):
+    width = weight_ref.shape[1]
+    blocks = [blocks_ref[i] for i in range(blocks_ref.shape[0])]
+    total_ref[...] = project_blocks((0, 2, 4, 6), blocks, weight_ref, width)
+
+
+def second_half(
+    own_ref, other_ref, total_ref, weight_ref, gain_ref, rope_ref, query_ref, *, model_width
+):
+    width = weight_ref.shape[1]
+    count = own_ref.shape[0]
+    blocks = [other_ref[i] for i in range(count)]
+    projected = total_ref[...] + project_blocks((1, 3, 5, 7), blocks, weight_ref, width)
+    squares = sum(
+        lane_sum(ref[i, :, width:].astype(jnp.float32), 0)
+        for ref in (own_ref, other_ref)
+        for i in range(count)
+    )
+    projected = projected * lax.rsqrt(squares / model_width + EPSILON)
+    head_dim = gain_ref.shape[1]
+    cosine = rope_ref[:, :head_dim]
+    sine = rope_ref[:, head_dim:]
+    for head in range(width // head_dim):
+        place = slice(head * head_dim, (head + 1) * head_dim)
+        query = projected[:, place]
+        mean = jnp.mean(query * query, axis=1, keepdims=True)
+        query = query * lax.rsqrt(mean + EPSILON) * gain_ref[...]
+        turned = pltpu.roll(query, head_dim // 2, 1)
+        query_ref[:, place] = (query * cosine + turned * sine).astype(jnp.bfloat16)
+
+
+def attend_head(i, query, key_ref, value_ref, swapped_ref, range_ref):
+    me = lax.axis_index("pack")
+    tokens = key_ref.shape[0]
+    head_dim = 128
+    heads = swapped_ref.shape[1] // (2 * head_dim)
+    grouped = jnp.concatenate(
+        [query[:, h * head_dim : (h + 1) * head_dim] for h in range(query.shape[1] // head_dim)],
+        axis=0,
+    )
+    group = query.shape[1] // head_dim
+    column = pl.ds(pl.multiple_of((me ^ (2 * i)) * head_dim, head_dim), head_dim)
+    keys = (key_ref[:, column], swapped_ref[:, i * head_dim : (i + 1) * head_dim])
+    values = (
+        value_ref[:, column],
+        swapped_ref[:, (heads + i) * head_dim : (heads + i + 1) * head_dim],
+    )
+    scores = []
+    masks = []
+    for part, owner in enumerate((me, me ^ 1)):
+        index = lax.broadcasted_iota(jnp.int32, (query.shape[0], tokens), 1) + owner * tokens
+        index = index.astype(jnp.float32)
+        mask = (index >= range_ref[:, :1]) & (index < range_ref[:, 128:129])
+        mask = jnp.concatenate([mask.astype(jnp.float32)] * group, axis=0) > 0.5
+        raw = lax.dot_general(
+            grouped, keys[part], (((1,), (1,)), ((), ())), preferred_element_type=jnp.float32
+        )
+        scores.append(jnp.where(mask, raw * (head_dim**-0.5), MASKED_LOGIT))
+        masks.append(mask)
+    highest = jnp.maximum(
+        jnp.max(scores[0], axis=1, keepdims=True), jnp.max(scores[1], axis=1, keepdims=True)
+    )
+    total = 0.0
+    numerators = 0.0
+    for part in range(2):
+        weights = jnp.where(masks[part], jnp.exp(scores[part] - highest), 0.0)
+        total = total + jnp.sum(weights, axis=1, keepdims=True)
+        numerators = numerators + jnp.dot(
+            weights.astype(jnp.bfloat16), values[part], preferred_element_type=jnp.float32
+        )
+    return highest, total, numerators
+
+
+def attend_others(*refs):
+    query_refs, refs = refs[:3], refs[3:]
+    key_ref, value_ref, swapped_ref, range_ref = refs[:4]
+    rows = query_refs[0].shape[0]
+    for i, (query_ref, out_ref) in enumerate(zip(query_refs, refs[4:])):
+        highest, total, numerators = attend_head(
+            i + 1, query_ref[...], key_ref, value_ref, swapped_ref, range_ref
+        )
+        stats = []
+        for h in range(query_ref.shape[1] // 128):
+            part = slice(h * rows, (h + 1) * rows)
+            out_ref[:, h * 128 : (h + 1) * 128] = numerators[part].astype(jnp.bfloat16)
+            stats += [highest[part], total[part]]
+        out_ref[:, query_ref.shape[1] :] = lane_pieces(stats)
+
+
+def attend_own(query_ref, key_ref, value_ref, swapped_ref, range_ref, out_ref, stats_ref):
+    highest, total, numerators = attend_head(
+        0, query_ref[...], key_ref, value_ref, swapped_ref, range_ref
+    )
+    out_ref[...] = numerators
+    stats_ref[:, :128] = jnp.broadcast_to(highest, (highest.shape[0], 128))
+    stats_ref[:, 128:] = jnp.broadcast_to(total, (highest.shape[0], 128))
+
+
+def join_and_project(
+    own_ref, stats_ref, first_ref, second_ref, third_ref, weight_ref, attended_ref, out_ref
+):
+    me = lax.axis_index("pack")
+    rows, width = attended_ref.shape
+    others = (first_ref, second_ref, third_ref)
+    for h in range(width // 128):
+        part = slice(h * rows, (h + 1) * rows)
+        place = slice(h * 128, (h + 1) * 128)
+        maxima = [stats_ref[part, :1]]
+        totals = [stats_ref[part, 128:129]]
+        numerators = [own_ref[part, :]]
+        for ref in others:
+            stats = ref[:, width:].astype(jnp.float32)
+            maxima.append(lane_sum(stats, 2 * h))
+            totals.append(lane_sum(stats, 2 * h + 1))
+            numerators.append(ref[:, place].astype(jnp.float32))
+        highest = maxima[0]
+        for value in maxima[1:]:
+            highest = jnp.maximum(highest, value)
+        denominator = 0.0
+        summed = 0.0
+        for value, total, numerator in zip(maxima, totals, numerators):
+            factor = jnp.exp(value - highest)
+            denominator = denominator + total * factor
+            summed = summed + numerator * factor
+        attended_ref[:, place] = (summed / denominator).astype(jnp.bfloat16)
+    attended = attended_ref[...]
+    for i in range(out_ref.shape[0]):
+        column = pl.ds(pl.multiple_of((me ^ 1 ^ (2 * i)) * width, width), width)
+        out_ref[i] = jnp.dot(
+            attended, weight_ref[:, column], preferred_element_type=jnp.float32
+        ).astype(jnp.bfloat16)
+
+
+def project_own(attended_ref, weight_ref, out_ref):
+    me = lax.axis_index("pack")
+    width = attended_ref.shape[1]
+    attended = attended_ref[...]
+    for i in range(out_ref.shape[0]):
+        column = pl.ds(pl.multiple_of((me ^ (2 * i)) * width, width), width)
+        out_ref[i] = jnp.dot(attended, weight_ref[:, column], preferred_element_type=jnp.float32)
+
+
+def add_cores(own_ref, other_ref, hidden_ref, kept_ref, *sent_refs):
+    kept_ref[...] = (
+        hidden_ref[...].astype(jnp.float32) + own_ref[0] + other_ref[0].astype(jnp.float32)
+    )
+    for i, ref in enumerate(sent_refs):
+        ref[...] = (own_ref[i + 1] + other_ref[i + 1].astype(jnp.float32)).astype(jnp.bfloat16)
+
+
+def finish_hidden(kept_ref, first_ref, second_ref, third_ref, gain_ref, sent_ref, scaled_ref, square_ref):
+    hidden = kept_ref[...]
+    for ref in (first_ref, second_ref, third_ref):
+        hidden = hidden + ref[...].astype(jnp.float32)
+    scaled = hidden * gain_ref[...]
+    scaled_ref[...] = scaled
+    sent_ref[...] = scaled.astype(jnp.bfloat16)
+    square_ref[...] = jnp.broadcast_to(
+        jnp.sum(hidden * hidden, axis=1, keepdims=True), square_ref.shape
+    )
+
+
+def gram_part(first_ref, second_ref, third_ref, fourth_ref, square_ref, vectors_ref, out_ref):
+    rows = first_ref.shape[0]
+    for i, ref in enumerate((first_ref, second_ref, third_ref, fourth_ref)):
+        vectors_ref[i * rows : (i + 1) * rows, :] = ref[...]
+    vectors = vectors_ref[...]
+    gram = lax.dot_general(
+        vectors, vectors, (((1,), (1,)), ((), ())), preferred_element_type=jnp.float32
+    )
+    half = gram.shape[0] // 2
+    out_ref[:half, : 2 * half] = gram[:half]
+    out_ref[:half, 2 * half :] = gram[half:]
+    out_ref[half:, :] = square_ref[...]
+
+
+def add_two(first_ref, second_ref, out_ref):
+    out_ref[...] = first_ref[...] + second_ref[...]
+
+
+def losses_and_gradient(
+    a_ref,
+    b_ref,
+    c_ref,
+    d_ref,
+    vectors_ref,
+    scaled_ref,
+    gain_ref,
+    partner_ref,
+    pooled_ref,
+    loss_ref,
+    grad_ref,
+    *,
+    model_width,
+):
+    group = lax.axis_index("dp")
+    me = lax.axis_index("pack")
+    count = vectors_ref.shape[0]
+    rows = scaled_ref.shape[0]
+    half = count // 2
+    summed = a_ref[...] + b_ref[...] + c_ref[...] + d_ref[...]
+    gram = jnp.concatenate([summed[:half, :count], summed[:half, count:]], axis=0)
+    squares = summed[half:, :1]
+    shape = (count, count)
+    row = lax.broadcasted_iota(jnp.int32, shape, 0)
+    column = lax.broadcasted_iota(jnp.int32, shape, 1)
+    row_id = ((group ^ (row // rows)) * rows) + row % rows
+    column_id = ((group ^ (column // rows)) * rows) + column % rows
+    partners = jnp.broadcast_to(partner_ref[...], shape)
+    row_partner = jnp.sum(
+        jnp.where(column == row_id, partners, 0).astype(jnp.float32), axis=1, keepdims=True
+    )
+    column_partner = jnp.sum(
+        jnp.where(row_id == column_id, row_partner, 0.0), axis=0, keepdims=True
+    )
+    own_partner = column_id.astype(jnp.float32) == row_partner
+    other_partner = row_id.astype(jnp.float32) == column_partner
+    diagonal = row == column
+    on_diagonal = jnp.where(diagonal, gram, 0.0)
+    row_scale = lax.rsqrt(jnp.sum(on_diagonal, axis=1, keepdims=True))
+    column_scale = lax.rsqrt(jnp.sum(on_diagonal, axis=0, keepdims=True))
+    cosines = gram * row_scale * column_scale
+    scaled_cosines = cosines * (1.0 / SOFTMAX_WARMTH)
+    logits = jnp.where(diagonal, MASKED_LOGIT, scaled_cosines)
+    row_high = jnp.max(logits, axis=1, keepdims=True)
+    row_lse = row_high + jnp.log(jnp.sum(jnp.exp(logits - row_high), axis=1, keepdims=True))
+    column_high = jnp.max(logits, axis=0, keepdims=True)
+    column_lse = column_high + jnp.log(
+        jnp.sum(jnp.exp(logits - column_high), axis=0, keepdims=True)
+    )
+    loss = row_lse - jnp.sum(jnp.where(own_partner, logits, 0.0), axis=1, keepdims=True)
+    own = loss_ref.shape[0]
+    index = lax.broadcasted_iota(jnp.int32, (count, 1), 0)
+    for i in range(own):
+        loss_ref[i] = jnp.sum(jnp.where(index == me * own + i, loss, 0.0))
+    weights = (
+        jnp.exp(logits - row_lse)
+        + jnp.exp(logits - column_lse)
+        - own_partner.astype(jnp.float32)
+        - other_partner.astype(jnp.float32)
+    )[:rows]
+    inner = jnp.sum(weights * cosines[:rows], axis=1, keepdims=True)
+    scaled_weights = weights * column_scale
+    upper = scaled_weights.astype(jnp.bfloat16)
+    lower = (scaled_weights - upper.astype(jnp.float32)).astype(jnp.bfloat16)
+    vectors = vectors_ref[...]
+    gradient = jnp.dot(upper, vectors, preferred_element_type=jnp.float32) + jnp.dot(
+        lower, vectors, preferred_element_type=jnp.float32
+    )
+    own_scale = row_scale[:rows]
+    scaled = scaled_ref[...]
+    gradient = (gradient - scaled * (own_scale * inner)) * own_scale
+    grad_ref[...] = (gradient * (gain_ref[...] * (model_width**0.5 / SOFTMAX_WARMTH))).astype(
+        jnp.bfloat16
+    )
+    pooled_ref[...] = (scaled * lax.rsqrt(squares / model_width + EPSILON)).astype(jnp.bfloat16)
+
+
+def chip_pairs(
+    hidden_in,
+    attn_gain,
+    w_query,
+    query_gain,
+    cached_keys,
+    cached_values,
+    w_out,
+    final_gain,
+    lengths,
+    pack_order,
+    partner,
+):
+    pack_size = lax.axis_size("pack")
+    stmts, width = hidden_in.shape
+    model_width = width * pack_size
+    head_dim = query_gain.shape[0]
+    tokens = cached_keys.shape[0]
+    chips = pack_size // 2
+    total = partner.shape[0]
+    bf16 = jnp.bfloat16
+    f32 = jnp.float32
+    attn_gain = attn_gain[None]
+    final_gain = final_gain[None]
+    query_gain = query_gain[None]
+    half = np.arange(head_dim // 2)
+    frequency = (ROPE_BASE ** (-half * 2.0 / head_dim)).astype(np.float32)
+    frequency = jnp.asarray(np.concatenate([frequency, frequency])[None])
+
+    message = in_vmem(
+        prepare_inputs, shaped((stmts, width + 128), bf16), hidden_in, attn_gain
+    )
+    blocks = [message] + [flip(message, "pack", 2 * i) for i in range(1, chips)]
+    blocks = in_vmem(join_blocks, shaped((chips,) + message.shape, bf16), *blocks)
+    others = flip(blocks, "pack", 1)
+    rope, ranges = in_vmem(
+        positions_and_ranges,
+        (shaped((stmts, 2 * head_dim), f32), shaped((stmts, 256), f32)),
+        frequency,
+        lengths,
+        pack_order,
+    )
+    anywhere = pl.BlockSpec(memory_space=pl.ANY)
+    swapped = pl.pallas_call(
+        send_heads,
+        out_shape=shaped((tokens, 2 * chips * head_dim), bf16),
+        in_specs=[anywhere] * 2,
+        out_specs=anywhere,
+        scratch_shapes=[pltpu.SemaphoreType.DMA((2 * chips,))],
+        compiler_params=pltpu.CompilerParams(vmem_limit_bytes=4 << 20),
+        cost_estimate=pl.CostEstimate(flops=0, bytes_accessed=2 << 20, transcendentals=0),
+    )(cached_keys, cached_values)
+    swapped = flip(swapped, "pack", 1)
+    projected = in_vmem(
+        first_half, shaped((stmts, width), f32), blocks, w_query, limit=16, flops=1 << 27
+    )
+    queries = in_vmem(
+        lambda *refs: second_half(*refs, model_width=model_width),
+        shaped((stmts, width), bf16),
+        blocks,
+        others,
+        projected,
+        w_query,
+        query_gain,
+        rope,
+        limit=16,
+        flops=1 << 27,
+    )
+    received = [flip(queries, "pack", 2 * i) for i in range(1, chips)]
+    sent = in_vmem(
+        attend_others,
+        (shaped((stmts, width + 128), bf16),) * (chips - 1),
+        *received,
+        cached_keys,
+        cached_values,
+        swapped,
+        ranges,
+        flops=1 << 27,
+    )
+    partials = [flip(part, "pack", 2 * (i + 1)) for i, part in enumerate(sent)]
+    group_rows = stmts * (width // head_dim)
+    own_part, own_stats = in_vmem(
+        attend_own,
+        (shaped((group_rows, head_dim), f32), shaped((group_rows, 256), f32)),
+        queries,
+        cached_keys,
+        cached_values,
+        swapped,
+        ranges,
+        flops=1 << 26,
+    )
+    attended, to_core = in_vmem(
+        join_and_project,
+        (shaped((stmts, width), bf16), shaped((chips, stmts, width), bf16)),
+        own_part,
+        own_stats,
+        *partials,
+        w_out,
+        limit=16,
+        flops=1 << 27,
+    )
+    from_core = flip(to_core, "pack", 1)
+    own_out = in_vmem(
+        project_own,
+        shaped((chips, stmts, width), f32),
+        attended,
+        w_out,
+        limit=16,
+        flops=1 << 27,
+    )
+    kept, *to_chips = in_vmem(
+        add_cores,
+        (shaped((stmts, width), f32),) + (shaped((stmts, width), bf16),) * (chips - 1),
+        own_out,
+        from_core,
+        hidden_in,
+    )
+    from_chips = [flip(part, "pack", 2 * (i + 1)) for i, part in enumerate(to_chips)]
+    vector, scaled, squares = in_vmem(
+        finish_hidden,
+        (shaped((stmts, width), bf16), shaped((stmts, width), f32), shaped((stmts, 128), f32)),
+        kept,
+        *from_chips,
+        final_gain,
+    )
+    vectors = [vector] + [flip(vector, "dp", i) for i in range(1, lax.axis_size("dp"))]
+    vectors, gram = in_vmem(
+        gram_part,
+        (shaped((total, width), bf16), shaped((total // 2 + stmts, 128), f32)),
+        *vectors,
+        squares,
+    )
+    gram = in_vmem(add_two, shaped(gram.shape, f32), gram, flip(gram, "pack", 1))
+    grams = [gram] + [flip(gram, "pack", 2 * i) for i in range(1, chips)]
+    whole = pl.BlockSpec(memory_space=pltpu.VMEM)
+    pooled, loss_rows, grad_hidden = pl.pallas_call(
+        lambda *refs: losses_and_gradient(*refs, model_width=model_width),
+        out_shape=(
+            shaped((stmts, width), bf16),
+            shaped((stmts // pack_size,), f32),
+            shaped((stmts, width), bf16),
+        ),
+        in_specs=[whole] * 8,
+        out_specs=(whole, pl.BlockSpec(memory_space=pltpu.SMEM), whole),
+        compiler_params=pltpu.CompilerParams(vmem_limit_bytes=8 << 20),
+    )(*grams, vectors, scaled, final_gain, partner[None])
+    return (pooled, loss_rows, grad_hidden)
 
 
 def local(
@@ -226,6 +744,7 @@
 
 
 def solution(mesh):
+    body = chip_pairs if mesh.shape["pack"] == 8 and mesh.shape["dp"] == 4 else local
     in_specs = (
         P("dp", "pack"),
         P("pack"),
@@ -240,4 +759,4 @@
         P(),
     )
     out_specs = (P("dp", "pack"), P(("dp", "pack")), P("dp", "pack"))
-    return jax.shard_map(local, mesh=mesh, in_specs=in_specs, out_specs=out_specs, check_vma=False)
+    return jax.shard_map(body, mesh=mesh, in_specs=in_specs, out_specs=out_specs, check_vma=False)

time: 82 us -> 67.2 us (0.82)
  blocking collectives: 27.4 us -> 0 us
  starting transfers between devices: 13.1 us -> 27 us
  matrix products: 7.4 us -> 0 us
  other arithmetic: 6.91 us -> 0 us
  waiting for transfers between devices: 20 us -> 26 us
  Pallas kernels: 0 us -> 5.35 us
  local copies, waits for them, and re-layouts: 5.44 us -> 7.75 us
    ppermute x0 -> x22, starting transfers between devices: none -> 27 us  [flip(): return lax.ppermute(array, axis, [(i, i ^ offset) for i in range(size)])]
    ppermute x0 -> x22, waiting for transfers between devices: none -> 26 us  [flip(): return lax.ppermute(array, axis, [(i, i ^ offset) for i in range(size)])]
    all_to_all x3 -> x0, waiting for transfers between devices: 20 us -> none  [gather_blocks(): lax.all_to_all(jnp.broadcast_to(block[None], (size,) + block.shape), axis...]
    all_to_all x2 -> x0, blocking collectives: 19.2 us -> none  [the longest x1 9.67 us: local(): message = lax.all_to_all(message, 'pack', 0, 0)]
    all_to_all x3 -> x0, starting transfers between devices: 13.1 us -> none  [gather_blocks(): lax.all_to_all(jnp.broadcast_to(block[None], (size,) + block.shape), axis...]
    all_gather x1 -> x0, blocking collectives: 8.24 us -> none  [local(): lax.all_gather(scaled_out.astype(jnp.bfloat16), 'dp', axis=0, tiled=True)]
    dot_general x6 -> x0, matrix products: 7.4 us -> none  [the longest x1 2.85 us: local(): jnp.dot(attended.reshape(stmt_count, width), w_out, preferred_element_typ...]
    unnamed x16 -> x30, local copies, waits for them, and re-layouts: 0.41 us -> 7.75 us
  transfers between devices with their start and end apart: 3 -> 22, of which waited for: 3 -> 15; matrix products, arithmetic and copies ran while one was open for 4% -> 0% of each run, Pallas kernels for 0% -> 3%
where the time goes in v2:
time: 67.2 us; the launch traced here: 66.9 us
  starting transfers between devices  27 us (40%)
  waiting for transfers between devices  26 us (39%)
  local copies, waits for them, and re-layouts  7.75 us (12%)
  Pallas kernels  5.35 us (8%)
  between operations  0.77 us (1%)
    ppermute x22, starting transfers between devices, flip(): return lax.ppermute(array, axis, [(i, i ^ offset) for i in range(size)])  27 us
    ppermute x22, waiting for transfers between devices, flip(): return lax.ppermute(array, axis, [(i, i ^ offset) for i in range(size)])  26 us
    unnamed x30, local copies, waits for them, and re-layouts  7.75 us
    pallas_call x13, Pallas kernels, in_vmem(): pl.pallas_call(body, out_shape=outputs, in_specs=[whole] * len(operands),...  3.98 us
  transfers between devices with their start and end apart: 22, of which 15 were waited for; matrix products, arithmetic and copies ran while one was open for 0% of the time, Pallas kernels for 3%

profile of v2, /device:TPU:0, one launch (start us, length us, event | category | flops | bytes accessed | tf_op | source)
XLA Modules:
  0.0 66.9 jit_solution(3374082848956266382)
XLA Ops:
  0.6 1.1 %copy-done.2 = bf16[320,1024]{1,0:T(8,128)(2,1)S(1)} copy-done((bf16[320,1024]{1,0:T(8,128)(2,1)S(1)}, bf16[320,1024]{1,0:T(8,128)(2,1)}, u32[]{:S(2)}) %copy-start.2) | copy-done | bytes 655384
  1.7 1.1 %copy-done.4 = bf16[320,1024]{1,0:T(8,128)(2,1)S(1)} copy-done((bf16[320,1024]{1,0:T(8,128)(2,1)S(1)}, bf16[320,1024]{1,0:T(8,128)(2,1)}, u32[]{:S(2)}) %copy-start.4) | copy-done | bytes 655384
  2.8 0.3 shard_map.144
  3.1 0.5 collective-permute-start.4
  3.6 0.7 %copy-done.6 = bf16[16,512]{1,0:T(8,128)(2,1)S(1)} copy-done((bf16[16,512]{1,0:T(8,128)(2,1)S(1)}, bf16[16,512]{1,0:T(8,128)(2,1)}, u32[]{:S(2)}) %copy-start.6) | copy-done | bytes 16408
  4.3 0.7 %copy-done.9 = f32[512]{0:T(512)S(1)} copy-done((f32[512]{0:T(512)S(1)}, f32[512]{0:T(512)}, u32[]{:S(2)}) %copy-start.9) | copy-done | bytes 2072
  5.1 2.6 %collective-permute-start = (bf16[16,640]{1,0:T(8,128)(2,1)S(1)}, bf16[16,640]{1,0:T(8,128)(2,1)S(1)}, u32[]{:S(2)}, u32[]{:S(2)}) collective-permute-start(bf16[16,640]{1,0:T(8,128)(2,1)S(1)} %shard_map.139.refs_0_), channel_id=1, source_target_pairs={{0,2},{1,3},{2,0},{3,1},{4,6},{5,7},{6,4},{7,5},{8,10},{9,11},{10,... | collective-permute-start | bytes 61448 | tf_op jit(solution)/shard_map/ppermute | solution.py:108
  7.7 2.6 %collective-permute-start.1 = (bf16[16,640]{1,0:T(8,128)(2,1)S(1)}, bf16[16,640]{1,0:T(8,128)(2,1)S(1)}, u32[]{:S(2)}, u32[]{:S(2)}) collective-permute-start(bf16[16,640]{1,0:T(8,128)(2,1)S(1)} %shard_map.139.refs_0_), channel_id=1, source_target_pairs={{0,4},{1,5},{2,6},{3,7},{4,0},{5,1},{6,2},{7,3},{8,12},{9,13},{10,... | collective-permute-start | bytes 61448 | tf_op jit(solution)/shard_map/ppermute | solution.py:108
  10.3 2.1 %collective-permute-done.1.refs_2_ = bf16[16,640]{1,0:T(8,128)(2,1)S(1)} collective-permute-done((bf16[16,640]{1,0:T(8,128)(2,1)S(1)}, bf16[16,640]{1,0:T(8,128)(2,1)S(1)}, u32[]{:S(2)}, u32[]{:S(2)}) %collective-permute-start.1) | collective-permute-done | bytes 20512 | tf_op jit(solution)/shard_map/ppermute | solution.py:108
  12.4 3.5 %collective-permute-done.2.refs_3_ = bf16[16,640]{1,0:T(8,128)(2,1)S(1)} collective-permute-done((bf16[16,640]{1,0:T(8,128)(2,1)S(1)}, bf16[16,640]{1,0:T(8,128)(2,1)S(1)}, u32[]{:S(2)}, u32[]{:S(2)}) %collective-permute-start.2) | collective-permute-done | bytes 20512 | tf_op jit(solution)/shard_map/ppermute | solution.py:108
  16.0 0.6 copy-done.12
  16.6 0.7 copy-done.13
  17.3 0.7 copy-done.14
  18.1 2.2 %copy-done = bf16[4096,512]{1,0:T(8,128)(2,1)S(1)} copy-done((bf16[4096,512]{1,0:T(8,128)(2,1)S(1)}, bf16[4096,512]{1,0:T(8,128)(2,1)}, u32[]{:S(2)}) %copy-start) | copy-done | bytes 4194328
  20.3 0.4 shard_map.141.refs_2_
  20.7 0.6 shard_map.143.query_ref
  21.3 0.8 %collective-permute-start.6 = (bf16[16,512]{1,0:T(8,128)(2,1)S(1)}, bf16[16,512]{1,0:T(8,128)(2,1)S(1)}, u32[]{:S(2)}, u32[]{:S(2)}) collective-permute-start(bf16[16,512]{1,0:T(8,128)(2,1)S(1)} %shard_map.143.query_ref), channel_id=1, source_target_pairs={{0,4},{1,5},{2,6},{3,7},{4,0},{5,1},{6,2},{7,3},{8,12},{9,13},{10,... | collective-permute-start | bytes 49160 | tf_op jit(solution)/shard_map/ppermute | solution.py:108
  22.1 3.6 %collective-permute-start.7 = (bf16[16,512]{1,0:T(8,128)(2,1)S(1)}, bf16[16,512]{1,0:T(8,128)(2,1)S(1)}, u32[]{:S(2)}, u32[]{:S(2)}) collective-permute-start(bf16[16,512]{1,0:T(8,128)(2,1)S(1)} %shard_map.143.query_ref), channel_id=1, source_target_pairs={{0,6},{1,7},{2,4},{3,5},{4,2},{5,3},{6,0},{7,1},{8,14},{9,15},{10,... | collective-permute-start | bytes 49160 | tf_op jit(solution)/shard_map/ppermute | solution.py:108
  25.7 0.3 collective-permute-done.6.refs_1_
  26.0 1.6 %collective-permute-done.7.refs_2_ = bf16[16,512]{1,0:T(8,128)(2,1)S(1)} collective-permute-done((bf16[16,512]{1,0:T(8,128)(2,1)S(1)}, bf16[16,512]{1,0:T(8,128)(2,1)S(1)}, u32[]{:S(2)}, u32[]{:S(2)}) %collective-permute-start.7) | collective-permute-done | bytes 16416 | tf_op jit(solution)/shard_map/ppermute | solution.py:108
  27.6 1.1 %shard_map.146 = (bf16[16,640]{1,0:T(8,128)(2,1)S(1)}, bf16[16,640]{1,0:T(8,128)(2,1)S(1)}, bf16[16,640]{1,0:T(8,128)(2,1)S(1)}) custom-call(bf16[16,512]{1,0:T(8,128)(2,1)S(1)} %collective-permute-done.5.refs_0_, bf16[16,512]{1,0:T(8,128)(2,1)S(1)} %collective-permute-done.6.refs_1_, bf16[16,512]{1,0:T(8,128)(2,1)S(1)} %collective-permute-done.7.refs_2_, ...), custom_call_target="tpu_custom_call" | custom-call | flops 134217728 | bytes 2031616 | tf_op jit(solution)/shard_map/pallas_call | solution.py:114
  28.7 0.4 collective-permute-start.8
  29.1 3.8 %collective-permute-start.9 = (bf16[16,640]{1,0:T(8,128)(2,1)S(1)}, bf16[16,640]{1,0:T(8,128)(2,1)S(1)}, u32[]{:S(2)}, u32[]{:S(2)}) collective-permute-start(bf16[16,640]{1,0:T(8,128)(2,1)S(1)} %get-tuple-element.26), channel_id=1, source_target_pairs={{0,4},{1,5},{2,6},{3,7},{4,0},{5,1},{6,2},{7,3},{8,12},{9,13},{10,... | collective-permute-start | bytes 61448 | tf_op jit(solution)/shard_map/ppermute | solution.py:108
  32.9 0.2 collective-permute-start.10
  33.2 0.4 shard_map.145
  33.6 1.1 %collective-permute-done.9.second_ref = bf16[16,640]{1,0:T(8,128)(2,1)S(1)} collective-permute-done((bf16[16,640]{1,0:T(8,128)(2,1)S(1)}, bf16[16,640]{1,0:T(8,128)(2,1)S(1)}, u32[]{:S(2)}, u32[]{:S(2)}) %collective-permute-start.9) | collective-permute-done | bytes 20512 | tf_op jit(solution)/shard_map/ppermute | solution.py:108
  34.7 3.8 %collective-permute-done.10.third_ref = bf16[16,640]{1,0:T(8,128)(2,1)S(1)} collective-permute-done((bf16[16,640]{1,0:T(8,128)(2,1)S(1)}, bf16[16,640]{1,0:T(8,128)(2,1)S(1)}, u32[]{:S(2)}, u32[]{:S(2)}) %collective-permute-start.10) | collective-permute-done | bytes 20512 | tf_op jit(solution)/shard_map/ppermute | solution.py:108
  38.5 0.6 shard_map.147
  39.1 0.4 shard_map.148.own_ref
  39.5 0.9 %collective-permute-done.11.other_ref = bf16[4,16,512]{2,1,0:T(8,128)(2,1)S(1)} collective-permute-done((bf16[4,16,512]{2,1,0:T(8,128)(2,1)S(1)}, bf16[4,16,512]{2,1,0:T(8,128)(2,1)S(1)}, u32[]{:S(2)}, u32[]{:S(2)}) %collective-permute-start.11) | collective-permute-done | bytes 65568 | tf_op jit(solution)/shard_map/ppermute | solution.py:108
  40.5 0.8 %collective-permute-start.13 = (bf16[16,512]{1,0:T(8,128)(2,1)S(1)}, bf16[16,512]{1,0:T(8,128)(2,1)S(1)}, u32[]{:S(2)}, u32[]{:S(2)}) collective-permute-start(bf16[16,512]{1,0:T(8,128)(2,1)S(1)} %get-tuple-element.32), channel_id=1, source_target_pairs={{0,4},{1,5},{2,6},{3,7},{4,0},{5,1},{6,2},{7,3},{8,12},{9,13},{10,... | collective-permute-start | bytes 49160 | tf_op jit(solution)/shard_map/ppermute | solution.py:108
  41.2 3.6 %collective-permute-start.14 = (bf16[16,512]{1,0:T(8,128)(2,1)S(1)}, bf16[16,512]{1,0:T(8,128)(2,1)S(1)}, u32[]{:S(2)}, u32[]{:S(2)}) collective-permute-start(bf16[16,512]{1,0:T(8,128)(2,1)S(1)} %get-tuple-element.33), channel_id=1, source_target_pairs={{0,6},{1,7},{2,4},{3,5},{4,2},{5,3},{6,0},{7,1},{8,14},{9,15},{10,... | collective-permute-start | bytes 49160 | tf_op jit(solution)/shard_map/ppermute | solution.py:108
  44.8 0.3 collective-permute-done.13.second_ref
  45.2 1.6 %collective-permute-done.14.third_ref = bf16[16,512]{1,0:T(8,128)(2,1)S(1)} collective-permute-done((bf16[16,512]{1,0:T(8,128)(2,1)S(1)}, bf16[16,512]{1,0:T(8,128)(2,1)S(1)}, u32[]{:S(2)}, u32[]{:S(2)}) %collective-permute-start.14) | collective-permute-done | bytes 16416 | tf_op jit(solution)/shard_map/ppermute | solution.py:108
  46.9 1.5 %collective-permute-start.15 = (bf16[16,512]{1,0:T(8,128)(2,1)S(1)}, bf16[16,512]{1,0:T(8,128)(2,1)S(1)}, u32[]{:S(2)}, u32[]{:S(2)}) collective-permute-start(bf16[16,512]{1,0:T(8,128)(2,1)S(1)} %get-tuple-element.34.first_ref), channel_id=1, source_target_pairs={{0,8},{8,0},{16,24},{24,16},{1,9},{9,1},{17,25},{25,17},{2,10},{10... | collective-permute-start | bytes 49160 | tf_op jit(solution)/shard_map/ppermute | solution.py:108
  48.4 1.5 %collective-permute-start.16 = (bf16[16,512]{1,0:T(8,128)(2,1)S(1)}, bf16[16,512]{1,0:T(8,128)(2,1)S(1)}, u32[]{:S(2)}, u32[]{:S(2)}) collective-permute-start(bf16[16,512]{1,0:T(8,128)(2,1)S(1)} %get-tuple-element.34.first_ref), channel_id=1, source_target_pairs={{0,16},{8,24},{16,0},{24,8},{1,17},{9,25},{17,1},{25,9},{2,18},{10... | collective-permute-start | bytes 49160 | tf_op jit(solution)/shard_map/ppermute | solution.py:108
  49.9 0.5 collective-permute-start.17
  50.4 0.3 collective-permute-done.15.second_ref
  50.7 1.4 %collective-permute-done.16.third_ref = bf16[16,512]{1,0:T(8,128)(2,1)S(1)} collective-permute-done((bf16[16,512]{1,0:T(8,128)(2,1)S(1)}, bf16[16,512]{1,0:T(8,128)(2,1)S(1)}, u32[]{:S(2)}, u32[]{:S(2)}) %collective-permute-start.16) | collective-permute-done | bytes 16416 | tf_op jit(solution)/shard_map/ppermute | solution.py:108
  52.1 2.4 %collective-permute-done.17.fourth_ref = bf16[16,512]{1,0:T(8,128)(2,1)S(1)} collective-permute-done((bf16[16,512]{1,0:T(8,128)(2,1)S(1)}, bf16[16,512]{1,0:T(8,128)(2,1)S(1)}, u32[]{:S(2)}, u32[]{:S(2)}) %collective-permute-start.17) | collective-permute-done | bytes 16416 | tf_op jit(solution)/shard_map/ppermute | solution.py:108
  54.5 0.2 shard_map.151
  54.7 1.2 %collective-permute-done.18.second_ref = f32[48,128]{1,0:T(8,128)S(1)} collective-permute-done((f32[48,128]{1,0:T(8,128)S(1)}, f32[48,128]{1,0:T(8,128)S(1)}, u32[]{:S(2)}, u32[]{:S(2)}) %collective-permute-start.18) | collective-permute-done | bytes 24608 | tf_op jit(solution)/shard_map/ppermute | solution.py:108
  55.9 0.3 collective-permute-start.19
  56.3 3.8 %collective-permute-start.20 = (f32[48,128]{1,0:T(8,128)S(1)}, f32[48,128]{1,0:T(8,128)S(1)}, u32[]{:S(2)}, u32[]{:S(2)}) collective-permute-start(f32[48,128]{1,0:T(8,128)S(1)} %shard_map.152.refs_0_), channel_id=1, source_target_pairs={{0,4},{1,5},{2,6},{3,7},{4,0},{5,1},{6,2},{7,3},{8,12},{9,13},{10,... | collective-permute-start | bytes 73736 | tf_op jit(solution)/shard_map/ppermute | solution.py:108
  60.1 0.2 collective-permute-start.21
  60.3 1.6 %collective-permute-done.20.refs_2_ = f32[48,128]{1,0:T(8,128)S(1)} collective-permute-done((f32[48,128]{1,0:T(8,128)S(1)}, f32[48,128]{1,0:T(8,128)S(1)}, u32[]{:S(2)}, u32[]{:S(2)}) %collective-permute-start.20) | collective-permute-done | bytes 24608 | tf_op jit(solution)/shard_map/ppermute | solution.py:108
  61.9 3.8 %collective-permute-done.21.refs_3_ = f32[48,128]{1,0:T(8,128)S(1)} collective-permute-done((f32[48,128]{1,0:T(8,128)S(1)}, f32[48,128]{1,0:T(8,128)S(1)}, u32[]{:S(2)}, u32[]{:S(2)}) %collective-permute-start.21) | collective-permute-done | bytes 24608 | tf_op jit(solution)/shard_map/ppermute | solution.py:108
  65.7 1.1 %shard_map.153 = (bf16[16,512]{1,0:T(8,128)(2,1)}, f32[2]{0:T(128)}, bf16[16,512]{1,0:T(8,128)(2,1)}) custom-call(f32[48,128]{1,0:T(8,128)S(1)} %shard_map.152.refs_0_, f32[48,128]{1,0:T(8,128)S(1)} %collective-permute-done.19.refs_1_, f32[48,128]{1,0:T(8,128)S(1)} %collective-permute-done.20.refs_2_, f32[48,128]{1,0:T(8,128)S(1)} %collective-permute-done.21.refs_3_, ...), custom_call_target="tpu_custom_call" | custom-call | tf_op jit(solution)/shard_map/pallas_call | solution.py:608
  (41 shorter events, 0.7 us)
Async XLA Ops:
  0.6 1.1 %copy-start.2 = (bf16[320,1024]{1,0:T(8,128)(2,1)S(1)}, bf16[320,1024]{1,0:T(8,128)(2,1)}, u32[]{:S(2)}) copy-start(bf16[320,1024]{1,0:T(8,128)(2,1)} %refs_3_.3) | copy-start | bytes 1966084
  1.7 1.1 %copy-start.4 = (bf16[320,1024]{1,0:T(8,128)(2,1)S(1)}, bf16[320,1024]{1,0:T(8,128)(2,1)}, u32[]{:S(2)}) copy-start(bf16[320,1024]{1,0:T(8,128)(2,1)} %refs_4_.1) | copy-start | bytes 1966084
  2.8 17.8 %copy-start.10 = (f32[128]{0:T(128)S(1)}, f32[128]{0:T(128)}, u32[]{:S(2)}) copy-start(f32[128]{0:T(128)} %param.15) | copy-start | bytes 1540
  3.1 24.5 %collective-permute-start.4 = (bf16[320,1024]{1,0:T(8,128)(2,1)S(1)}, bf16[320,1024]{1,0:T(8,128)(2,1)S(1)}, u32[]{:S(2)}, u32[]{:S(2)}) collective-permute-start(bf16[320,1024]{1,0:T(8,128)(2,1)S(1)} %shard_map.144), channel_id=1, source_target_pairs={{0,1},{1,0},{2,3},{3,2},{4,5},{5,4},{6,7},{7,6},{8,9},{9,8},{10,11... | collective-permute-start | bytes 1966088 | tf_op jit(solution)/shard_map/ppermute | solution.py:108
  3.6 0.7 %copy-start.6 = (bf16[16,512]{1,0:T(8,128)(2,1)S(1)}, bf16[16,512]{1,0:T(8,128)(2,1)}, u32[]{:S(2)}) copy-start(bf16[16,512]{1,0:T(8,128)(2,1)} %hidden_ref.3) | copy-start | bytes 49156
  4.3 0.7 %copy-start.9 = (f32[512]{0:T(512)S(1)}, f32[512]{0:T(512)}, u32[]{:S(2)}) copy-start(f32[512]{0:T(512)} %param.13) | copy-start | bytes 6148
  5.1 5.2 %collective-permute-start = (bf16[16,640]{1,0:T(8,128)(2,1)S(1)}, bf16[16,640]{1,0:T(8,128)(2,1)S(1)}, u32[]{:S(2)}, u32[]{:S(2)}) collective-permute-start(bf16[16,640]{1,0:T(8,128)(2,1)S(1)} %shard_map.139.refs_0_), channel_id=1, source_target_pairs={{0,2},{1,3},{2,0},{3,1},{4,6},{5,7},{6,4},{7,5},{8,10},{9,11},{10,... | collective-permute-start | bytes 61448 | tf_op jit(solution)/shard_map/ppermute | solution.py:108
  7.7 4.7 %collective-permute-start.1 = (bf16[16,640]{1,0:T(8,128)(2,1)S(1)}, bf16[16,640]{1,0:T(8,128)(2,1)S(1)}, u32[]{:S(2)}, u32[]{:S(2)}) collective-permute-start(bf16[16,640]{1,0:T(8,128)(2,1)S(1)} %shard_map.139.refs_0_), channel_id=1, source_target_pairs={{0,4},{1,5},{2,6},{3,7},{4,0},{5,1},{6,2},{7,3},{8,12},{9,13},{10,... | collective-permute-start | bytes 61448 | tf_op jit(solution)/shard_map/ppermute | solution.py:108
  10.3 5.6 %collective-permute-start.2 = (bf16[16,640]{1,0:T(8,128)(2,1)S(1)}, bf16[16,640]{1,0:T(8,128)(2,1)S(1)}, u32[]{:S(2)}, u32[]{:S(2)}) collective-permute-start(bf16[16,640]{1,0:T(8,128)(2,1)S(1)} %shard_map.139.refs_0_), channel_id=1, source_target_pairs={{0,6},{1,7},{2,4},{3,5},{4,2},{5,3},{6,0},{7,1},{8,14},{9,15},{10,... | collective-permute-start | bytes 61448 | tf_op jit(solution)/shard_map/ppermute | solution.py:108
  15.9 4.8 %collective-permute-start.3 = (bf16[4,16,640]{2,1,0:T(8,128)(2,1)S(1)}, bf16[4,16,640]{2,1,0:T(8,128)(2,1)S(1)}, u32[]{:S(2)}, u32[]{:S(2)}) collective-permute-start(bf16[4,16,640]{2,1,0:T(8,128)(2,1)S(1)} %shard_map.140.blocks_ref.refs_0_), channel_id=1, source_target_pairs={{0,1},{1,0},{2,3},{3,2},{4,5},{5,4},{6,7},{7,6},{8,9},{9,8},{10,11... | collective-permute-start | bytes 245768 | tf_op jit(solution)/shard_map/ppermute | solution.py:108
  15.9 0.7 copy-start.12
  16.6 0.7 copy-start.13
  17.3 0.7 copy-start.14
  18.1 2.2 %copy-start = (bf16[4096,512]{1,0:T(8,128)(2,1)S(1)}, bf16[4096,512]{1,0:T(8,128)(2,1)}, u32[]{:S(2)}) copy-start(bf16[4096,512]{1,0:T(8,128)(2,1)} %refs_3_.2) | copy-start | bytes 12582916
  20.3 7.4 %copy-start.3 = (bf16[320,1024]{1,0:T(8,128)(2,1)S(1)}, bf16[320,1024]{1,0:T(8,128)(2,1)}, u32[]{:S(2)}) copy-start(bf16[320,1024]{1,0:T(8,128)(2,1)} %refs_3_.3) | copy-start | bytes 1966084
  20.3 7.4 %copy-start.5 = (bf16[320,1024]{1,0:T(8,128)(2,1)S(1)}, bf16[320,1024]{1,0:T(8,128)(2,1)}, u32[]{:S(2)}) copy-start(bf16[320,1024]{1,0:T(8,128)(2,1)} %refs_4_.1) | copy-start | bytes 1966084
  20.6 17.9 %copy-start.1 = (bf16[512,4096]{1,0:T(8,128)(2,1)S(1)}, bf16[512,4096]{1,0:T(8,128)(2,1)}, u32[]{:S(2)}) copy-start(bf16[512,4096]{1,0:T(8,128)(2,1)} %weight_ref.5) | copy-start | bytes 12582916
  21.2 4.5 %collective-permute-start.5 = (bf16[16,512]{1,0:T(8,128)(2,1)S(1)}, bf16[16,512]{1,0:T(8,128)(2,1)S(1)}, u32[]{:S(2)}, u32[]{:S(2)}) collective-permute-start(bf16[16,512]{1,0:T(8,128)(2,1)S(1)} %shard_map.143.query_ref), channel_id=1, source_target_pairs={{0,2},{1,3},{2,0},{3,1},{4,6},{5,7},{6,4},{7,5},{8,10},{9,11},{10,... | collective-permute-start | bytes 49160 | tf_op jit(solution)/shard_map/ppermute | solution.py:108
  21.3 4.7 %collective-permute-start.6 = (bf16[16,512]{1,0:T(8,128)(2,1)S(1)}, bf16[16,512]{1,0:T(8,128)(2,1)S(1)}, u32[]{:S(2)}, u32[]{:S(2)}) collective-permute-start(bf16[16,512]{1,0:T(8,128)(2,1)S(1)} %shard_map.143.query_ref), channel_id=1, source_target_pairs={{0,4},{1,5},{2,6},{3,7},{4,0},{5,1},{6,2},{7,3},{8,12},{9,13},{10,... | collective-permute-start | bytes 49160 | tf_op jit(solution)/shard_map/ppermute | solution.py:108
  22.1 5.5 %collective-permute-start.7 = (bf16[16,512]{1,0:T(8,128)(2,1)S(1)}, bf16[16,512]{1,0:T(8,128)(2,1)S(1)}, u32[]{:S(2)}, u32[]{:S(2)}) collective-permute-start(bf16[16,512]{1,0:T(8,128)(2,1)S(1)} %shard_map.143.query_ref), channel_id=1, source_target_pairs={{0,6},{1,7},{2,4},{3,5},{4,2},{5,3},{6,0},{7,1},{8,14},{9,15},{10,... | collective-permute-start | bytes 49160 | tf_op jit(solution)/shard_map/ppermute | solution.py:108
  28.7 4.9 %collective-permute-start.8 = (bf16[16,640]{1,0:T(8,128)(2,1)S(1)}, bf16[16,640]{1,0:T(8,128)(2,1)S(1)}, u32[]{:S(2)}, u32[]{:S(2)}) collective-permute-start(bf16[16,640]{1,0:T(8,128)(2,1)S(1)} %get-tuple-element.25), channel_id=1, source_target_pairs={{0,2},{1,3},{2,0},{3,1},{4,6},{5,7},{6,4},{7,5},{8,10},{9,11},{10,... | collective-permute-start | bytes 61448 | tf_op jit(solution)/shard_map/ppermute | solution.py:108
  29.1 5.6 %collective-permute-start.9 = (bf16[16,640]{1,0:T(8,128)(2,1)S(1)}, bf16[16,640]{1,0:T(8,128)(2,1)S(1)}, u32[]{:S(2)}, u32[]{:S(2)}) collective-permute-start(bf16[16,640]{1,0:T(8,128)(2,1)S(1)} %get-tuple-element.26), channel_id=1, source_target_pairs={{0,4},{1,5},{2,6},{3,7},{4,0},{5,1},{6,2},{7,3},{8,12},{9,13},{10,... | collective-permute-start | bytes 61448 | tf_op jit(solution)/shard_map/ppermute | solution.py:108
  32.9 5.6 %collective-permute-start.10 = (bf16[16,640]{1,0:T(8,128)(2,1)S(1)}, bf16[16,640]{1,0:T(8,128)(2,1)S(1)}, u32[]{:S(2)}, u32[]{:S(2)}) collective-permute-start(bf16[16,640]{1,0:T(8,128)(2,1)S(1)} %get-tuple-element.27), channel_id=1, source_target_pairs={{0,6},{1,7},{2,4},{3,5},{4,2},{5,3},{6,0},{7,1},{8,14},{9,15},{10,... | collective-permute-start | bytes 61448 | tf_op jit(solution)/shard_map/ppermute | solution.py:108
  38.5 1.8 %copy-start.7 = (bf16[16,512]{1,0:T(8,128)(2,1)S(1)}, bf16[16,512]{1,0:T(8,128)(2,1)}, u32[]{:S(2)}) copy-start(bf16[16,512]{1,0:T(8,128)(2,1)} %hidden_ref.3) | copy-start | bytes 49156
  38.5 8.3 %copy-start.8 = (f32[512]{0:T(512)S(1)}, f32[512]{0:T(512)}, u32[]{:S(2)}) copy-start(f32[512]{0:T(512)} %param.19) | copy-start | bytes 6148
  38.5 27.2 %copy-start.11 = (s32[64]{0:T(128)S(1)}, s32[64]{0:T(128)}, u32[]{:S(2)}) copy-start(s32[64]{0:T(128)} %param.22) | copy-start | bytes 772
  39.1 1.3 %collective-permute-start.11 = (bf16[4,16,512]{2,1,0:T(8,128)(2,1)S(1)}, bf16[4,16,512]{2,1,0:T(8,128)(2,1)S(1)}, u32[]{:S(2)}, u32[]{:S(2)}) collective-permute-start(bf16[4,16,512]{2,1,0:T(8,128)(2,1)S(1)} %get-tuple-element.29), channel_id=1, source_target_pairs={{0,1},{1,0},{2,3},{3,2},{4,5},{5,4},{6,7},{7,6},{8,9},{9,8},{10,11... | collective-permute-start | bytes 196616 | tf_op jit(solution)/shard_map/ppermute | solution.py:108
  40.4 4.5 %collective-permute-start.12 = (bf16[16,512]{1,0:T(8,128)(2,1)S(1)}, bf16[16,512]{1,0:T(8,128)(2,1)S(1)}, u32[]{:S(2)}, u32[]{:S(2)}) collective-permute-start(bf16[16,512]{1,0:T(8,128)(2,1)S(1)} %get-tuple-element.31), channel_id=1, source_target_pairs={{0,2},{1,3},{2,0},{3,1},{4,6},{5,7},{6,4},{7,5},{8,10},{9,11},{10,... | collective-permute-start | bytes 49160 | tf_op jit(solution)/shard_map/ppermute | solution.py:108
  40.5 4.7 %collective-permute-start.13 = (bf16[16,512]{1,0:T(8,128)(2,1)S(1)}, bf16[16,512]{1,0:T(8,128)(2,1)S(1)}, u32[]{:S(2)}, u32[]{:S(2)}) collective-permute-start(bf16[16,512]{1,0:T(8,128)(2,1)S(1)} %get-tuple-element.32), channel_id=1, source_target_pairs={{0,4},{1,5},{2,6},{3,7},{4,0},{5,1},{6,2},{7,3},{8,12},{9,13},{10,... | collective-permute-start | bytes 49160 | tf_op jit(solution)/shard_map/ppermute | solution.py:108
  41.2 5.5 %collective-permute-start.14 = (bf16[16,512]{1,0:T(8,128)(2,1)S(1)}, bf16[16,512]{1,0:T(8,128)(2,1)S(1)}, u32[]{:S(2)}, u32[]{:S(2)}) collective-permute-start(bf16[16,512]{1,0:T(8,128)(2,1)S(1)} %get-tuple-element.33), channel_id=1, source_target_pairs={{0,6},{1,7},{2,4},{3,5},{4,2},{5,3},{6,0},{7,1},{8,14},{9,15},{10,... | collective-permute-start | bytes 49160 | tf_op jit(solution)/shard_map/ppermute | solution.py:108
  46.9 3.8 %collective-permute-start.15 = (bf16[16,512]{1,0:T(8,128)(2,1)S(1)}, bf16[16,512]{1,0:T(8,128)(2,1)S(1)}, u32[]{:S(2)}, u32[]{:S(2)}) collective-permute-start(bf16[16,512]{1,0:T(8,128)(2,1)S(1)} %get-tuple-element.34.first_ref), channel_id=1, source_target_pairs={{0,8},{8,0},{16,24},{24,16},{1,9},{9,1},{17,25},{25,17},{2,10},{10... | collective-permute-start | bytes 49160 | tf_op jit(solution)/shard_map/ppermute | solution.py:108
  48.4 3.7 %collective-permute-start.16 = (bf16[16,512]{1,0:T(8,128)(2,1)S(1)}, bf16[16,512]{1,0:T(8,128)(2,1)S(1)}, u32[]{:S(2)}, u32[]{:S(2)}) collective-permute-start(bf16[16,512]{1,0:T(8,128)(2,1)S(1)} %get-tuple-element.34.first_ref), channel_id=1, source_target_pairs={{0,16},{8,24},{16,0},{24,8},{1,17},{9,25},{17,1},{25,9},{2,18},{10... | collective-permute-start | bytes 49160 | tf_op jit(solution)/shard_map/ppermute | solution.py:108
  49.9 4.6 %collective-permute-start.17 = (bf16[16,512]{1,0:T(8,128)(2,1)S(1)}, bf16[16,512]{1,0:T(8,128)(2,1)S(1)}, u32[]{:S(2)}, u32[]{:S(2)}) collective-permute-start(bf16[16,512]{1,0:T(8,128)(2,1)S(1)} %get-tuple-element.34.first_ref), channel_id=1, source_target_pairs={{0,24},{8,16},{16,8},{24,0},{1,25},{9,17},{17,9},{25,1},{2,26},{10... | collective-permute-start | bytes 49160 | tf_op jit(solution)/shard_map/ppermute | solution.py:108
  54.7 1.2 %collective-permute-start.18 = (f32[48,128]{1,0:T(8,128)S(1)}, f32[48,128]{1,0:T(8,128)S(1)}, u32[]{:S(2)}, u32[]{:S(2)}) collective-permute-start(f32[48,128]{1,0:T(8,128)S(1)} %get-tuple-element.36.first_ref), channel_id=1, source_target_pairs={{0,1},{1,0},{2,3},{3,2},{4,5},{5,4},{6,7},{7,6},{8,9},{9,8},{10,11... | collective-permute-start | bytes 73736 | tf_op jit(solution)/shard_map/ppermute | solution.py:108
  55.9 4.4 %collective-permute-start.19 = (f32[48,128]{1,0:T(8,128)S(1)}, f32[48,128]{1,0:T(8,128)S(1)}, u32[]{:S(2)}, u32[]{:S(2)}) collective-permute-start(f32[48,128]{1,0:T(8,128)S(1)} %shard_map.152.refs_0_), channel_id=1, source_target_pairs={{0,2},{1,3},{2,0},{3,1},{4,6},{5,7},{6,4},{7,5},{8,10},{9,11},{10,... | collective-permute-start | bytes 73736 | tf_op jit(solution)/shard_map/ppermute | solution.py:108
  56.3 5.6 %collective-permute-start.20 = (f32[48,128]{1,0:T(8,128)S(1)}, f32[48,128]{1,0:T(8,128)S(1)}, u32[]{:S(2)}, u32[]{:S(2)}) collective-permute-start(f32[48,128]{1,0:T(8,128)S(1)} %shard_map.152.refs_0_), channel_id=1, source_target_pairs={{0,4},{1,5},{2,6},{3,7},{4,0},{5,1},{6,2},{7,3},{8,12},{9,13},{10,... | collective-permute-start | bytes 73736 | tf_op jit(solution)/shard_map/ppermute | solution.py:108
  60.1 5.6 %collective-permute-start.21 = (f32[48,128]{1,0:T(8,128)S(1)}, f32[48,128]{1,0:T(8,128)S(1)}, u32[]{:S(2)}, u32[]{:S(2)}) collective-permute-start(f32[48,128]{1,0:T(8,128)S(1)} %shard_map.152.refs_0_), channel_id=1, source_target_pairs={{0,6},{1,7},{2,4},{3,5},{4,2},{5,3},{6,0},{7,1},{8,14},{9,15},{10,... | collective-permute-start | bytes 73736 | tf_op jit(solution)/shard_map/ppermute | solution.py:108

commit v3 on v2

--- a/solution.py
+++ b/solution.py
@@ -144,14 +144,22 @@
     return jnp.sum(jnp.where(own, block, 0.0), axis=1, keepdims=True)
 
 
-def prepare_inputs(hidden_ref, gain_ref, message_ref):
+def open_window(out_ref):
+    out_ref[...] = jnp.zeros_like(out_ref)
+
+
+def prepare_inputs(window_ref, hidden_ref, gain_ref, message_ref):
+    del window_ref
     inputs = hidden_ref[...].astype(jnp.float32)
     width = inputs.shape[1]
     message_ref[:, :width] = (inputs * gain_ref[...]).astype(jnp.bfloat16)
     message_ref[:, width:] = lane_pieces([jnp.sum(inputs * inputs, axis=1, keepdims=True)])
 
 
-def positions_and_ranges(frequency_ref, lengths_ref, order_ref, rope_ref, range_ref):
+def positions_and_ranges(
+    message_ref, frequency_ref, lengths_ref, order_ref, rope_ref, range_ref
+):
+    del message_ref
     count = lengths_ref.shape[1]
     half = frequency_ref.shape[1] // 2
     row = lax.broadcasted_iota(jnp.int32, (count, count), 0)
@@ -172,7 +180,8 @@
     rope_ref[:, 2 * half :] = jnp.where(lane < half, -sine, sine)
 
 
-def send_heads(key_ref, value_ref, out_ref, semaphore):
+def send_heads(message_ref, key_ref, value_ref, out_ref, semaphore):
+    del message_ref
     me = lax.axis_index("pack")
     heads = out_ref.shape[1] // 256
     copies = []
@@ -192,39 +201,40 @@
         copy.wait()
 
 
-def project_blocks(offsets, blocks, weight_ref, width):
+def project_blocks(offsets, blocks, weight_ref):
     me = lax.axis_index("pack")
-    total = None
+    width = weight_ref.shape[1]
+    total = 0.0
     for offset, block in zip(offsets, blocks):
         rows = pl.ds(pl.multiple_of((me ^ offset) * width, width), width)
-        part = jnp.dot(
-            block[:, :width].astype(jnp.bfloat16),
-            weight_ref[rows, :],
-            preferred_element_type=jnp.float32,
+        total = total + jnp.dot(
+            block[:, :width], weight_ref[rows, :], preferred_element_type=jnp.float32
         )
-        total = part if total is None else total + part
     return total
+
+
+def project_first(message_ref, weight_ref, total_ref):
+    total_ref[...] = project_blocks((0,), [message_ref], weight_ref)
 
 
 def join_blocks(*refs):
     out_ref = refs[-1]
-    for i, ref in enumerate(refs[:-1]):
-        out_ref[i] = ref[...]
-
-
-def first_half(blocks_ref, weight_ref, total_ref):
-    width = weight_ref.shape[1]
-    blocks = [blocks_ref[i] for i in range(blocks_ref.shape[0])]
-    total_ref[...] = project_blocks((0, 2, 4, 6), blocks, weight_ref, width)
+    for i in range(out_ref.shape[0]):
+        out_ref[i] = refs[i][...]
+
+
+def first_half(blocks_ref, own_ref, weight_ref, total_ref):
+    blocks = [blocks_ref.at[i] for i in range(1, blocks_ref.shape[0])]
+    total_ref[...] = own_ref[...] + project_blocks((2, 4, 6), blocks, weight_ref)
 
 
 def second_half(
     own_ref, other_ref, total_ref, weight_ref, gain_ref, rope_ref, query_ref, *, model_width
 ):
-    width = weight_ref.shape[1]
+    width = total_ref.shape[1]
     count = own_ref.shape[0]
-    blocks = [other_ref[i] for i in range(count)]
-    projected = total_ref[...] + project_blocks((1, 3, 5, 7), blocks, weight_ref, width)
+    blocks = [other_ref.at[i] for i in range(count)]
+    projected = total_ref[...] + project_blocks((1, 3, 5, 7), blocks, weight_ref)
     squares = sum(
         lane_sum(ref[i, :, width:].astype(jnp.float32), 0)
         for ref in (own_ref, other_ref)
@@ -499,33 +509,57 @@
     frequency = (ROPE_BASE ** (-half * 2.0 / head_dim)).astype(np.float32)
     frequency = jnp.asarray(np.concatenate([frequency, frequency])[None])
 
+    whole = pl.BlockSpec(memory_space=pltpu.VMEM)
+    anywhere = pl.BlockSpec(memory_space=pl.ANY)
+    window = pl.pallas_call(
+        open_window,
+        out_shape=shaped((8, 128), f32),
+        out_specs=whole,
+        compiler_params=pltpu.CompilerParams(vmem_limit_bytes=1 << 20),
+        cost_estimate=pl.CostEstimate(flops=1 << 34, bytes_accessed=0, transcendentals=0),
+    )()
     message = in_vmem(
-        prepare_inputs, shaped((stmts, width + 128), bf16), hidden_in, attn_gain
+        prepare_inputs, shaped((stmts, width + 128), bf16), window, hidden_in, attn_gain
     )
     blocks = [message] + [flip(message, "pack", 2 * i) for i in range(1, chips)]
-    blocks = in_vmem(join_blocks, shaped((chips,) + message.shape, bf16), *blocks)
-    others = flip(blocks, "pack", 1)
+    own_projected = in_vmem(
+        project_first, shaped((stmts, width), f32), message, w_query, limit=16, flops=1 << 26
+    )
     rope, ranges = in_vmem(
         positions_and_ranges,
         (shaped((stmts, 2 * head_dim), f32), shaped((stmts, 256), f32)),
+        message,
         frequency,
         lengths,
         pack_order,
     )
-    anywhere = pl.BlockSpec(memory_space=pl.ANY)
+    blocks = in_vmem(
+        join_blocks,
+        shaped((chips,) + message.shape, bf16),
+        *blocks,
+        own_projected,
+        rope,
+    )
+    others = flip(blocks, "pack", 1)
+    projected = in_vmem(
+        first_half,
+        shaped((stmts, width), f32),
+        blocks,
+        own_projected,
+        w_query,
+        limit=16,
+        flops=1 << 27,
+    )
     swapped = pl.pallas_call(
         send_heads,
         out_shape=shaped((tokens, 2 * chips * head_dim), bf16),
-        in_specs=[anywhere] * 2,
-        out_specs=anywhere,
+        in_specs=[whole] + [anywhere] * 2,
+        out_specs=whole,
         scratch_shapes=[pltpu.SemaphoreType.DMA((2 * chips,))],
         compiler_params=pltpu.CompilerParams(vmem_limit_bytes=4 << 20),
         cost_estimate=pl.CostEstimate(flops=0, bytes_accessed=2 << 20, transcendentals=0),
-    )(cached_keys, cached_values)
+    )(projected, cached_keys, cached_values)
     swapped = flip(swapped, "pack", 1)
-    projected = in_vmem(
-        first_half, shaped((stmts, width), f32), blocks, w_query, limit=16, flops=1 << 27
-    )
     queries = in_vmem(
         lambda *refs: second_half(*refs, model_width=model_width),
         shaped((stmts, width), bf16),
@@ -536,7 +570,7 @@
         query_gain,
         rope,
         limit=16,
-        flops=1 << 27,
+        flops=1 << 36,
     )
     received = [flip(queries, "pack", 2 * i) for i in range(1, chips)]
     sent = in_vmem(
@@ -604,7 +638,6 @@
     )
     gram = in_vmem(add_two, shaped(gram.shape, f32), gram, flip(gram, "pack", 1))
     grams = [gram] + [flip(gram, "pack", 2 * i) for i in range(1, chips)]
-    whole = pl.BlockSpec(memory_space=pltpu.VMEM)
     pooled, loss_rows, grad_hidden = pl.pallas_call(
         lambda *refs: losses_and_gradient(*refs, model_width=model_width),
         out_shape=(

time: 67.2 us -> 60.3 us (0.90)
  local copies, waits for them, and re-layouts: 7.75 us -> 0.71 us
    unnamed x30 -> x24, local copies, waits for them, and re-layouts: 7.75 us -> 0.71 us
    pallas_call x13 -> x14, Pallas kernels: 3.98 us -> 4.08 us  [in_vmem(): pl.pallas_call(body, out_shape=outputs, in_specs=[whole] * len(operands),...]
  transfers between devices with their start and end apart: 22 -> 22, of which waited for: 15 -> 16; matrix products, arithmetic and copies ran while one was open for 0% -> 0% of each run, Pallas kernels for 3% -> 4%
where the time goes in v3:
time: 60.3 us; the launch traced here: 60.2 us
  starting transfers between devices  27.5 us (46%)
  waiting for transfers between devices  25.7 us (43%)
  Pallas kernels  5.48 us (9%)
  between operations  0.8 us (1%)
  local copies, waits for them, and re-layouts  0.71 us (1%)
    ppermute x22, starting transfers between devices, flip(): return lax.ppermute(array, axis, [(i, i ^ offset) for i in range(size)])  27.5 us
    ppermute x22, waiting for transfers between devices, flip(): return lax.ppermute(array, axis, [(i, i ^ offset) for i in range(size)])  25.7 us
    pallas_call x14, Pallas kernels, in_vmem(): pl.pallas_call(body, out_shape=outputs, in_specs=[whole] * len(operands),...  4.08 us
  transfers between devices with their start and end apart: 22, of which 16 were waited for; matrix products, arithmetic and copies ran while one was open for 0% of the time, Pallas kernels for 4%

profile of v3, /device:TPU:0, one launch (start us, length us, event | category | flops | bytes accessed | tf_op | source)
XLA Modules:
  0.0 60.2 jit_solution(15462789785584679093)
XLA Ops:
  0.7 0.7 %copy-done.4 = bf16[16,512]{1,0:T(8,128)(2,1)S(1)} copy-done((bf16[16,512]{1,0:T(8,128)(2,1)S(1)}, bf16[16,512]{1,0:T(8,128)(2,1)}, u32[]{:S(2)}) %copy-start.4) | copy-done | bytes 16408
  1.4 0.1 shard_map.140.message_ref.refs_0_
  1.5 3.0 %collective-permute-start = (bf16[16,640]{1,0:T(8,128)(2,1)S(1)}, bf16[16,640]{1,0:T(8,128)(2,1)S(1)}, u32[]{:S(2)}, u32[]{:S(2)}) collective-permute-start(bf16[16,640]{1,0:T(8,128)(2,1)S(1)} %shard_map.140.message_ref.refs_0_), channel_id=1, source_target_pairs={{0,2},{1,3},{2,0},{3,1},{4,6},{5,7},{6,4},{7,5},{8,10},{9,11},{10,... | collective-permute-start | bytes 61448 | tf_op jit(solution)/shard_map/ppermute | solution.py:108
  4.5 2.6 %collective-permute-start.1 = (bf16[16,640]{1,0:T(8,128)(2,1)S(1)}, bf16[16,640]{1,0:T(8,128)(2,1)S(1)}, u32[]{:S(2)}, u32[]{:S(2)}) collective-permute-start(bf16[16,640]{1,0:T(8,128)(2,1)S(1)} %shard_map.140.message_ref.refs_0_), channel_id=1, source_target_pairs={{0,4},{1,5},{2,6},{3,7},{4,0},{5,1},{6,2},{7,3},{8,12},{9,13},{10,... | collective-permute-start | bytes 61448 | tf_op jit(solution)/shard_map/ppermute | solution.py:108
  7.1 0.2 shard_map.142
  7.3 0.2 shard_map.141.refs_4_.own_ref
  7.5 1.9 %collective-permute-done.1.refs_2_ = bf16[16,640]{1,0:T(8,128)(2,1)S(1)} collective-permute-done((bf16[16,640]{1,0:T(8,128)(2,1)S(1)}, bf16[16,640]{1,0:T(8,128)(2,1)S(1)}, u32[]{:S(2)}, u32[]{:S(2)}) %collective-permute-start.1) | collective-permute-done | bytes 20512 | tf_op jit(solution)/shard_map/ppermute | solution.py:108
  9.4 3.3 %collective-permute-done.2.refs_3_ = bf16[16,640]{1,0:T(8,128)(2,1)S(1)} collective-permute-done((bf16[16,640]{1,0:T(8,128)(2,1)S(1)}, bf16[16,640]{1,0:T(8,128)(2,1)S(1)}, u32[]{:S(2)}, u32[]{:S(2)}) %collective-permute-start.2) | collective-permute-done | bytes 20512 | tf_op jit(solution)/shard_map/ppermute | solution.py:108
  12.7 0.1 collective-permute-start.3
  12.7 0.3 shard_map.144.refs_2_.message_ref
  13.1 0.3 shard_map.146
  13.4 0.6 collective-permute-start.4
  13.9 0.1 collective-permute-done.3.refs_1_
  14.0 0.5 shard_map.145.query_ref
  14.6 0.1 collective-permute-start.5
  14.7 0.8 %collective-permute-start.6 = (bf16[16,512]{1,0:T(8,128)(2,1)S(1)}, bf16[16,512]{1,0:T(8,128)(2,1)S(1)}, u32[]{:S(2)}, u32[]{:S(2)}) collective-permute-start(bf16[16,512]{1,0:T(8,128)(2,1)S(1)} %shard_map.145.query_ref), channel_id=1, source_target_pairs={{0,4},{1,5},{2,6},{3,7},{4,0},{5,1},{6,2},{7,3},{8,12},{9,13},{10,... | collective-permute-start | bytes 49160 | tf_op jit(solution)/shard_map/ppermute | solution.py:108
  15.4 3.6 %collective-permute-start.7 = (bf16[16,512]{1,0:T(8,128)(2,1)S(1)}, bf16[16,512]{1,0:T(8,128)(2,1)S(1)}, u32[]{:S(2)}, u32[]{:S(2)}) collective-permute-start(bf16[16,512]{1,0:T(8,128)(2,1)S(1)} %shard_map.145.query_ref), channel_id=1, source_target_pairs={{0,6},{1,7},{2,4},{3,5},{4,2},{5,3},{6,0},{7,1},{8,14},{9,15},{10,... | collective-permute-start | bytes 49160 | tf_op jit(solution)/shard_map/ppermute | solution.py:108
  19.0 0.3 collective-permute-done.6.refs_1_
  19.4 1.6 %collective-permute-done.7.refs_2_ = bf16[16,512]{1,0:T(8,128)(2,1)S(1)} collective-permute-done((bf16[16,512]{1,0:T(8,128)(2,1)S(1)}, bf16[16,512]{1,0:T(8,128)(2,1)S(1)}, u32[]{:S(2)}, u32[]{:S(2)}) %collective-permute-start.7) | collective-permute-done | bytes 16416 | tf_op jit(solution)/shard_map/ppermute | solution.py:108
  21.0 1.1 %shard_map.148 = (bf16[16,640]{1,0:T(8,128)(2,1)S(1)}, bf16[16,640]{1,0:T(8,128)(2,1)S(1)}, bf16[16,640]{1,0:T(8,128)(2,1)S(1)}) custom-call(bf16[16,512]{1,0:T(8,128)(2,1)S(1)} %collective-permute-done.5.refs_0_, bf16[16,512]{1,0:T(8,128)(2,1)S(1)} %collective-permute-done.6.refs_1_, bf16[16,512]{1,0:T(8,128)(2,1)S(1)} %collective-permute-done.7.refs_2_, ...), custom_call_target="tpu_custom_call" | custom-call | flops 134217728 | bytes 2031616 | tf_op jit(solution)/shard_map/pallas_call | solution.py:114
  22.0 0.4 collective-permute-start.8
  22.4 3.8 %collective-permute-start.9 = (bf16[16,640]{1,0:T(8,128)(2,1)S(1)}, bf16[16,640]{1,0:T(8,128)(2,1)S(1)}, u32[]{:S(2)}, u32[]{:S(2)}) collective-permute-start(bf16[16,640]{1,0:T(8,128)(2,1)S(1)} %get-tuple-element.26), channel_id=1, source_target_pairs={{0,4},{1,5},{2,6},{3,7},{4,0},{5,1},{6,2},{7,3},{8,12},{9,13},{10,... | collective-permute-start | bytes 61448 | tf_op jit(solution)/shard_map/ppermute | solution.py:108
  26.3 0.2 collective-permute-start.10
  26.5 0.4 shard_map.147
  26.9 1.1 %collective-permute-done.9.second_ref = bf16[16,640]{1,0:T(8,128)(2,1)S(1)} collective-permute-done((bf16[16,640]{1,0:T(8,128)(2,1)S(1)}, bf16[16,640]{1,0:T(8,128)(2,1)S(1)}, u32[]{:S(2)}, u32[]{:S(2)}) %collective-permute-start.9) | collective-permute-done | bytes 20512 | tf_op jit(solution)/shard_map/ppermute | solution.py:108
  28.0 3.8 %collective-permute-done.10.third_ref = bf16[16,640]{1,0:T(8,128)(2,1)S(1)} collective-permute-done((bf16[16,640]{1,0:T(8,128)(2,1)S(1)}, bf16[16,640]{1,0:T(8,128)(2,1)S(1)}, u32[]{:S(2)}, u32[]{:S(2)}) %collective-permute-start.10) | collective-permute-done | bytes 20512 | tf_op jit(solution)/shard_map/ppermute | solution.py:108
  31.9 0.6 shard_map.149
  32.4 0.4 shard_map.150.own_ref
  32.8 0.9 %collective-permute-done.11.other_ref = bf16[4,16,512]{2,1,0:T(8,128)(2,1)S(1)} collective-permute-done((bf16[4,16,512]{2,1,0:T(8,128)(2,1)S(1)}, bf16[4,16,512]{2,1,0:T(8,128)(2,1)S(1)}, u32[]{:S(2)}, u32[]{:S(2)}) %collective-permute-start.11) | collective-permute-done | bytes 65568 | tf_op jit(solution)/shard_map/ppermute | solution.py:108
  33.8 0.8 %collective-permute-start.13 = (bf16[16,512]{1,0:T(8,128)(2,1)S(1)}, bf16[16,512]{1,0:T(8,128)(2,1)S(1)}, u32[]{:S(2)}, u32[]{:S(2)}) collective-permute-start(bf16[16,512]{1,0:T(8,128)(2,1)S(1)} %get-tuple-element.32), channel_id=1, source_target_pairs={{0,4},{1,5},{2,6},{3,7},{4,0},{5,1},{6,2},{7,3},{8,12},{9,13},{10,... | collective-permute-start | bytes 49160 | tf_op jit(solution)/shard_map/ppermute | solution.py:108
  34.6 3.6 %collective-permute-start.14 = (bf16[16,512]{1,0:T(8,128)(2,1)S(1)}, bf16[16,512]{1,0:T(8,128)(2,1)S(1)}, u32[]{:S(2)}, u32[]{:S(2)}) collective-permute-start(bf16[16,512]{1,0:T(8,128)(2,1)S(1)} %get-tuple-element.33), channel_id=1, source_target_pairs={{0,6},{1,7},{2,4},{3,5},{4,2},{5,3},{6,0},{7,1},{8,14},{9,15},{10,... | collective-permute-start | bytes 49160 | tf_op jit(solution)/shard_map/ppermute | solution.py:108
  38.2 0.3 collective-permute-done.13.second_ref
  38.5 1.6 %collective-permute-done.14.third_ref = bf16[16,512]{1,0:T(8,128)(2,1)S(1)} collective-permute-done((bf16[16,512]{1,0:T(8,128)(2,1)S(1)}, bf16[16,512]{1,0:T(8,128)(2,1)S(1)}, u32[]{:S(2)}, u32[]{:S(2)}) %collective-permute-start.14) | collective-permute-done | bytes 16416 | tf_op jit(solution)/shard_map/ppermute | solution.py:108
  40.1 0.1 shard_map.152
  40.2 1.5 %collective-permute-start.15 = (bf16[16,512]{1,0:T(8,128)(2,1)S(1)}, bf16[16,512]{1,0:T(8,128)(2,1)S(1)}, u32[]{:S(2)}, u32[]{:S(2)}) collective-permute-start(bf16[16,512]{1,0:T(8,128)(2,1)S(1)} %get-tuple-element.34.first_ref), channel_id=1, source_target_pairs={{0,8},{8,0},{16,24},{24,16},{1,9},{9,1},{17,25},{25,17},{2,10},{10... | collective-permute-start | bytes 49160 | tf_op jit(solution)/shard_map/ppermute | solution.py:108
  41.7 1.5 %collective-permute-start.16 = (bf16[16,512]{1,0:T(8,128)(2,1)S(1)}, bf16[16,512]{1,0:T(8,128)(2,1)S(1)}, u32[]{:S(2)}, u32[]{:S(2)}) collective-permute-start(bf16[16,512]{1,0:T(8,128)(2,1)S(1)} %get-tuple-element.34.first_ref), channel_id=1, source_target_pairs={{0,16},{8,24},{16,0},{24,8},{1,17},{9,25},{17,1},{25,9},{2,18},{10... | collective-permute-start | bytes 49160 | tf_op jit(solution)/shard_map/ppermute | solution.py:108
  43.2 0.5 collective-permute-start.17
  43.7 0.3 collective-permute-done.15.second_ref
  44.0 1.4 %collective-permute-done.16.third_ref = bf16[16,512]{1,0:T(8,128)(2,1)S(1)} collective-permute-done((bf16[16,512]{1,0:T(8,128)(2,1)S(1)}, bf16[16,512]{1,0:T(8,128)(2,1)S(1)}, u32[]{:S(2)}, u32[]{:S(2)}) %collective-permute-start.16) | collective-permute-done | bytes 16416 | tf_op jit(solution)/shard_map/ppermute | solution.py:108
  45.4 2.4 %collective-permute-done.17.fourth_ref = bf16[16,512]{1,0:T(8,128)(2,1)S(1)} collective-permute-done((bf16[16,512]{1,0:T(8,128)(2,1)S(1)}, bf16[16,512]{1,0:T(8,128)(2,1)S(1)}, u32[]{:S(2)}, u32[]{:S(2)}) %collective-permute-start.17) | collective-permute-done | bytes 16416 | tf_op jit(solution)/shard_map/ppermute | solution.py:108
  47.8 0.2 shard_map.153
  48.1 1.2 %collective-permute-done.18.second_ref = f32[48,128]{1,0:T(8,128)S(1)} collective-permute-done((f32[48,128]{1,0:T(8,128)S(1)}, f32[48,128]{1,0:T(8,128)S(1)}, u32[]{:S(2)}, u32[]{:S(2)}) %collective-permute-start.18) | collective-permute-done | bytes 24608 | tf_op jit(solution)/shard_map/ppermute | solution.py:108
  49.3 0.3 collective-permute-start.19
  49.6 3.8 %collective-permute-start.20 = (f32[48,128]{1,0:T(8,128)S(1)}, f32[48,128]{1,0:T(8,128)S(1)}, u32[]{:S(2)}, u32[]{:S(2)}) collective-permute-start(f32[48,128]{1,0:T(8,128)S(1)} %shard_map.154.refs_0_), channel_id=1, source_target_pairs={{0,4},{1,5},{2,6},{3,7},{4,0},{5,1},{6,2},{7,3},{8,12},{9,13},{10,... | collective-permute-start | bytes 73736 | tf_op jit(solution)/shard_map/ppermute | solution.py:108
  53.4 0.2 collective-permute-start.21
  53.7 1.6 %collective-permute-done.20.refs_2_ = f32[48,128]{1,0:T(8,128)S(1)} collective-permute-done((f32[48,128]{1,0:T(8,128)S(1)}, f32[48,128]{1,0:T(8,128)S(1)}, u32[]{:S(2)}, u32[]{:S(2)}) %collective-permute-start.20) | collective-permute-done | bytes 24608 | tf_op jit(solution)/shard_map/ppermute | solution.py:108
  55.3 3.8 %collective-permute-done.21.refs_3_ = f32[48,128]{1,0:T(8,128)S(1)} collective-permute-done((f32[48,128]{1,0:T(8,128)S(1)}, f32[48,128]{1,0:T(8,128)S(1)}, u32[]{:S(2)}, u32[]{:S(2)}) %collective-permute-start.21) | collective-permute-done | bytes 24608 | tf_op jit(solution)/shard_map/ppermute | solution.py:108
  59.1 1.1 %shard_map.155 = (bf16[16,512]{1,0:T(8,128)(2,1)}, f32[2]{0:T(128)}, bf16[16,512]{1,0:T(8,128)(2,1)}) custom-call(f32[48,128]{1,0:T(8,128)S(1)} %shard_map.154.refs_0_, f32[48,128]{1,0:T(8,128)S(1)} %collective-permute-done.19.refs_1_, f32[48,128]{1,0:T(8,128)S(1)} %collective-permute-done.20.refs_2_, f32[48,128]{1,0:T(8,128)S(1)} %collective-permute-done.21.refs_3_, ...), custom_call_target="tpu_custom_call" | custom-call | tf_op jit(solution)/shard_map/pallas_call | solution.py:641
  (37 shorter events, 0.2 us)
Async XLA Ops:
  0.6 6.5 %copy-start.10 = (f32[1,128]{1,0:T(1,128)S(1)}, f32[1,128]{1,0:T(1,128)}, u32[]{:S(2)}) copy-start(f32[1,128]{1,0:T(1,128)} %constant.2.clone.frequency_ref) | copy-start | bytes 1540
  0.6 0.7 %copy-start.4 = (bf16[16,512]{1,0:T(8,128)(2,1)S(1)}, bf16[16,512]{1,0:T(8,128)(2,1)}, u32[]{:S(2)}) copy-start(bf16[16,512]{1,0:T(8,128)(2,1)} %hidden_ref.3) | copy-start | bytes 49156
  0.7 0.7 %copy-start.6 = (f32[512]{0:T(512)S(1)}, f32[512]{0:T(512)}, u32[]{:S(2)}) copy-start(f32[512]{0:T(512)} %param.13) | copy-start | bytes 6148
  0.7 6.4 %copy-start.8 = (s32[1,16]{1,0:T(1,128)S(1)}, s32[1,16]{1,0:T(1,128)}, u32[]{:S(2)}) copy-start(s32[1,16]{1,0:T(1,128)} %lengths_ref.1) | copy-start | bytes 196
  0.7 6.4 %copy-start.9 = (s32[1,16]{1,0:T(1,128)S(1)}, s32[1,16]{1,0:T(1,128)}, u32[]{:S(2)}) copy-start(s32[1,16]{1,0:T(1,128)} %order_ref.1) | copy-start | bytes 196
  0.7 6.6 %copy-start = (bf16[4096,512]{1,0:T(8,128)(2,1)S(1)}, bf16[4096,512]{1,0:T(8,128)(2,1)}, u32[]{:S(2)}) copy-start(bf16[4096,512]{1,0:T(8,128)(2,1)} %refs_3_.2) | copy-start | bytes 12582916
  1.5 6.0 %collective-permute-start = (bf16[16,640]{1,0:T(8,128)(2,1)S(1)}, bf16[16,640]{1,0:T(8,128)(2,1)S(1)}, u32[]{:S(2)}, u32[]{:S(2)}) collective-permute-start(bf16[16,640]{1,0:T(8,128)(2,1)S(1)} %shard_map.140.message_ref.refs_0_), channel_id=1, source_target_pairs={{0,2},{1,3},{2,0},{3,1},{4,6},{5,7},{6,4},{7,5},{8,10},{9,11},{10,... | collective-permute-start | bytes 61448 | tf_op jit(solution)/shard_map/ppermute | solution.py:108
  4.5 4.9 %collective-permute-start.1 = (bf16[16,640]{1,0:T(8,128)(2,1)S(1)}, bf16[16,640]{1,0:T(8,128)(2,1)S(1)}, u32[]{:S(2)}, u32[]{:S(2)}) collective-permute-start(bf16[16,640]{1,0:T(8,128)(2,1)S(1)} %shard_map.140.message_ref.refs_0_), channel_id=1, source_target_pairs={{0,4},{1,5},{2,6},{3,7},{4,0},{5,1},{6,2},{7,3},{8,12},{9,13},{10,... | collective-permute-start | bytes 61448 | tf_op jit(solution)/shard_map/ppermute | solution.py:108
  7.1 5.6 %collective-permute-start.2 = (bf16[16,640]{1,0:T(8,128)(2,1)S(1)}, bf16[16,640]{1,0:T(8,128)(2,1)S(1)}, u32[]{:S(2)}, u32[]{:S(2)}) collective-permute-start(bf16[16,640]{1,0:T(8,128)(2,1)S(1)} %shard_map.140.message_ref.refs_0_), channel_id=1, source_target_pairs={{0,6},{1,7},{2,4},{3,5},{4,2},{5,3},{6,0},{7,1},{8,14},{9,15},{10,... | collective-permute-start | bytes 61448 | tf_op jit(solution)/shard_map/ppermute | solution.py:108
  7.3 5.8 %copy-start.2 = (bf16[320,1024]{1,0:T(8,128)(2,1)S(1)}, bf16[320,1024]{1,0:T(8,128)(2,1)}, u32[]{:S(2)}) copy-start(bf16[320,1024]{1,0:T(8,128)(2,1)} %refs_3_.3) | copy-start | bytes 1966084
  7.3 5.8 %copy-start.3 = (bf16[320,1024]{1,0:T(8,128)(2,1)S(1)}, bf16[320,1024]{1,0:T(8,128)(2,1)}, u32[]{:S(2)}) copy-start(bf16[320,1024]{1,0:T(8,128)(2,1)} %refs_4_.1) | copy-start | bytes 1966084
  7.5 6.6 %copy-start.11 = (f32[128]{0:T(128)S(1)}, f32[128]{0:T(128)}, u32[]{:S(2)}) copy-start(f32[128]{0:T(128)} %param.15) | copy-start | bytes 1540
  12.7 1.3 %collective-permute-start.3 = (bf16[4,16,640]{2,1,0:T(8,128)(2,1)S(1)}, bf16[4,16,640]{2,1,0:T(8,128)(2,1)S(1)}, u32[]{:S(2)}, u32[]{:S(2)}) collective-permute-start(bf16[4,16,640]{2,1,0:T(8,128)(2,1)S(1)} %shard_map.143.blocks_ref.refs_0_), channel_id=1, source_target_pairs={{0,1},{1,0},{2,3},{3,2},{4,5},{5,4},{6,7},{7,6},{8,9},{9,8},{10,11... | collective-permute-start | bytes 245768 | tf_op jit(solution)/shard_map/ppermute | solution.py:108
  13.4 7.6 %collective-permute-start.4 = (bf16[320,1024]{1,0:T(8,128)(2,1)S(1)}, bf16[320,1024]{1,0:T(8,128)(2,1)S(1)}, u32[]{:S(2)}, u32[]{:S(2)}) collective-permute-start(bf16[320,1024]{1,0:T(8,128)(2,1)S(1)} %shard_map.146), channel_id=1, source_target_pairs={{0,1},{1,0},{2,3},{3,2},{4,5},{5,4},{6,7},{7,6},{8,9},{9,8},{10,11... | collective-permute-start | bytes 1966088 | tf_op jit(solution)/shard_map/ppermute | solution.py:108
  14.0 17.8 %copy-start.1 = (bf16[512,4096]{1,0:T(8,128)(2,1)S(1)}, bf16[512,4096]{1,0:T(8,128)(2,1)}, u32[]{:S(2)}) copy-start(bf16[512,4096]{1,0:T(8,128)(2,1)} %weight_ref.7) | copy-start | bytes 12582916
  14.6 4.5 %collective-permute-start.5 = (bf16[16,512]{1,0:T(8,128)(2,1)S(1)}, bf16[16,512]{1,0:T(8,128)(2,1)S(1)}, u32[]{:S(2)}, u32[]{:S(2)}) collective-permute-start(bf16[16,512]{1,0:T(8,128)(2,1)S(1)} %shard_map.145.query_ref), channel_id=1, source_target_pairs={{0,2},{1,3},{2,0},{3,1},{4,6},{5,7},{6,4},{7,5},{8,10},{9,11},{10,... | collective-permute-start | bytes 49160 | tf_op jit(solution)/shard_map/ppermute | solution.py:108
  14.7 4.7 %collective-permute-start.6 = (bf16[16,512]{1,0:T(8,128)(2,1)S(1)}, bf16[16,512]{1,0:T(8,128)(2,1)S(1)}, u32[]{:S(2)}, u32[]{:S(2)}) collective-permute-start(bf16[16,512]{1,0:T(8,128)(2,1)S(1)} %shard_map.145.query_ref), channel_id=1, source_target_pairs={{0,4},{1,5},{2,6},{3,7},{4,0},{5,1},{6,2},{7,3},{8,12},{9,13},{10,... | collective-permute-start | bytes 49160 | tf_op jit(solution)/shard_map/ppermute | solution.py:108
  15.4 5.5 %collective-permute-start.7 = (bf16[16,512]{1,0:T(8,128)(2,1)S(1)}, bf16[16,512]{1,0:T(8,128)(2,1)S(1)}, u32[]{:S(2)}, u32[]{:S(2)}) collective-permute-start(bf16[16,512]{1,0:T(8,128)(2,1)S(1)} %shard_map.145.query_ref), channel_id=1, source_target_pairs={{0,6},{1,7},{2,4},{3,5},{4,2},{5,3},{6,0},{7,1},{8,14},{9,15},{10,... | collective-permute-start | bytes 49160 | tf_op jit(solution)/shard_map/ppermute | solution.py:108
  22.0 4.9 %collective-permute-start.8 = (bf16[16,640]{1,0:T(8,128)(2,1)S(1)}, bf16[16,640]{1,0:T(8,128)(2,1)S(1)}, u32[]{:S(2)}, u32[]{:S(2)}) collective-permute-start(bf16[16,640]{1,0:T(8,128)(2,1)S(1)} %get-tuple-element.25), channel_id=1, source_target_pairs={{0,2},{1,3},{2,0},{3,1},{4,6},{5,7},{6,4},{7,5},{8,10},{9,11},{10,... | collective-permute-start | bytes 61448 | tf_op jit(solution)/shard_map/ppermute | solution.py:108
  22.4 5.6 %collective-permute-start.9 = (bf16[16,640]{1,0:T(8,128)(2,1)S(1)}, bf16[16,640]{1,0:T(8,128)(2,1)S(1)}, u32[]{:S(2)}, u32[]{:S(2)}) collective-permute-start(bf16[16,640]{1,0:T(8,128)(2,1)S(1)} %get-tuple-element.26), channel_id=1, source_target_pairs={{0,4},{1,5},{2,6},{3,7},{4,0},{5,1},{6,2},{7,3},{8,12},{9,13},{10,... | collective-permute-start | bytes 61448 | tf_op jit(solution)/shard_map/ppermute | solution.py:108
  26.3 5.6 %collective-permute-start.10 = (bf16[16,640]{1,0:T(8,128)(2,1)S(1)}, bf16[16,640]{1,0:T(8,128)(2,1)S(1)}, u32[]{:S(2)}, u32[]{:S(2)}) collective-permute-start(bf16[16,640]{1,0:T(8,128)(2,1)S(1)} %get-tuple-element.27), channel_id=1, source_target_pairs={{0,6},{1,7},{2,4},{3,5},{4,2},{5,3},{6,0},{7,1},{8,14},{9,15},{10,... | collective-permute-start | bytes 61448 | tf_op jit(solution)/shard_map/ppermute | solution.py:108
  31.9 8.2 %copy-start.5 = (f32[512]{0:T(512)S(1)}, f32[512]{0:T(512)}, u32[]{:S(2)}) copy-start(f32[512]{0:T(512)} %param.19) | copy-start | bytes 6148
  31.9 27.2 %copy-start.7 = (s32[64]{0:T(128)S(1)}, s32[64]{0:T(128)}, u32[]{:S(2)}) copy-start(s32[64]{0:T(128)} %param.22) | copy-start | bytes 772
  32.4 1.3 %collective-permute-start.11 = (bf16[4,16,512]{2,1,0:T(8,128)(2,1)S(1)}, bf16[4,16,512]{2,1,0:T(8,128)(2,1)S(1)}, u32[]{:S(2)}, u32[]{:S(2)}) collective-permute-start(bf16[4,16,512]{2,1,0:T(8,128)(2,1)S(1)} %get-tuple-element.29), channel_id=1, source_target_pairs={{0,1},{1,0},{2,3},{3,2},{4,5},{5,4},{6,7},{7,6},{8,9},{9,8},{10,11... | collective-permute-start | bytes 196616 | tf_op jit(solution)/shard_map/ppermute | solution.py:108
  33.7 4.5 %collective-permute-start.12 = (bf16[16,512]{1,0:T(8,128)(2,1)S(1)}, bf16[16,512]{1,0:T(8,128)(2,1)S(1)}, u32[]{:S(2)}, u32[]{:S(2)}) collective-permute-start(bf16[16,512]{1,0:T(8,128)(2,1)S(1)} %get-tuple-element.31), channel_id=1, source_target_pairs={{0,2},{1,3},{2,0},{3,1},{4,6},{5,7},{6,4},{7,5},{8,10},{9,11},{10,... | collective-permute-start | bytes 49160 | tf_op jit(solution)/shard_map/ppermute | solution.py:108
  33.8 4.7 %collective-permute-start.13 = (bf16[16,512]{1,0:T(8,128)(2,1)S(1)}, bf16[16,512]{1,0:T(8,128)(2,1)S(1)}, u32[]{:S(2)}, u32[]{:S(2)}) collective-permute-start(bf16[16,512]{1,0:T(8,128)(2,1)S(1)} %get-tuple-element.32), channel_id=1, source_target_pairs={{0,4},{1,5},{2,6},{3,7},{4,0},{5,1},{6,2},{7,3},{8,12},{9,13},{10,... | collective-permute-start | bytes 49160 | tf_op jit(solution)/shard_map/ppermute | solution.py:108
  34.6 5.5 %collective-permute-start.14 = (bf16[16,512]{1,0:T(8,128)(2,1)S(1)}, bf16[16,512]{1,0:T(8,128)(2,1)S(1)}, u32[]{:S(2)}, u32[]{:S(2)}) collective-permute-start(bf16[16,512]{1,0:T(8,128)(2,1)S(1)} %get-tuple-element.33), channel_id=1, source_target_pairs={{0,6},{1,7},{2,4},{3,5},{4,2},{5,3},{6,0},{7,1},{8,14},{9,15},{10,... | collective-permute-start | bytes 49160 | tf_op jit(solution)/shard_map/ppermute | solution.py:108
  40.2 3.8 %collective-permute-start.15 = (bf16[16,512]{1,0:T(8,128)(2,1)S(1)}, bf16[16,512]{1,0:T(8,128)(2,1)S(1)}, u32[]{:S(2)}, u32[]{:S(2)}) collective-permute-start(bf16[16,512]{1,0:T(8,128)(2,1)S(1)} %get-tuple-element.34.first_ref), channel_id=1, source_target_pairs={{0,8},{8,0},{16,24},{24,16},{1,9},{9,1},{17,25},{25,17},{2,10},{10... | collective-permute-start | bytes 49160 | tf_op jit(solution)/shard_map/ppermute | solution.py:108
  41.7 3.7 %collective-permute-start.16 = (bf16[16,512]{1,0:T(8,128)(2,1)S(1)}, bf16[16,512]{1,0:T(8,128)(2,1)S(1)}, u32[]{:S(2)}, u32[]{:S(2)}) collective-permute-start(bf16[16,512]{1,0:T(8,128)(2,1)S(1)} %get-tuple-element.34.first_ref), channel_id=1, source_target_pairs={{0,16},{8,24},{16,0},{24,8},{1,17},{9,25},{17,1},{25,9},{2,18},{10... | collective-permute-start | bytes 49160 | tf_op jit(solution)/shard_map/ppermute | solution.py:108
  43.2 4.6 %collective-permute-start.17 = (bf16[16,512]{1,0:T(8,128)(2,1)S(1)}, bf16[16,512]{1,0:T(8,128)(2,1)S(1)}, u32[]{:S(2)}, u32[]{:S(2)}) collective-permute-start(bf16[16,512]{1,0:T(8,128)(2,1)S(1)} %get-tuple-element.34.first_ref), channel_id=1, source_target_pairs={{0,24},{8,16},{16,8},{24,0},{1,25},{9,17},{17,9},{25,1},{2,26},{10... | collective-permute-start | bytes 49160 | tf_op jit(solution)/shard_map/ppermute | solution.py:108
  48.0 1.2 %collective-permute-start.18 = (f32[48,128]{1,0:T(8,128)S(1)}, f32[48,128]{1,0:T(8,128)S(1)}, u32[]{:S(2)}, u32[]{:S(2)}) collective-permute-start(f32[48,128]{1,0:T(8,128)S(1)} %get-tuple-element.36.first_ref), channel_id=1, source_target_pairs={{0,1},{1,0},{2,3},{3,2},{4,5},{5,4},{6,7},{7,6},{8,9},{9,8},{10,11... | collective-permute-start | bytes 73736 | tf_op jit(solution)/shard_map/ppermute | solution.py:108
  49.3 4.4 %collective-permute-start.19 = (f32[48,128]{1,0:T(8,128)S(1)}, f32[48,128]{1,0:T(8,128)S(1)}, u32[]{:S(2)}, u32[]{:S(2)}) collective-permute-start(f32[48,128]{1,0:T(8,128)S(1)} %shard_map.154.refs_0_), channel_id=1, source_target_pairs={{0,2},{1,3},{2,0},{3,1},{4,6},{5,7},{6,4},{7,5},{8,10},{9,11},{10,... | collective-permute-start | bytes 73736 | tf_op jit(solution)/shard_map/ppermute | solution.py:108
  49.6 5.6 %collective-permute-start.20 = (f32[48,128]{1,0:T(8,128)S(1)}, f32[48,128]{1,0:T(8,128)S(1)}, u32[]{:S(2)}, u32[]{:S(2)}) collective-permute-start(f32[48,128]{1,0:T(8,128)S(1)} %shard_map.154.refs_0_), channel_id=1, source_target_pairs={{0,4},{1,5},{2,6},{3,7},{4,0},{5,1},{6,2},{7,3},{8,12},{9,13},{10,... | collective-permute-start | bytes 73736 | tf_op jit(solution)/shard_map/ppermute | solution.py:108
  53.4 5.6 %collective-permute-start.21 = (f32[48,128]{1,0:T(8,128)S(1)}, f32[48,128]{1,0:T(8,128)S(1)}, u32[]{:S(2)}, u32[]{:S(2)}) collective-permute-start(f32[48,128]{1,0:T(8,128)S(1)} %shard_map.154.refs_0_), channel_id=1, source_target_pairs={{0,6},{1,7},{2,4},{3,5},{4,2},{5,3},{6,0},{7,1},{8,14},{9,15},{10,... | collective-permute-start | bytes 73736 | tf_op jit(solution)/shard_map/ppermute | solution.py:108

commit v4 on v1

--- a/solution.py
+++ b/solution.py
@@ -2,6 +2,8 @@
 import jax
 import jax.numpy as jnp
 from jax import lax
+from jax.experimental import pallas as pl
+from jax.experimental.pallas import tpu as pltpu
 from jax.sharding import PartitionSpec as P
 
 EPSILON = 1e-06
@@ -99,6 +101,639 @@
         block_sum.reshape(stmt_count, head_count),
         numerators.reshape(stmt_count, head_count, head_dim),
     )
+
+
+def flip(array, axis, offset):
+    size = lax.axis_size(axis)
+    return lax.ppermute(array, axis, [(i, i ^ offset) for i in range(size)])
+
+
+def in_vmem(body, outputs, *operands, limit=8, flops=1_000_000):
+    whole = pl.BlockSpec(memory_space=pltpu.VMEM)
+    moved = sum(operand.size * operand.dtype.itemsize for operand in operands)
+    return pl.pallas_call(
+        body,
+        out_shape=outputs,
+        in_specs=[whole] * len(operands),
+        out_specs=jax.tree.map(lambda _: whole, outputs),
+        compiler_params=pltpu.CompilerParams(vmem_limit_bytes=limit << 20),
+        cost_estimate=pl.CostEstimate(flops=flops, bytes_accessed=moved, transcendentals=0),
+    )(*operands)
+
+
+def shaped(shape, kind):
+    return jax.ShapeDtypeStruct(shape, kind)
+
+
+def lane_pieces(values, width=128):
+    rows = values[0].shape[0]
+    lane = lax.broadcasted_iota(jnp.int32, (rows, width), 1)
+    out = jnp.zeros((rows, width), jnp.float32)
+    for place, value in enumerate(values):
+        rest = value
+        for part in range(3):
+            piece = rest.astype(jnp.bfloat16).astype(jnp.float32)
+            out = jnp.where(lane == 3 * place + part, piece, out)
+            rest = rest - piece
+    return out.astype(jnp.bfloat16)
+
+
+def lane_sum(block, place):
+    lane = lax.broadcasted_iota(jnp.int32, block.shape, 1)
+    own = (lane >= 3 * place) & (lane < 3 * place + 3)
+    return jnp.sum(jnp.where(own, block, 0.0), axis=1, keepdims=True)
+
+
+def open_window(out_ref):
+    out_ref[...] = jnp.zeros_like(out_ref)
+
+
+def prepare_inputs(window_ref, hidden_ref, gain_ref, message_ref):
+    del window_ref
+    inputs = hidden_ref[...].astype(jnp.float32)
+    width = inputs.shape[1]
+    message_ref[:, :width] = (inputs * gain_ref[...]).astype(jnp.bfloat16)
+    message_ref[:, width:] = lane_pieces([jnp.sum(inputs * inputs, axis=1, keepdims=True)])
+
+
+def positions_and_ranges(
+    message_ref, frequency_ref, lengths_ref, order_ref, rope_ref, range_ref
+):
+    del message_ref
+    count = lengths_ref.shape[1]
+    half = frequency_ref.shape[1] // 2
+    row = lax.broadcasted_iota(jnp.int32, (count, count), 0)
+    column = lax.broadcasted_iota(jnp.int32, (count, count), 1)
+    lengths = jnp.broadcast_to(lengths_ref[...], (count, count)).astype(jnp.float32)
+    length = jnp.sum(jnp.where(row == column, lengths, 0.0), axis=1, keepdims=True)
+    order = jnp.broadcast_to(order_ref[...], (count, count))
+    placed = order == row
+    slot = jnp.sum(jnp.where(placed, column, 0).astype(jnp.float32), axis=1, keepdims=True)
+    packed = jnp.sum(jnp.where(placed, length, 0.0), axis=0, keepdims=True)
+    earlier = column.astype(jnp.float32) < slot
+    start = jnp.sum(jnp.where(earlier, packed, 0.0), axis=1, keepdims=True)
+    range_ref[:, :128] = jnp.broadcast_to(start, (count, 128))
+    range_ref[:, 128:] = jnp.broadcast_to(start + length, (count, 128))
+    cosine, sine = cosine_and_sine((length - 1.0) * frequency_ref[...])
+    lane = lax.broadcasted_iota(jnp.int32, cosine.shape, 1)
+    rope_ref[:, : 2 * half] = cosine
+    rope_ref[:, 2 * half :] = jnp.where(lane < half, -sine, sine)
+
+
+def core_number():
+    return lax.axis_index("pack") & 1
+
+
+def chip_number():
+    return lax.axis_index("pack") >> 1
+
+
+def send_across(array, axis, offset, sender):
+    groups, pack = lax.axis_size("dp"), lax.axis_size("pack")
+    pairs = []
+    for group in range(groups):
+        for place in range(pack):
+            if place % 2 != sender:
+                target = (group, place ^ 1)
+            elif axis == "dp":
+                target = (group ^ offset, place ^ 1)
+            else:
+                target = (group, place ^ (2 * offset) ^ 1)
+            pairs.append((group * pack + place, target[0] * pack + target[1]))
+    return lax.ppermute(array, ("dp", "pack"), pairs)
+
+
+def copy_tokens(_, key_ref, value_ref, out_ref):
+    out_ref[0] = key_ref[...]
+    out_ref[1] = value_ref[...]
+
+
+def join_cores(own_ref, other_ref, pair_ref):
+    core = core_number()
+    pair_ref[core] = own_ref[...]
+    pair_ref[1 - core] = other_ref[...]
+
+
+def join_blocks(*refs):
+    out_ref = refs[-1]
+    for i in range(out_ref.shape[0]):
+        out_ref[i] = refs[i][...]
+
+
+def project_pair(pair_ref, offset, weight_ref):
+    chip = chip_number() ^ offset
+    width = weight_ref.shape[1]
+    total = 0.0
+    for core in range(2):
+        rows = pl.ds(pl.multiple_of((2 * chip + core) * width, width), width)
+        total = total + jnp.dot(
+            pair_ref[core, :, :width], weight_ref[rows, :], preferred_element_type=jnp.float32
+        )
+    return total
+
+
+def project_own_pair(pair_ref, weight_ref, total_ref):
+    total_ref[...] = project_pair(pair_ref, 0, weight_ref)
+
+
+def make_queries(
+    pair_ref, blocks_ref, total_ref, weight_ref, gain_ref, rope_ref, query_ref, *, core, model_width
+):
+    width = total_ref.shape[1]
+    head_dim = gain_ref.shape[1]
+
+    @pl.when(core_number() == core)
+    def _():
+        projected = total_ref[...]
+        squares = jnp.zeros((total_ref.shape[0], 1), jnp.float32)
+        for j in range(2):
+            squares = squares + lane_sum(pair_ref[j, :, width:].astype(jnp.float32), 0)
+        for i in range(blocks_ref.shape[0]):
+            projected = projected + project_pair(blocks_ref.at[i], i + 1, weight_ref)
+            for j in range(2):
+                squares = squares + lane_sum(blocks_ref[i, j, :, width:].astype(jnp.float32), 0)
+        projected = projected * lax.rsqrt(squares / model_width + EPSILON)
+        cosine = rope_ref[:, :head_dim]
+        sine = rope_ref[:, head_dim:]
+        for head in range(width // head_dim):
+            place = slice(head * head_dim, (head + 1) * head_dim)
+            query = projected[:, place]
+            mean = jnp.mean(query * query, axis=1, keepdims=True)
+            query = query * lax.rsqrt(mean + EPSILON) * gain_ref[...]
+            turned = pltpu.roll(query, head_dim // 2, 1)
+            query_ref[:, place] = (query * cosine + turned * sine).astype(jnp.bfloat16)
+
+
+def join_queries(first_ref, second_ref, out_ref):
+    width = first_ref.shape[1]
+    out_ref[:, :width] = first_ref[...]
+    out_ref[:, width:] = second_ref[...]
+
+
+def token_masks(range_ref, tokens, group):
+    me = lax.axis_index("pack")
+    masks = []
+    for owner in (me, me ^ 1):
+        index = lax.broadcasted_iota(jnp.int32, (range_ref.shape[0], tokens), 1) + owner * tokens
+        index = index.astype(jnp.float32)
+        mask = (index >= range_ref[:, :1]) & (index < range_ref[:, 128:129])
+        masks.append(jnp.concatenate([mask.astype(jnp.float32)] * group, axis=0) > 0.5)
+    return masks
+
+
+def attend_head(query, head, key_ref, value_ref, other_ref, masks):
+    head_dim = 128
+    group = query.shape[1] // head_dim
+    grouped = jnp.concatenate(
+        [query[:, h * head_dim : (h + 1) * head_dim] for h in range(group)], axis=0
+    )
+    column = pl.ds(pl.multiple_of(head * head_dim, head_dim), head_dim)
+    keys = (key_ref[:, column], other_ref[0, :, column])
+    values = (value_ref[:, column], other_ref[1, :, column])
+    scores = []
+    for part in range(2):
+        raw = lax.dot_general(
+            grouped, keys[part], (((1,), (1,)), ((), ())), preferred_element_type=jnp.float32
+        )
+        scores.append(jnp.where(masks[part], raw * (head_dim**-0.5), MASKED_LOGIT))
+    highest = jnp.maximum(
+        jnp.max(scores[0], axis=1, keepdims=True), jnp.max(scores[1], axis=1, keepdims=True)
+    )
+    total = 0.0
+    numerators = 0.0
+    for part in range(2):
+        weights = jnp.exp(scores[part] - highest)
+        total = total + jnp.sum(weights, axis=1, keepdims=True)
+        numerators = numerators + jnp.dot(
+            weights.astype(jnp.bfloat16), values[part], preferred_element_type=jnp.float32
+        )
+    return highest, total, numerators
+
+
+def attend_remote(*refs):
+    query_refs, refs = refs[:3], refs[3:]
+    key_ref, value_ref, other_ref, range_ref = refs[:4]
+
+    @pl.when(core_number() == 1)
+    def _():
+        rows = query_refs[0].shape[0]
+        width = query_refs[0].shape[1] // 2
+        masks = token_masks(range_ref, key_ref.shape[0], width // 128)
+        for i, (query_ref, out_ref) in enumerate(zip(query_refs, refs[4:])):
+            stats = []
+            for j in range(2):
+                head = 2 * (chip_number() ^ (i + 1)) + j
+                query = query_ref[:, j * width : (j + 1) * width]
+                highest, total, numerators = attend_head(
+                    query, head, key_ref, value_ref, other_ref, masks
+                )
+                for h in range(width // 128):
+                    part = slice(h * rows, (h + 1) * rows)
+                    place = slice(j * width + h * 128, j * width + (h + 1) * 128)
+                    out_ref[:, place] = numerators[part].astype(jnp.bfloat16)
+                    stats += [highest[part], total[part]]
+            out_ref[:, 2 * width :] = lane_pieces(stats)
+
+
+def attend_own(query_ref, key_ref, value_ref, other_ref, range_ref, out_ref, stats_ref):
+    @pl.when(core_number() == 0)
+    def _():
+        width = query_ref.shape[1] // 2
+        masks = token_masks(range_ref, key_ref.shape[0], width // 128)
+        for j in range(2):
+            query = query_ref[:, j * width : (j + 1) * width]
+            highest, total, numerators = attend_head(
+                query, 2 * chip_number() + j, key_ref, value_ref, other_ref, masks
+            )
+            out_ref[j] = numerators
+            stats_ref[j, :, :128] = jnp.broadcast_to(highest, (highest.shape[0], 128))
+            stats_ref[j, :, 128:] = jnp.broadcast_to(total, (highest.shape[0], 128))
+
+
+def merge_partials(
+    own_ref, stats_ref, first_ref, second_ref, third_ref, attended_ref, other_attended_ref
+):
+    @pl.when(core_number() == 0)
+    def _():
+        rows, width = attended_ref.shape
+        others = (first_ref, second_ref, third_ref)
+        stats = [ref[:, 2 * width :].astype(jnp.float32) for ref in others]
+        for j, out_ref in enumerate((attended_ref, other_attended_ref)):
+            for h in range(width // 128):
+                part = slice(h * rows, (h + 1) * rows)
+                place = slice(h * 128, (h + 1) * 128)
+                far_place = slice(j * width + h * 128, j * width + (h + 1) * 128)
+                slot = 2 * (j * (width // 128) + h)
+                maxima = [stats_ref[j, part, :1]] + [lane_sum(s, slot) for s in stats]
+                totals = [stats_ref[j, part, 128:129]] + [lane_sum(s, slot + 1) for s in stats]
+                numerators = [own_ref[j, part, :]]
+                numerators += [ref[:, far_place].astype(jnp.float32) for ref in others]
+                highest = maxima[0]
+                for value in maxima[1:]:
+                    highest = jnp.maximum(highest, value)
+                denominator = 0.0
+                summed = 0.0
+                for value, total, numerator in zip(maxima, totals, numerators):
+                    factor = jnp.exp(value - highest)
+                    denominator = denominator + total * factor
+                    summed = summed + numerator * factor
+                out_ref[:, place] = (summed / denominator).astype(jnp.bfloat16)
+
+
+def project_out(attended_ref, weight_ref, *refs, core, offsets):
+    out_ref = refs[-1]
+
+    @pl.when(core_number() == core)
+    def _():
+        width = out_ref.shape[2]
+        attended = attended_ref[...]
+        for i, offset in enumerate(offsets):
+            column = pl.ds(pl.multiple_of((chip_number() ^ offset) * width, width), width)
+            out_ref[i] = jnp.dot(
+                attended, weight_ref[:, column], preferred_element_type=jnp.float32
+            ).astype(out_ref.dtype)
+
+
+def add_partials(own_ref, other_ref, *out_refs, first):
+    for i, out_ref in enumerate(out_refs):
+        total = own_ref[first + i] + other_ref[i].astype(jnp.float32)
+        out_ref[...] = total.astype(out_ref.dtype)
+
+
+def finish_hidden(
+    kept_ref,
+    first_ref,
+    second_ref,
+    third_ref,
+    own_ref,
+    other_ref,
+    own_gain_ref,
+    other_gain_ref,
+    sent_ref,
+    state_ref,
+):
+    width = own_ref.shape[1]
+
+    @pl.when(core_number() == 1)
+    def _():
+        squares = 0.0
+        inputs = (other_ref, own_ref)
+        gains = (other_gain_ref, own_gain_ref)
+        for core in range(2):
+            place = slice(core * width, (core + 1) * width)
+            hidden = inputs[core][...].astype(jnp.float32) + kept_ref[:, place]
+            for ref in (first_ref, second_ref, third_ref):
+                hidden = hidden + ref[:, place].astype(jnp.float32)
+            scaled = hidden * gains[core][...]
+            state_ref[:, place] = scaled
+            sent_ref[:, place] = scaled.astype(jnp.bfloat16)
+            squares = squares + jnp.sum(hidden * hidden, axis=1, keepdims=True)
+        state_ref[:, 2 * width :] = jnp.broadcast_to(squares, (squares.shape[0], 128))
+
+
+def gram_part(state_ref, first_ref, second_ref, third_ref, out_ref, near_ref, far_ref):
+    @pl.when(core_number() == 0)
+    def _():
+        rows = first_ref.shape[0]
+        width = near_ref.shape[1]
+        near_ref[:rows] = state_ref[:, :width].astype(jnp.bfloat16)
+        far_ref[:rows] = state_ref[:, width : 2 * width].astype(jnp.bfloat16)
+        for i, ref in enumerate((first_ref, second_ref, third_ref)):
+            near_ref[(i + 1) * rows : (i + 2) * rows] = ref[:, :width]
+            far_ref[(i + 1) * rows : (i + 2) * rows] = ref[:, width:]
+        gram = 0.0
+        for ref in (near_ref, far_ref):
+            vectors = ref[...]
+            gram = gram + lax.dot_general(
+                vectors, vectors, (((1,), (1,)), ((), ())), preferred_element_type=jnp.float32
+            )
+        half = gram.shape[0] // 2
+        out_ref[:half, : 2 * half] = gram[:half]
+        out_ref[:half, 2 * half :] = gram[half:]
+        out_ref[half:, :] = state_ref[:, 2 * width :]
+
+
+def sum_grams(own_ref, first_ref, second_ref, third_ref, out_ref):
+    out_ref[...] = own_ref[...] + first_ref[...] + second_ref[...] + third_ref[...]
+
+
+def losses_and_gradient(
+    summed_ref,
+    other_summed_ref,
+    near_ref,
+    other_far_ref,
+    state_ref,
+    other_state_ref,
+    gain_ref,
+    partner_ref,
+    pooled_ref,
+    loss_ref,
+    grad_ref,
+    *,
+    model_width,
+):
+    group = lax.axis_index("dp")
+    me = lax.axis_index("pack")
+    first_core = core_number() == 0
+    count, width = near_ref.shape
+    rows = state_ref.shape[0]
+    half = count // 2
+    summed = jnp.where(first_core, other_summed_ref[...], summed_ref[...])
+    gram = jnp.concatenate([summed[:half, :count], summed[:half, count:]], axis=0)
+    squares = summed[half:, :1]
+    shape = (count, count)
+    row = lax.broadcasted_iota(jnp.int32, shape, 0)
+    column = lax.broadcasted_iota(jnp.int32, shape, 1)
+    row_id = ((group ^ (row // rows)) * rows) + row % rows
+    column_id = ((group ^ (column // rows)) * rows) + column % rows
+    partners = jnp.broadcast_to(partner_ref[...], shape)
+    row_partner = jnp.sum(
+        jnp.where(column == row_id, partners, 0).astype(jnp.float32), axis=1, keepdims=True
+    )
+    column_partner = jnp.sum(
+        jnp.where(row_id == column_id, row_partner, 0.0), axis=0, keepdims=True
+    )
+    own_partner = column_id.astype(jnp.float32) == row_partner
+    other_partner = row_id.astype(jnp.float32) == column_partner
+    diagonal = row == column
+    on_diagonal = jnp.where(diagonal, gram, 0.0)
+    row_scale = lax.rsqrt(jnp.sum(on_diagonal, axis=1, keepdims=True))
+    column_scale = lax.rsqrt(jnp.sum(on_diagonal, axis=0, keepdims=True))
+    cosines = gram * row_scale * column_scale
+    logits = jnp.where(diagonal, MASKED_LOGIT, cosines * (1.0 / SOFTMAX_WARMTH))
+    row_high = jnp.max(logits, axis=1, keepdims=True)
+    row_lse = row_high + jnp.log(jnp.sum(jnp.exp(logits - row_high), axis=1, keepdims=True))
+    column_high = jnp.max(logits, axis=0, keepdims=True)
+    column_lse = column_high + jnp.log(
+        jnp.sum(jnp.exp(logits - column_high), axis=0, keepdims=True)
+    )
+    loss = row_lse - jnp.sum(jnp.where(own_partner, logits, 0.0), axis=1, keepdims=True)
+    own = loss_ref.shape[0]
+    index = lax.broadcasted_iota(jnp.int32, (count, 1), 0)
+    for i in range(own):
+        loss_ref[i] = jnp.sum(jnp.where(index == me * own + i, loss, 0.0))
+    weights = (
+        jnp.exp(logits - row_lse)
+        + jnp.exp(logits - column_lse)
+        - own_partner.astype(jnp.float32)
+        - other_partner.astype(jnp.float32)
+    )[:rows]
+    inner = jnp.sum(weights * cosines[:rows], axis=1, keepdims=True)
+    scaled_weights = weights * column_scale
+    upper = scaled_weights.astype(jnp.bfloat16)
+    lower = (scaled_weights - upper.astype(jnp.float32)).astype(jnp.bfloat16)
+    own_scale = row_scale[:rows]
+    pooled_scale = lax.rsqrt(squares / model_width + EPSILON)
+    grad_gain = gain_ref[...] * (model_width**0.5 / SOFTMAX_WARMTH)
+
+    def write(vectors, scaled):
+        gradient = jnp.dot(upper, vectors, preferred_element_type=jnp.float32) + jnp.dot(
+            lower, vectors, preferred_element_type=jnp.float32
+        )
+        gradient = (gradient - scaled * (own_scale * inner)) * own_scale
+        grad_ref[...] = (gradient * grad_gain).astype(jnp.bfloat16)
+        pooled_ref[...] = (scaled * pooled_scale).astype(jnp.bfloat16)
+
+    @pl.when(first_core)
+    def _():
+        write(near_ref[...], other_state_ref[:, :width])
+
+    @pl.when(core_number() == 1)
+    def _():
+        write(other_far_ref[...], state_ref[:, width : 2 * width])
+
+
+def core_roles(
+    hidden_in,
+    attn_gain,
+    w_query,
+    query_gain,
+    cached_keys,
+    cached_values,
+    w_out,
+    final_gain,
+    lengths,
+    pack_order,
+    partner,
+):
+    pack_size = lax.axis_size("pack")
+    stmts, width = hidden_in.shape
+    model_width = width * pack_size
+    head_dim = query_gain.shape[0]
+    tokens = cached_keys.shape[0]
+    chips = pack_size // 2
+    others = range(1, chips)
+    total = partner.shape[0]
+    bf16 = jnp.bfloat16
+    f32 = jnp.float32
+    final_gain = final_gain[None]
+    query_gain = query_gain[None]
+    half = np.arange(head_dim // 2)
+    frequency = (ROPE_BASE ** (-half * 2.0 / head_dim)).astype(np.float32)
+    frequency = jnp.asarray(np.concatenate([frequency, frequency])[None])
+    whole = pl.BlockSpec(memory_space=pltpu.VMEM)
+
+    window = pl.pallas_call(
+        open_window,
+        out_shape=shaped((8, 128), f32),
+        out_specs=whole,
+        compiler_params=pltpu.CompilerParams(vmem_limit_bytes=1 << 20),
+        cost_estimate=pl.CostEstimate(flops=1 << 34, bytes_accessed=0, transcendentals=0),
+    )()
+    message = in_vmem(
+        prepare_inputs, shaped((stmts, width + 128), bf16), window, hidden_in, attn_gain[None]
+    )
+    pair = in_vmem(
+        join_cores, shaped((2,) + message.shape, bf16), message, flip(message, "pack", 1)
+    )
+    received = [send_across(pair, "pack", k, 0) for k in others]
+    own_projected = in_vmem(
+        project_own_pair, shaped((stmts, width), f32), pair, w_query, limit=16, flops=1 << 26
+    )
+    rope, ranges = in_vmem(
+        positions_and_ranges,
+        (shaped((stmts, 2 * head_dim), f32), shaped((stmts, 256), f32)),
+        message,
+        frequency,
+        lengths,
+        pack_order,
+    )
+    blocks = in_vmem(
+        join_blocks, shaped((chips - 1,) + pair.shape, bf16), *received, own_projected, rope
+    )
+    flipped_blocks = flip(blocks, "pack", 1)
+
+    def queries_on(core, blocks, flops):
+        return in_vmem(
+            lambda *refs: make_queries(*refs, core=core, model_width=model_width),
+            shaped((stmts, width), bf16),
+            pair,
+            blocks,
+            own_projected,
+            w_query,
+            query_gain,
+            rope,
+            limit=16,
+            flops=flops,
+        )
+
+    late_queries = queries_on(1, blocks, 1 << 27)
+    held = in_vmem(
+        copy_tokens,
+        shaped((2,) + cached_keys.shape, bf16),
+        late_queries,
+        cached_keys,
+        cached_values,
+    )
+    other_held = flip(held, "pack", 1)
+    second_queries = flip(late_queries, "pack", 1)
+    first_queries = queries_on(0, flipped_blocks, 1 << 36)
+    queries = in_vmem(
+        join_queries, shaped((stmts, 2 * width), bf16), first_queries, second_queries
+    )
+    received = [send_across(queries, "pack", k, 0) for k in others]
+    group_rows = stmts * (width // head_dim)
+    own_part, own_stats = in_vmem(
+        attend_own,
+        (shaped((2, group_rows, head_dim), f32), shaped((2, group_rows, 256), f32)),
+        queries,
+        cached_keys,
+        cached_values,
+        other_held,
+        ranges,
+        flops=1 << 27,
+    )
+    partials = in_vmem(
+        attend_remote,
+        (shaped((stmts, 2 * width + 128), bf16),) * (chips - 1),
+        *received,
+        cached_keys,
+        cached_values,
+        other_held,
+        ranges,
+        flops=1 << 28,
+    )
+    received = [send_across(part, "pack", k, 1) for k, part in zip(others, partials)]
+    attended, other_attended = in_vmem(
+        merge_partials,
+        (shaped((stmts, width), bf16),) * 2,
+        own_part,
+        own_stats,
+        *received,
+    )
+    other_attended = flip(other_attended, "pack", 1)
+
+    def projected_on(core, attended, offsets, kind, *after):
+        return in_vmem(
+            lambda *refs: project_out(*refs, core=core, offsets=offsets),
+            shaped((len(offsets), stmts, 2 * width), kind),
+            attended,
+            w_out,
+            *after,
+            limit=16,
+            flops=1 << 27,
+        )
+
+    own_out = projected_on(0, attended, (1, 2, 3, 0), f32)
+    early = projected_on(1, other_attended, (1, 2), bf16, own_out)
+    late = projected_on(1, other_attended, (3, 0), bf16, early)
+    early = flip(early, "pack", 1)
+    late = flip(late, "pack", 1)
+    chip_part = shaped((stmts, 2 * width), bf16)
+    to_chips = in_vmem(
+        lambda *refs: add_partials(*refs, first=0), (chip_part, chip_part), own_out, early
+    )
+    last, kept = in_vmem(
+        lambda *refs: add_partials(*refs, first=2),
+        (chip_part, shaped((stmts, 2 * width), f32)),
+        own_out,
+        late,
+    )
+    other_kept = flip(kept, "pack", 1)
+    received = [send_across(part, "pack", k, 0) for k, part in zip(others, (*to_chips, last))]
+    vector, state = in_vmem(
+        finish_hidden,
+        (shaped((stmts, 2 * width), bf16), shaped((stmts, 2 * width + 128), f32)),
+        other_kept,
+        *received,
+        hidden_in,
+        flip(hidden_in, "pack", 1),
+        final_gain,
+        flip(final_gain, "pack", 1),
+    )
+    other_state = flip(state, "pack", 1)
+    received = [send_across(vector, "dp", k, 1) for k in range(1, lax.axis_size("dp"))]
+    gram, near, far = in_vmem(
+        gram_part,
+        (shaped((total // 2 + stmts, 128), f32),) + (shaped((total, width), bf16),) * 2,
+        other_state,
+        *received,
+    )
+    other_far = flip(far, "pack", 1)
+    other_gram = flip(gram, "pack", 1)
+    received = [send_across(gram, "pack", k, 0) for k in others]
+    summed = in_vmem(sum_grams, shaped(gram.shape, f32), other_gram, *received)
+    pooled, loss_rows, grad_hidden = pl.pallas_call(
+        lambda *refs: losses_and_gradient(*refs, model_width=model_width),
+        out_shape=(
+            shaped((stmts, width), bf16),
+            shaped((stmts // pack_size,), f32),
+            shaped((stmts, width), bf16),
+        ),
+        in_specs=[whole] * 8,
+        out_specs=(whole, pl.BlockSpec(memory_space=pltpu.SMEM), whole),
+        compiler_params=pltpu.CompilerParams(vmem_limit_bytes=8 << 20),
+    )(
+        summed,
+        flip(summed, "pack", 1),
+        near,
+        other_far,
+        state,
+        other_state,
+        final_gain,
+        partner[None],
+    )
+    return (pooled, loss_rows, grad_hidden)
 
 
 def local(
@@ -226,6 +861,7 @@
 
 
 def solution(mesh):
+    body = core_roles if mesh.shape["pack"] == 8 and mesh.shape["dp"] == 4 else local
     in_specs = (
         P("dp", "pack"),
         P("pack"),
@@ -240,4 +876,4 @@
         P(),
     )
     out_specs = (P("dp", "pack"), P(("dp", "pack")), P("dp", "pack"))
-    return jax.shard_map(local, mesh=mesh, in_specs=in_specs, out_specs=out_specs, check_vma=False)
+    return jax.shard_map(body, mesh=mesh, in_specs=in_specs, out_specs=out_specs, check_vma=False)

time: 82 us -> 50.5 us (0.62)
  blocking collectives: 27.4 us -> 0 us
  starting transfers between devices: 13.1 us -> 27.2 us
  matrix products: 7.4 us -> 0 us
  other arithmetic: 6.91 us -> 0 us
  local copies, waits for them, and re-layouts: 5.44 us -> 0.71 us
  Pallas kernels: 0 us -> 4.36 us
  waiting for transfers between devices: 20 us -> 17.2 us
    ppermute x0 -> x32, starting transfers between devices: none -> 27.2 us  [the longest x18 19.2 us: send_across(): return lax.ppermute(array, ('dp', 'pack'), pairs)]
    all_to_all x3 -> x0, waiting for transfers between devices: 20 us -> none  [gather_blocks(): lax.all_to_all(jnp.broadcast_to(block[None], (size,) + block.shape), axis...]
    all_to_all x2 -> x0, blocking collectives: 19.2 us -> none  [the longest x1 9.67 us: local(): message = lax.all_to_all(message, 'pack', 0, 0)]
    ppermute x0 -> x32, waiting for transfers between devices: none -> 17.2 us  [the longest x18 11.9 us: send_across(): return lax.ppermute(array, ('dp', 'pack'), pairs)]
    all_to_all x3 -> x0, starting transfers between devices: 13.1 us -> none  [gather_blocks(): lax.all_to_all(jnp.broadcast_to(block[None], (size,) + block.shape), axis...]
    all_gather x1 -> x0, blocking collectives: 8.24 us -> none  [local(): lax.all_gather(scaled_out.astype(jnp.bfloat16), 'dp', axis=0, tiled=True)]
    dot_general x6 -> x0, matrix products: 7.4 us -> none  [the longest x1 2.85 us: local(): jnp.dot(attended.reshape(stmt_count, width), w_out, preferred_element_typ...]
    pallas_call x0 -> x22, Pallas kernels: none -> 4.36 us  [the longest x20 3.26 us: in_vmem(): pl.pallas_call(body, out_shape=outputs, in_specs=[whole] * len(operands),...]
  transfers between devices with their start and end apart: 3 -> 32, of which waited for: 3 -> 15; matrix products, arithmetic and copies ran while one was open for 4% -> 0% of each run, Pallas kernels for 0% -> 5%
where the time goes in v4:
time: 50.5 us; the launch traced here: 50.3 us
  starting transfers between devices  27.2 us (54%)
  waiting for transfers between devices  17.2 us (34%)
  Pallas kernels  4.36 us (9%)
  between operations  0.86 us (2%)
  local copies, waits for them, and re-layouts  0.71 us (1%)
    ppermute x18, starting transfers between devices, send_across(): return lax.ppermute(array, ('dp', 'pack'), pairs)  19.2 us
    ppermute x18, waiting for transfers between devices, send_across(): return lax.ppermute(array, ('dp', 'pack'), pairs)  11.9 us
    ppermute x14, starting transfers between devices, flip(): return lax.ppermute(array, axis, [(i, i ^ offset) for i in range(size)])  7.96 us
    ppermute x14, waiting for transfers between devices, flip(): return lax.ppermute(array, axis, [(i, i ^ offset) for i in range(size)])  5.24 us
    pallas_call x20, Pallas kernels, in_vmem(): pl.pallas_call(body, out_shape=outputs, in_specs=[whole] * len(operands),...  3.26 us
    pallas_call x1, Pallas kernels, core_roles(): pl.pallas_call(lambda *refs: losses_and_gradient(*refs, model_width=model...  1.1 us
  transfers between devices with their start and end apart: 32, of which 15 were waited for; matrix products, arithmetic and copies ran while one was open for 0% of the time, Pallas kernels for 5%

profile of v4, /device:TPU:0, one launch (start us, length us, event | category | flops | bytes accessed | tf_op | source)
XLA Modules:
  0.0 50.3 jit_solution(2243413840377227666)
XLA Ops:
  0.7 0.7 %copy-done.4 = bf16[16,512]{1,0:T(8,128)(2,1)S(1)} copy-done((bf16[16,512]{1,0:T(8,128)(2,1)S(1)}, bf16[16,512]{1,0:T(8,128)(2,1)}, u32[]{:S(2)}) %copy-start.4) | copy-done | bytes 16408
  1.5 0.5 collective-permute-start
  1.9 0.8 %collective-permute-done.other_ref = bf16[16,640]{1,0:T(8,128)(2,1)S(1)} collective-permute-done((bf16[16,640]{1,0:T(8,128)(2,1)S(1)}, bf16[16,640]{1,0:T(8,128)(2,1)S(1)}, u32[]{:S(2)}, u32[]{:S(2)}) %collective-permute-start) | collective-permute-done | bytes 20512 | tf_op jit(solution)/shard_map/ppermute | solution.py:108
  2.8 2.7 %collective-permute-start.1 = (bf16[2,16,640]{2,1,0:T(8,128)(2,1)S(1)}, bf16[2,16,640]{2,1,0:T(8,128)(2,1)S(1)}, u32[]{:S(2)}, u32[]{:S(2)}) collective-permute-start(bf16[2,16,640]{2,1,0:T(8,128)(2,1)S(1)} %shard_map.141.pair_ref.refs_0_), channel_id=1, source_target_pairs={{0,3},{1,0},{2,1},{3,2},{4,7},{5,4},{6,5},{7,6},{8,11},{9,8},{10,9... | collective-permute-start | bytes 122888 | tf_op jit(solution)/shard_map/ppermute | solution.py:203
  5.5 1.4 %collective-permute-start.2 = (bf16[2,16,640]{2,1,0:T(8,128)(2,1)S(1)}, bf16[2,16,640]{2,1,0:T(8,128)(2,1)S(1)}, u32[]{:S(2)}, u32[]{:S(2)}) collective-permute-start(bf16[2,16,640]{2,1,0:T(8,128)(2,1)S(1)} %shard_map.141.pair_ref.refs_0_), channel_id=1, source_target_pairs={{0,5},{1,0},{2,7},{3,2},{4,1},{5,4},{6,3},{7,6},{8,13},{9,8},{10,1... | collective-permute-start | bytes 122888 | tf_op jit(solution)/shard_map/ppermute | solution.py:203
  6.8 1.2 %collective-permute-start.3 = (bf16[2,16,640]{2,1,0:T(8,128)(2,1)S(1)}, bf16[2,16,640]{2,1,0:T(8,128)(2,1)S(1)}, u32[]{:S(2)}, u32[]{:S(2)}) collective-permute-start(bf16[2,16,640]{2,1,0:T(8,128)(2,1)S(1)} %shard_map.141.pair_ref.refs_0_), channel_id=1, source_target_pairs={{0,7},{1,0},{2,5},{3,2},{4,3},{5,4},{6,1},{7,6},{8,15},{9,8},{10,1... | collective-permute-start | bytes 122888 | tf_op jit(solution)/shard_map/ppermute | solution.py:203
  8.1 0.2 shard_map.143
  8.2 0.2 shard_map.142.refs_3_.refs_2_
  8.5 1.2 %collective-permute-done.3.refs_2_ = bf16[2,16,640]{2,1,0:T(8,128)(2,1)S(1)} collective-permute-done((bf16[2,16,640]{2,1,0:T(8,128)(2,1)S(1)}, bf16[2,16,640]{2,1,0:T(8,128)(2,1)S(1)}, u32[]{:S(2)}, u32[]{:S(2)}) %collective-permute-start.3) | collective-permute-done | bytes 40992 | tf_op jit(solution)/shard_map/ppermute | solution.py:203
  9.7 1.5 %collective-permute-start.4 = (bf16[3,2,16,640]{3,2,1,0:T(8,128)(2,1)S(1)}, bf16[3,2,16,640]{3,2,1,0:T(8,128)(2,1)S(1)}, u32[]{:S(2)}, u32[]{:S(2)}) collective-permute-start(bf16[3,2,16,640]{3,2,1,0:T(8,128)(2,1)S(1)} %shard_map.144.refs_1_), channel_id=1, source_target_pairs={{0,1},{1,0},{2,3},{3,2},{4,5},{5,4},{6,7},{7,6},{8,9},{9,8},{10,11... | collective-permute-start | bytes 368648 | tf_op jit(solution)/shard_map/ppermute | solution.py:108
  11.3 0.8 %collective-permute-start.5 = (bf16[16,512]{1,0:T(8,128)(2,1)S(1)}, bf16[16,512]{1,0:T(8,128)(2,1)S(1)}, u32[]{:S(2)}, u32[]{:S(2)}) collective-permute-start(bf16[16,512]{1,0:T(8,128)(2,1)S(1)} %shard_map.146._), channel_id=1, source_target_pairs={{0,1},{1,0},{2,3},{3,2},{4,5},{5,4},{6,7},{7,6},{8,9},{9,8},{10,11... | collective-permute-start | bytes 49160 | tf_op jit(solution)/shard_map/ppermute | solution.py:108
  12.2 0.1 collective-permute-start.6
  12.3 0.7 %shard_map.145.first_ref = bf16[16,512]{1,0:T(8,128)(2,1)S(1)} custom-call(bf16[2,16,640]{2,1,0:T(8,128)(2,1)S(1)} %shard_map.141.pair_ref.refs_0_, bf16[3,2,16,640]{3,2,1,0:T(8,128)(2,1)S(1)} %collective-permute-done.4.refs_1_, f32[16,512]{1,0:T(8,128)S(1)} %shard_map.142.refs_3_.refs_2_, bf16[4096,512]{1,0:T(8,128)(2,1)S(1)} %copy-done.1, ...), custom_call_target="tpu_custom_call" | custom-call | flops 68719476736 | bytes 4407808 | tf_op jit(solution)/shard_map/pallas_call | solution.py:114
  13.1 1.3 %collective-permute-start.8 = (bf16[16,1024]{1,0:T(8,128)(2,1)S(1)}, bf16[16,1024]{1,0:T(8,128)(2,1)S(1)}, u32[]{:S(2)}, u32[]{:S(2)}) collective-permute-start(bf16[16,1024]{1,0:T(8,128)(2,1)S(1)} %shard_map.147.query_ref), channel_id=1, source_target_pairs={{0,5},{1,0},{2,7},{3,2},{4,1},{5,4},{6,3},{7,6},{8,13},{9,8},{10,1... | collective-permute-start | bytes 98312 | tf_op jit(solution)/shard_map/ppermute | solution.py:203
  14.4 1.4 %collective-permute-start.9 = (bf16[16,1024]{1,0:T(8,128)(2,1)S(1)}, bf16[16,1024]{1,0:T(8,128)(2,1)S(1)}, u32[]{:S(2)}, u32[]{:S(2)}) collective-permute-start(bf16[16,1024]{1,0:T(8,128)(2,1)S(1)} %shard_map.147.query_ref), channel_id=1, source_target_pairs={{0,7},{1,0},{2,5},{3,2},{4,3},{5,4},{6,1},{7,6},{8,15},{9,8},{10,1... | collective-permute-start | bytes 98312 | tf_op jit(solution)/shard_map/ppermute | solution.py:203
  15.8 0.2 collective-permute-done.8.refs_1_
  16.0 1.4 %collective-permute-done.9.refs_2_ = bf16[16,1024]{1,0:T(8,128)(2,1)S(1)} collective-permute-done((bf16[16,1024]{1,0:T(8,128)(2,1)S(1)}, bf16[16,1024]{1,0:T(8,128)(2,1)S(1)}, u32[]{:S(2)}, u32[]{:S(2)}) %collective-permute-start.9) | collective-permute-done | bytes 32800 | tf_op jit(solution)/shard_map/ppermute | solution.py:203
  17.4 3.3 %collective-permute-start.10 = (bf16[16,1152]{1,0:T(8,128)(2,1)S(1)}, bf16[16,1152]{1,0:T(8,128)(2,1)S(1)}, u32[]{:S(2)}, u32[]{:S(2)}) collective-permute-start(bf16[16,1152]{1,0:T(8,128)(2,1)S(1)} %get-tuple-element.25), channel_id=1, source_target_pairs={{0,1},{1,2},{2,3},{3,0},{4,5},{5,6},{6,7},{7,4},{8,9},{9,10},{10,1... | collective-permute-start | bytes 110600 | tf_op jit(solution)/shard_map/ppermute | solution.py:203
  20.8 1.1 %collective-permute-start.12 = (bf16[16,1152]{1,0:T(8,128)(2,1)S(1)}, bf16[16,1152]{1,0:T(8,128)(2,1)S(1)}, u32[]{:S(2)}, u32[]{:S(2)}) collective-permute-start(bf16[16,1152]{1,0:T(8,128)(2,1)S(1)} %get-tuple-element.27), channel_id=1, source_target_pairs={{0,1},{1,6},{2,3},{3,4},{4,5},{5,2},{6,7},{7,0},{8,9},{9,14},{10,1... | collective-permute-start | bytes 110600 | tf_op jit(solution)/shard_map/ppermute | solution.py:203
  21.9 0.7 %shard_map.149 = (f32[2,64,128]{2,1,0:T(8,128)S(1)}, f32[2,64,256]{2,1,0:T(8,128)S(1)}) custom-call(bf16[16,1024]{1,0:T(8,128)(2,1)S(1)} %shard_map.147.query_ref, bf16[320,1024]{1,0:T(8,128)(2,1)S(1)} %copy-done.2, bf16[320,1024]{1,0:T(8,128)(2,1)S(1)} %copy-done.3, bf16[2,320,1024]{2,1,0:T(8,128)(2,1)S(1)} %collective-permute-done.6.other_ref.refs_5_, ...), custom_call_target="tpu_custom_call" | custom-call | flops 134217728 | bytes 2670592 | tf_op jit(solution)/shard_map/pallas_call | solution.py:114
  22.6 2.7 %collective-permute-done.11.second_ref = bf16[16,1152]{1,0:T(8,128)(2,1)S(1)} collective-permute-done((bf16[16,1152]{1,0:T(8,128)(2,1)S(1)}, bf16[16,1152]{1,0:T(8,128)(2,1)S(1)}, u32[]{:S(2)}, u32[]{:S(2)}) %collective-permute-start.11) | collective-permute-done | bytes 36896 | tf_op jit(solution)/shard_map/ppermute | solution.py:203
  25.3 0.8 %collective-permute-done.12.third_ref = bf16[16,1152]{1,0:T(8,128)(2,1)S(1)} collective-permute-done((bf16[16,1152]{1,0:T(8,128)(2,1)S(1)}, bf16[16,1152]{1,0:T(8,128)(2,1)S(1)}, u32[]{:S(2)}, u32[]{:S(2)}) %collective-permute-start.12) | collective-permute-done | bytes 36896 | tf_op jit(solution)/shard_map/ppermute | solution.py:203
  26.1 0.3 shard_map.151
  26.5 0.7 %shard_map.152.refs_2_.refs_0_ = f32[4,16,1024]{2,1,0:T(8,128)S(1)} custom-call(bf16[16,512]{1,0:T(8,128)(2,1)S(1)} %get-tuple-element.28.refs_0_, bf16[512,4096]{1,0:T(8,128)(2,1)S(1)} %copy-done), custom_call_target="tpu_custom_call" | custom-call | flops 134217728 | bytes 4210688 | tf_op jit(solution)/shard_map/pallas_call | solution.py:114
  27.1 0.5 collective-permute-done.13.refs_0_
  27.6 0.9 %collective-permute-start.14 = (bf16[2,16,1024]{2,1,0:T(8,128)(2,1)S(1)}, bf16[2,16,1024]{2,1,0:T(8,128)(2,1)S(1)}, u32[]{:S(2)}, u32[]{:S(2)}) collective-permute-start(bf16[2,16,1024]{2,1,0:T(8,128)(2,1)S(1)} %shard_map.154), channel_id=1, source_target_pairs={{0,1},{1,0},{2,3},{3,2},{4,5},{5,4},{6,7},{7,6},{8,9},{9,8},{10,11... | collective-permute-start | bytes 196616 | tf_op jit(solution)/shard_map/ppermute | solution.py:108
  28.6 0.9 %collective-permute-done.14.refs_1_ = bf16[2,16,1024]{2,1,0:T(8,128)(2,1)S(1)} collective-permute-done((bf16[2,16,1024]{2,1,0:T(8,128)(2,1)S(1)}, bf16[2,16,1024]{2,1,0:T(8,128)(2,1)S(1)}, u32[]{:S(2)}, u32[]{:S(2)}) %collective-permute-start.14) | collective-permute-done | bytes 65568 | tf_op jit(solution)/shard_map/ppermute | solution.py:108
  29.5 0.4 collective-permute-start.15
  29.9 0.4 collective-permute-start.17
  30.3 0.7 %collective-permute-start.18 = (bf16[16,1024]{1,0:T(8,128)(2,1)S(1)}, bf16[16,1024]{1,0:T(8,128)(2,1)S(1)}, u32[]{:S(2)}, u32[]{:S(2)}) collective-permute-start(bf16[16,1024]{1,0:T(8,128)(2,1)S(1)} %get-tuple-element.32), channel_id=1, source_target_pairs={{0,5},{1,0},{2,7},{3,2},{4,1},{5,4},{6,3},{7,6},{8,13},{9,8},{10,1... | collective-permute-start | bytes 98312 | tf_op jit(solution)/shard_map/ppermute | solution.py:203
  31.1 1.5 %collective-permute-start.19 = (bf16[16,1024]{1,0:T(8,128)(2,1)S(1)}, bf16[16,1024]{1,0:T(8,128)(2,1)S(1)}, u32[]{:S(2)}, u32[]{:S(2)}) collective-permute-start(bf16[16,1024]{1,0:T(8,128)(2,1)S(1)} %get-tuple-element.33), channel_id=1, source_target_pairs={{0,7},{1,0},{2,5},{3,2},{4,3},{5,4},{6,1},{7,6},{8,15},{9,8},{10,1... | collective-permute-start | bytes 98312 | tf_op jit(solution)/shard_map/ppermute | solution.py:203
  32.6 1.2 %collective-permute-done.21.other_gain_ref = f32[1,512]{1,0:T(1,128)S(1)} collective-permute-done((f32[1,512]{1,0:T(1,128)S(1)}, f32[1,512]{1,0:T(1,128)S(1)}, u32[]{:S(2)}, u32[]{:S(2)}) %collective-permute-start.21) | collective-permute-done | bytes 2080 | tf_op jit(solution)/shard_map/ppermute | solution.py:108
  33.8 0.2 collective-permute-start.20
  33.9 1.0 %collective-permute-done.20.other_ref = bf16[16,512]{1,0:T(8,128)(2,1)S(1)} collective-permute-done((bf16[16,512]{1,0:T(8,128)(2,1)S(1)}, bf16[16,512]{1,0:T(8,128)(2,1)S(1)}, u32[]{:S(2)}, u32[]{:S(2)}) %collective-permute-start.20) | collective-permute-done | bytes 16416 | tf_op jit(solution)/shard_map/ppermute | solution.py:108
  35.0 1.1 %collective-permute-start.22 = (f32[16,1152]{1,0:T(8,128)S(1)}, f32[16,1152]{1,0:T(8,128)S(1)}, u32[]{:S(2)}, u32[]{:S(2)}) collective-permute-start(f32[16,1152]{1,0:T(8,128)S(1)} %get-tuple-element.34.refs_4_), channel_id=1, source_target_pairs={{0,1},{1,0},{2,3},{3,2},{4,5},{5,4},{6,7},{7,6},{8,9},{9,8},{10,11... | collective-permute-start | bytes 221192 | tf_op jit(solution)/shard_map/ppermute | solution.py:108
  36.2 1.5 %collective-permute-start.24 = (bf16[16,1024]{1,0:T(8,128)(2,1)S(1)}, bf16[16,1024]{1,0:T(8,128)(2,1)S(1)}, u32[]{:S(2)}, u32[]{:S(2)}) collective-permute-start(bf16[16,1024]{1,0:T(8,128)(2,1)S(1)} %get-tuple-element.35), channel_id=1, source_target_pairs={{0,1},{1,16},{2,3},{3,18},{4,5},{5,20},{6,7},{7,22},{8,9},{9,24},{... | collective-permute-start | bytes 98312 | tf_op jit(solution)/shard_map/ppermute | solution.py:203
  37.7 0.1 collective-permute-start.25
  37.8 1.6 %collective-permute-done.23.first_ref = bf16[16,1024]{1,0:T(8,128)(2,1)S(1)} collective-permute-done((bf16[16,1024]{1,0:T(8,128)(2,1)S(1)}, bf16[16,1024]{1,0:T(8,128)(2,1)S(1)}, u32[]{:S(2)}, u32[]{:S(2)}) %collective-permute-start.23) | collective-permute-done | bytes 32800 | tf_op jit(solution)/shard_map/ppermute | solution.py:203
  39.4 1.0 %collective-permute-done.24.second_ref = bf16[16,1024]{1,0:T(8,128)(2,1)S(1)} collective-permute-done((bf16[16,1024]{1,0:T(8,128)(2,1)S(1)}, bf16[16,1024]{1,0:T(8,128)(2,1)S(1)}, u32[]{:S(2)}, u32[]{:S(2)}) %collective-permute-start.24) | collective-permute-done | bytes 32800 | tf_op jit(solution)/shard_map/ppermute | solution.py:203
  40.4 1.5 %collective-permute-done.25.third_ref = bf16[16,1024]{1,0:T(8,128)(2,1)S(1)} collective-permute-done((bf16[16,1024]{1,0:T(8,128)(2,1)S(1)}, bf16[16,1024]{1,0:T(8,128)(2,1)S(1)}, u32[]{:S(2)}, u32[]{:S(2)}) %collective-permute-start.25) | collective-permute-done | bytes 32800 | tf_op jit(solution)/shard_map/ppermute | solution.py:203
  41.9 0.2 shard_map.158
  42.2 0.5 collective-permute-start.26
  42.7 0.8 %collective-permute-start.28 = (f32[48,128]{1,0:T(8,128)S(1)}, f32[48,128]{1,0:T(8,128)S(1)}, u32[]{:S(2)}, u32[]{:S(2)}) collective-permute-start(f32[48,128]{1,0:T(8,128)S(1)} %get-tuple-element.36), channel_id=1, source_target_pairs={{0,5},{1,0},{2,7},{3,2},{4,1},{5,4},{6,3},{7,6},{8,13},{9,8},{10,1... | collective-permute-start | bytes 73736 | tf_op jit(solution)/shard_map/ppermute | solution.py:203
  43.5 1.5 %collective-permute-start.29 = (f32[48,128]{1,0:T(8,128)S(1)}, f32[48,128]{1,0:T(8,128)S(1)}, u32[]{:S(2)}, u32[]{:S(2)}) collective-permute-start(f32[48,128]{1,0:T(8,128)S(1)} %get-tuple-element.36), channel_id=1, source_target_pairs={{0,7},{1,0},{2,5},{3,2},{4,3},{5,4},{6,1},{7,6},{8,15},{9,8},{10,1... | collective-permute-start | bytes 73736 | tf_op jit(solution)/shard_map/ppermute | solution.py:203
  45.0 1.5 %collective-permute-done.29.third_ref = f32[48,128]{1,0:T(8,128)S(1)} collective-permute-done((f32[48,128]{1,0:T(8,128)S(1)}, f32[48,128]{1,0:T(8,128)S(1)}, u32[]{:S(2)}, u32[]{:S(2)}) %collective-permute-start.29) | collective-permute-done | bytes 24608 | tf_op jit(solution)/shard_map/ppermute | solution.py:203
  46.5 1.8 %collective-permute-start.30 = (f32[48,128]{1,0:T(8,128)S(1)}, f32[48,128]{1,0:T(8,128)S(1)}, u32[]{:S(2)}, u32[]{:S(2)}) collective-permute-start(f32[48,128]{1,0:T(8,128)S(1)} %shard_map.159.refs_0_), channel_id=1, source_target_pairs={{0,1},{1,0},{2,3},{3,2},{4,5},{5,4},{6,7},{7,6},{8,9},{9,8},{10,11... | collective-permute-start | bytes 73736 | tf_op jit(solution)/shard_map/ppermute | solution.py:108
  48.3 0.8 %collective-permute-done.30.refs_1_ = f32[48,128]{1,0:T(8,128)S(1)} collective-permute-done((f32[48,128]{1,0:T(8,128)S(1)}, f32[48,128]{1,0:T(8,128)S(1)}, u32[]{:S(2)}, u32[]{:S(2)}) %collective-permute-start.30) | collective-permute-done | bytes 24608 | tf_op jit(solution)/shard_map/ppermute | solution.py:108
  49.2 1.1 %shard_map.160 = (bf16[16,512]{1,0:T(8,128)(2,1)}, f32[2]{0:T(128)}, bf16[16,512]{1,0:T(8,128)(2,1)}) custom-call(f32[48,128]{1,0:T(8,128)S(1)} %shard_map.159.refs_0_, f32[48,128]{1,0:T(8,128)S(1)} %collective-permute-done.30.refs_1_, bf16[64,512]{1,0:T(8,128)(2,1)S(1)} %get-tuple-element.37.refs_2_, bf16[64,512]{1,0:T(8,128)(2,1)S(1)} %collective-permute-done.31.refs_3_, ...), custom_call_target="tpu_custom_call" | custom-call | tf_op jit(solution)/shard_map/pallas_call | solution.py:716
  (62 shorter events, 0.7 us)
Async XLA Ops:
  0.6 7.4 %copy-start.11 = (f32[1,128]{1,0:T(1,128)S(1)}, f32[1,128]{1,0:T(1,128)}, u32[]{:S(2)}) copy-start(f32[1,128]{1,0:T(1,128)} %constant.2.clone.frequency_ref) | copy-start | bytes 1540
  0.6 0.7 %copy-start.4 = (bf16[16,512]{1,0:T(8,128)(2,1)S(1)}, bf16[16,512]{1,0:T(8,128)(2,1)}, u32[]{:S(2)}) copy-start(bf16[16,512]{1,0:T(8,128)(2,1)} %own_ref.1) | copy-start | bytes 49156
  0.7 0.7 %copy-start.6 = (f32[512]{0:T(512)S(1)}, f32[512]{0:T(512)}, u32[]{:S(2)}) copy-start(f32[512]{0:T(512)} %param.13) | copy-start | bytes 6148
  0.7 7.4 %copy-start.9 = (s32[1,16]{1,0:T(1,128)S(1)}, s32[1,16]{1,0:T(1,128)}, u32[]{:S(2)}) copy-start(s32[1,16]{1,0:T(1,128)} %lengths_ref.1) | copy-start | bytes 196
  0.7 7.4 %copy-start.10 = (s32[1,16]{1,0:T(1,128)S(1)}, s32[1,16]{1,0:T(1,128)}, u32[]{:S(2)}) copy-start(s32[1,16]{1,0:T(1,128)} %order_ref.1) | copy-start | bytes 196
  0.7 7.5 %copy-start.1 = (bf16[4096,512]{1,0:T(8,128)(2,1)S(1)}, bf16[4096,512]{1,0:T(8,128)(2,1)}, u32[]{:S(2)}) copy-start(bf16[4096,512]{1,0:T(8,128)(2,1)} %refs_3_.4) | copy-start | bytes 12582916
  0.7 10.6 %copy-start.7 = (f32[128]{0:T(128)S(1)}, f32[128]{0:T(128)}, u32[]{:S(2)}) copy-start(f32[128]{0:T(128)} %param.15) | copy-start | bytes 1540
  1.5 1.3 %collective-permute-start = (bf16[16,640]{1,0:T(8,128)(2,1)S(1)}, bf16[16,640]{1,0:T(8,128)(2,1)S(1)}, u32[]{:S(2)}, u32[]{:S(2)}) collective-permute-start(bf16[16,640]{1,0:T(8,128)(2,1)S(1)} %shard_map.140.own_ref.message_ref), channel_id=1, source_target_pairs={{0,1},{1,0},{2,3},{3,2},{4,5},{5,4},{6,7},{7,6},{8,9},{9,8},{10,11... | collective-permute-start | bytes 61448 | tf_op jit(solution)/shard_map/ppermute | solution.py:108
  2.8 5.7 %collective-permute-start.1 = (bf16[2,16,640]{2,1,0:T(8,128)(2,1)S(1)}, bf16[2,16,640]{2,1,0:T(8,128)(2,1)S(1)}, u32[]{:S(2)}, u32[]{:S(2)}) collective-permute-start(bf16[2,16,640]{2,1,0:T(8,128)(2,1)S(1)} %shard_map.141.pair_ref.refs_0_), channel_id=1, source_target_pairs={{0,3},{1,0},{2,1},{3,2},{4,7},{5,4},{6,5},{7,6},{8,11},{9,8},{10,9... | collective-permute-start | bytes 122888 | tf_op jit(solution)/shard_map/ppermute | solution.py:203
  5.5 3.0 %collective-permute-start.2 = (bf16[2,16,640]{2,1,0:T(8,128)(2,1)S(1)}, bf16[2,16,640]{2,1,0:T(8,128)(2,1)S(1)}, u32[]{:S(2)}, u32[]{:S(2)}) collective-permute-start(bf16[2,16,640]{2,1,0:T(8,128)(2,1)S(1)} %shard_map.141.pair_ref.refs_0_), channel_id=1, source_target_pairs={{0,5},{1,0},{2,7},{3,2},{4,1},{5,4},{6,3},{7,6},{8,13},{9,8},{10,1... | collective-permute-start | bytes 122888 | tf_op jit(solution)/shard_map/ppermute | solution.py:203
  6.8 2.9 %collective-permute-start.3 = (bf16[2,16,640]{2,1,0:T(8,128)(2,1)S(1)}, bf16[2,16,640]{2,1,0:T(8,128)(2,1)S(1)}, u32[]{:S(2)}, u32[]{:S(2)}) collective-permute-start(bf16[2,16,640]{2,1,0:T(8,128)(2,1)S(1)} %shard_map.141.pair_ref.refs_0_), channel_id=1, source_target_pairs={{0,7},{1,0},{2,5},{3,2},{4,3},{5,4},{6,1},{7,6},{8,15},{9,8},{10,1... | collective-permute-start | bytes 122888 | tf_op jit(solution)/shard_map/ppermute | solution.py:203
  8.2 3.8 %copy-start.2 = (bf16[320,1024]{1,0:T(8,128)(2,1)S(1)}, bf16[320,1024]{1,0:T(8,128)(2,1)}, u32[]{:S(2)}) copy-start(bf16[320,1024]{1,0:T(8,128)(2,1)} %refs_3_.5) | copy-start | bytes 1966084
  8.2 3.8 %copy-start.3 = (bf16[320,1024]{1,0:T(8,128)(2,1)S(1)}, bf16[320,1024]{1,0:T(8,128)(2,1)}, u32[]{:S(2)}) copy-start(bf16[320,1024]{1,0:T(8,128)(2,1)} %refs_4_.1) | copy-start | bytes 1966084
  9.7 2.5 %collective-permute-start.4 = (bf16[3,2,16,640]{3,2,1,0:T(8,128)(2,1)S(1)}, bf16[3,2,16,640]{3,2,1,0:T(8,128)(2,1)S(1)}, u32[]{:S(2)}, u32[]{:S(2)}) collective-permute-start(bf16[3,2,16,640]{3,2,1,0:T(8,128)(2,1)S(1)} %shard_map.144.refs_1_), channel_id=1, source_target_pairs={{0,1},{1,0},{2,3},{3,2},{4,5},{5,4},{6,7},{7,6},{8,9},{9,8},{10,11... | collective-permute-start | bytes 368648 | tf_op jit(solution)/shard_map/ppermute | solution.py:108
  11.3 1.7 %collective-permute-start.5 = (bf16[16,512]{1,0:T(8,128)(2,1)S(1)}, bf16[16,512]{1,0:T(8,128)(2,1)S(1)}, u32[]{:S(2)}, u32[]{:S(2)}) collective-permute-start(bf16[16,512]{1,0:T(8,128)(2,1)S(1)} %shard_map.146._), channel_id=1, source_target_pairs={{0,1},{1,0},{2,3},{3,2},{4,5},{5,4},{6,7},{7,6},{8,9},{9,8},{10,11... | collective-permute-start | bytes 49160 | tf_op jit(solution)/shard_map/ppermute | solution.py:108
  12.2 5.2 %collective-permute-start.6 = (bf16[2,320,1024]{2,1,0:T(8,128)(2,1)S(1)}, bf16[2,320,1024]{2,1,0:T(8,128)(2,1)S(1)}, u32[]{:S(2)}, u32[]{:S(2)}) collective-permute-start(bf16[2,320,1024]{2,1,0:T(8,128)(2,1)S(1)} %shard_map.148), channel_id=1, source_target_pairs={{0,1},{1,0},{2,3},{3,2},{4,5},{5,4},{6,7},{7,6},{8,9},{9,8},{10,11... | collective-permute-start | bytes 3932168 | tf_op jit(solution)/shard_map/ppermute | solution.py:108
  13.0 13.5 %copy-start = (bf16[512,4096]{1,0:T(8,128)(2,1)S(1)}, bf16[512,4096]{1,0:T(8,128)(2,1)}, u32[]{:S(2)}) copy-start(bf16[512,4096]{1,0:T(8,128)(2,1)} %refs_1_.5) | copy-start | bytes 12582916
  13.0 2.8 %collective-permute-start.7 = (bf16[16,1024]{1,0:T(8,128)(2,1)S(1)}, bf16[16,1024]{1,0:T(8,128)(2,1)S(1)}, u32[]{:S(2)}, u32[]{:S(2)}) collective-permute-start(bf16[16,1024]{1,0:T(8,128)(2,1)S(1)} %shard_map.147.query_ref), channel_id=1, source_target_pairs={{0,3},{1,0},{2,1},{3,2},{4,7},{5,4},{6,5},{7,6},{8,11},{9,8},{10,9... | collective-permute-start | bytes 98312 | tf_op jit(solution)/shard_map/ppermute | solution.py:203
  13.1 2.9 %collective-permute-start.8 = (bf16[16,1024]{1,0:T(8,128)(2,1)S(1)}, bf16[16,1024]{1,0:T(8,128)(2,1)S(1)}, u32[]{:S(2)}, u32[]{:S(2)}) collective-permute-start(bf16[16,1024]{1,0:T(8,128)(2,1)S(1)} %shard_map.147.query_ref), channel_id=1, source_target_pairs={{0,5},{1,0},{2,7},{3,2},{4,1},{5,4},{6,3},{7,6},{8,13},{9,8},{10,1... | collective-permute-start | bytes 98312 | tf_op jit(solution)/shard_map/ppermute | solution.py:203
  14.4 3.0 %collective-permute-start.9 = (bf16[16,1024]{1,0:T(8,128)(2,1)S(1)}, bf16[16,1024]{1,0:T(8,128)(2,1)S(1)}, u32[]{:S(2)}, u32[]{:S(2)}) collective-permute-start(bf16[16,1024]{1,0:T(8,128)(2,1)S(1)} %shard_map.147.query_ref), channel_id=1, source_target_pairs={{0,7},{1,0},{2,5},{3,2},{4,3},{5,4},{6,1},{7,6},{8,15},{9,8},{10,1... | collective-permute-start | bytes 98312 | tf_op jit(solution)/shard_map/ppermute | solution.py:203
  17.4 5.2 %collective-permute-start.10 = (bf16[16,1152]{1,0:T(8,128)(2,1)S(1)}, bf16[16,1152]{1,0:T(8,128)(2,1)S(1)}, u32[]{:S(2)}, u32[]{:S(2)}) collective-permute-start(bf16[16,1152]{1,0:T(8,128)(2,1)S(1)} %get-tuple-element.25), channel_id=1, source_target_pairs={{0,1},{1,2},{2,3},{3,0},{4,5},{5,6},{6,7},{7,4},{8,9},{9,10},{10,1... | collective-permute-start | bytes 110600 | tf_op jit(solution)/shard_map/ppermute | solution.py:203
  20.7 4.6 %collective-permute-start.11 = (bf16[16,1152]{1,0:T(8,128)(2,1)S(1)}, bf16[16,1152]{1,0:T(8,128)(2,1)S(1)}, u32[]{:S(2)}, u32[]{:S(2)}) collective-permute-start(bf16[16,1152]{1,0:T(8,128)(2,1)S(1)} %get-tuple-element.26), channel_id=1, source_target_pairs={{0,1},{1,4},{2,3},{3,6},{4,5},{5,0},{6,7},{7,2},{8,9},{9,12},{10,1... | collective-permute-start | bytes 110600 | tf_op jit(solution)/shard_map/ppermute | solution.py:203
  20.8 5.3 %collective-permute-start.12 = (bf16[16,1152]{1,0:T(8,128)(2,1)S(1)}, bf16[16,1152]{1,0:T(8,128)(2,1)S(1)}, u32[]{:S(2)}, u32[]{:S(2)}) collective-permute-start(bf16[16,1152]{1,0:T(8,128)(2,1)S(1)} %get-tuple-element.27), channel_id=1, source_target_pairs={{0,1},{1,6},{2,3},{3,4},{4,5},{5,2},{6,7},{7,0},{8,9},{9,14},{10,1... | collective-permute-start | bytes 110600 | tf_op jit(solution)/shard_map/ppermute | solution.py:203
  26.4 1.2 %collective-permute-start.13 = (bf16[16,512]{1,0:T(8,128)(2,1)S(1)}, bf16[16,512]{1,0:T(8,128)(2,1)S(1)}, u32[]{:S(2)}, u32[]{:S(2)}) collective-permute-start(bf16[16,512]{1,0:T(8,128)(2,1)S(1)} %get-tuple-element.29), channel_id=1, source_target_pairs={{0,1},{1,0},{2,3},{3,2},{4,5},{5,4},{6,7},{7,6},{8,9},{9,8},{10,11... | collective-permute-start | bytes 49160 | tf_op jit(solution)/shard_map/ppermute | solution.py:108
  27.1 5.5 %copy-start.5 = (f32[512]{0:T(512)S(1)}, f32[512]{0:T(512)}, u32[]{:S(2)}) copy-start(f32[512]{0:T(512)} %param.19) | copy-start | bytes 6148
  27.1 22.1 %copy-start.8 = (s32[64]{0:T(128)S(1)}, s32[64]{0:T(128)}, u32[]{:S(2)}) copy-start(s32[64]{0:T(128)} %param.22) | copy-start | bytes 772
  27.6 1.8 %collective-permute-start.14 = (bf16[2,16,1024]{2,1,0:T(8,128)(2,1)S(1)}, bf16[2,16,1024]{2,1,0:T(8,128)(2,1)S(1)}, u32[]{:S(2)}, u32[]{:S(2)}) collective-permute-start(bf16[2,16,1024]{2,1,0:T(8,128)(2,1)S(1)} %shard_map.154), channel_id=1, source_target_pairs={{0,1},{1,0},{2,3},{3,2},{4,5},{5,4},{6,7},{7,6},{8,9},{9,8},{10,11... | collective-permute-start | bytes 196616 | tf_op jit(solution)/shard_map/ppermute | solution.py:108
  28.6 1.3 %collective-permute-start.16 = (bf16[2,16,1024]{2,1,0:T(8,128)(2,1)S(1)}, bf16[2,16,1024]{2,1,0:T(8,128)(2,1)S(1)}, u32[]{:S(2)}, u32[]{:S(2)}) collective-permute-start(bf16[2,16,1024]{2,1,0:T(8,128)(2,1)S(1)} %shard_map.153.refs_2_), channel_id=1, source_target_pairs={{0,1},{1,0},{2,3},{3,2},{4,5},{5,4},{6,7},{7,6},{8,9},{9,8},{10,11... | collective-permute-start | bytes 196616 | tf_op jit(solution)/shard_map/ppermute | solution.py:108
  29.5 5.5 %collective-permute-start.15 = (f32[16,1024]{1,0:T(8,128)S(1)}, f32[16,1024]{1,0:T(8,128)S(1)}, u32[]{:S(2)}, u32[]{:S(2)}) collective-permute-start(f32[16,1024]{1,0:T(8,128)S(1)} %get-tuple-element.30), channel_id=1, source_target_pairs={{0,1},{1,0},{2,3},{3,2},{4,5},{5,4},{6,7},{7,6},{8,9},{9,8},{10,11... | collective-permute-start | bytes 196616 | tf_op jit(solution)/shard_map/ppermute | solution.py:108
  29.9 5.0 %collective-permute-start.17 = (bf16[16,1024]{1,0:T(8,128)(2,1)S(1)}, bf16[16,1024]{1,0:T(8,128)(2,1)S(1)}, u32[]{:S(2)}, u32[]{:S(2)}) collective-permute-start(bf16[16,1024]{1,0:T(8,128)(2,1)S(1)} %get-tuple-element.31), channel_id=1, source_target_pairs={{0,3},{1,0},{2,1},{3,2},{4,7},{5,4},{6,5},{7,6},{8,11},{9,8},{10,9... | collective-permute-start | bytes 98312 | tf_op jit(solution)/shard_map/ppermute | solution.py:203
  30.3 4.6 %collective-permute-start.18 = (bf16[16,1024]{1,0:T(8,128)(2,1)S(1)}, bf16[16,1024]{1,0:T(8,128)(2,1)S(1)}, u32[]{:S(2)}, u32[]{:S(2)}) collective-permute-start(bf16[16,1024]{1,0:T(8,128)(2,1)S(1)} %get-tuple-element.32), channel_id=1, source_target_pairs={{0,5},{1,0},{2,7},{3,2},{4,1},{5,4},{6,3},{7,6},{8,13},{9,8},{10,1... | collective-permute-start | bytes 98312 | tf_op jit(solution)/shard_map/ppermute | solution.py:203
  31.1 3.9 %collective-permute-start.19 = (bf16[16,1024]{1,0:T(8,128)(2,1)S(1)}, bf16[16,1024]{1,0:T(8,128)(2,1)S(1)}, u32[]{:S(2)}, u32[]{:S(2)}) collective-permute-start(bf16[16,1024]{1,0:T(8,128)(2,1)S(1)} %get-tuple-element.33), channel_id=1, source_target_pairs={{0,7},{1,0},{2,5},{3,2},{4,3},{5,4},{6,1},{7,6},{8,15},{9,8},{10,1... | collective-permute-start | bytes 98312 | tf_op jit(solution)/shard_map/ppermute | solution.py:203
  32.6 1.2 %collective-permute-start.21 = (f32[1,512]{1,0:T(1,128)S(1)}, f32[1,512]{1,0:T(1,128)S(1)}, u32[]{:S(2)}, u32[]{:S(2)}) collective-permute-start(f32[1,512]{1,0:T(1,128)S(1)} %bitcast.4), channel_id=1, source_target_pairs={{0,1},{1,0},{2,3},{3,2},{4,5},{5,4},{6,7},{7,6},{8,9},{9,8},{10,11... | collective-permute-start | bytes 6152 | tf_op jit(solution)/shard_map/ppermute | solution.py:108
  33.8 1.2 %collective-permute-start.20 = (bf16[16,512]{1,0:T(8,128)(2,1)S(1)}, bf16[16,512]{1,0:T(8,128)(2,1)S(1)}, u32[]{:S(2)}, u32[]{:S(2)}) collective-permute-start(bf16[16,512]{1,0:T(8,128)(2,1)S(1)} %copy-done.4), channel_id=1, source_target_pairs={{0,1},{1,0},{2,3},{3,2},{4,5},{5,4},{6,7},{7,6},{8,9},{9,8},{10,11... | collective-permute-start | bytes 49160 | tf_op jit(solution)/shard_map/ppermute | solution.py:108
  35.0 6.9 %collective-permute-start.22 = (f32[16,1152]{1,0:T(8,128)S(1)}, f32[16,1152]{1,0:T(8,128)S(1)}, u32[]{:S(2)}, u32[]{:S(2)}) collective-permute-start(f32[16,1152]{1,0:T(8,128)S(1)} %get-tuple-element.34.refs_4_), channel_id=1, source_target_pairs={{0,1},{1,0},{2,3},{3,2},{4,5},{5,4},{6,7},{7,6},{8,9},{9,8},{10,11... | collective-permute-start | bytes 221192 | tf_op jit(solution)/shard_map/ppermute | solution.py:108
  36.1 3.3 %collective-permute-start.23 = (bf16[16,1024]{1,0:T(8,128)(2,1)S(1)}, bf16[16,1024]{1,0:T(8,128)(2,1)S(1)}, u32[]{:S(2)}, u32[]{:S(2)}) collective-permute-start(bf16[16,1024]{1,0:T(8,128)(2,1)S(1)} %get-tuple-element.35), channel_id=1, source_target_pairs={{0,1},{1,8},{2,3},{3,10},{4,5},{5,12},{6,7},{7,14},{8,9},{9,0},{10... | collective-permute-start | bytes 98312 | tf_op jit(solution)/shard_map/ppermute | solution.py:203
  36.2 4.3 %collective-permute-start.24 = (bf16[16,1024]{1,0:T(8,128)(2,1)S(1)}, bf16[16,1024]{1,0:T(8,128)(2,1)S(1)}, u32[]{:S(2)}, u32[]{:S(2)}) collective-permute-start(bf16[16,1024]{1,0:T(8,128)(2,1)S(1)} %get-tuple-element.35), channel_id=1, source_target_pairs={{0,1},{1,16},{2,3},{3,18},{4,5},{5,20},{6,7},{7,22},{8,9},{9,24},{... | collective-permute-start | bytes 98312 | tf_op jit(solution)/shard_map/ppermute | solution.py:203
  37.7 4.2 %collective-permute-start.25 = (bf16[16,1024]{1,0:T(8,128)(2,1)S(1)}, bf16[16,1024]{1,0:T(8,128)(2,1)S(1)}, u32[]{:S(2)}, u32[]{:S(2)}) collective-permute-start(bf16[16,1024]{1,0:T(8,128)(2,1)S(1)} %get-tuple-element.35), channel_id=1, source_target_pairs={{0,1},{1,24},{2,3},{3,26},{4,5},{5,28},{6,7},{7,30},{8,9},{9,16},{... | collective-permute-start | bytes 98312 | tf_op jit(solution)/shard_map/ppermute | solution.py:203
  42.2 7.0 %collective-permute-start.31 = (bf16[64,512]{1,0:T(8,128)(2,1)S(1)}, bf16[64,512]{1,0:T(8,128)(2,1)S(1)}, u32[]{:S(2)}, u32[]{:S(2)}) collective-permute-start(bf16[64,512]{1,0:T(8,128)(2,1)S(1)} %get-tuple-element.38), channel_id=1, source_target_pairs={{0,1},{1,0},{2,3},{3,2},{4,5},{5,4},{6,7},{7,6},{8,9},{9,8},{10,11... | collective-permute-start | bytes 196616 | tf_op jit(solution)/shard_map/ppermute | solution.py:108
  42.2 2.8 %collective-permute-start.26 = (f32[48,128]{1,0:T(8,128)S(1)}, f32[48,128]{1,0:T(8,128)S(1)}, u32[]{:S(2)}, u32[]{:S(2)}) collective-permute-start(f32[48,128]{1,0:T(8,128)S(1)} %get-tuple-element.36), channel_id=1, source_target_pairs={{0,1},{1,0},{2,3},{3,2},{4,5},{5,4},{6,7},{7,6},{8,9},{9,8},{10,11... | collective-permute-start | bytes 73736 | tf_op jit(solution)/shard_map/ppermute | solution.py:108
  42.7 2.3 %collective-permute-start.27 = (f32[48,128]{1,0:T(8,128)S(1)}, f32[48,128]{1,0:T(8,128)S(1)}, u32[]{:S(2)}, u32[]{:S(2)}) collective-permute-start(f32[48,128]{1,0:T(8,128)S(1)} %get-tuple-element.36), channel_id=1, source_target_pairs={{0,3},{1,0},{2,1},{3,2},{4,7},{5,4},{6,5},{7,6},{8,11},{9,8},{10,9... | collective-permute-start | bytes 73736 | tf_op jit(solution)/shard_map/ppermute | solution.py:203
  42.7 2.3 %collective-permute-start.28 = (f32[48,128]{1,0:T(8,128)S(1)}, f32[48,128]{1,0:T(8,128)S(1)}, u32[]{:S(2)}, u32[]{:S(2)}) collective-permute-start(f32[48,128]{1,0:T(8,128)S(1)} %get-tuple-element.36), channel_id=1, source_target_pairs={{0,5},{1,0},{2,7},{3,2},{4,1},{5,4},{6,3},{7,6},{8,13},{9,8},{10,1... | collective-permute-start | bytes 73736 | tf_op jit(solution)/shard_map/ppermute | solution.py:203
  43.5 3.0 %collective-permute-start.29 = (f32[48,128]{1,0:T(8,128)S(1)}, f32[48,128]{1,0:T(8,128)S(1)}, u32[]{:S(2)}, u32[]{:S(2)}) collective-permute-start(f32[48,128]{1,0:T(8,128)S(1)} %get-tuple-element.36), channel_id=1, source_target_pairs={{0,7},{1,0},{2,5},{3,2},{4,3},{5,4},{6,1},{7,6},{8,15},{9,8},{10,1... | collective-permute-start | bytes 73736 | tf_op jit(solution)/shard_map/ppermute | solution.py:203
  46.5 2.7 %collective-permute-start.30 = (f32[48,128]{1,0:T(8,128)S(1)}, f32[48,128]{1,0:T(8,128)S(1)}, u32[]{:S(2)}, u32[]{:S(2)}) collective-permute-start(f32[48,128]{1,0:T(8,128)S(1)} %shard_map.159.refs_0_), channel_id=1, source_target_pairs={{0,1},{1,0},{2,3},{3,2},{4,5},{5,4},{6,7},{7,6},{8,9},{9,8},{10,11... | collective-permute-start | bytes 73736 | tf_op jit(solution)/shard_map/ppermute | solution.py:108

commit v5 on v4

--- a/solution.py
+++ b/solution.py
@@ -180,6 +180,9 @@
     rope_ref[:, 2 * half :] = jnp.where(lane < half, -sine, sine)
 
 
+LOG2_E = 1.4426950408889634
+
+
 def core_number():
     return lax.axis_index("pack") & 1
 
@@ -216,8 +219,9 @@
 
 def join_blocks(*refs):
     out_ref = refs[-1]
-    for i in range(out_ref.shape[0]):
-        out_ref[i] = refs[i][...]
+    count = out_ref.shape[0]
+    for i in range(count):
+        out_ref[count - 1 - i] = refs[i][...]
 
 
 def project_pair(pair_ref, offset, weight_ref):
@@ -281,52 +285,68 @@
     return masks
 
 
-def attend_head(query, head, key_ref, value_ref, other_ref, masks):
+def attend_heads(queries, heads, key_ref, value_ref, other_ref, masks):
     head_dim = 128
-    group = query.shape[1] // head_dim
-    grouped = jnp.concatenate(
-        [query[:, h * head_dim : (h + 1) * head_dim] for h in range(group)], axis=0
-    )
-    column = pl.ds(pl.multiple_of(head * head_dim, head_dim), head_dim)
-    keys = (key_ref[:, column], other_ref[0, :, column])
-    values = (value_ref[:, column], other_ref[1, :, column])
+    scale = head_dim**-0.5
     scores = []
-    for part in range(2):
-        raw = lax.dot_general(
-            grouped, keys[part], (((1,), (1,)), ((), ())), preferred_element_type=jnp.float32
-        )
-        scores.append(jnp.where(masks[part], raw * (head_dim**-0.5), MASKED_LOGIT))
-    highest = jnp.maximum(
-        jnp.max(scores[0], axis=1, keepdims=True), jnp.max(scores[1], axis=1, keepdims=True)
-    )
-    total = 0.0
-    numerators = 0.0
-    for part in range(2):
-        weights = jnp.exp(scores[part] - highest)
-        total = total + jnp.sum(weights, axis=1, keepdims=True)
-        numerators = numerators + jnp.dot(
-            weights.astype(jnp.bfloat16), values[part], preferred_element_type=jnp.float32
-        )
-    return highest, total, numerators
+    columns = []
+    for query, head in zip(queries, heads):
+        grouped = jnp.concatenate(
+            [query[:, i : i + head_dim] for i in range(0, query.shape[1], head_dim)], axis=0
+        )
+        column = pl.ds(pl.multiple_of(head * head_dim, head_dim), head_dim)
+        columns.append(column)
+        raw = [
+            lax.dot_general(
+                grouped, keys, (((1,), (1,)), ((), ())), preferred_element_type=jnp.float32
+            )
+            for keys in (key_ref[:, column], other_ref[0, :, column])
+        ]
+        scores.append([jnp.where(mask, part, MASKED_LOGIT) for mask, part in zip(masks, raw)])
+    maxima = [
+        jnp.maximum(
+            jnp.max(first, axis=1, keepdims=True), jnp.max(second, axis=1, keepdims=True)
+        )
+        for first, second in scores
+    ]
+    weights = [
+        [jnp.exp2((part - highest) * (scale * LOG2_E)) for part in parts]
+        for parts, highest in zip(scores, maxima)
+    ]
+    out = []
+    for parts, highest, column in zip(weights, maxima, columns):
+        total = jnp.sum(parts[0], axis=1, keepdims=True) + jnp.sum(
+            parts[1], axis=1, keepdims=True
+        )
+        numerators = jnp.dot(
+            parts[0].astype(jnp.bfloat16), value_ref[:, column], preferred_element_type=jnp.float32
+        ) + jnp.dot(
+            parts[1].astype(jnp.bfloat16),
+            other_ref[1, :, column],
+            preferred_element_type=jnp.float32,
+        )
+        out.append((highest * scale, total, numerators))
+    return out
 
 
 def attend_remote(*refs):
     query_refs, refs = refs[:3], refs[3:]
     key_ref, value_ref, other_ref, range_ref = refs[:4]
+    out_refs = refs[4:]
 
     @pl.when(core_number() == 1)
     def _():
         rows = query_refs[0].shape[0]
         width = query_refs[0].shape[1] // 2
         masks = token_masks(range_ref, key_ref.shape[0], width // 128)
-        for i, (query_ref, out_ref) in enumerate(zip(query_refs, refs[4:])):
+        for i, (query_ref, out_ref) in enumerate(zip(query_refs, out_refs)):
+            chip = chip_number() ^ (3 - i)
+            queries = [query_ref[:, :width], query_ref[:, width:]]
+            parts = attend_heads(
+                queries, (2 * chip, 2 * chip + 1), key_ref, value_ref, other_ref, masks
+            )
             stats = []
-            for j in range(2):
-                head = 2 * (chip_number() ^ (i + 1)) + j
-                query = query_ref[:, j * width : (j + 1) * width]
-                highest, total, numerators = attend_head(
-                    query, head, key_ref, value_ref, other_ref, masks
-                )
+            for j, (highest, total, numerators) in enumerate(parts):
                 for h in range(width // 128):
                     part = slice(h * rows, (h + 1) * rows)
                     place = slice(j * width + h * 128, j * width + (h + 1) * 128)
@@ -340,34 +360,39 @@
     def _():
         width = query_ref.shape[1] // 2
         masks = token_masks(range_ref, key_ref.shape[0], width // 128)
-        for j in range(2):
-            query = query_ref[:, j * width : (j + 1) * width]
-            highest, total, numerators = attend_head(
-                query, 2 * chip_number() + j, key_ref, value_ref, other_ref, masks
-            )
+        chip = chip_number()
+        parts = attend_heads(
+            [query_ref[:, :width], query_ref[:, width:]],
+            (2 * chip, 2 * chip + 1),
+            key_ref,
+            value_ref,
+            other_ref,
+            masks,
+        )
+        for j, (highest, total, numerators) in enumerate(parts):
             out_ref[j] = numerators
             stats_ref[j, :, :128] = jnp.broadcast_to(highest, (highest.shape[0], 128))
             stats_ref[j, :, 128:] = jnp.broadcast_to(total, (highest.shape[0], 128))
 
 
-def merge_partials(
-    own_ref, stats_ref, first_ref, second_ref, third_ref, attended_ref, other_attended_ref
-):
+def merge_partials(third_ref, second_ref, first_ref, own_ref, stats_ref, *refs):
+    attended_ref = refs[-1]
+
     @pl.when(core_number() == 0)
     def _():
-        rows, width = attended_ref.shape
+        rows = attended_ref.shape[0]
+        width = attended_ref.shape[1] // 2
         others = (first_ref, second_ref, third_ref)
         stats = [ref[:, 2 * width :].astype(jnp.float32) for ref in others]
-        for j, out_ref in enumerate((attended_ref, other_attended_ref)):
+        for j in range(2):
             for h in range(width // 128):
                 part = slice(h * rows, (h + 1) * rows)
-                place = slice(h * 128, (h + 1) * 128)
-                far_place = slice(j * width + h * 128, j * width + (h + 1) * 128)
+                place = slice(j * width + h * 128, j * width + (h + 1) * 128)
                 slot = 2 * (j * (width // 128) + h)
                 maxima = [stats_ref[j, part, :1]] + [lane_sum(s, slot) for s in stats]
                 totals = [stats_ref[j, part, 128:129]] + [lane_sum(s, slot + 1) for s in stats]
                 numerators = [own_ref[j, part, :]]
-                numerators += [ref[:, far_place].astype(jnp.float32) for ref in others]
+                numerators += [ref[:, place].astype(jnp.float32) for ref in others]
                 highest = maxima[0]
                 for value in maxima[1:]:
                     highest = jnp.maximum(highest, value)
@@ -377,40 +402,40 @@
                     factor = jnp.exp(value - highest)
                     denominator = denominator + total * factor
                     summed = summed + numerator * factor
-                out_ref[:, place] = (summed / denominator).astype(jnp.bfloat16)
-
-
-def project_out(attended_ref, weight_ref, *refs, core, offsets):
+                attended_ref[:, place] = (summed / denominator).astype(jnp.bfloat16)
+
+
+def copy_weights(_, weight_ref, out_ref):
+    out_ref[...] = weight_ref[...]
+
+
+def project_out(attended_ref, weight_ref, other_weight_ref, *refs, offset):
     out_ref = refs[-1]
 
-    @pl.when(core_number() == core)
+    @pl.when(core_number() == 0)
     def _():
-        width = out_ref.shape[2]
-        attended = attended_ref[...]
-        for i, offset in enumerate(offsets):
-            column = pl.ds(pl.multiple_of((chip_number() ^ offset) * width, width), width)
-            out_ref[i] = jnp.dot(
-                attended, weight_ref[:, column], preferred_element_type=jnp.float32
-            ).astype(out_ref.dtype)
-
-
-def add_partials(own_ref, other_ref, *out_refs, first):
-    for i, out_ref in enumerate(out_refs):
-        total = own_ref[first + i] + other_ref[i].astype(jnp.float32)
+        width = attended_ref.shape[1] // 2
+        column = pl.ds(pl.multiple_of((chip_number() ^ offset) * 2 * width, 2 * width), 2 * width)
+        total = jnp.dot(
+            attended_ref[:, :width], weight_ref[:, column], preferred_element_type=jnp.float32
+        ) + jnp.dot(
+            attended_ref[:, width:], other_weight_ref[:, column], preferred_element_type=jnp.float32
+        )
         out_ref[...] = total.astype(out_ref.dtype)
 
 
 def finish_hidden(
+    third_ref,
+    second_ref,
+    first_ref,
     kept_ref,
-    first_ref,
-    second_ref,
-    third_ref,
     own_ref,
     other_ref,
     own_gain_ref,
     other_gain_ref,
     sent_ref,
-    state_ref,
+    scaled_ref,
+    other_scaled_ref,
 ):
     width = own_ref.shape[1]
 
@@ -421,49 +446,73 @@
         gains = (other_gain_ref, own_gain_ref)
         for core in range(2):
             place = slice(core * width, (core + 1) * width)
-            hidden = inputs[core][...].astype(jnp.float32) + kept_ref[:, place]
-            for ref in (first_ref, second_ref, third_ref):
+            hidden = inputs[core][...].astype(jnp.float32)
+            for ref in (kept_ref, first_ref, second_ref, third_ref):
                 hidden = hidden + ref[:, place].astype(jnp.float32)
             scaled = hidden * gains[core][...]
-            state_ref[:, place] = scaled
+            (other_scaled_ref, scaled_ref)[core][...] = scaled
             sent_ref[:, place] = scaled.astype(jnp.bfloat16)
             squares = squares + jnp.sum(hidden * hidden, axis=1, keepdims=True)
-        state_ref[:, 2 * width :] = jnp.broadcast_to(squares, (squares.shape[0], 128))
-
-
-def gram_part(state_ref, first_ref, second_ref, third_ref, out_ref, near_ref, far_ref):
+        sent_ref[:, 2 * width :] = lane_pieces([squares])
+
+
+def gram_part(third_ref, second_ref, first_ref, own_ref, _, out_ref, near_ref, far_ref):
     @pl.when(core_number() == 0)
     def _():
-        rows = first_ref.shape[0]
-        width = near_ref.shape[1]
-        near_ref[:rows] = state_ref[:, :width].astype(jnp.bfloat16)
-        far_ref[:rows] = state_ref[:, width : 2 * width].astype(jnp.bfloat16)
-        for i, ref in enumerate((first_ref, second_ref, third_ref)):
-            near_ref[(i + 1) * rows : (i + 2) * rows] = ref[:, :width]
-            far_ref[(i + 1) * rows : (i + 2) * rows] = ref[:, width:]
+        rows = own_ref.shape[0]
+        width = far_ref.shape[1]
+        refs = (own_ref, first_ref, second_ref, third_ref)
+        for i, ref in enumerate(refs):
+            near_ref[i * rows : (i + 1) * rows] = ref[:, :width]
+        for i, ref in enumerate(refs[1:]):
+            far_ref[i * rows : (i + 1) * rows] = ref[:, width : 2 * width]
+        far = jnp.concatenate([ref[:, width : 2 * width] for ref in refs], axis=0)
+        squares = lane_sum(own_ref[:, 2 * width :].astype(jnp.float32), 0)
         gram = 0.0
-        for ref in (near_ref, far_ref):
-            vectors = ref[...]
+        for vectors in (near_ref[...], far):
             gram = gram + lax.dot_general(
                 vectors, vectors, (((1,), (1,)), ((), ())), preferred_element_type=jnp.float32
             )
         half = gram.shape[0] // 2
         out_ref[:half, : 2 * half] = gram[:half]
         out_ref[:half, 2 * half :] = gram[half:]
-        out_ref[half:, :] = state_ref[:, 2 * width :]
-
-
-def sum_grams(own_ref, first_ref, second_ref, third_ref, out_ref):
+        out_ref[half:, :] = jnp.broadcast_to(squares, (rows, 128))
+
+
+def sum_grams(third_ref, second_ref, first_ref, own_ref, *refs):
+    out_ref = refs[-1]
     out_ref[...] = own_ref[...] + first_ref[...] + second_ref[...] + third_ref[...]
+
+
+def partner_masks(partner_ref, out_ref, *, rows):
+    group = lax.axis_index("dp")
+    shape = out_ref.shape[1:]
+    row = lax.broadcasted_iota(jnp.int32, shape, 0)
+    column = lax.broadcasted_iota(jnp.int32, shape, 1)
+    row_id = ((group ^ (row // rows)) * rows) + row % rows
+    column_id = ((group ^ (column // rows)) * rows) + column % rows
+    partners = jnp.broadcast_to(partner_ref[...], shape)
+    row_partner = jnp.sum(
+        jnp.where(column == row_id, partners, 0).astype(jnp.float32), axis=1, keepdims=True
+    )
+    column_partner = jnp.sum(
+        jnp.where(row_id == column_id, row_partner, 0.0), axis=0, keepdims=True
+    )
+    own_partner = column_id.astype(jnp.float32) == row_partner
+    other_partner = row_id.astype(jnp.float32) == column_partner
+    own_partner = own_partner.astype(jnp.float32)
+    out_ref[0] = own_partner
+    out_ref[1] = own_partner + other_partner.astype(jnp.float32)
 
 
 def losses_and_gradient(
     summed_ref,
     other_summed_ref,
     near_ref,
+    sent_ref,
     other_far_ref,
-    state_ref,
-    other_state_ref,
+    scaled_ref,
+    other_scaled_ref,
     gain_ref,
     partner_ref,
     pooled_ref,
@@ -472,11 +521,10 @@
     *,
     model_width,
 ):
-    group = lax.axis_index("dp")
     me = lax.axis_index("pack")
     first_core = core_number() == 0
     count, width = near_ref.shape
-    rows = state_ref.shape[0]
+    rows = scaled_ref.shape[0]
     half = count // 2
     summed = jnp.where(first_core, other_summed_ref[...], summed_ref[...])
     gram = jnp.concatenate([summed[:half, :count], summed[:half, count:]], axis=0)
@@ -484,17 +532,6 @@
     shape = (count, count)
     row = lax.broadcasted_iota(jnp.int32, shape, 0)
     column = lax.broadcasted_iota(jnp.int32, shape, 1)
-    row_id = ((group ^ (row // rows)) * rows) + row % rows
-    column_id = ((group ^ (column // rows)) * rows) + column % rows
-    partners = jnp.broadcast_to(partner_ref[...], shape)
-    row_partner = jnp.sum(
-        jnp.where(column == row_id, partners, 0).astype(jnp.float32), axis=1, keepdims=True
-    )
-    column_partner = jnp.sum(
-        jnp.where(row_id == column_id, row_partner, 0.0), axis=0, keepdims=True
-    )
-    own_partner = column_id.astype(jnp.float32) == row_partner
-    other_partner = row_id.astype(jnp.float32) == column_partner
     diagonal = row == column
     on_diagonal = jnp.where(diagonal, gram, 0.0)
     row_scale = lax.rsqrt(jnp.sum(on_diagonal, axis=1, keepdims=True))
@@ -507,7 +544,8 @@
     column_lse = column_high + jnp.log(
         jnp.sum(jnp.exp(logits - column_high), axis=0, keepdims=True)
     )
-    loss = row_lse - jnp.sum(jnp.where(own_partner, logits, 0.0), axis=1, keepdims=True)
+    target = jnp.sum(partner_ref[0] * logits, axis=1, keepdims=True)
+    loss = row_lse - target
     own = loss_ref.shape[0]
     index = lax.broadcasted_iota(jnp.int32, (count, 1), 0)
     for i in range(own):
@@ -515,8 +553,7 @@
     weights = (
         jnp.exp(logits - row_lse)
         + jnp.exp(logits - column_lse)
-        - own_partner.astype(jnp.float32)
-        - other_partner.astype(jnp.float32)
+        - partner_ref[1]
     )[:rows]
     inner = jnp.sum(weights * cosines[:rows], axis=1, keepdims=True)
     scaled_weights = weights * column_scale
@@ -536,11 +573,12 @@
 
     @pl.when(first_core)
     def _():
-        write(near_ref[...], other_state_ref[:, :width])
+        write(near_ref[...], other_scaled_ref[...])
 
     @pl.when(core_number() == 1)
     def _():
-        write(other_far_ref[...], state_ref[:, width : 2 * width])
+        vectors = jnp.concatenate((sent_ref[:, width : 2 * width], other_far_ref[...]), axis=0)
+        write(vectors, scaled_ref[...])
 
 
 def core_roles(
@@ -599,7 +637,7 @@
         pack_order,
     )
     blocks = in_vmem(
-        join_blocks, shaped((chips - 1,) + pair.shape, bf16), *received, own_projected, rope
+        join_blocks, shaped((chips - 1,) + pair.shape, bf16), *received[::-1], own_projected, rope
     )
     flipped_blocks = flip(blocks, "pack", 1)
 
@@ -631,6 +669,9 @@
     queries = in_vmem(
         join_queries, shaped((stmts, 2 * width), bf16), first_queries, second_queries
     )
+    other_weights = flip(
+        in_vmem(copy_weights, shaped(w_out.shape, bf16), queries, w_out, limit=16), "pack", 1
+    )
     received = [send_across(queries, "pack", k, 0) for k in others]
     group_rows = stmts * (width // head_dim)
     own_part, own_stats = in_vmem(
@@ -646,73 +687,79 @@
     partials = in_vmem(
         attend_remote,
         (shaped((stmts, 2 * width + 128), bf16),) * (chips - 1),
-        *received,
+        *received[::-1],
         cached_keys,
         cached_values,
         other_held,
         ranges,
-        flops=1 << 28,
-    )
-    received = [send_across(part, "pack", k, 1) for k, part in zip(others, partials)]
-    attended, other_attended = in_vmem(
+        flops=1 << 36,
+    )
+    received = [send_across(part, "pack", k, 1) for k, part in zip(others, partials[::-1])]
+    other_hidden_in = flip(hidden_in, "pack", 1)
+    other_gain = flip(final_gain, "pack", 1)
+    attended = in_vmem(
         merge_partials,
-        (shaped((stmts, width), bf16),) * 2,
+        shaped((stmts, 2 * width), bf16),
+        *received[::-1],
         own_part,
         own_stats,
-        *received,
-    )
-    other_attended = flip(other_attended, "pack", 1)
-
-    def projected_on(core, attended, offsets, kind, *after):
+        other_hidden_in,
+        other_gain,
+    )
+
+    def projected_to(offset, kind, *after):
         return in_vmem(
-            lambda *refs: project_out(*refs, core=core, offsets=offsets),
-            shaped((len(offsets), stmts, 2 * width), kind),
+            lambda *refs: project_out(*refs, offset=offset),
+            shaped((stmts, 2 * width), kind),
             attended,
             w_out,
+            other_weights,
             *after,
             limit=16,
             flops=1 << 27,
         )
 
-    own_out = projected_on(0, attended, (1, 2, 3, 0), f32)
-    early = projected_on(1, other_attended, (1, 2), bf16, own_out)
-    late = projected_on(1, other_attended, (3, 0), bf16, early)
-    early = flip(early, "pack", 1)
-    late = flip(late, "pack", 1)
-    chip_part = shaped((stmts, 2 * width), bf16)
-    to_chips = in_vmem(
-        lambda *refs: add_partials(*refs, first=0), (chip_part, chip_part), own_out, early
-    )
-    last, kept = in_vmem(
-        lambda *refs: add_partials(*refs, first=2),
-        (chip_part, shaped((stmts, 2 * width), f32)),
-        own_out,
-        late,
-    )
-    other_kept = flip(kept, "pack", 1)
-    received = [send_across(part, "pack", k, 0) for k, part in zip(others, (*to_chips, last))]
-    vector, state = in_vmem(
+    third = projected_to(3, bf16)
+    second = projected_to(2, bf16, third)
+    first = projected_to(1, bf16, second)
+    kept = projected_to(0, bf16, first)
+    received = [send_across(part, "pack", k, 0) for k, part in zip(others, (first, second, third))]
+    vector, scaled, far_scaled = in_vmem(
         finish_hidden,
-        (shaped((stmts, 2 * width), bf16), shaped((stmts, 2 * width + 128), f32)),
-        other_kept,
-        *received,
+        (shaped((stmts, 2 * width + 128), bf16),) + (shaped((stmts, width), f32),) * 2,
+        *received[::-1],
+        flip(kept, "pack", 1),
         hidden_in,
-        flip(hidden_in, "pack", 1),
+        other_hidden_in,
         final_gain,
-        flip(final_gain, "pack", 1),
-    )
-    other_state = flip(state, "pack", 1)
+        other_gain,
+    )
     received = [send_across(vector, "dp", k, 1) for k in range(1, lax.axis_size("dp"))]
+    other_scaled = flip(far_scaled, "pack", 1)
     gram, near, far = in_vmem(
         gram_part,
-        (shaped((total // 2 + stmts, 128), f32),) + (shaped((total, width), bf16),) * 2,
-        other_state,
-        *received,
-    )
+        (
+            shaped((total // 2 + stmts, 128), f32),
+            shaped((total, width), bf16),
+            shaped((total - stmts, width), bf16),
+        ),
+        *received[::-1],
+        flip(vector, "pack", 1),
+        other_scaled,
+    )
+    received = [send_across(gram, "pack", k, 0) for k in others]
     other_far = flip(far, "pack", 1)
-    other_gram = flip(gram, "pack", 1)
-    received = [send_across(gram, "pack", k, 0) for k in others]
-    summed = in_vmem(sum_grams, shaped(gram.shape, f32), other_gram, *received)
+    summed = in_vmem(
+        sum_grams,
+        shaped(gram.shape, f32),
+        *received[::-1],
+        flip(gram, "pack", 1),
+    )
+    masks = in_vmem(
+        lambda *refs: partner_masks(*refs, rows=stmts),
+        shaped((2, total, total), f32),
+        partner[None],
+    )
     pooled, loss_rows, grad_hidden = pl.pallas_call(
         lambda *refs: losses_and_gradient(*refs, model_width=model_width),
         out_shape=(
@@ -720,18 +767,19 @@
             shaped((stmts // pack_size,), f32),
             shaped((stmts, width), bf16),
         ),
-        in_specs=[whole] * 8,
+        in_specs=[whole] * 9,
         out_specs=(whole, pl.BlockSpec(memory_space=pltpu.SMEM), whole),
         compiler_params=pltpu.CompilerParams(vmem_limit_bytes=8 << 20),
     )(
         summed,
         flip(summed, "pack", 1),
         near,
+        vector,
         other_far,
-        state,
-        other_state,
+        scaled,
+        other_scaled,
         final_gain,
-        partner[None],
+        masks,
     )
     return (pooled, loss_rows, grad_hidden)
 

time: 50.5 us -> 42.4 us (0.84)
  waiting for transfers between devices: 17.2 us -> 12.3 us
  starting transfers between devices: 27.2 us -> 23.1 us
  Pallas kernels: 4.36 us -> 5.34 us
    ppermute x18, waiting for transfers between devices: 11.9 us -> 8.21 us  [send_across(): return lax.ppermute(array, ('dp', 'pack'), pairs)]
    ppermute x18, starting transfers between devices: 19.2 us -> 17 us  [send_across(): return lax.ppermute(array, ('dp', 'pack'), pairs)]
    ppermute x14 -> x13, starting transfers between devices: 7.96 us -> 6.14 us  [flip(): return lax.ppermute(array, axis, [(i, i ^ offset) for i in range(size)])]
    ppermute x14 -> x13, waiting for transfers between devices: 5.24 us -> 4.07 us  [flip(): return lax.ppermute(array, axis, [(i, i ^ offset) for i in range(size)])]
    pallas_call x20 -> x21, Pallas kernels: 3.26 us -> 4.24 us  [in_vmem(): pl.pallas_call(body, out_shape=outputs, in_specs=[whole] * len(operands),...]
  transfers between devices with their start and end apart: 32 -> 31, of which waited for: 15 -> 18; matrix products, arithmetic and copies ran while one was open for 0% -> 0% of each run, Pallas kernels for 5% -> 8%
where the time goes in v5:
time: 42.4 us; the launch traced here: 42.2 us
  starting transfers between devices  23.1 us (54%)
  waiting for transfers between devices  12.3 us (29%)
  Pallas kernels  5.34 us (13%)
  between operations  0.83 us (2%)
  local copies, waits for them, and re-layouts  0.71 us (2%)
    ppermute x18, starting transfers between devices, send_across(): return lax.ppermute(array, ('dp', 'pack'), pairs)  17 us
    ppermute x18, waiting for transfers between devices, send_across(): return lax.ppermute(array, ('dp', 'pack'), pairs)  8.21 us
    ppermute x13, starting transfers between devices, flip(): return lax.ppermute(array, axis, [(i, i ^ offset) for i in range(size)])  6.14 us
    pallas_call x21, Pallas kernels, in_vmem(): pl.pallas_call(body, out_shape=outputs, in_specs=[whole] * len(operands),...  4.24 us
    ppermute x13, waiting for transfers between devices, flip(): return lax.ppermute(array, axis, [(i, i ^ offset) for i in range(size)])  4.07 us
    pallas_call x1, Pallas kernels, core_roles(): pl.pallas_call(lambda *refs: losses_and_gradient(*refs, model_width=model...  1.1 us
  transfers between devices with their start and end apart: 31, of which 18 were waited for; matrix products, arithmetic and copies ran while one was open for 0% of the time, Pallas kernels for 8%

profile of v5, /device:TPU:0, one launch (start us, length us, event | category | flops | bytes accessed | tf_op | source)
XLA Modules:
  0.0 42.2 jit_solution(6976868799562386292)
XLA Ops:
  0.7 0.7 %copy-done.4 = bf16[16,512]{1,0:T(8,128)(2,1)S(1)} copy-done((bf16[16,512]{1,0:T(8,128)(2,1)S(1)}, bf16[16,512]{1,0:T(8,128)(2,1)}, u32[]{:S(2)}) %copy-start.4) | copy-done | bytes 16408
  1.5 0.5 %collective-permute-start = (bf16[16,640]{1,0:T(8,128)(2,1)S(1)}, bf16[16,640]{1,0:T(8,128)(2,1)S(1)}, u32[]{:S(2)}, u32[]{:S(2)}) collective-permute-start(bf16[16,640]{1,0:T(8,128)(2,1)S(1)} %shard_map.140.own_ref.message_ref), channel_id=1, source_target_pairs={{0,1},{1,0},{2,3},{3,2},{4,5},{5,4},{6,7},{7,6},{8,9},{9,8},{10,11... | collective-permute-start | bytes 61448 | tf_op jit(solution)/shard_map/ppermute | solution.py:108
  1.9 0.8 %collective-permute-done.other_ref = bf16[16,640]{1,0:T(8,128)(2,1)S(1)} collective-permute-done((bf16[16,640]{1,0:T(8,128)(2,1)S(1)}, bf16[16,640]{1,0:T(8,128)(2,1)S(1)}, u32[]{:S(2)}, u32[]{:S(2)}) %collective-permute-start) | collective-permute-done | bytes 20512 | tf_op jit(solution)/shard_map/ppermute | solution.py:108
  2.8 4.7 %collective-permute-start.1 = (bf16[2,16,640]{2,1,0:T(8,128)(2,1)S(1)}, bf16[2,16,640]{2,1,0:T(8,128)(2,1)S(1)}, u32[]{:S(2)}, u32[]{:S(2)}) collective-permute-start(bf16[2,16,640]{2,1,0:T(8,128)(2,1)S(1)} %shard_map.141.pair_ref.refs_0_), channel_id=1, source_target_pairs={{0,7},{1,0},{2,5},{3,2},{4,3},{5,4},{6,1},{7,6},{8,15},{9,8},{10,1... | collective-permute-start | bytes 122888 | tf_op jit(solution)/shard_map/ppermute | solution.py:206
  7.7 0.2 shard_map.142.refs_3_.refs_2_
  7.9 1.2 %collective-permute-done.1.refs_0_ = bf16[2,16,640]{2,1,0:T(8,128)(2,1)S(1)} collective-permute-done((bf16[2,16,640]{2,1,0:T(8,128)(2,1)S(1)}, bf16[2,16,640]{2,1,0:T(8,128)(2,1)S(1)}, u32[]{:S(2)}, u32[]{:S(2)}) %collective-permute-start.1) | collective-permute-done | bytes 40992 | tf_op jit(solution)/shard_map/ppermute | solution.py:206
  9.2 0.4 collective-permute-done.2.refs_1_
  9.5 0.4 collective-permute-done.3.refs_2_
  9.9 1.6 %collective-permute-start.4 = (bf16[3,2,16,640]{3,2,1,0:T(8,128)(2,1)S(1)}, bf16[3,2,16,640]{3,2,1,0:T(8,128)(2,1)S(1)}, u32[]{:S(2)}, u32[]{:S(2)}) collective-permute-start(bf16[3,2,16,640]{3,2,1,0:T(8,128)(2,1)S(1)} %shard_map.144.refs_1_), channel_id=1, source_target_pairs={{0,1},{1,0},{2,3},{3,2},{4,5},{5,4},{6,7},{7,6},{8,9},{9,8},{10,11... | collective-permute-start | bytes 368648 | tf_op jit(solution)/shard_map/ppermute | solution.py:108
  11.5 0.8 %collective-permute-start.5 = (bf16[16,512]{1,0:T(8,128)(2,1)S(1)}, bf16[16,512]{1,0:T(8,128)(2,1)S(1)}, u32[]{:S(2)}, u32[]{:S(2)}) collective-permute-start(bf16[16,512]{1,0:T(8,128)(2,1)S(1)} %shard_map.146._), channel_id=1, source_target_pairs={{0,1},{1,0},{2,3},{3,2},{4,5},{5,4},{6,7},{7,6},{8,9},{9,8},{10,11... | collective-permute-start | bytes 49160 | tf_op jit(solution)/shard_map/ppermute | solution.py:108
  12.5 0.7 %shard_map.145.first_ref = bf16[16,512]{1,0:T(8,128)(2,1)S(1)} custom-call(bf16[2,16,640]{2,1,0:T(8,128)(2,1)S(1)} %shard_map.141.pair_ref.refs_0_, bf16[3,2,16,640]{3,2,1,0:T(8,128)(2,1)S(1)} %collective-permute-done.4.refs_1_, f32[16,512]{1,0:T(8,128)S(1)} %shard_map.142.refs_3_.refs_2_, bf16[4096,512]{1,0:T(8,128)(2,1)S(1)} %copy-done.1, ...), custom_call_target="tpu_custom_call" | custom-call | flops 68719476736 | bytes 4407808 | tf_op jit(solution)/shard_map/pallas_call | solution.py:114
  13.2 1.6 %collective-permute-start.6 = (bf16[16,1024]{1,0:T(8,128)(2,1)S(1)}, bf16[16,1024]{1,0:T(8,128)(2,1)S(1)}, u32[]{:S(2)}, u32[]{:S(2)}) collective-permute-start(bf16[16,1024]{1,0:T(8,128)(2,1)S(1)} %shard_map.147.query_ref._), channel_id=1, source_target_pairs={{0,7},{1,0},{2,5},{3,2},{4,3},{5,4},{6,1},{7,6},{8,15},{9,8},{10,1... | collective-permute-start | bytes 98312 | tf_op jit(solution)/shard_map/ppermute | solution.py:206
  15.0 0.3 shard_map.152
  15.3 0.4 collective-permute-start.15
  15.6 0.7 %collective-permute-done.6.refs_0_ = bf16[16,1024]{1,0:T(8,128)(2,1)S(1)} collective-permute-done((bf16[16,1024]{1,0:T(8,128)(2,1)S(1)}, bf16[16,1024]{1,0:T(8,128)(2,1)S(1)}, u32[]{:S(2)}, u32[]{:S(2)}) %collective-permute-start.6) | collective-permute-done | bytes 32800 | tf_op jit(solution)/shard_map/ppermute | solution.py:206
  16.4 0.3 collective-permute-done.7.refs_1_
  16.7 0.3 collective-permute-done.8.refs_2_
  17.0 3.3 %collective-permute-start.10 = (bf16[16,1152]{1,0:T(8,128)(2,1)S(1)}, bf16[16,1152]{1,0:T(8,128)(2,1)S(1)}, u32[]{:S(2)}, u32[]{:S(2)}) collective-permute-start(bf16[16,1152]{1,0:T(8,128)(2,1)S(1)} %get-tuple-element.18), channel_id=1, source_target_pairs={{0,1},{1,6},{2,3},{3,4},{4,5},{5,2},{6,7},{7,0},{8,9},{9,14},{10,1... | collective-permute-start | bytes 110600 | tf_op jit(solution)/shard_map/ppermute | solution.py:206
  20.4 0.9 %collective-permute-start.12 = (bf16[16,1152]{1,0:T(8,128)(2,1)S(1)}, bf16[16,1152]{1,0:T(8,128)(2,1)S(1)}, u32[]{:S(2)}, u32[]{:S(2)}) collective-permute-start(bf16[16,1152]{1,0:T(8,128)(2,1)S(1)} %get-tuple-element.20), channel_id=1, source_target_pairs={{0,1},{1,2},{2,3},{3,0},{4,5},{5,6},{6,7},{7,4},{8,9},{9,10},{10,1... | collective-permute-start | bytes 110600 | tf_op jit(solution)/shard_map/ppermute | solution.py:206
  21.3 1.3 %collective-permute-done.14.refs_1_.other_gain_ref = f32[1,512]{1,0:T(1,128)S(1)} collective-permute-done((f32[1,512]{1,0:T(1,128)S(1)}, f32[1,512]{1,0:T(1,128)S(1)}, u32[]{:S(2)}, u32[]{:S(2)}) %collective-permute-start.14) | collective-permute-done | bytes 2080 | tf_op jit(solution)/shard_map/ppermute | solution.py:108
  22.6 0.4 collective-permute-start.13
  23.0 0.5 %shard_map.150 = (f32[2,64,128]{2,1,0:T(8,128)S(1)}, f32[2,64,256]{2,1,0:T(8,128)S(1)}) custom-call(bf16[16,1024]{1,0:T(8,128)(2,1)S(1)} %shard_map.147.query_ref._, bf16[320,1024]{1,0:T(8,128)(2,1)S(1)} %copy-done.2, bf16[320,1024]{1,0:T(8,128)(2,1)S(1)} %copy-done.3, bf16[2,320,1024]{2,1,0:T(8,128)(2,1)S(1)} %collective-permute-done.9.refs_5_.other_ref, ...), custom_call_target="tpu_custom_call" | custom-call | flops 134217728 | bytes 2670592 | tf_op jit(solution)/shard_map/pallas_call | solution.py:114
  23.4 0.3 collective-permute-done.13.refs_0_.other_ref
  23.8 1.2 %collective-permute-done.11.second_ref = bf16[16,1152]{1,0:T(8,128)(2,1)S(1)} collective-permute-done((bf16[16,1152]{1,0:T(8,128)(2,1)S(1)}, bf16[16,1152]{1,0:T(8,128)(2,1)S(1)}, u32[]{:S(2)}, u32[]{:S(2)}) %collective-permute-start.11) | collective-permute-done | bytes 36896 | tf_op jit(solution)/shard_map/ppermute | solution.py:206
  25.0 0.3 shard_map.151.refs_0_
  25.3 0.4 shard_map.153.refs_3_
  25.7 0.3 collective-permute-start.16
  26.0 0.4 shard_map.154.refs_3_
  26.4 0.8 %collective-permute-start.17 = (bf16[16,1024]{1,0:T(8,128)(2,1)S(1)}, bf16[16,1024]{1,0:T(8,128)(2,1)S(1)}, u32[]{:S(2)}, u32[]{:S(2)}) collective-permute-start(bf16[16,1024]{1,0:T(8,128)(2,1)S(1)} %shard_map.154.refs_3_), channel_id=1, source_target_pairs={{0,5},{1,0},{2,7},{3,2},{4,1},{5,4},{6,3},{7,6},{8,13},{9,8},{10,1... | collective-permute-start | bytes 98312 | tf_op jit(solution)/shard_map/ppermute | solution.py:206
  27.1 0.4 shard_map.155.refs_3_
  27.5 0.4 shard_map.156
  28.0 0.7 %collective-permute-done.17.second_ref = bf16[16,1024]{1,0:T(8,128)(2,1)S(1)} collective-permute-done((bf16[16,1024]{1,0:T(8,128)(2,1)S(1)}, bf16[16,1024]{1,0:T(8,128)(2,1)S(1)}, u32[]{:S(2)}, u32[]{:S(2)}) %collective-permute-start.17) | collective-permute-done | bytes 32800 | tf_op jit(solution)/shard_map/ppermute | solution.py:206
  28.7 0.4 collective-permute-done.18.first_ref
  29.1 1.8 %collective-permute-start.20 = (bf16[16,1152]{1,0:T(8,128)(2,1)S(1)}, bf16[16,1152]{1,0:T(8,128)(2,1)S(1)}, u32[]{:S(2)}, u32[]{:S(2)}) collective-permute-start(bf16[16,1152]{1,0:T(8,128)(2,1)S(1)} %get-tuple-element.23.refs_3_), channel_id=1, source_target_pairs={{0,1},{1,24},{2,3},{3,26},{4,5},{5,28},{6,7},{7,30},{8,9},{9,16},{... | collective-permute-start | bytes 110600 | tf_op jit(solution)/shard_map/ppermute | solution.py:206
  30.9 0.8 %collective-permute-start.21 = (bf16[16,1152]{1,0:T(8,128)(2,1)S(1)}, bf16[16,1152]{1,0:T(8,128)(2,1)S(1)}, u32[]{:S(2)}, u32[]{:S(2)}) collective-permute-start(bf16[16,1152]{1,0:T(8,128)(2,1)S(1)} %get-tuple-element.23.refs_3_), channel_id=1, source_target_pairs={{0,1},{1,16},{2,3},{3,18},{4,5},{5,20},{6,7},{7,22},{8,9},{9,24},{... | collective-permute-start | bytes 110600 | tf_op jit(solution)/shard_map/ppermute | solution.py:206
  31.7 0.9 %collective-permute-start.22 = (bf16[16,1152]{1,0:T(8,128)(2,1)S(1)}, bf16[16,1152]{1,0:T(8,128)(2,1)S(1)}, u32[]{:S(2)}, u32[]{:S(2)}) collective-permute-start(bf16[16,1152]{1,0:T(8,128)(2,1)S(1)} %get-tuple-element.23.refs_3_), channel_id=1, source_target_pairs={{0,1},{1,8},{2,3},{3,10},{4,5},{5,12},{6,7},{7,14},{8,9},{9,0},{10... | collective-permute-start | bytes 110600 | tf_op jit(solution)/shard_map/ppermute | solution.py:206
  32.6 0.5 %collective-permute-start.24 = (f32[16,512]{1,0:T(8,128)S(1)}, f32[16,512]{1,0:T(8,128)S(1)}, u32[]{:S(2)}, u32[]{:S(2)}) collective-permute-start(f32[16,512]{1,0:T(8,128)S(1)} %get-tuple-element.24), channel_id=1, source_target_pairs={{0,1},{1,0},{2,3},{3,2},{4,5},{5,4},{6,7},{7,6},{8,9},{9,8},{10,11... | collective-permute-start | bytes 98312 | tf_op jit(solution)/shard_map/ppermute | solution.py:108
  33.1 0.9 %collective-permute-done.24._.refs_6_ = f32[16,512]{1,0:T(8,128)S(1)} collective-permute-done((f32[16,512]{1,0:T(8,128)S(1)}, f32[16,512]{1,0:T(8,128)S(1)}, u32[]{:S(2)}, u32[]{:S(2)}) %collective-permute-start.24) | collective-permute-done | bytes 32800 | tf_op jit(solution)/shard_map/ppermute | solution.py:108
  33.9 0.8 %collective-permute-done.20.third_ref = bf16[16,1152]{1,0:T(8,128)(2,1)S(1)} collective-permute-done((bf16[16,1152]{1,0:T(8,128)(2,1)S(1)}, bf16[16,1152]{1,0:T(8,128)(2,1)S(1)}, u32[]{:S(2)}, u32[]{:S(2)}) %collective-permute-start.20) | collective-permute-done | bytes 36896 | tf_op jit(solution)/shard_map/ppermute | solution.py:206
  34.7 0.6 %collective-permute-done.22.first_ref = bf16[16,1152]{1,0:T(8,128)(2,1)S(1)} collective-permute-done((bf16[16,1152]{1,0:T(8,128)(2,1)S(1)}, bf16[16,1152]{1,0:T(8,128)(2,1)S(1)}, u32[]{:S(2)}, u32[]{:S(2)}) %collective-permute-start.22) | collective-permute-done | bytes 36896 | tf_op jit(solution)/shard_map/ppermute | solution.py:206
  35.3 0.2 shard_map.158
  35.7 1.4 %collective-permute-start.26 = (f32[48,128]{1,0:T(8,128)S(1)}, f32[48,128]{1,0:T(8,128)S(1)}, u32[]{:S(2)}, u32[]{:S(2)}) collective-permute-start(f32[48,128]{1,0:T(8,128)S(1)} %get-tuple-element.25), channel_id=1, source_target_pairs={{0,5},{1,0},{2,7},{3,2},{4,1},{5,4},{6,3},{7,6},{8,13},{9,8},{10,1... | collective-permute-start | bytes 73736 | tf_op jit(solution)/shard_map/ppermute | solution.py:206
  37.2 0.5 %collective-permute-start.28 = (f32[48,128]{1,0:T(8,128)S(1)}, f32[48,128]{1,0:T(8,128)S(1)}, u32[]{:S(2)}, u32[]{:S(2)}) collective-permute-start(f32[48,128]{1,0:T(8,128)S(1)} %get-tuple-element.25), channel_id=1, source_target_pairs={{0,1},{1,0},{2,3},{3,2},{4,5},{5,4},{6,7},{7,6},{8,9},{9,8},{10,11... | collective-permute-start | bytes 73736 | tf_op jit(solution)/shard_map/ppermute | solution.py:108
  37.7 1.0 %collective-permute-done.26.second_ref = f32[48,128]{1,0:T(8,128)S(1)} collective-permute-done((f32[48,128]{1,0:T(8,128)S(1)}, f32[48,128]{1,0:T(8,128)S(1)}, u32[]{:S(2)}, u32[]{:S(2)}) %collective-permute-start.26) | collective-permute-done | bytes 24608 | tf_op jit(solution)/shard_map/ppermute | solution.py:206
  38.7 0.2 collective-permute-done.27.first_ref
  38.9 1.3 %collective-permute-start.29 = (f32[48,128]{1,0:T(8,128)S(1)}, f32[48,128]{1,0:T(8,128)S(1)}, u32[]{:S(2)}, u32[]{:S(2)}) collective-permute-start(f32[48,128]{1,0:T(8,128)S(1)} %shard_map.159.refs_0_), channel_id=1, source_target_pairs={{0,1},{1,0},{2,3},{3,2},{4,5},{5,4},{6,7},{7,6},{8,9},{9,8},{10,11... | collective-permute-start | bytes 73736 | tf_op jit(solution)/shard_map/ppermute | solution.py:108
  40.4 0.7 %collective-permute-done.29.refs_1_ = f32[48,128]{1,0:T(8,128)S(1)} collective-permute-done((f32[48,128]{1,0:T(8,128)S(1)}, f32[48,128]{1,0:T(8,128)S(1)}, u32[]{:S(2)}, u32[]{:S(2)}) %collective-permute-start.29) | collective-permute-done | bytes 24608 | tf_op jit(solution)/shard_map/ppermute | solution.py:108
  41.1 1.1 %shard_map.161 = (bf16[16,512]{1,0:T(8,128)(2,1)}, f32[2]{0:T(128)}, bf16[16,512]{1,0:T(8,128)(2,1)}) custom-call(f32[48,128]{1,0:T(8,128)S(1)} %shard_map.159.refs_0_, f32[48,128]{1,0:T(8,128)S(1)} %collective-permute-done.29.refs_1_, bf16[64,512]{1,0:T(8,128)(2,1)S(1)} %get-tuple-element.26.refs_2_, bf16[16,1152]{1,0:T(8,128)(2,1)S(1)} %get-tuple-element.23.refs_3_, ...), custom_call_target="tpu_custom_call" | custom-call | tf_op jit(solution)/shard_map/pallas_call | solution.py:763
  (61 shorter events, 1.3 us)
Async XLA Ops:
  0.6 6.9 %copy-start.11 = (f32[1,128]{1,0:T(1,128)S(1)}, f32[1,128]{1,0:T(1,128)}, u32[]{:S(2)}) copy-start(f32[1,128]{1,0:T(1,128)} %constant.2.clone.frequency_ref) | copy-start | bytes 1540
  0.6 0.7 %copy-start.4 = (bf16[16,512]{1,0:T(8,128)(2,1)S(1)}, bf16[16,512]{1,0:T(8,128)(2,1)}, u32[]{:S(2)}) copy-start(bf16[16,512]{1,0:T(8,128)(2,1)} %own_ref.1) | copy-start | bytes 49156
  0.7 0.7 %copy-start.6 = (f32[512]{0:T(512)S(1)}, f32[512]{0:T(512)}, u32[]{:S(2)}) copy-start(f32[512]{0:T(512)} %param.13) | copy-start | bytes 6148
  0.7 6.8 %copy-start.9 = (s32[1,16]{1,0:T(1,128)S(1)}, s32[1,16]{1,0:T(1,128)}, u32[]{:S(2)}) copy-start(s32[1,16]{1,0:T(1,128)} %lengths_ref.1) | copy-start | bytes 196
  0.7 6.8 %copy-start.10 = (s32[1,16]{1,0:T(1,128)S(1)}, s32[1,16]{1,0:T(1,128)}, u32[]{:S(2)}) copy-start(s32[1,16]{1,0:T(1,128)} %order_ref.1) | copy-start | bytes 196
  0.7 7.0 %copy-start.1 = (bf16[4096,512]{1,0:T(8,128)(2,1)S(1)}, bf16[4096,512]{1,0:T(8,128)(2,1)}, u32[]{:S(2)}) copy-start(bf16[4096,512]{1,0:T(8,128)(2,1)} %refs_3_.4) | copy-start | bytes 12582916
  0.7 10.8 %copy-start.7 = (f32[128]{0:T(128)S(1)}, f32[128]{0:T(128)}, u32[]{:S(2)}) copy-start(f32[128]{0:T(128)} %param.15) | copy-start | bytes 1540
  1.5 1.3 %collective-permute-start = (bf16[16,640]{1,0:T(8,128)(2,1)S(1)}, bf16[16,640]{1,0:T(8,128)(2,1)S(1)}, u32[]{:S(2)}, u32[]{:S(2)}) collective-permute-start(bf16[16,640]{1,0:T(8,128)(2,1)S(1)} %shard_map.140.own_ref.message_ref), channel_id=1, source_target_pairs={{0,1},{1,0},{2,3},{3,2},{4,5},{5,4},{6,7},{7,6},{8,9},{9,8},{10,11... | collective-permute-start | bytes 61448 | tf_op jit(solution)/shard_map/ppermute | solution.py:108
  2.8 6.4 %collective-permute-start.1 = (bf16[2,16,640]{2,1,0:T(8,128)(2,1)S(1)}, bf16[2,16,640]{2,1,0:T(8,128)(2,1)S(1)}, u32[]{:S(2)}, u32[]{:S(2)}) collective-permute-start(bf16[2,16,640]{2,1,0:T(8,128)(2,1)S(1)} %shard_map.141.pair_ref.refs_0_), channel_id=1, source_target_pairs={{0,7},{1,0},{2,5},{3,2},{4,3},{5,4},{6,1},{7,6},{8,15},{9,8},{10,1... | collective-permute-start | bytes 122888 | tf_op jit(solution)/shard_map/ppermute | solution.py:206
  7.5 2.1 %collective-permute-start.2 = (bf16[2,16,640]{2,1,0:T(8,128)(2,1)S(1)}, bf16[2,16,640]{2,1,0:T(8,128)(2,1)S(1)}, u32[]{:S(2)}, u32[]{:S(2)}) collective-permute-start(bf16[2,16,640]{2,1,0:T(8,128)(2,1)S(1)} %shard_map.141.pair_ref.refs_0_), channel_id=1, source_target_pairs={{0,5},{1,0},{2,7},{3,2},{4,1},{5,4},{6,3},{7,6},{8,13},{9,8},{10,1... | collective-permute-start | bytes 122888 | tf_op jit(solution)/shard_map/ppermute | solution.py:206
  7.5 2.4 %collective-permute-start.3 = (bf16[2,16,640]{2,1,0:T(8,128)(2,1)S(1)}, bf16[2,16,640]{2,1,0:T(8,128)(2,1)S(1)}, u32[]{:S(2)}, u32[]{:S(2)}) collective-permute-start(bf16[2,16,640]{2,1,0:T(8,128)(2,1)S(1)} %shard_map.141.pair_ref.refs_0_), channel_id=1, source_target_pairs={{0,3},{1,0},{2,1},{3,2},{4,7},{5,4},{6,5},{7,6},{8,11},{9,8},{10,9... | collective-permute-start | bytes 122888 | tf_op jit(solution)/shard_map/ppermute | solution.py:206
  7.7 4.6 %copy-start.2 = (bf16[320,1024]{1,0:T(8,128)(2,1)S(1)}, bf16[320,1024]{1,0:T(8,128)(2,1)}, u32[]{:S(2)}) copy-start(bf16[320,1024]{1,0:T(8,128)(2,1)} %key_ref.3) | copy-start | bytes 1966084
  7.7 4.6 %copy-start.3 = (bf16[320,1024]{1,0:T(8,128)(2,1)S(1)}, bf16[320,1024]{1,0:T(8,128)(2,1)}, u32[]{:S(2)}) copy-start(bf16[320,1024]{1,0:T(8,128)(2,1)} %value_ref.3) | copy-start | bytes 1966084
  9.9 2.6 %collective-permute-start.4 = (bf16[3,2,16,640]{3,2,1,0:T(8,128)(2,1)S(1)}, bf16[3,2,16,640]{3,2,1,0:T(8,128)(2,1)S(1)}, u32[]{:S(2)}, u32[]{:S(2)}) collective-permute-start(bf16[3,2,16,640]{3,2,1,0:T(8,128)(2,1)S(1)} %shard_map.144.refs_1_), channel_id=1, source_target_pairs={{0,1},{1,0},{2,3},{3,2},{4,5},{5,4},{6,7},{7,6},{8,9},{9,8},{10,11... | collective-permute-start | bytes 368648 | tf_op jit(solution)/shard_map/ppermute | solution.py:108
  11.5 1.7 %collective-permute-start.5 = (bf16[16,512]{1,0:T(8,128)(2,1)S(1)}, bf16[16,512]{1,0:T(8,128)(2,1)S(1)}, u32[]{:S(2)}, u32[]{:S(2)}) collective-permute-start(bf16[16,512]{1,0:T(8,128)(2,1)S(1)} %shard_map.146._), channel_id=1, source_target_pairs={{0,1},{1,0},{2,3},{3,2},{4,5},{5,4},{6,7},{7,6},{8,9},{9,8},{10,11... | collective-permute-start | bytes 49160 | tf_op jit(solution)/shard_map/ppermute | solution.py:108
  12.4 2.6 %copy-start = (bf16[512,4096]{1,0:T(8,128)(2,1)S(1)}, bf16[512,4096]{1,0:T(8,128)(2,1)}, u32[]{:S(2)}) copy-start(bf16[512,4096]{1,0:T(8,128)(2,1)} %refs_1_.7) | copy-start | bytes 12582916
  12.4 4.6 %collective-permute-start.9 = (bf16[2,320,1024]{2,1,0:T(8,128)(2,1)S(1)}, bf16[2,320,1024]{2,1,0:T(8,128)(2,1)S(1)}, u32[]{:S(2)}, u32[]{:S(2)}) collective-permute-start(bf16[2,320,1024]{2,1,0:T(8,128)(2,1)S(1)} %shard_map.148), channel_id=1, source_target_pairs={{0,1},{1,0},{2,3},{3,2},{4,5},{5,4},{6,7},{7,6},{8,9},{9,8},{10,11... | collective-permute-start | bytes 3932168 | tf_op jit(solution)/shard_map/ppermute | solution.py:108
  13.2 3.2 %collective-permute-start.6 = (bf16[16,1024]{1,0:T(8,128)(2,1)S(1)}, bf16[16,1024]{1,0:T(8,128)(2,1)S(1)}, u32[]{:S(2)}, u32[]{:S(2)}) collective-permute-start(bf16[16,1024]{1,0:T(8,128)(2,1)S(1)} %shard_map.147.query_ref._), channel_id=1, source_target_pairs={{0,7},{1,0},{2,5},{3,2},{4,3},{5,4},{6,1},{7,6},{8,15},{9,8},{10,1... | collective-permute-start | bytes 98312 | tf_op jit(solution)/shard_map/ppermute | solution.py:206
  14.8 1.9 %collective-permute-start.7 = (bf16[16,1024]{1,0:T(8,128)(2,1)S(1)}, bf16[16,1024]{1,0:T(8,128)(2,1)S(1)}, u32[]{:S(2)}, u32[]{:S(2)}) collective-permute-start(bf16[16,1024]{1,0:T(8,128)(2,1)S(1)} %shard_map.147.query_ref._), channel_id=1, source_target_pairs={{0,5},{1,0},{2,7},{3,2},{4,1},{5,4},{6,3},{7,6},{8,13},{9,8},{10,1... | collective-permute-start | bytes 98312 | tf_op jit(solution)/shard_map/ppermute | solution.py:206
  14.8 2.2 %collective-permute-start.8 = (bf16[16,1024]{1,0:T(8,128)(2,1)S(1)}, bf16[16,1024]{1,0:T(8,128)(2,1)S(1)}, u32[]{:S(2)}, u32[]{:S(2)}) collective-permute-start(bf16[16,1024]{1,0:T(8,128)(2,1)S(1)} %shard_map.147.query_ref._), channel_id=1, source_target_pairs={{0,3},{1,0},{2,1},{3,2},{4,7},{5,4},{6,5},{7,6},{8,11},{9,8},{10,9... | collective-permute-start | bytes 98312 | tf_op jit(solution)/shard_map/ppermute | solution.py:206
  15.3 10.0 %collective-permute-start.15 = (bf16[512,4096]{1,0:T(8,128)(2,1)S(1)}, bf16[512,4096]{1,0:T(8,128)(2,1)S(1)}, u32[]{:S(2)}, u32[]{:S(2)}) collective-permute-start(bf16[512,4096]{1,0:T(8,128)(2,1)S(1)} %shard_map.152), channel_id=1, source_target_pairs={{0,1},{1,0},{2,3},{3,2},{4,5},{5,4},{6,7},{7,6},{8,9},{9,8},{10,11... | collective-permute-start | bytes 12582920 | tf_op jit(solution)/shard_map/ppermute | solution.py:108
  17.0 4.3 %copy-start.5 = (f32[512]{0:T(512)S(1)}, f32[512]{0:T(512)}, u32[]{:S(2)}) copy-start(f32[512]{0:T(512)} %param.19) | copy-start | bytes 6148
  17.0 6.8 %collective-permute-start.10 = (bf16[16,1152]{1,0:T(8,128)(2,1)S(1)}, bf16[16,1152]{1,0:T(8,128)(2,1)S(1)}, u32[]{:S(2)}, u32[]{:S(2)}) collective-permute-start(bf16[16,1152]{1,0:T(8,128)(2,1)S(1)} %get-tuple-element.18), channel_id=1, source_target_pairs={{0,1},{1,6},{2,3},{3,4},{4,5},{5,2},{6,7},{7,0},{8,9},{9,14},{10,1... | collective-permute-start | bytes 110600 | tf_op jit(solution)/shard_map/ppermute | solution.py:206
  20.3 4.7 %collective-permute-start.11 = (bf16[16,1152]{1,0:T(8,128)(2,1)S(1)}, bf16[16,1152]{1,0:T(8,128)(2,1)S(1)}, u32[]{:S(2)}, u32[]{:S(2)}) collective-permute-start(bf16[16,1152]{1,0:T(8,128)(2,1)S(1)} %get-tuple-element.19), channel_id=1, source_target_pairs={{0,1},{1,4},{2,3},{3,6},{4,5},{5,0},{6,7},{7,2},{8,9},{9,12},{10,1... | collective-permute-start | bytes 110600 | tf_op jit(solution)/shard_map/ppermute | solution.py:206
  20.4 4.6 %collective-permute-start.12 = (bf16[16,1152]{1,0:T(8,128)(2,1)S(1)}, bf16[16,1152]{1,0:T(8,128)(2,1)S(1)}, u32[]{:S(2)}, u32[]{:S(2)}) collective-permute-start(bf16[16,1152]{1,0:T(8,128)(2,1)S(1)} %get-tuple-element.20), channel_id=1, source_target_pairs={{0,1},{1,2},{2,3},{3,0},{4,5},{5,6},{6,7},{7,4},{8,9},{9,10},{10,1... | collective-permute-start | bytes 110600 | tf_op jit(solution)/shard_map/ppermute | solution.py:206
  21.3 1.3 %collective-permute-start.14 = (f32[1,512]{1,0:T(1,128)S(1)}, f32[1,512]{1,0:T(1,128)S(1)}, u32[]{:S(2)}, u32[]{:S(2)}) collective-permute-start(f32[1,512]{1,0:T(1,128)S(1)} %bitcast.4), channel_id=1, source_target_pairs={{0,1},{1,0},{2,3},{3,2},{4,5},{5,4},{6,7},{7,6},{8,9},{9,8},{10,11... | collective-permute-start | bytes 6152 | tf_op jit(solution)/shard_map/ppermute | solution.py:108
  22.6 1.2 %collective-permute-start.13 = (bf16[16,512]{1,0:T(8,128)(2,1)S(1)}, bf16[16,512]{1,0:T(8,128)(2,1)S(1)}, u32[]{:S(2)}, u32[]{:S(2)}) collective-permute-start(bf16[16,512]{1,0:T(8,128)(2,1)S(1)} %copy-done.4), channel_id=1, source_target_pairs={{0,1},{1,0},{2,3},{3,2},{4,5},{5,4},{6,7},{7,6},{8,9},{9,8},{10,11... | collective-permute-start | bytes 49160 | tf_op jit(solution)/shard_map/ppermute | solution.py:108
  25.7 2.4 %collective-permute-start.16 = (bf16[16,1024]{1,0:T(8,128)(2,1)S(1)}, bf16[16,1024]{1,0:T(8,128)(2,1)S(1)}, u32[]{:S(2)}, u32[]{:S(2)}) collective-permute-start(bf16[16,1024]{1,0:T(8,128)(2,1)S(1)} %shard_map.153.refs_3_), channel_id=1, source_target_pairs={{0,7},{1,0},{2,5},{3,2},{4,3},{5,4},{6,1},{7,6},{8,15},{9,8},{10,1... | collective-permute-start | bytes 98312 | tf_op jit(solution)/shard_map/ppermute | solution.py:206
  26.4 2.4 %collective-permute-start.17 = (bf16[16,1024]{1,0:T(8,128)(2,1)S(1)}, bf16[16,1024]{1,0:T(8,128)(2,1)S(1)}, u32[]{:S(2)}, u32[]{:S(2)}) collective-permute-start(bf16[16,1024]{1,0:T(8,128)(2,1)S(1)} %shard_map.154.refs_3_), channel_id=1, source_target_pairs={{0,5},{1,0},{2,7},{3,2},{4,1},{5,4},{6,3},{7,6},{8,13},{9,8},{10,1... | collective-permute-start | bytes 98312 | tf_op jit(solution)/shard_map/ppermute | solution.py:206
  27.5 12.8 %copy-start.8 = (s32[64]{0:T(128)S(1)}, s32[64]{0:T(128)}, u32[]{:S(2)}) copy-start(s32[64]{0:T(128)} %param.22) | copy-start | bytes 772
  27.5 1.6 %collective-permute-start.18 = (bf16[16,1024]{1,0:T(8,128)(2,1)S(1)}, bf16[16,1024]{1,0:T(8,128)(2,1)S(1)}, u32[]{:S(2)}, u32[]{:S(2)}) collective-permute-start(bf16[16,1024]{1,0:T(8,128)(2,1)S(1)} %shard_map.155.refs_3_), channel_id=1, source_target_pairs={{0,3},{1,0},{2,1},{3,2},{4,7},{5,4},{6,5},{7,6},{8,11},{9,8},{10,9... | collective-permute-start | bytes 98312 | tf_op jit(solution)/shard_map/ppermute | solution.py:206
  27.9 1.2 %collective-permute-start.19 = (bf16[16,1024]{1,0:T(8,128)(2,1)S(1)}, bf16[16,1024]{1,0:T(8,128)(2,1)S(1)}, u32[]{:S(2)}, u32[]{:S(2)}) collective-permute-start(bf16[16,1024]{1,0:T(8,128)(2,1)S(1)} %shard_map.156), channel_id=1, source_target_pairs={{0,1},{1,0},{2,3},{3,2},{4,5},{5,4},{6,7},{7,6},{8,9},{9,8},{10,11... | collective-permute-start | bytes 98312 | tf_op jit(solution)/shard_map/ppermute | solution.py:108
  29.1 5.6 %collective-permute-start.20 = (bf16[16,1152]{1,0:T(8,128)(2,1)S(1)}, bf16[16,1152]{1,0:T(8,128)(2,1)S(1)}, u32[]{:S(2)}, u32[]{:S(2)}) collective-permute-start(bf16[16,1152]{1,0:T(8,128)(2,1)S(1)} %get-tuple-element.23.refs_3_), channel_id=1, source_target_pairs={{0,1},{1,24},{2,3},{3,26},{4,5},{5,28},{6,7},{7,30},{8,9},{9,16},{... | collective-permute-start | bytes 110600 | tf_op jit(solution)/shard_map/ppermute | solution.py:206
  30.9 3.8 %collective-permute-start.21 = (bf16[16,1152]{1,0:T(8,128)(2,1)S(1)}, bf16[16,1152]{1,0:T(8,128)(2,1)S(1)}, u32[]{:S(2)}, u32[]{:S(2)}) collective-permute-start(bf16[16,1152]{1,0:T(8,128)(2,1)S(1)} %get-tuple-element.23.refs_3_), channel_id=1, source_target_pairs={{0,1},{1,16},{2,3},{3,18},{4,5},{5,20},{6,7},{7,22},{8,9},{9,24},{... | collective-permute-start | bytes 110600 | tf_op jit(solution)/shard_map/ppermute | solution.py:206
  31.7 3.6 %collective-permute-start.22 = (bf16[16,1152]{1,0:T(8,128)(2,1)S(1)}, bf16[16,1152]{1,0:T(8,128)(2,1)S(1)}, u32[]{:S(2)}, u32[]{:S(2)}) collective-permute-start(bf16[16,1152]{1,0:T(8,128)(2,1)S(1)} %get-tuple-element.23.refs_3_), channel_id=1, source_target_pairs={{0,1},{1,8},{2,3},{3,10},{4,5},{5,12},{6,7},{7,14},{8,9},{9,0},{10... | collective-permute-start | bytes 110600 | tf_op jit(solution)/shard_map/ppermute | solution.py:206
  32.5 2.7 %collective-permute-start.23 = (bf16[16,1152]{1,0:T(8,128)(2,1)S(1)}, bf16[16,1152]{1,0:T(8,128)(2,1)S(1)}, u32[]{:S(2)}, u32[]{:S(2)}) collective-permute-start(bf16[16,1152]{1,0:T(8,128)(2,1)S(1)} %get-tuple-element.23.refs_3_), channel_id=1, source_target_pairs={{0,1},{1,0},{2,3},{3,2},{4,5},{5,4},{6,7},{7,6},{8,9},{9,8},{10,11... | collective-permute-start | bytes 110600 | tf_op jit(solution)/shard_map/ppermute | solution.py:108
  32.6 1.3 %collective-permute-start.24 = (f32[16,512]{1,0:T(8,128)S(1)}, f32[16,512]{1,0:T(8,128)S(1)}, u32[]{:S(2)}, u32[]{:S(2)}) collective-permute-start(f32[16,512]{1,0:T(8,128)S(1)} %get-tuple-element.24), channel_id=1, source_target_pairs={{0,1},{1,0},{2,3},{3,2},{4,5},{5,4},{6,7},{7,6},{8,9},{9,8},{10,11... | collective-permute-start | bytes 98312 | tf_op jit(solution)/shard_map/ppermute | solution.py:108
  35.5 2.2 %collective-permute-start.25 = (f32[48,128]{1,0:T(8,128)S(1)}, f32[48,128]{1,0:T(8,128)S(1)}, u32[]{:S(2)}, u32[]{:S(2)}) collective-permute-start(f32[48,128]{1,0:T(8,128)S(1)} %get-tuple-element.25), channel_id=1, source_target_pairs={{0,7},{1,0},{2,5},{3,2},{4,3},{5,4},{6,1},{7,6},{8,15},{9,8},{10,1... | collective-permute-start | bytes 73736 | tf_op jit(solution)/shard_map/ppermute | solution.py:206
  35.7 3.0 %collective-permute-start.26 = (f32[48,128]{1,0:T(8,128)S(1)}, f32[48,128]{1,0:T(8,128)S(1)}, u32[]{:S(2)}, u32[]{:S(2)}) collective-permute-start(f32[48,128]{1,0:T(8,128)S(1)} %get-tuple-element.25), channel_id=1, source_target_pairs={{0,5},{1,0},{2,7},{3,2},{4,1},{5,4},{6,3},{7,6},{8,13},{9,8},{10,1... | collective-permute-start | bytes 73736 | tf_op jit(solution)/shard_map/ppermute | solution.py:206
  37.2 1.8 %collective-permute-start.27 = (f32[48,128]{1,0:T(8,128)S(1)}, f32[48,128]{1,0:T(8,128)S(1)}, u32[]{:S(2)}, u32[]{:S(2)}) collective-permute-start(f32[48,128]{1,0:T(8,128)S(1)} %get-tuple-element.25), channel_id=1, source_target_pairs={{0,3},{1,0},{2,1},{3,2},{4,7},{5,4},{6,5},{7,6},{8,11},{9,8},{10,9... | collective-permute-start | bytes 73736 | tf_op jit(solution)/shard_map/ppermute | solution.py:206
  37.2 1.8 %collective-permute-start.28 = (f32[48,128]{1,0:T(8,128)S(1)}, f32[48,128]{1,0:T(8,128)S(1)}, u32[]{:S(2)}, u32[]{:S(2)}) collective-permute-start(f32[48,128]{1,0:T(8,128)S(1)} %get-tuple-element.25), channel_id=1, source_target_pairs={{0,1},{1,0},{2,3},{3,2},{4,5},{5,4},{6,7},{7,6},{8,9},{9,8},{10,11... | collective-permute-start | bytes 73736 | tf_op jit(solution)/shard_map/ppermute | solution.py:108
  37.7 2.7 %collective-permute-start.30 = (bf16[48,512]{1,0:T(8,128)(2,1)S(1)}, bf16[48,512]{1,0:T(8,128)(2,1)S(1)}, u32[]{:S(2)}, u32[]{:S(2)}) collective-permute-start(bf16[48,512]{1,0:T(8,128)(2,1)S(1)} %get-tuple-element.27), channel_id=1, source_target_pairs={{0,1},{1,0},{2,3},{3,2},{4,5},{5,4},{6,7},{7,6},{8,9},{9,8},{10,11... | collective-permute-start | bytes 147464 | tf_op jit(solution)/shard_map/ppermute | solution.py:108
  38.9 2.2 %collective-permute-start.29 = (f32[48,128]{1,0:T(8,128)S(1)}, f32[48,128]{1,0:T(8,128)S(1)}, u32[]{:S(2)}, u32[]{:S(2)}) collective-permute-start(f32[48,128]{1,0:T(8,128)S(1)} %shard_map.159.refs_0_), channel_id=1, source_target_pairs={{0,1},{1,0},{2,3},{3,2},{4,5},{5,4},{6,7},{7,6},{8,9},{9,8},{10,11... | collective-permute-start | bytes 73736 | tf_op jit(solution)/shard_map/ppermute | solution.py:108

commit v6 on v5

--- a/solution.py
+++ b/solution.py
@@ -125,25 +125,6 @@
     return jax.ShapeDtypeStruct(shape, kind)
 
 
-def lane_pieces(values, width=128):
-    rows = values[0].shape[0]
-    lane = lax.broadcasted_iota(jnp.int32, (rows, width), 1)
-    out = jnp.zeros((rows, width), jnp.float32)
-    for place, value in enumerate(values):
-        rest = value
-        for part in range(3):
-            piece = rest.astype(jnp.bfloat16).astype(jnp.float32)
-            out = jnp.where(lane == 3 * place + part, piece, out)
-            rest = rest - piece
-    return out.astype(jnp.bfloat16)
-
-
-def lane_sum(block, place):
-    lane = lax.broadcasted_iota(jnp.int32, block.shape, 1)
-    own = (lane >= 3 * place) & (lane < 3 * place + 3)
-    return jnp.sum(jnp.where(own, block, 0.0), axis=1, keepdims=True)
-
-
 def open_window(out_ref):
     out_ref[...] = jnp.zeros_like(out_ref)
 
@@ -153,7 +134,7 @@
     inputs = hidden_ref[...].astype(jnp.float32)
     width = inputs.shape[1]
     message_ref[:, :width] = (inputs * gain_ref[...]).astype(jnp.bfloat16)
-    message_ref[:, width:] = lane_pieces([jnp.sum(inputs * inputs, axis=1, keepdims=True)])
+    message_ref[:, width:] = pack_statistics([jnp.sum(inputs * inputs, axis=1, keepdims=True)])
 
 
 def positions_and_ranges(
@@ -183,6 +164,24 @@
 LOG2_E = 1.4426950408889634
 
 
+def pack_statistics(values):
+    rows = values[0].shape[0]
+    lane = lax.broadcasted_iota(jnp.int32, (rows, 128), 1)
+    rest = jnp.zeros((rows, 128), jnp.float32)
+    for place, value in enumerate(values):
+        rest = jnp.where(lane == place, value, rest)
+    out = rest.astype(jnp.bfloat16).astype(jnp.float32)
+    for part in (1, 2):
+        rest = rest - rest.astype(jnp.bfloat16).astype(jnp.float32)
+        out = out + pltpu.roll(rest.astype(jnp.bfloat16).astype(jnp.float32), 32 * part, 1)
+    return out.astype(jnp.bfloat16)
+
+
+def unpack_statistics(block):
+    block = block.astype(jnp.float32)
+    return block + pltpu.roll(block, 96, 1) + pltpu.roll(block, 64, 1)
+
+
 def core_number():
     return lax.axis_index("pack") & 1
 
@@ -213,8 +212,16 @@
 
 def join_cores(own_ref, other_ref, pair_ref):
     core = core_number()
-    pair_ref[core] = own_ref[...]
-    pair_ref[1 - core] = other_ref[...]
+    width = own_ref.shape[1] - 128
+    refs = (own_ref, other_ref)
+    squares = sum(unpack_statistics(ref[:, width:])[:, :1] for ref in refs)
+    pair_ref[:, 2 * width :] = pack_statistics([squares])
+    for first in range(2):
+
+        @pl.when(core == first)
+        def _():
+            pair_ref[:, :width] = refs[first][:, :width]
+            pair_ref[:, width : 2 * width] = refs[1 - first][:, :width]
 
 
 def join_blocks(*refs):
@@ -226,14 +233,11 @@
 
 def project_pair(pair_ref, offset, weight_ref):
     chip = chip_number() ^ offset
-    width = weight_ref.shape[1]
-    total = 0.0
-    for core in range(2):
-        rows = pl.ds(pl.multiple_of((2 * chip + core) * width, width), width)
-        total = total + jnp.dot(
-            pair_ref[core, :, :width], weight_ref[rows, :], preferred_element_type=jnp.float32
-        )
-    return total
+    width = 2 * weight_ref.shape[1]
+    rows = pl.ds(pl.multiple_of(chip * width, width), width)
+    return jnp.dot(
+        pair_ref[:, :width], weight_ref[rows, :], preferred_element_type=jnp.float32
+    )
 
 
 def project_own_pair(pair_ref, weight_ref, total_ref):
@@ -249,13 +253,11 @@
     @pl.when(core_number() == core)
     def _():
         projected = total_ref[...]
-        squares = jnp.zeros((total_ref.shape[0], 1), jnp.float32)
-        for j in range(2):
-            squares = squares + lane_sum(pair_ref[j, :, width:].astype(jnp.float32), 0)
+        squares = unpack_statistics(pair_ref[:, 2 * width :])
         for i in range(blocks_ref.shape[0]):
             projected = projected + project_pair(blocks_ref.at[i], i + 1, weight_ref)
-            for j in range(2):
-                squares = squares + lane_sum(blocks_ref[i, j, :, width:].astype(jnp.float32), 0)
+            squares = squares + unpack_statistics(blocks_ref[i, :, 2 * width :])
+        squares = squares[:, :1]
         projected = projected * lax.rsqrt(squares / model_width + EPSILON)
         cosine = rope_ref[:, :head_dim]
         sine = rope_ref[:, head_dim:]
@@ -329,30 +331,26 @@
     return out
 
 
-def attend_remote(*refs):
-    query_refs, refs = refs[:3], refs[3:]
-    key_ref, value_ref, other_ref, range_ref = refs[:4]
-    out_refs = refs[4:]
+def attend_remote(query_ref, key_ref, value_ref, other_ref, range_ref, *refs, offset):
+    out_ref = refs[-1]
 
     @pl.when(core_number() == 1)
     def _():
-        rows = query_refs[0].shape[0]
-        width = query_refs[0].shape[1] // 2
+        rows = query_ref.shape[0]
+        width = query_ref.shape[1] // 2
         masks = token_masks(range_ref, key_ref.shape[0], width // 128)
-        for i, (query_ref, out_ref) in enumerate(zip(query_refs, out_refs)):
-            chip = chip_number() ^ (3 - i)
-            queries = [query_ref[:, :width], query_ref[:, width:]]
-            parts = attend_heads(
-                queries, (2 * chip, 2 * chip + 1), key_ref, value_ref, other_ref, masks
-            )
-            stats = []
-            for j, (highest, total, numerators) in enumerate(parts):
-                for h in range(width // 128):
-                    part = slice(h * rows, (h + 1) * rows)
-                    place = slice(j * width + h * 128, j * width + (h + 1) * 128)
-                    out_ref[:, place] = numerators[part].astype(jnp.bfloat16)
-                    stats += [highest[part], total[part]]
-            out_ref[:, 2 * width :] = lane_pieces(stats)
+        chip = chip_number() ^ offset
+        queries = [query_ref[:, :width], query_ref[:, width:]]
+        heads = (2 * chip, 2 * chip + 1)
+        parts = attend_heads(queries, heads, key_ref, value_ref, other_ref, masks)
+        stats = []
+        for j, (highest, total, numerators) in enumerate(parts):
+            for h in range(width // 128):
+                part = slice(h * rows, (h + 1) * rows)
+                place = slice(j * width + h * 128, j * width + (h + 1) * 128)
+                out_ref[:, place] = numerators[part].astype(jnp.bfloat16)
+                stats += [highest[part], total[part]]
+        out_ref[:, 2 * width :] = pack_statistics(stats)
 
 
 def attend_own(query_ref, key_ref, value_ref, other_ref, range_ref, out_ref, stats_ref):
@@ -383,14 +381,15 @@
         rows = attended_ref.shape[0]
         width = attended_ref.shape[1] // 2
         others = (first_ref, second_ref, third_ref)
-        stats = [ref[:, 2 * width :].astype(jnp.float32) for ref in others]
+        stats = [unpack_statistics(ref[:, 2 * width :]) for ref in others]
         for j in range(2):
             for h in range(width // 128):
                 part = slice(h * rows, (h + 1) * rows)
                 place = slice(j * width + h * 128, j * width + (h + 1) * 128)
                 slot = 2 * (j * (width // 128) + h)
-                maxima = [stats_ref[j, part, :1]] + [lane_sum(s, slot) for s in stats]
-                totals = [stats_ref[j, part, 128:129]] + [lane_sum(s, slot + 1) for s in stats]
+                maxima = [stats_ref[j, part, :1]] + [s[:, slot : slot + 1] for s in stats]
+                totals = [stats_ref[j, part, 128:129]]
+                totals += [s[:, slot + 1 : slot + 2] for s in stats]
                 numerators = [own_ref[j, part, :]]
                 numerators += [ref[:, place].astype(jnp.float32) for ref in others]
                 highest = maxima[0]
@@ -453,7 +452,7 @@
             (other_scaled_ref, scaled_ref)[core][...] = scaled
             sent_ref[:, place] = scaled.astype(jnp.bfloat16)
             squares = squares + jnp.sum(hidden * hidden, axis=1, keepdims=True)
-        sent_ref[:, 2 * width :] = lane_pieces([squares])
+        sent_ref[:, 2 * width :] = pack_statistics([squares])
 
 
 def gram_part(third_ref, second_ref, first_ref, own_ref, _, out_ref, near_ref, far_ref):
@@ -467,7 +466,7 @@
         for i, ref in enumerate(refs[1:]):
             far_ref[i * rows : (i + 1) * rows] = ref[:, width : 2 * width]
         far = jnp.concatenate([ref[:, width : 2 * width] for ref in refs], axis=0)
-        squares = lane_sum(own_ref[:, 2 * width :].astype(jnp.float32), 0)
+        squares = unpack_statistics(own_ref[:, 2 * width :])[:, :1]
         gram = 0.0
         for vectors in (near_ref[...], far):
             gram = gram + lax.dot_general(
@@ -537,24 +536,17 @@
     row_scale = lax.rsqrt(jnp.sum(on_diagonal, axis=1, keepdims=True))
     column_scale = lax.rsqrt(jnp.sum(on_diagonal, axis=0, keepdims=True))
     cosines = gram * row_scale * column_scale
-    logits = jnp.where(diagonal, MASKED_LOGIT, cosines * (1.0 / SOFTMAX_WARMTH))
-    row_high = jnp.max(logits, axis=1, keepdims=True)
-    row_lse = row_high + jnp.log(jnp.sum(jnp.exp(logits - row_high), axis=1, keepdims=True))
-    column_high = jnp.max(logits, axis=0, keepdims=True)
-    column_lse = column_high + jnp.log(
-        jnp.sum(jnp.exp(logits - column_high), axis=0, keepdims=True)
-    )
+    logits = cosines * (1.0 / SOFTMAX_WARMTH)
+    powers = jnp.where(diagonal, 0.0, jnp.exp(logits))
+    row_sum = jnp.sum(powers, axis=1, keepdims=True)
+    column_sum = jnp.sum(powers, axis=0, keepdims=True)
+    weights = (powers * (1.0 / row_sum + 1.0 / column_sum) - partner_ref[1])[:rows]
     target = jnp.sum(partner_ref[0] * logits, axis=1, keepdims=True)
-    loss = row_lse - target
+    loss = jnp.log(row_sum) - target
     own = loss_ref.shape[0]
     index = lax.broadcasted_iota(jnp.int32, (count, 1), 0)
     for i in range(own):
         loss_ref[i] = jnp.sum(jnp.where(index == me * own + i, loss, 0.0))
-    weights = (
-        jnp.exp(logits - row_lse)
-        + jnp.exp(logits - column_lse)
-        - partner_ref[1]
-    )[:rows]
     inner = jnp.sum(weights * cosines[:rows], axis=1, keepdims=True)
     scaled_weights = weights * column_scale
     upper = scaled_weights.astype(jnp.bfloat16)
@@ -622,7 +614,7 @@
         prepare_inputs, shaped((stmts, width + 128), bf16), window, hidden_in, attn_gain[None]
     )
     pair = in_vmem(
-        join_cores, shaped((2,) + message.shape, bf16), message, flip(message, "pack", 1)
+        join_cores, shaped((stmts, 2 * width + 128), bf16), message, flip(message, "pack", 1)
     )
     received = [send_across(pair, "pack", k, 0) for k in others]
     own_projected = in_vmem(
@@ -684,16 +676,21 @@
         ranges,
         flops=1 << 27,
     )
-    partials = in_vmem(
-        attend_remote,
-        (shaped((stmts, 2 * width + 128), bf16),) * (chips - 1),
-        *received[::-1],
-        cached_keys,
-        cached_values,
-        other_held,
-        ranges,
-        flops=1 << 36,
-    )
+    partials = []
+    for k, part in zip(others[::-1], received[::-1]):
+        partials.append(
+            in_vmem(
+                lambda *refs, offset=k: attend_remote(*refs, offset=offset),
+                shaped((stmts, 2 * width + 128), bf16),
+                part,
+                cached_keys,
+                cached_values,
+                other_held,
+                ranges,
+                *partials[-1:],
+                flops=1 << 34,
+            )
+        )
     received = [send_across(part, "pack", k, 1) for k, part in zip(others, partials[::-1])]
     other_hidden_in = flip(hidden_in, "pack", 1)
     other_gain = flip(final_gain, "pack", 1)

time: 42.4 us -> 42.6 us (level)
  waiting for transfers between devices: 12.3 us -> 11.7 us
  Pallas kernels: 5.34 us -> 5.78 us
    ppermute x18, waiting for transfers between devices: 8.21 us -> 6.48 us  [send_across(): return lax.ppermute(array, ('dp', 'pack'), pairs)]
    ppermute x13, waiting for transfers between devices: 4.07 us -> 5.22 us  [flip(): return lax.ppermute(array, axis, [(i, i ^ offset) for i in range(size)])]
    pallas_call x21 -> x23, Pallas kernels: 4.24 us -> 4.76 us  [in_vmem(): pl.pallas_call(body, out_shape=outputs, in_specs=[whole] * len(operands),...]
    ppermute x13, starting transfers between devices: 6.14 us -> 6.61 us  [flip(): return lax.ppermute(array, axis, [(i, i ^ offset) for i in range(size)])]
  transfers between devices with their start and end apart: 31 -> 31, of which waited for: 18 -> 15; matrix products, arithmetic and copies ran while one was open for 0% -> 0% of each run, Pallas kernels for 8% -> 9%
where the time goes in v6:
time: 42.6 us; the launch traced here: 42.4 us
  starting transfers between devices  23.4 us (55%)
  waiting for transfers between devices  11.7 us (27%)
  Pallas kernels  5.78 us (14%)
  between operations  0.85 us (2%)
  local copies, waits for them, and re-layouts  0.71 us (2%)
    ppermute x18, starting transfers between devices, send_across(): return lax.ppermute(array, ('dp', 'pack'), pairs)  16.8 us
    ppermute x13, starting transfers between devices, flip(): return lax.ppermute(array, axis, [(i, i ^ offset) for i in range(size)])  6.61 us
    ppermute x18, waiting for transfers between devices, send_across(): return lax.ppermute(array, ('dp', 'pack'), pairs)  6.48 us
    ppermute x13, waiting for transfers between devices, flip(): return lax.ppermute(array, axis, [(i, i ^ offset) for i in range(size)])  5.22 us
    pallas_call x23, Pallas kernels, in_vmem(): pl.pallas_call(body, out_shape=outputs, in_specs=[whole] * len(operands),...  4.76 us
    pallas_call x1, Pallas kernels, core_roles(): pl.pallas_call(lambda *refs: losses_and_gradient(*refs, model_width=model...  1.02 us
  transfers between devices with their start and end apart: 31, of which 15 were waited for; matrix products, arithmetic and copies ran while one was open for 0% of the time, Pallas kernels for 9%

profile of v6, /device:TPU:0, one launch (start us, length us, event | category | flops | bytes accessed | tf_op | source)
XLA Modules:
  0.0 42.4 jit_solution(550522938780615136)
XLA Ops:
  0.7 0.7 %copy-done.4 = bf16[16,512]{1,0:T(8,128)(2,1)S(1)} copy-done((bf16[16,512]{1,0:T(8,128)(2,1)S(1)}, bf16[16,512]{1,0:T(8,128)(2,1)}, u32[]{:S(2)}) %copy-start.4) | copy-done | bytes 16408
  1.5 0.5 %collective-permute-start = (bf16[16,640]{1,0:T(8,128)(2,1)S(1)}, bf16[16,640]{1,0:T(8,128)(2,1)S(1)}, u32[]{:S(2)}, u32[]{:S(2)}) collective-permute-start(bf16[16,640]{1,0:T(8,128)(2,1)S(1)} %shard_map.140.own_ref.message_ref), channel_id=1, source_target_pairs={{0,1},{1,0},{2,3},{3,2},{4,5},{5,4},{6,7},{7,6},{8,9},{9,8},{10,11... | collective-permute-start | bytes 61448 | tf_op jit(solution)/shard_map/ppermute | solution.py:108
  2.0 0.8 %collective-permute-done.other_ref = bf16[16,640]{1,0:T(8,128)(2,1)S(1)} collective-permute-done((bf16[16,640]{1,0:T(8,128)(2,1)S(1)}, bf16[16,640]{1,0:T(8,128)(2,1)S(1)}, u32[]{:S(2)}, u32[]{:S(2)}) %collective-permute-start) | collective-permute-done | bytes 20512 | tf_op jit(solution)/shard_map/ppermute | solution.py:108
  2.8 0.2 shard_map.141.pair_ref.refs_0_
  3.1 4.7 %collective-permute-start.1 = (bf16[16,1152]{1,0:T(8,128)(2,1)S(1)}, bf16[16,1152]{1,0:T(8,128)(2,1)S(1)}, u32[]{:S(2)}, u32[]{:S(2)}) collective-permute-start(bf16[16,1152]{1,0:T(8,128)(2,1)S(1)} %shard_map.141.pair_ref.refs_0_), channel_id=1, source_target_pairs={{0,7},{1,0},{2,5},{3,2},{4,3},{5,4},{6,1},{7,6},{8,15},{9,8},{10,1... | collective-permute-start | bytes 110600 | tf_op jit(solution)/shard_map/ppermute | solution.py:205
  7.8 0.2 shard_map.143
  8.0 0.2 shard_map.142.refs_3_.refs_2_
  8.2 1.2 %collective-permute-done.1.refs_0_ = bf16[16,1152]{1,0:T(8,128)(2,1)S(1)} collective-permute-done((bf16[16,1152]{1,0:T(8,128)(2,1)S(1)}, bf16[16,1152]{1,0:T(8,128)(2,1)S(1)}, u32[]{:S(2)}, u32[]{:S(2)}) %collective-permute-start.1) | collective-permute-done | bytes 36896 | tf_op jit(solution)/shard_map/ppermute | solution.py:205
  9.4 0.3 collective-permute-done.2.refs_1_
  9.8 0.3 collective-permute-done.3.refs_2_
  10.1 1.6 %collective-permute-start.4 = (bf16[3,16,1152]{2,1,0:T(8,128)(2,1)S(1)}, bf16[3,16,1152]{2,1,0:T(8,128)(2,1)S(1)}, u32[]{:S(2)}, u32[]{:S(2)}) collective-permute-start(bf16[3,16,1152]{2,1,0:T(8,128)(2,1)S(1)} %shard_map.144.refs_1_), channel_id=1, source_target_pairs={{0,1},{1,0},{2,3},{3,2},{4,5},{5,4},{6,7},{7,6},{8,9},{9,8},{10,11... | collective-permute-start | bytes 331784 | tf_op jit(solution)/shard_map/ppermute | solution.py:108
  11.7 0.8 %collective-permute-start.5 = (bf16[16,512]{1,0:T(8,128)(2,1)S(1)}, bf16[16,512]{1,0:T(8,128)(2,1)S(1)}, u32[]{:S(2)}, u32[]{:S(2)}) collective-permute-start(bf16[16,512]{1,0:T(8,128)(2,1)S(1)} %shard_map.146._), channel_id=1, source_target_pairs={{0,1},{1,0},{2,3},{3,2},{4,5},{5,4},{6,7},{7,6},{8,9},{9,8},{10,11... | collective-permute-start | bytes 49160 | tf_op jit(solution)/shard_map/ppermute | solution.py:108
  12.7 0.7 %shard_map.145.first_ref = bf16[16,512]{1,0:T(8,128)(2,1)S(1)} custom-call(bf16[16,1152]{1,0:T(8,128)(2,1)S(1)} %shard_map.141.pair_ref.refs_0_, bf16[3,16,1152]{2,1,0:T(8,128)(2,1)S(1)} %collective-permute-done.4.refs_1_, f32[16,512]{1,0:T(8,128)S(1)} %shard_map.142.refs_3_.refs_2_, bf16[4096,512]{1,0:T(8,128)(2,1)S(1)} %copy-done.1, f32[1,128]{1,0:T(1,128)S(1)} %bitcast.9, ...), custom_call_target="tpu_custom_call" | custom-call | flops 68719476736 | bytes 4391424 | tf_op jit(solution)/shard_map/pallas_call | solution.py:114
  13.5 1.6 %collective-permute-start.6 = (bf16[16,1024]{1,0:T(8,128)(2,1)S(1)}, bf16[16,1024]{1,0:T(8,128)(2,1)S(1)}, u32[]{:S(2)}, u32[]{:S(2)}) collective-permute-start(bf16[16,1024]{1,0:T(8,128)(2,1)S(1)} %shard_map.147.query_ref._), channel_id=1, source_target_pairs={{0,7},{1,0},{2,5},{3,2},{4,3},{5,4},{6,1},{7,6},{8,15},{9,8},{10,1... | collective-permute-start | bytes 98312 | tf_op jit(solution)/shard_map/ppermute | solution.py:205
  15.0 0.2 collective-permute-start.11
  15.2 0.3 shard_map.154
  15.5 0.4 collective-permute-start.15
  15.9 0.7 %collective-permute-done.6.refs_0_ = bf16[16,1024]{1,0:T(8,128)(2,1)S(1)} collective-permute-done((bf16[16,1024]{1,0:T(8,128)(2,1)S(1)}, bf16[16,1024]{1,0:T(8,128)(2,1)S(1)}, u32[]{:S(2)}, u32[]{:S(2)}) %collective-permute-start.6) | collective-permute-done | bytes 32800 | tf_op jit(solution)/shard_map/ppermute | solution.py:205
  16.6 2.8 %collective-permute-start.8 = (bf16[16,1152]{1,0:T(8,128)(2,1)S(1)}, bf16[16,1152]{1,0:T(8,128)(2,1)S(1)}, u32[]{:S(2)}, u32[]{:S(2)}) collective-permute-start(bf16[16,1152]{1,0:T(8,128)(2,1)S(1)} %shard_map.149.refs_5_), channel_id=1, source_target_pairs={{0,1},{1,6},{2,3},{3,4},{4,5},{5,2},{6,7},{7,0},{8,9},{9,14},{10,1... | collective-permute-start | bytes 110600 | tf_op jit(solution)/shard_map/ppermute | solution.py:205
  19.5 0.6 %collective-permute-start.10 = (bf16[16,1152]{1,0:T(8,128)(2,1)S(1)}, bf16[16,1152]{1,0:T(8,128)(2,1)S(1)}, u32[]{:S(2)}, u32[]{:S(2)}) collective-permute-start(bf16[16,1152]{1,0:T(8,128)(2,1)S(1)} %shard_map.150.refs_5_), channel_id=1, source_target_pairs={{0,1},{1,4},{2,3},{3,6},{4,5},{5,0},{6,7},{7,2},{8,9},{9,12},{10,1... | collective-permute-start | bytes 110600 | tf_op jit(solution)/shard_map/ppermute | solution.py:205
  20.1 0.6 %collective-permute-start.12 = (bf16[16,1152]{1,0:T(8,128)(2,1)S(1)}, bf16[16,1152]{1,0:T(8,128)(2,1)S(1)}, u32[]{:S(2)}, u32[]{:S(2)}) collective-permute-start(bf16[16,1152]{1,0:T(8,128)(2,1)S(1)} %shard_map.151), channel_id=1, source_target_pairs={{0,1},{1,2},{2,3},{3,0},{4,5},{5,6},{6,7},{7,4},{8,9},{9,10},{10,1... | collective-permute-start | bytes 110600 | tf_op jit(solution)/shard_map/ppermute | solution.py:205
  20.7 2.1 %collective-permute-done.14.refs_1_.other_gain_ref = f32[1,512]{1,0:T(1,128)S(1)} collective-permute-done((f32[1,512]{1,0:T(1,128)S(1)}, f32[1,512]{1,0:T(1,128)S(1)}, u32[]{:S(2)}, u32[]{:S(2)}) %collective-permute-start.14) | collective-permute-done | bytes 2080 | tf_op jit(solution)/shard_map/ppermute | solution.py:108
  22.8 0.4 collective-permute-start.13
  23.2 0.5 %shard_map.152 = (f32[2,64,128]{2,1,0:T(8,128)S(1)}, f32[2,64,256]{2,1,0:T(8,128)S(1)}) custom-call(bf16[16,1024]{1,0:T(8,128)(2,1)S(1)} %shard_map.147.query_ref._, bf16[320,1024]{1,0:T(8,128)(2,1)S(1)} %copy-done.2, bf16[320,1024]{1,0:T(8,128)(2,1)S(1)} %copy-done.3, bf16[2,320,1024]{2,1,0:T(8,128)(2,1)S(1)} %collective-permute-done.7.refs_3_.other_ref, ...), custom_call_target="tpu_custom_call" | custom-call | flops 134217728 | bytes 2670592 | tf_op jit(solution)/shard_map/pallas_call | solution.py:114
  23.7 0.3 collective-permute-done.13.refs_0_.other_ref
  24.0 0.5 %shard_map.153.refs_0_ = bf16[16,1024]{1,0:T(8,128)(2,1)S(1)} custom-call(bf16[16,1152]{1,0:T(8,128)(2,1)S(1)} %collective-permute-done.8.third_ref, bf16[16,1152]{1,0:T(8,128)(2,1)S(1)} %collective-permute-done.10.second_ref, bf16[16,1152]{1,0:T(8,128)(2,1)S(1)} %collective-permute-done.12.first_ref, f32[2,64,128]{2,1,0:T(8,128)S(1)} %get-tuple-element.15.own_ref, ...), custom_call_target="tpu_custom_call" | custom-call | flops 1000000 | bytes 325632 | tf_op jit(solution)/shard_map/pallas_call | solution.py:114
  24.6 0.4 shard_map.155.refs_3_
  25.0 1.3 %collective-permute-start.16 = (bf16[16,1024]{1,0:T(8,128)(2,1)S(1)}, bf16[16,1024]{1,0:T(8,128)(2,1)S(1)}, u32[]{:S(2)}, u32[]{:S(2)}) collective-permute-start(bf16[16,1024]{1,0:T(8,128)(2,1)S(1)} %shard_map.155.refs_3_), channel_id=1, source_target_pairs={{0,7},{1,0},{2,5},{3,2},{4,3},{5,4},{6,1},{7,6},{8,15},{9,8},{10,1... | collective-permute-start | bytes 98312 | tf_op jit(solution)/shard_map/ppermute | solution.py:205
  26.2 0.4 shard_map.156.refs_3_
  26.6 1.0 %collective-permute-start.17 = (bf16[16,1024]{1,0:T(8,128)(2,1)S(1)}, bf16[16,1024]{1,0:T(8,128)(2,1)S(1)}, u32[]{:S(2)}, u32[]{:S(2)}) collective-permute-start(bf16[16,1024]{1,0:T(8,128)(2,1)S(1)} %shard_map.156.refs_3_), channel_id=1, source_target_pairs={{0,5},{1,0},{2,7},{3,2},{4,1},{5,4},{6,3},{7,6},{8,13},{9,8},{10,1... | collective-permute-start | bytes 98312 | tf_op jit(solution)/shard_map/ppermute | solution.py:205
  27.6 0.4 shard_map.157.refs_3_
  28.0 0.4 shard_map.158
  28.5 0.7 %collective-permute-done.17.second_ref = bf16[16,1024]{1,0:T(8,128)(2,1)S(1)} collective-permute-done((bf16[16,1024]{1,0:T(8,128)(2,1)S(1)}, bf16[16,1024]{1,0:T(8,128)(2,1)S(1)}, u32[]{:S(2)}, u32[]{:S(2)}) %collective-permute-start.17) | collective-permute-done | bytes 32800 | tf_op jit(solution)/shard_map/ppermute | solution.py:205
  29.2 0.4 collective-permute-done.18.first_ref
  29.6 1.1 %collective-permute-start.20 = (bf16[16,1152]{1,0:T(8,128)(2,1)S(1)}, bf16[16,1152]{1,0:T(8,128)(2,1)S(1)}, u32[]{:S(2)}, u32[]{:S(2)}) collective-permute-start(bf16[16,1152]{1,0:T(8,128)(2,1)S(1)} %get-tuple-element.17.refs_3_), channel_id=1, source_target_pairs={{0,1},{1,24},{2,3},{3,26},{4,5},{5,28},{6,7},{7,30},{8,9},{9,16},{... | collective-permute-start | bytes 110600 | tf_op jit(solution)/shard_map/ppermute | solution.py:205
  30.7 1.5 %collective-permute-start.21 = (bf16[16,1152]{1,0:T(8,128)(2,1)S(1)}, bf16[16,1152]{1,0:T(8,128)(2,1)S(1)}, u32[]{:S(2)}, u32[]{:S(2)}) collective-permute-start(bf16[16,1152]{1,0:T(8,128)(2,1)S(1)} %get-tuple-element.17.refs_3_), channel_id=1, source_target_pairs={{0,1},{1,16},{2,3},{3,18},{4,5},{5,20},{6,7},{7,22},{8,9},{9,24},{... | collective-permute-start | bytes 110600 | tf_op jit(solution)/shard_map/ppermute | solution.py:205
  32.3 0.5 %collective-permute-start.23 = (bf16[16,1152]{1,0:T(8,128)(2,1)S(1)}, bf16[16,1152]{1,0:T(8,128)(2,1)S(1)}, u32[]{:S(2)}, u32[]{:S(2)}) collective-permute-start(bf16[16,1152]{1,0:T(8,128)(2,1)S(1)} %get-tuple-element.17.refs_3_), channel_id=1, source_target_pairs={{0,1},{1,0},{2,3},{3,2},{4,5},{5,4},{6,7},{7,6},{8,9},{9,8},{10,11... | collective-permute-start | bytes 110600 | tf_op jit(solution)/shard_map/ppermute | solution.py:108
  32.8 1.2 %collective-permute-done.24._.refs_6_ = f32[16,512]{1,0:T(8,128)S(1)} collective-permute-done((f32[16,512]{1,0:T(8,128)S(1)}, f32[16,512]{1,0:T(8,128)S(1)}, u32[]{:S(2)}, u32[]{:S(2)}) %collective-permute-start.24) | collective-permute-done | bytes 32800 | tf_op jit(solution)/shard_map/ppermute | solution.py:108
  34.0 0.4 collective-permute-done.20.third_ref
  34.5 1.1 %collective-permute-done.22.first_ref = bf16[16,1152]{1,0:T(8,128)(2,1)S(1)} collective-permute-done((bf16[16,1152]{1,0:T(8,128)(2,1)S(1)}, bf16[16,1152]{1,0:T(8,128)(2,1)S(1)}, u32[]{:S(2)}, u32[]{:S(2)}) %collective-permute-start.22) | collective-permute-done | bytes 36896 | tf_op jit(solution)/shard_map/ppermute | solution.py:205
  35.6 0.2 shard_map.160
  35.8 1.4 %collective-permute-start.26 = (f32[48,128]{1,0:T(8,128)S(1)}, f32[48,128]{1,0:T(8,128)S(1)}, u32[]{:S(2)}, u32[]{:S(2)}) collective-permute-start(f32[48,128]{1,0:T(8,128)S(1)} %get-tuple-element.19), channel_id=1, source_target_pairs={{0,5},{1,0},{2,7},{3,2},{4,1},{5,4},{6,3},{7,6},{8,13},{9,8},{10,1... | collective-permute-start | bytes 73736 | tf_op jit(solution)/shard_map/ppermute | solution.py:205
  37.2 0.5 %collective-permute-start.28 = (f32[48,128]{1,0:T(8,128)S(1)}, f32[48,128]{1,0:T(8,128)S(1)}, u32[]{:S(2)}, u32[]{:S(2)}) collective-permute-start(f32[48,128]{1,0:T(8,128)S(1)} %get-tuple-element.19), channel_id=1, source_target_pairs={{0,1},{1,0},{2,3},{3,2},{4,5},{5,4},{6,7},{7,6},{8,9},{9,8},{10,11... | collective-permute-start | bytes 73736 | tf_op jit(solution)/shard_map/ppermute | solution.py:108
  37.7 1.0 %collective-permute-done.26.second_ref = f32[48,128]{1,0:T(8,128)S(1)} collective-permute-done((f32[48,128]{1,0:T(8,128)S(1)}, f32[48,128]{1,0:T(8,128)S(1)}, u32[]{:S(2)}, u32[]{:S(2)}) %collective-permute-start.26) | collective-permute-done | bytes 24608 | tf_op jit(solution)/shard_map/ppermute | solution.py:205
  38.7 0.2 collective-permute-done.27.first_ref
  38.9 1.6 %collective-permute-start.29 = (f32[48,128]{1,0:T(8,128)S(1)}, f32[48,128]{1,0:T(8,128)S(1)}, u32[]{:S(2)}, u32[]{:S(2)}) collective-permute-start(f32[48,128]{1,0:T(8,128)S(1)} %shard_map.161.refs_0_), channel_id=1, source_target_pairs={{0,1},{1,0},{2,3},{3,2},{4,5},{5,4},{6,7},{7,6},{8,9},{9,8},{10,11... | collective-permute-start | bytes 73736 | tf_op jit(solution)/shard_map/ppermute | solution.py:108
  40.7 0.7 %collective-permute-done.29.refs_1_ = f32[48,128]{1,0:T(8,128)S(1)} collective-permute-done((f32[48,128]{1,0:T(8,128)S(1)}, f32[48,128]{1,0:T(8,128)S(1)}, u32[]{:S(2)}, u32[]{:S(2)}) %collective-permute-start.29) | collective-permute-done | bytes 24608 | tf_op jit(solution)/shard_map/ppermute | solution.py:108
  41.4 1.0 %shard_map.163 = (bf16[16,512]{1,0:T(8,128)(2,1)}, f32[2]{0:T(128)}, bf16[16,512]{1,0:T(8,128)(2,1)}) custom-call(f32[48,128]{1,0:T(8,128)S(1)} %shard_map.161.refs_0_, f32[48,128]{1,0:T(8,128)S(1)} %collective-permute-done.29.refs_1_, bf16[64,512]{1,0:T(8,128)(2,1)S(1)} %get-tuple-element.20.refs_2_, bf16[16,1152]{1,0:T(8,128)(2,1)S(1)} %get-tuple-element.17.refs_3_, ...), custom_call_target="tpu_custom_call" | custom-call | tf_op jit(solution)/shard_map/pallas_call | solution.py:760
  (63 shorter events, 1.0 us)
Async XLA Ops:
  0.6 7.1 %copy-start.11 = (f32[1,128]{1,0:T(1,128)S(1)}, f32[1,128]{1,0:T(1,128)}, u32[]{:S(2)}) copy-start(f32[1,128]{1,0:T(1,128)} %constant.2.clone.frequency_ref) | copy-start | bytes 1540
  0.6 0.7 %copy-start.4 = (bf16[16,512]{1,0:T(8,128)(2,1)S(1)}, bf16[16,512]{1,0:T(8,128)(2,1)}, u32[]{:S(2)}) copy-start(bf16[16,512]{1,0:T(8,128)(2,1)} %own_ref.1) | copy-start | bytes 49156
  0.7 0.7 %copy-start.6 = (f32[512]{0:T(512)S(1)}, f32[512]{0:T(512)}, u32[]{:S(2)}) copy-start(f32[512]{0:T(512)} %param.13) | copy-start | bytes 6148
  0.7 7.1 %copy-start.9 = (s32[1,16]{1,0:T(1,128)S(1)}, s32[1,16]{1,0:T(1,128)}, u32[]{:S(2)}) copy-start(s32[1,16]{1,0:T(1,128)} %lengths_ref.1) | copy-start | bytes 196
  0.7 7.1 %copy-start.10 = (s32[1,16]{1,0:T(1,128)S(1)}, s32[1,16]{1,0:T(1,128)}, u32[]{:S(2)}) copy-start(s32[1,16]{1,0:T(1,128)} %order_ref.1) | copy-start | bytes 196
  0.7 7.3 %copy-start.1 = (bf16[4096,512]{1,0:T(8,128)(2,1)S(1)}, bf16[4096,512]{1,0:T(8,128)(2,1)}, u32[]{:S(2)}) copy-start(bf16[4096,512]{1,0:T(8,128)(2,1)} %refs_3_.3) | copy-start | bytes 12582916
  0.7 11.0 %copy-start.7 = (f32[128]{0:T(128)S(1)}, f32[128]{0:T(128)}, u32[]{:S(2)}) copy-start(f32[128]{0:T(128)} %param.15) | copy-start | bytes 1540
  1.5 1.3 %collective-permute-start = (bf16[16,640]{1,0:T(8,128)(2,1)S(1)}, bf16[16,640]{1,0:T(8,128)(2,1)S(1)}, u32[]{:S(2)}, u32[]{:S(2)}) collective-permute-start(bf16[16,640]{1,0:T(8,128)(2,1)S(1)} %shard_map.140.own_ref.message_ref), channel_id=1, source_target_pairs={{0,1},{1,0},{2,3},{3,2},{4,5},{5,4},{6,7},{7,6},{8,9},{9,8},{10,11... | collective-permute-start | bytes 61448 | tf_op jit(solution)/shard_map/ppermute | solution.py:108
  3.1 6.4 %collective-permute-start.1 = (bf16[16,1152]{1,0:T(8,128)(2,1)S(1)}, bf16[16,1152]{1,0:T(8,128)(2,1)S(1)}, u32[]{:S(2)}, u32[]{:S(2)}) collective-permute-start(bf16[16,1152]{1,0:T(8,128)(2,1)S(1)} %shard_map.141.pair_ref.refs_0_), channel_id=1, source_target_pairs={{0,7},{1,0},{2,5},{3,2},{4,3},{5,4},{6,1},{7,6},{8,15},{9,8},{10,1... | collective-permute-start | bytes 110600 | tf_op jit(solution)/shard_map/ppermute | solution.py:205
  7.8 2.0 %collective-permute-start.2 = (bf16[16,1152]{1,0:T(8,128)(2,1)S(1)}, bf16[16,1152]{1,0:T(8,128)(2,1)S(1)}, u32[]{:S(2)}, u32[]{:S(2)}) collective-permute-start(bf16[16,1152]{1,0:T(8,128)(2,1)S(1)} %shard_map.141.pair_ref.refs_0_), channel_id=1, source_target_pairs={{0,5},{1,0},{2,7},{3,2},{4,1},{5,4},{6,3},{7,6},{8,13},{9,8},{10,1... | collective-permute-start | bytes 110600 | tf_op jit(solution)/shard_map/ppermute | solution.py:205
  7.8 2.3 %collective-permute-start.3 = (bf16[16,1152]{1,0:T(8,128)(2,1)S(1)}, bf16[16,1152]{1,0:T(8,128)(2,1)S(1)}, u32[]{:S(2)}, u32[]{:S(2)}) collective-permute-start(bf16[16,1152]{1,0:T(8,128)(2,1)S(1)} %shard_map.141.pair_ref.refs_0_), channel_id=1, source_target_pairs={{0,3},{1,0},{2,1},{3,2},{4,7},{5,4},{6,5},{7,6},{8,11},{9,8},{10,9... | collective-permute-start | bytes 110600 | tf_op jit(solution)/shard_map/ppermute | solution.py:205
  8.0 4.6 %copy-start.2 = (bf16[320,1024]{1,0:T(8,128)(2,1)S(1)}, bf16[320,1024]{1,0:T(8,128)(2,1)}, u32[]{:S(2)}) copy-start(bf16[320,1024]{1,0:T(8,128)(2,1)} %key_ref.3) | copy-start | bytes 1966084
  8.0 4.6 %copy-start.3 = (bf16[320,1024]{1,0:T(8,128)(2,1)S(1)}, bf16[320,1024]{1,0:T(8,128)(2,1)}, u32[]{:S(2)}) copy-start(bf16[320,1024]{1,0:T(8,128)(2,1)} %value_ref.3) | copy-start | bytes 1966084
  10.1 2.6 %collective-permute-start.4 = (bf16[3,16,1152]{2,1,0:T(8,128)(2,1)S(1)}, bf16[3,16,1152]{2,1,0:T(8,128)(2,1)S(1)}, u32[]{:S(2)}, u32[]{:S(2)}) collective-permute-start(bf16[3,16,1152]{2,1,0:T(8,128)(2,1)S(1)} %shard_map.144.refs_1_), channel_id=1, source_target_pairs={{0,1},{1,0},{2,3},{3,2},{4,5},{5,4},{6,7},{7,6},{8,9},{9,8},{10,11... | collective-permute-start | bytes 331784 | tf_op jit(solution)/shard_map/ppermute | solution.py:108
  11.7 1.7 %collective-permute-start.5 = (bf16[16,512]{1,0:T(8,128)(2,1)S(1)}, bf16[16,512]{1,0:T(8,128)(2,1)S(1)}, u32[]{:S(2)}, u32[]{:S(2)}) collective-permute-start(bf16[16,512]{1,0:T(8,128)(2,1)S(1)} %shard_map.146._), channel_id=1, source_target_pairs={{0,1},{1,0},{2,3},{3,2},{4,5},{5,4},{6,7},{7,6},{8,9},{9,8},{10,11... | collective-permute-start | bytes 49160 | tf_op jit(solution)/shard_map/ppermute | solution.py:108
  12.6 2.6 %copy-start = (bf16[512,4096]{1,0:T(8,128)(2,1)S(1)}, bf16[512,4096]{1,0:T(8,128)(2,1)}, u32[]{:S(2)}) copy-start(bf16[512,4096]{1,0:T(8,128)(2,1)} %refs_1_.13) | copy-start | bytes 12582916
  12.6 4.0 %collective-permute-start.7 = (bf16[2,320,1024]{2,1,0:T(8,128)(2,1)S(1)}, bf16[2,320,1024]{2,1,0:T(8,128)(2,1)S(1)}, u32[]{:S(2)}, u32[]{:S(2)}) collective-permute-start(bf16[2,320,1024]{2,1,0:T(8,128)(2,1)S(1)} %shard_map.148), channel_id=1, source_target_pairs={{0,1},{1,0},{2,3},{3,2},{4,5},{5,4},{6,7},{7,6},{8,9},{9,8},{10,11... | collective-permute-start | bytes 3932168 | tf_op jit(solution)/shard_map/ppermute | solution.py:108
  13.5 3.2 %collective-permute-start.6 = (bf16[16,1024]{1,0:T(8,128)(2,1)S(1)}, bf16[16,1024]{1,0:T(8,128)(2,1)S(1)}, u32[]{:S(2)}, u32[]{:S(2)}) collective-permute-start(bf16[16,1024]{1,0:T(8,128)(2,1)S(1)} %shard_map.147.query_ref._), channel_id=1, source_target_pairs={{0,7},{1,0},{2,5},{3,2},{4,3},{5,4},{6,1},{7,6},{8,15},{9,8},{10,1... | collective-permute-start | bytes 98312 | tf_op jit(solution)/shard_map/ppermute | solution.py:205
  15.0 4.4 %collective-permute-start.9 = (bf16[16,1024]{1,0:T(8,128)(2,1)S(1)}, bf16[16,1024]{1,0:T(8,128)(2,1)S(1)}, u32[]{:S(2)}, u32[]{:S(2)}) collective-permute-start(bf16[16,1024]{1,0:T(8,128)(2,1)S(1)} %shard_map.147.query_ref._), channel_id=1, source_target_pairs={{0,5},{1,0},{2,7},{3,2},{4,1},{5,4},{6,3},{7,6},{8,13},{9,8},{10,1... | collective-permute-start | bytes 98312 | tf_op jit(solution)/shard_map/ppermute | solution.py:205
  15.0 5.0 %collective-permute-start.11 = (bf16[16,1024]{1,0:T(8,128)(2,1)S(1)}, bf16[16,1024]{1,0:T(8,128)(2,1)S(1)}, u32[]{:S(2)}, u32[]{:S(2)}) collective-permute-start(bf16[16,1024]{1,0:T(8,128)(2,1)S(1)} %shard_map.147.query_ref._), channel_id=1, source_target_pairs={{0,3},{1,0},{2,1},{3,2},{4,7},{5,4},{6,5},{7,6},{8,11},{9,8},{10,9... | collective-permute-start | bytes 98312 | tf_op jit(solution)/shard_map/ppermute | solution.py:205
  15.5 9.1 %collective-permute-start.15 = (bf16[512,4096]{1,0:T(8,128)(2,1)S(1)}, bf16[512,4096]{1,0:T(8,128)(2,1)S(1)}, u32[]{:S(2)}, u32[]{:S(2)}) collective-permute-start(bf16[512,4096]{1,0:T(8,128)(2,1)S(1)} %shard_map.154), channel_id=1, source_target_pairs={{0,1},{1,0},{2,3},{3,2},{4,5},{5,4},{6,7},{7,6},{8,9},{9,8},{10,11... | collective-permute-start | bytes 12582920 | tf_op jit(solution)/shard_map/ppermute | solution.py:108
  16.6 7.4 %collective-permute-start.8 = (bf16[16,1152]{1,0:T(8,128)(2,1)S(1)}, bf16[16,1152]{1,0:T(8,128)(2,1)S(1)}, u32[]{:S(2)}, u32[]{:S(2)}) collective-permute-start(bf16[16,1152]{1,0:T(8,128)(2,1)S(1)} %shard_map.149.refs_5_), channel_id=1, source_target_pairs={{0,1},{1,6},{2,3},{3,4},{4,5},{5,2},{6,7},{7,0},{8,9},{9,14},{10,1... | collective-permute-start | bytes 110600 | tf_op jit(solution)/shard_map/ppermute | solution.py:205
  19.5 1.2 %copy-start.5 = (f32[512]{0:T(512)S(1)}, f32[512]{0:T(512)}, u32[]{:S(2)}) copy-start(f32[512]{0:T(512)} %param.19) | copy-start | bytes 6148
  19.5 4.6 %collective-permute-start.10 = (bf16[16,1152]{1,0:T(8,128)(2,1)S(1)}, bf16[16,1152]{1,0:T(8,128)(2,1)S(1)}, u32[]{:S(2)}, u32[]{:S(2)}) collective-permute-start(bf16[16,1152]{1,0:T(8,128)(2,1)S(1)} %shard_map.150.refs_5_), channel_id=1, source_target_pairs={{0,1},{1,4},{2,3},{3,6},{4,5},{5,0},{6,7},{7,2},{8,9},{9,12},{10,1... | collective-permute-start | bytes 110600 | tf_op jit(solution)/shard_map/ppermute | solution.py:205
  20.1 4.0 %collective-permute-start.12 = (bf16[16,1152]{1,0:T(8,128)(2,1)S(1)}, bf16[16,1152]{1,0:T(8,128)(2,1)S(1)}, u32[]{:S(2)}, u32[]{:S(2)}) collective-permute-start(bf16[16,1152]{1,0:T(8,128)(2,1)S(1)} %shard_map.151), channel_id=1, source_target_pairs={{0,1},{1,2},{2,3},{3,0},{4,5},{5,6},{6,7},{7,4},{8,9},{9,10},{10,1... | collective-permute-start | bytes 110600 | tf_op jit(solution)/shard_map/ppermute | solution.py:205
  20.7 2.2 %collective-permute-start.14 = (f32[1,512]{1,0:T(1,128)S(1)}, f32[1,512]{1,0:T(1,128)S(1)}, u32[]{:S(2)}, u32[]{:S(2)}) collective-permute-start(f32[1,512]{1,0:T(1,128)S(1)} %bitcast.4), channel_id=1, source_target_pairs={{0,1},{1,0},{2,3},{3,2},{4,5},{5,4},{6,7},{7,6},{8,9},{9,8},{10,11... | collective-permute-start | bytes 6152 | tf_op jit(solution)/shard_map/ppermute | solution.py:108
  22.8 1.2 %collective-permute-start.13 = (bf16[16,512]{1,0:T(8,128)(2,1)S(1)}, bf16[16,512]{1,0:T(8,128)(2,1)S(1)}, u32[]{:S(2)}, u32[]{:S(2)}) collective-permute-start(bf16[16,512]{1,0:T(8,128)(2,1)S(1)} %copy-done.4), channel_id=1, source_target_pairs={{0,1},{1,0},{2,3},{3,2},{4,5},{5,4},{6,7},{7,6},{8,9},{9,8},{10,11... | collective-permute-start | bytes 49160 | tf_op jit(solution)/shard_map/ppermute | solution.py:108
  25.0 3.5 %collective-permute-start.16 = (bf16[16,1024]{1,0:T(8,128)(2,1)S(1)}, bf16[16,1024]{1,0:T(8,128)(2,1)S(1)}, u32[]{:S(2)}, u32[]{:S(2)}) collective-permute-start(bf16[16,1024]{1,0:T(8,128)(2,1)S(1)} %shard_map.155.refs_3_), channel_id=1, source_target_pairs={{0,7},{1,0},{2,5},{3,2},{4,3},{5,4},{6,1},{7,6},{8,15},{9,8},{10,1... | collective-permute-start | bytes 98312 | tf_op jit(solution)/shard_map/ppermute | solution.py:205
  26.6 2.6 %collective-permute-start.17 = (bf16[16,1024]{1,0:T(8,128)(2,1)S(1)}, bf16[16,1024]{1,0:T(8,128)(2,1)S(1)}, u32[]{:S(2)}, u32[]{:S(2)}) collective-permute-start(bf16[16,1024]{1,0:T(8,128)(2,1)S(1)} %shard_map.156.refs_3_), channel_id=1, source_target_pairs={{0,5},{1,0},{2,7},{3,2},{4,1},{5,4},{6,3},{7,6},{8,13},{9,8},{10,1... | collective-permute-start | bytes 98312 | tf_op jit(solution)/shard_map/ppermute | solution.py:205
  28.0 12.6 %copy-start.8 = (s32[64]{0:T(128)S(1)}, s32[64]{0:T(128)}, u32[]{:S(2)}) copy-start(s32[64]{0:T(128)} %param.22) | copy-start | bytes 772
  28.0 1.6 %collective-permute-start.18 = (bf16[16,1024]{1,0:T(8,128)(2,1)S(1)}, bf16[16,1024]{1,0:T(8,128)(2,1)S(1)}, u32[]{:S(2)}, u32[]{:S(2)}) collective-permute-start(bf16[16,1024]{1,0:T(8,128)(2,1)S(1)} %shard_map.157.refs_3_), channel_id=1, source_target_pairs={{0,3},{1,0},{2,1},{3,2},{4,7},{5,4},{6,5},{7,6},{8,11},{9,8},{10,9... | collective-permute-start | bytes 98312 | tf_op jit(solution)/shard_map/ppermute | solution.py:205
  28.4 1.2 %collective-permute-start.19 = (bf16[16,1024]{1,0:T(8,128)(2,1)S(1)}, bf16[16,1024]{1,0:T(8,128)(2,1)S(1)}, u32[]{:S(2)}, u32[]{:S(2)}) collective-permute-start(bf16[16,1024]{1,0:T(8,128)(2,1)S(1)} %shard_map.158), channel_id=1, source_target_pairs={{0,1},{1,0},{2,3},{3,2},{4,5},{5,4},{6,7},{7,6},{8,9},{9,8},{10,11... | collective-permute-start | bytes 98312 | tf_op jit(solution)/shard_map/ppermute | solution.py:108
  29.6 4.8 %collective-permute-start.20 = (bf16[16,1152]{1,0:T(8,128)(2,1)S(1)}, bf16[16,1152]{1,0:T(8,128)(2,1)S(1)}, u32[]{:S(2)}, u32[]{:S(2)}) collective-permute-start(bf16[16,1152]{1,0:T(8,128)(2,1)S(1)} %get-tuple-element.17.refs_3_), channel_id=1, source_target_pairs={{0,1},{1,24},{2,3},{3,26},{4,5},{5,28},{6,7},{7,30},{8,9},{9,16},{... | collective-permute-start | bytes 110600 | tf_op jit(solution)/shard_map/ppermute | solution.py:205
  30.7 3.8 %collective-permute-start.21 = (bf16[16,1152]{1,0:T(8,128)(2,1)S(1)}, bf16[16,1152]{1,0:T(8,128)(2,1)S(1)}, u32[]{:S(2)}, u32[]{:S(2)}) collective-permute-start(bf16[16,1152]{1,0:T(8,128)(2,1)S(1)} %get-tuple-element.17.refs_3_), channel_id=1, source_target_pairs={{0,1},{1,16},{2,3},{3,18},{4,5},{5,20},{6,7},{7,22},{8,9},{9,24},{... | collective-permute-start | bytes 110600 | tf_op jit(solution)/shard_map/ppermute | solution.py:205
  32.2 3.4 %collective-permute-start.22 = (bf16[16,1152]{1,0:T(8,128)(2,1)S(1)}, bf16[16,1152]{1,0:T(8,128)(2,1)S(1)}, u32[]{:S(2)}, u32[]{:S(2)}) collective-permute-start(bf16[16,1152]{1,0:T(8,128)(2,1)S(1)} %get-tuple-element.17.refs_3_), channel_id=1, source_target_pairs={{0,1},{1,8},{2,3},{3,10},{4,5},{5,12},{6,7},{7,14},{8,9},{9,0},{10... | collective-permute-start | bytes 110600 | tf_op jit(solution)/shard_map/ppermute | solution.py:205
  32.3 3.2 %collective-permute-start.23 = (bf16[16,1152]{1,0:T(8,128)(2,1)S(1)}, bf16[16,1152]{1,0:T(8,128)(2,1)S(1)}, u32[]{:S(2)}, u32[]{:S(2)}) collective-permute-start(bf16[16,1152]{1,0:T(8,128)(2,1)S(1)} %get-tuple-element.17.refs_3_), channel_id=1, source_target_pairs={{0,1},{1,0},{2,3},{3,2},{4,5},{5,4},{6,7},{7,6},{8,9},{9,8},{10,11... | collective-permute-start | bytes 110600 | tf_op jit(solution)/shard_map/ppermute | solution.py:108
  32.8 1.2 %collective-permute-start.24 = (f32[16,512]{1,0:T(8,128)S(1)}, f32[16,512]{1,0:T(8,128)S(1)}, u32[]{:S(2)}, u32[]{:S(2)}) collective-permute-start(f32[16,512]{1,0:T(8,128)S(1)} %get-tuple-element.18), channel_id=1, source_target_pairs={{0,1},{1,0},{2,3},{3,2},{4,5},{5,4},{6,7},{7,6},{8,9},{9,8},{10,11... | collective-permute-start | bytes 98312 | tf_op jit(solution)/shard_map/ppermute | solution.py:108
  35.8 1.9 %collective-permute-start.25 = (f32[48,128]{1,0:T(8,128)S(1)}, f32[48,128]{1,0:T(8,128)S(1)}, u32[]{:S(2)}, u32[]{:S(2)}) collective-permute-start(f32[48,128]{1,0:T(8,128)S(1)} %get-tuple-element.19), channel_id=1, source_target_pairs={{0,7},{1,0},{2,5},{3,2},{4,3},{5,4},{6,1},{7,6},{8,15},{9,8},{10,1... | collective-permute-start | bytes 73736 | tf_op jit(solution)/shard_map/ppermute | solution.py:205
  35.8 2.9 %collective-permute-start.26 = (f32[48,128]{1,0:T(8,128)S(1)}, f32[48,128]{1,0:T(8,128)S(1)}, u32[]{:S(2)}, u32[]{:S(2)}) collective-permute-start(f32[48,128]{1,0:T(8,128)S(1)} %get-tuple-element.19), channel_id=1, source_target_pairs={{0,5},{1,0},{2,7},{3,2},{4,1},{5,4},{6,3},{7,6},{8,13},{9,8},{10,1... | collective-permute-start | bytes 73736 | tf_op jit(solution)/shard_map/ppermute | solution.py:205
  37.2 1.8 %collective-permute-start.27 = (f32[48,128]{1,0:T(8,128)S(1)}, f32[48,128]{1,0:T(8,128)S(1)}, u32[]{:S(2)}, u32[]{:S(2)}) collective-permute-start(f32[48,128]{1,0:T(8,128)S(1)} %get-tuple-element.19), channel_id=1, source_target_pairs={{0,3},{1,0},{2,1},{3,2},{4,7},{5,4},{6,5},{7,6},{8,11},{9,8},{10,9... | collective-permute-start | bytes 73736 | tf_op jit(solution)/shard_map/ppermute | solution.py:205
  37.2 1.8 %collective-permute-start.28 = (f32[48,128]{1,0:T(8,128)S(1)}, f32[48,128]{1,0:T(8,128)S(1)}, u32[]{:S(2)}, u32[]{:S(2)}) collective-permute-start(f32[48,128]{1,0:T(8,128)S(1)} %get-tuple-element.19), channel_id=1, source_target_pairs={{0,1},{1,0},{2,3},{3,2},{4,5},{5,4},{6,7},{7,6},{8,9},{9,8},{10,11... | collective-permute-start | bytes 73736 | tf_op jit(solution)/shard_map/ppermute | solution.py:108
  37.7 3.0 %collective-permute-start.30 = (bf16[48,512]{1,0:T(8,128)(2,1)S(1)}, bf16[48,512]{1,0:T(8,128)(2,1)S(1)}, u32[]{:S(2)}, u32[]{:S(2)}) collective-permute-start(bf16[48,512]{1,0:T(8,128)(2,1)S(1)} %get-tuple-element.21), channel_id=1, source_target_pairs={{0,1},{1,0},{2,3},{3,2},{4,5},{5,4},{6,7},{7,6},{8,9},{9,8},{10,11... | collective-permute-start | bytes 147464 | tf_op jit(solution)/shard_map/ppermute | solution.py:108
  38.9 2.5 %collective-permute-start.29 = (f32[48,128]{1,0:T(8,128)S(1)}, f32[48,128]{1,0:T(8,128)S(1)}, u32[]{:S(2)}, u32[]{:S(2)}) collective-permute-start(f32[48,128]{1,0:T(8,128)S(1)} %shard_map.161.refs_0_), channel_id=1, source_target_pairs={{0,1},{1,0},{2,3},{3,2},{4,5},{5,4},{6,7},{7,6},{8,9},{9,8},{10,11... | collective-permute-start | bytes 73736 | tf_op jit(solution)/shard_map/ppermute | solution.py:108

commit v7 on v6

--- a/solution.py
+++ b/solution.py
@@ -134,7 +134,9 @@
     inputs = hidden_ref[...].astype(jnp.float32)
     width = inputs.shape[1]
     message_ref[:, :width] = (inputs * gain_ref[...]).astype(jnp.bfloat16)
-    message_ref[:, width:] = pack_statistics([jnp.sum(inputs * inputs, axis=1, keepdims=True)])
+    message_ref[:, width:] = pack_statistics(
+        [jnp.sum(inputs * inputs, axis=1, keepdims=True)], core_number()
+    )
 
 
 def positions_and_ranges(
@@ -164,12 +166,12 @@
 LOG2_E = 1.4426950408889634
 
 
-def pack_statistics(values):
+def pack_statistics(values, first=0):
     rows = values[0].shape[0]
     lane = lax.broadcasted_iota(jnp.int32, (rows, 128), 1)
     rest = jnp.zeros((rows, 128), jnp.float32)
     for place, value in enumerate(values):
-        rest = jnp.where(lane == place, value, rest)
+        rest = jnp.where(lane == first + place, value, rest)
     out = rest.astype(jnp.bfloat16).astype(jnp.float32)
     for part in (1, 2):
         rest = rest - rest.astype(jnp.bfloat16).astype(jnp.float32)
@@ -177,9 +179,11 @@
     return out.astype(jnp.bfloat16)
 
 
-def unpack_statistics(block):
-    block = block.astype(jnp.float32)
-    return block + pltpu.roll(block, 96, 1) + pltpu.roll(block, 64, 1)
+def read_statistic(block, first, count=1):
+    lane = lax.broadcasted_iota(jnp.int32, block.shape, 1)
+    place = (lane & 31) - first
+    mine = (place >= 0) & (place < count) & (lane < 96)
+    return jnp.sum(jnp.where(mine, block.astype(jnp.float32), 0.0), axis=1, keepdims=True)
 
 
 def core_number():
@@ -214,8 +218,7 @@
     core = core_number()
     width = own_ref.shape[1] - 128
     refs = (own_ref, other_ref)
-    squares = sum(unpack_statistics(ref[:, width:])[:, :1] for ref in refs)
-    pair_ref[:, 2 * width :] = pack_statistics([squares])
+    pair_ref[:, 2 * width :] = own_ref[:, width:] + other_ref[:, width:]
     for first in range(2):
 
         @pl.when(core == first)
@@ -253,11 +256,11 @@
     @pl.when(core_number() == core)
     def _():
         projected = total_ref[...]
-        squares = unpack_statistics(pair_ref[:, 2 * width :])
+        squares = pair_ref[:, 2 * width :].astype(jnp.float32)
         for i in range(blocks_ref.shape[0]):
             projected = projected + project_pair(blocks_ref.at[i], i + 1, weight_ref)
-            squares = squares + unpack_statistics(blocks_ref[i, :, 2 * width :])
-        squares = squares[:, :1]
+            squares = squares + blocks_ref[i, :, 2 * width :].astype(jnp.float32)
+        squares = read_statistic(squares, 0, 2)
         projected = projected * lax.rsqrt(squares / model_width + EPSILON)
         cosine = rope_ref[:, :head_dim]
         sine = rope_ref[:, head_dim:]
@@ -381,15 +384,15 @@
         rows = attended_ref.shape[0]
         width = attended_ref.shape[1] // 2
         others = (first_ref, second_ref, third_ref)
-        stats = [unpack_statistics(ref[:, 2 * width :]) for ref in others]
+        stats = [ref[:, 2 * width :] for ref in others]
         for j in range(2):
             for h in range(width // 128):
                 part = slice(h * rows, (h + 1) * rows)
                 place = slice(j * width + h * 128, j * width + (h + 1) * 128)
                 slot = 2 * (j * (width // 128) + h)
-                maxima = [stats_ref[j, part, :1]] + [s[:, slot : slot + 1] for s in stats]
+                maxima = [stats_ref[j, part, :1]] + [read_statistic(s, slot) for s in stats]
                 totals = [stats_ref[j, part, 128:129]]
-                totals += [s[:, slot + 1 : slot + 2] for s in stats]
+                totals += [read_statistic(s, slot + 1) for s in stats]
                 numerators = [own_ref[j, part, :]]
                 numerators += [ref[:, place].astype(jnp.float32) for ref in others]
                 highest = maxima[0]
@@ -466,7 +469,7 @@
         for i, ref in enumerate(refs[1:]):
             far_ref[i * rows : (i + 1) * rows] = ref[:, width : 2 * width]
         far = jnp.concatenate([ref[:, width : 2 * width] for ref in refs], axis=0)
-        squares = unpack_statistics(own_ref[:, 2 * width :])[:, :1]
+        squares = read_statistic(own_ref[:, 2 * width :], 0)
         gram = 0.0
         for vectors in (near_ref[...], far):
             gram = gram + lax.dot_general(
@@ -628,8 +631,16 @@
         lengths,
         pack_order,
     )
+    other_hidden_in = flip(hidden_in, "pack", 1)
+    other_gain = flip(final_gain, "pack", 1)
     blocks = in_vmem(
-        join_blocks, shaped((chips - 1,) + pair.shape, bf16), *received[::-1], own_projected, rope
+        join_blocks,
+        shaped((chips - 1,) + pair.shape, bf16),
+        *received[::-1],
+        other_hidden_in,
+        other_gain,
+        own_projected,
+        rope,
     )
     flipped_blocks = flip(blocks, "pack", 1)
 
@@ -687,21 +698,17 @@
                 cached_values,
                 other_held,
                 ranges,
-                *partials[-1:],
+                *(partials[-1:] or (own_stats,)),
                 flops=1 << 34,
             )
         )
     received = [send_across(part, "pack", k, 1) for k, part in zip(others, partials[::-1])]
-    other_hidden_in = flip(hidden_in, "pack", 1)
-    other_gain = flip(final_gain, "pack", 1)
     attended = in_vmem(
         merge_partials,
         shaped((stmts, 2 * width), bf16),
         *received[::-1],
         own_part,
         own_stats,
-        other_hidden_in,
-        other_gain,
     )
 
     def projected_to(offset, kind, *after):

time: 42.6 us -> 41.1 us (0.965)
  waiting for transfers between devices: 11.7 us -> 11.1 us
  Pallas kernels: 5.78 us -> 5.33 us
    ppermute x13, waiting for transfers between devices: 5.22 us -> 3.11 us  [flip(): return lax.ppermute(array, axis, [(i, i ^ offset) for i in range(size)])]
    ppermute x18, waiting for transfers between devices: 6.48 us -> 7.94 us  [send_across(): return lax.ppermute(array, ('dp', 'pack'), pairs)]
    pallas_call x23, Pallas kernels: 4.76 us -> 4.3 us  [in_vmem(): pl.pallas_call(body, out_shape=outputs, in_specs=[whole] * len(operands),...]
  transfers between devices with their start and end apart: 31 -> 31, of which waited for: 15 -> 16; matrix products, arithmetic and copies ran while one was open for 0% -> 0% of each run, Pallas kernels for 9% -> 9%
where the time goes in v7:
time: 41.1 us; the launch traced here: 41 us
  starting transfers between devices  23.1 us (56%)
  waiting for transfers between devices  11.1 us (27%)
  Pallas kernels  5.33 us (13%)
  between operations  0.82 us (2%)
  local copies, waits for them, and re-layouts  0.7 us (2%)
    ppermute x18, starting transfers between devices, send_across(): return lax.ppermute(array, ('dp', 'pack'), pairs)  16.6 us
    ppermute x18, waiting for transfers between devices, send_across(): return lax.ppermute(array, ('dp', 'pack'), pairs)  7.94 us
    ppermute x13, starting transfers between devices, flip(): return lax.ppermute(array, axis, [(i, i ^ offset) for i in range(size)])  6.52 us
    pallas_call x23, Pallas kernels, in_vmem(): pl.pallas_call(body, out_shape=outputs, in_specs=[whole] * len(operands),...  4.3 us
    ppermute x13, waiting for transfers between devices, flip(): return lax.ppermute(array, axis, [(i, i ^ offset) for i in range(size)])  3.11 us
    pallas_call x1, Pallas kernels, core_roles(): pl.pallas_call(lambda *refs: losses_and_gradient(*refs, model_width=model...  1.02 us
  transfers between devices with their start and end apart: 31, of which 16 were waited for; matrix products, arithmetic and copies ran while one was open for 0% of the time, Pallas kernels for 9%

profile of v7, /device:TPU:0, one launch (start us, length us, event | category | flops | bytes accessed | tf_op | source)
XLA Modules:
  0.0 41.0 jit_solution(12176706806684689007)
XLA Ops:
  0.7 0.6 %copy-done.4 = bf16[16,512]{1,0:T(8,128)(2,1)S(1)} copy-done((bf16[16,512]{1,0:T(8,128)(2,1)S(1)}, bf16[16,512]{1,0:T(8,128)(2,1)}, u32[]{:S(2)}) %copy-start.4) | copy-done | bytes 16408
  1.5 0.5 %collective-permute-start = (bf16[16,640]{1,0:T(8,128)(2,1)S(1)}, bf16[16,640]{1,0:T(8,128)(2,1)S(1)}, u32[]{:S(2)}, u32[]{:S(2)}) collective-permute-start(bf16[16,640]{1,0:T(8,128)(2,1)S(1)} %shard_map.140.own_ref.message_ref), channel_id=1, source_target_pairs={{0,1},{1,0},{2,3},{3,2},{4,5},{5,4},{6,7},{7,6},{8,9},{9,8},{10,11... | collective-permute-start | bytes 61448 | tf_op jit(solution)/shard_map/ppermute | solution.py:108
  2.0 0.8 %collective-permute-done.other_ref = bf16[16,640]{1,0:T(8,128)(2,1)S(1)} collective-permute-done((bf16[16,640]{1,0:T(8,128)(2,1)S(1)}, bf16[16,640]{1,0:T(8,128)(2,1)S(1)}, u32[]{:S(2)}, u32[]{:S(2)}) %collective-permute-start) | collective-permute-done | bytes 20512 | tf_op jit(solution)/shard_map/ppermute | solution.py:108
  2.8 4.7 %collective-permute-start.1 = (bf16[16,1152]{1,0:T(8,128)(2,1)S(1)}, bf16[16,1152]{1,0:T(8,128)(2,1)S(1)}, u32[]{:S(2)}, u32[]{:S(2)}) collective-permute-start(bf16[16,1152]{1,0:T(8,128)(2,1)S(1)} %shard_map.141.pair_ref.refs_0_), channel_id=1, source_target_pairs={{0,7},{1,0},{2,5},{3,2},{4,3},{5,4},{6,1},{7,6},{8,15},{9,8},{10,1... | collective-permute-start | bytes 110600 | tf_op jit(solution)/shard_map/ppermute | solution.py:209
  7.6 0.5 %collective-permute-start.4 = (bf16[16,512]{1,0:T(8,128)(2,1)S(1)}, bf16[16,512]{1,0:T(8,128)(2,1)S(1)}, u32[]{:S(2)}, u32[]{:S(2)}) collective-permute-start(bf16[16,512]{1,0:T(8,128)(2,1)S(1)} %copy-done.4), channel_id=1, source_target_pairs={{0,1},{1,0},{2,3},{3,2},{4,5},{5,4},{6,7},{7,6},{8,9},{9,8},{10,11... | collective-permute-start | bytes 49160 | tf_op jit(solution)/shard_map/ppermute | solution.py:108
  8.3 0.2 shard_map.142.refs_5_.refs_2_
  8.6 0.7 %collective-permute-done.5.refs_4_.other_gain_ref = f32[1,512]{1,0:T(1,128)S(1)} collective-permute-done((f32[1,512]{1,0:T(1,128)S(1)}, f32[1,512]{1,0:T(1,128)S(1)}, u32[]{:S(2)}, u32[]{:S(2)}) %collective-permute-start.5) | collective-permute-done | bytes 2080 | tf_op jit(solution)/shard_map/ppermute | solution.py:108
  9.2 0.3 collective-permute-done.2.refs_1_
  9.5 0.3 collective-permute-done.3.refs_2_
  9.9 1.6 %collective-permute-start.6 = (bf16[3,16,1152]{2,1,0:T(8,128)(2,1)S(1)}, bf16[3,16,1152]{2,1,0:T(8,128)(2,1)S(1)}, u32[]{:S(2)}, u32[]{:S(2)}) collective-permute-start(bf16[3,16,1152]{2,1,0:T(8,128)(2,1)S(1)} %shard_map.144.refs_1_), channel_id=1, source_target_pairs={{0,1},{1,0},{2,3},{3,2},{4,5},{5,4},{6,7},{7,6},{8,9},{9,8},{10,11... | collective-permute-start | bytes 331784 | tf_op jit(solution)/shard_map/ppermute | solution.py:108
  11.5 0.8 %collective-permute-start.7 = (bf16[16,512]{1,0:T(8,128)(2,1)S(1)}, bf16[16,512]{1,0:T(8,128)(2,1)S(1)}, u32[]{:S(2)}, u32[]{:S(2)}) collective-permute-start(bf16[16,512]{1,0:T(8,128)(2,1)S(1)} %shard_map.146._), channel_id=1, source_target_pairs={{0,1},{1,0},{2,3},{3,2},{4,5},{5,4},{6,7},{7,6},{8,9},{9,8},{10,11... | collective-permute-start | bytes 49160 | tf_op jit(solution)/shard_map/ppermute | solution.py:108
  12.5 0.7 %shard_map.145.first_ref = bf16[16,512]{1,0:T(8,128)(2,1)S(1)} custom-call(bf16[16,1152]{1,0:T(8,128)(2,1)S(1)} %shard_map.141.pair_ref.refs_0_, bf16[3,16,1152]{2,1,0:T(8,128)(2,1)S(1)} %collective-permute-done.6.refs_1_, f32[16,512]{1,0:T(8,128)S(1)} %shard_map.142.refs_5_.refs_2_, bf16[4096,512]{1,0:T(8,128)(2,1)S(1)} %copy-done.1, f32[1,128]{1,0:T(1,128)S(1)} %bitcast.9, ...), custom_call_target="tpu_custom_call" | custom-call | flops 68719476736 | bytes 4391424 | tf_op jit(solution)/shard_map/pallas_call | solution.py:114
  13.2 1.6 %collective-permute-start.8 = (bf16[16,1024]{1,0:T(8,128)(2,1)S(1)}, bf16[16,1024]{1,0:T(8,128)(2,1)S(1)}, u32[]{:S(2)}, u32[]{:S(2)}) collective-permute-start(bf16[16,1024]{1,0:T(8,128)(2,1)S(1)} %shard_map.147.query_ref._), channel_id=1, source_target_pairs={{0,7},{1,0},{2,5},{3,2},{4,3},{5,4},{6,1},{7,6},{8,15},{9,8},{10,1... | collective-permute-start | bytes 98312 | tf_op jit(solution)/shard_map/ppermute | solution.py:209
  14.8 0.2 collective-permute-start.13
  15.0 0.3 shard_map.154
  15.2 0.4 collective-permute-start.15
  15.7 0.5 %shard_map.149 = (f32[2,64,128]{2,1,0:T(8,128)S(1)}, f32[2,64,256]{2,1,0:T(8,128)S(1)}) custom-call(bf16[16,1024]{1,0:T(8,128)(2,1)S(1)} %shard_map.147.query_ref._, bf16[320,1024]{1,0:T(8,128)(2,1)S(1)} %copy-done.2, bf16[320,1024]{1,0:T(8,128)(2,1)S(1)} %copy-done.3, bf16[2,320,1024]{2,1,0:T(8,128)(2,1)S(1)} %collective-permute-done.9.other_ref.refs_3_, ...), custom_call_target="tpu_custom_call" | custom-call | flops 134217728 | bytes 2670592 | tf_op jit(solution)/shard_map/pallas_call | solution.py:114
  16.2 0.2 collective-permute-done.8.refs_0_
  16.4 2.8 %collective-permute-start.10 = (bf16[16,1152]{1,0:T(8,128)(2,1)S(1)}, bf16[16,1152]{1,0:T(8,128)(2,1)S(1)}, u32[]{:S(2)}, u32[]{:S(2)}) collective-permute-start(bf16[16,1152]{1,0:T(8,128)(2,1)S(1)} %shard_map.150.refs_5_), channel_id=1, source_target_pairs={{0,1},{1,6},{2,3},{3,4},{4,5},{5,2},{6,7},{7,0},{8,9},{9,14},{10,1... | collective-permute-start | bytes 110600 | tf_op jit(solution)/shard_map/ppermute | solution.py:209
  19.2 0.6 %collective-permute-start.12 = (bf16[16,1152]{1,0:T(8,128)(2,1)S(1)}, bf16[16,1152]{1,0:T(8,128)(2,1)S(1)}, u32[]{:S(2)}, u32[]{:S(2)}) collective-permute-start(bf16[16,1152]{1,0:T(8,128)(2,1)S(1)} %shard_map.151.refs_5_), channel_id=1, source_target_pairs={{0,1},{1,4},{2,3},{3,6},{4,5},{5,0},{6,7},{7,2},{8,9},{9,12},{10,1... | collective-permute-start | bytes 110600 | tf_op jit(solution)/shard_map/ppermute | solution.py:209
  19.8 0.6 %collective-permute-start.14 = (bf16[16,1152]{1,0:T(8,128)(2,1)S(1)}, bf16[16,1152]{1,0:T(8,128)(2,1)S(1)}, u32[]{:S(2)}, u32[]{:S(2)}) collective-permute-start(bf16[16,1152]{1,0:T(8,128)(2,1)S(1)} %shard_map.152), channel_id=1, source_target_pairs={{0,1},{1,2},{2,3},{3,0},{4,5},{5,6},{6,7},{7,4},{8,9},{9,10},{10,1... | collective-permute-start | bytes 110600 | tf_op jit(solution)/shard_map/ppermute | solution.py:209
  20.4 2.1 %collective-permute-done.10.third_ref = bf16[16,1152]{1,0:T(8,128)(2,1)S(1)} collective-permute-done((bf16[16,1152]{1,0:T(8,128)(2,1)S(1)}, bf16[16,1152]{1,0:T(8,128)(2,1)S(1)}, u32[]{:S(2)}, u32[]{:S(2)}) %collective-permute-start.10) | collective-permute-done | bytes 36896 | tf_op jit(solution)/shard_map/ppermute | solution.py:209
  22.5 1.1 %collective-permute-done.12.second_ref = bf16[16,1152]{1,0:T(8,128)(2,1)S(1)} collective-permute-done((bf16[16,1152]{1,0:T(8,128)(2,1)S(1)}, bf16[16,1152]{1,0:T(8,128)(2,1)S(1)}, u32[]{:S(2)}, u32[]{:S(2)}) %collective-permute-start.12) | collective-permute-done | bytes 36896 | tf_op jit(solution)/shard_map/ppermute | solution.py:209
  23.8 0.3 shard_map.153.refs_0_
  24.1 0.4 shard_map.155.refs_3_
  24.5 0.3 collective-permute-start.16
  24.7 0.4 shard_map.156.refs_3_
  25.1 0.6 %collective-permute-start.17 = (bf16[16,1024]{1,0:T(8,128)(2,1)S(1)}, bf16[16,1024]{1,0:T(8,128)(2,1)S(1)}, u32[]{:S(2)}, u32[]{:S(2)}) collective-permute-start(bf16[16,1024]{1,0:T(8,128)(2,1)S(1)} %shard_map.156.refs_3_), channel_id=1, source_target_pairs={{0,5},{1,0},{2,7},{3,2},{4,1},{5,4},{6,3},{7,6},{8,13},{9,8},{10,1... | collective-permute-start | bytes 98312 | tf_op jit(solution)/shard_map/ppermute | solution.py:209
  25.7 0.4 shard_map.157.refs_3_
  26.1 0.4 shard_map.158
  26.6 0.7 %collective-permute-done.17.second_ref = bf16[16,1024]{1,0:T(8,128)(2,1)S(1)} collective-permute-done((bf16[16,1024]{1,0:T(8,128)(2,1)S(1)}, bf16[16,1024]{1,0:T(8,128)(2,1)S(1)}, u32[]{:S(2)}, u32[]{:S(2)}) %collective-permute-start.17) | collective-permute-done | bytes 32800 | tf_op jit(solution)/shard_map/ppermute | solution.py:209
  27.3 0.4 collective-permute-done.18.first_ref
  27.7 2.0 %collective-permute-start.20 = (bf16[16,1152]{1,0:T(8,128)(2,1)S(1)}, bf16[16,1152]{1,0:T(8,128)(2,1)S(1)}, u32[]{:S(2)}, u32[]{:S(2)}) collective-permute-start(bf16[16,1152]{1,0:T(8,128)(2,1)S(1)} %get-tuple-element.17.refs_3_), channel_id=1, source_target_pairs={{0,1},{1,24},{2,3},{3,26},{4,5},{5,28},{6,7},{7,30},{8,9},{9,16},{... | collective-permute-start | bytes 110600 | tf_op jit(solution)/shard_map/ppermute | solution.py:209
  29.7 0.6 %collective-permute-start.21 = (bf16[16,1152]{1,0:T(8,128)(2,1)S(1)}, bf16[16,1152]{1,0:T(8,128)(2,1)S(1)}, u32[]{:S(2)}, u32[]{:S(2)}) collective-permute-start(bf16[16,1152]{1,0:T(8,128)(2,1)S(1)} %get-tuple-element.17.refs_3_), channel_id=1, source_target_pairs={{0,1},{1,16},{2,3},{3,18},{4,5},{5,20},{6,7},{7,22},{8,9},{9,24},{... | collective-permute-start | bytes 110600 | tf_op jit(solution)/shard_map/ppermute | solution.py:209
  30.3 1.1 %collective-permute-start.22 = (bf16[16,1152]{1,0:T(8,128)(2,1)S(1)}, bf16[16,1152]{1,0:T(8,128)(2,1)S(1)}, u32[]{:S(2)}, u32[]{:S(2)}) collective-permute-start(bf16[16,1152]{1,0:T(8,128)(2,1)S(1)} %get-tuple-element.17.refs_3_), channel_id=1, source_target_pairs={{0,1},{1,8},{2,3},{3,10},{4,5},{5,12},{6,7},{7,14},{8,9},{9,0},{10... | collective-permute-start | bytes 110600 | tf_op jit(solution)/shard_map/ppermute | solution.py:209
  31.4 0.5 %collective-permute-start.24 = (f32[16,512]{1,0:T(8,128)S(1)}, f32[16,512]{1,0:T(8,128)S(1)}, u32[]{:S(2)}, u32[]{:S(2)}) collective-permute-start(f32[16,512]{1,0:T(8,128)S(1)} %get-tuple-element.18), channel_id=1, source_target_pairs={{0,1},{1,0},{2,3},{3,2},{4,5},{5,4},{6,7},{7,6},{8,9},{9,8},{10,11... | collective-permute-start | bytes 98312 | tf_op jit(solution)/shard_map/ppermute | solution.py:108
  31.9 0.9 %collective-permute-done.24._.refs_6_ = f32[16,512]{1,0:T(8,128)S(1)} collective-permute-done((f32[16,512]{1,0:T(8,128)S(1)}, f32[16,512]{1,0:T(8,128)S(1)}, u32[]{:S(2)}, u32[]{:S(2)}) %collective-permute-start.24) | collective-permute-done | bytes 32800 | tf_op jit(solution)/shard_map/ppermute | solution.py:108
  32.7 0.8 %collective-permute-done.20.third_ref = bf16[16,1152]{1,0:T(8,128)(2,1)S(1)} collective-permute-done((bf16[16,1152]{1,0:T(8,128)(2,1)S(1)}, bf16[16,1152]{1,0:T(8,128)(2,1)S(1)}, u32[]{:S(2)}, u32[]{:S(2)}) %collective-permute-start.20) | collective-permute-done | bytes 36896 | tf_op jit(solution)/shard_map/ppermute | solution.py:209
  33.5 0.6 %collective-permute-done.22.first_ref = bf16[16,1152]{1,0:T(8,128)(2,1)S(1)} collective-permute-done((bf16[16,1152]{1,0:T(8,128)(2,1)S(1)}, bf16[16,1152]{1,0:T(8,128)(2,1)S(1)}, u32[]{:S(2)}, u32[]{:S(2)}) %collective-permute-start.22) | collective-permute-done | bytes 36896 | tf_op jit(solution)/shard_map/ppermute | solution.py:209
  34.1 0.2 shard_map.160
  34.4 0.4 collective-permute-start.25
  34.8 1.2 %collective-permute-start.26 = (f32[48,128]{1,0:T(8,128)S(1)}, f32[48,128]{1,0:T(8,128)S(1)}, u32[]{:S(2)}, u32[]{:S(2)}) collective-permute-start(f32[48,128]{1,0:T(8,128)S(1)} %get-tuple-element.19), channel_id=1, source_target_pairs={{0,5},{1,0},{2,7},{3,2},{4,1},{5,4},{6,3},{7,6},{8,13},{9,8},{10,1... | collective-permute-start | bytes 73736 | tf_op jit(solution)/shard_map/ppermute | solution.py:209
  35.9 0.5 %collective-permute-start.28 = (f32[48,128]{1,0:T(8,128)S(1)}, f32[48,128]{1,0:T(8,128)S(1)}, u32[]{:S(2)}, u32[]{:S(2)}) collective-permute-start(f32[48,128]{1,0:T(8,128)S(1)} %get-tuple-element.19), channel_id=1, source_target_pairs={{0,1},{1,0},{2,3},{3,2},{4,5},{5,4},{6,7},{7,6},{8,9},{9,8},{10,11... | collective-permute-start | bytes 73736 | tf_op jit(solution)/shard_map/ppermute | solution.py:108
  36.5 1.0 %collective-permute-done.26.second_ref = f32[48,128]{1,0:T(8,128)S(1)} collective-permute-done((f32[48,128]{1,0:T(8,128)S(1)}, f32[48,128]{1,0:T(8,128)S(1)}, u32[]{:S(2)}, u32[]{:S(2)}) %collective-permute-start.26) | collective-permute-done | bytes 24608 | tf_op jit(solution)/shard_map/ppermute | solution.py:209
  37.5 0.2 collective-permute-done.27.first_ref
  37.7 1.4 %collective-permute-start.29 = (f32[48,128]{1,0:T(8,128)S(1)}, f32[48,128]{1,0:T(8,128)S(1)}, u32[]{:S(2)}, u32[]{:S(2)}) collective-permute-start(f32[48,128]{1,0:T(8,128)S(1)} %shard_map.161.refs_0_), channel_id=1, source_target_pairs={{0,1},{1,0},{2,3},{3,2},{4,5},{5,4},{6,7},{7,6},{8,9},{9,8},{10,11... | collective-permute-start | bytes 73736 | tf_op jit(solution)/shard_map/ppermute | solution.py:108
  39.2 0.7 %collective-permute-done.29.refs_1_ = f32[48,128]{1,0:T(8,128)S(1)} collective-permute-done((f32[48,128]{1,0:T(8,128)S(1)}, f32[48,128]{1,0:T(8,128)S(1)}, u32[]{:S(2)}, u32[]{:S(2)}) %collective-permute-start.29) | collective-permute-done | bytes 24608 | tf_op jit(solution)/shard_map/ppermute | solution.py:108
  40.0 1.0 %shard_map.163 = (bf16[16,512]{1,0:T(8,128)(2,1)}, f32[2]{0:T(128)}, bf16[16,512]{1,0:T(8,128)(2,1)}) custom-call(f32[48,128]{1,0:T(8,128)S(1)} %shard_map.161.refs_0_, f32[48,128]{1,0:T(8,128)S(1)} %collective-permute-done.29.refs_1_, bf16[64,512]{1,0:T(8,128)(2,1)S(1)} %get-tuple-element.20.refs_2_, bf16[16,1152]{1,0:T(8,128)(2,1)S(1)} %get-tuple-element.17.refs_3_, ...), custom_call_target="tpu_custom_call" | custom-call | tf_op jit(solution)/shard_map/pallas_call | solution.py:767
  (63 shorter events, 1.1 us)
Async XLA Ops:
  0.6 7.5 %copy-start.11 = (f32[1,128]{1,0:T(1,128)S(1)}, f32[1,128]{1,0:T(1,128)}, u32[]{:S(2)}) copy-start(f32[1,128]{1,0:T(1,128)} %constant.2.clone.frequency_ref) | copy-start | bytes 1540
  0.6 0.7 %copy-start.4 = (bf16[16,512]{1,0:T(8,128)(2,1)S(1)}, bf16[16,512]{1,0:T(8,128)(2,1)}, u32[]{:S(2)}) copy-start(bf16[16,512]{1,0:T(8,128)(2,1)} %own_ref.1) | copy-start | bytes 49156
  0.7 0.7 %copy-start.6 = (f32[512]{0:T(512)S(1)}, f32[512]{0:T(512)}, u32[]{:S(2)}) copy-start(f32[512]{0:T(512)} %param.13) | copy-start | bytes 6148
  0.7 7.4 %copy-start.5 = (f32[512]{0:T(512)S(1)}, f32[512]{0:T(512)}, u32[]{:S(2)}) copy-start(f32[512]{0:T(512)} %param.19) | copy-start | bytes 6148
  0.7 7.5 %copy-start.9 = (s32[1,16]{1,0:T(1,128)S(1)}, s32[1,16]{1,0:T(1,128)}, u32[]{:S(2)}) copy-start(s32[1,16]{1,0:T(1,128)} %lengths_ref.1) | copy-start | bytes 196
  0.7 7.5 %copy-start.10 = (s32[1,16]{1,0:T(1,128)S(1)}, s32[1,16]{1,0:T(1,128)}, u32[]{:S(2)}) copy-start(s32[1,16]{1,0:T(1,128)} %order_ref.1) | copy-start | bytes 196
  0.7 7.6 %copy-start.1 = (bf16[4096,512]{1,0:T(8,128)(2,1)S(1)}, bf16[4096,512]{1,0:T(8,128)(2,1)}, u32[]{:S(2)}) copy-start(bf16[4096,512]{1,0:T(8,128)(2,1)} %refs_3_.3) | copy-start | bytes 12582916
  0.7 10.8 %copy-start.7 = (f32[128]{0:T(128)S(1)}, f32[128]{0:T(128)}, u32[]{:S(2)}) copy-start(f32[128]{0:T(128)} %param.15) | copy-start | bytes 1540
  1.5 1.3 %collective-permute-start = (bf16[16,640]{1,0:T(8,128)(2,1)S(1)}, bf16[16,640]{1,0:T(8,128)(2,1)S(1)}, u32[]{:S(2)}, u32[]{:S(2)}) collective-permute-start(bf16[16,640]{1,0:T(8,128)(2,1)S(1)} %shard_map.140.own_ref.message_ref), channel_id=1, source_target_pairs={{0,1},{1,0},{2,3},{3,2},{4,5},{5,4},{6,7},{7,6},{8,9},{9,8},{10,11... | collective-permute-start | bytes 61448 | tf_op jit(solution)/shard_map/ppermute | solution.py:108
  2.8 6.4 %collective-permute-start.1 = (bf16[16,1152]{1,0:T(8,128)(2,1)S(1)}, bf16[16,1152]{1,0:T(8,128)(2,1)S(1)}, u32[]{:S(2)}, u32[]{:S(2)}) collective-permute-start(bf16[16,1152]{1,0:T(8,128)(2,1)S(1)} %shard_map.141.pair_ref.refs_0_), channel_id=1, source_target_pairs={{0,7},{1,0},{2,5},{3,2},{4,3},{5,4},{6,1},{7,6},{8,15},{9,8},{10,1... | collective-permute-start | bytes 110600 | tf_op jit(solution)/shard_map/ppermute | solution.py:209
  7.6 2.0 %collective-permute-start.2 = (bf16[16,1152]{1,0:T(8,128)(2,1)S(1)}, bf16[16,1152]{1,0:T(8,128)(2,1)S(1)}, u32[]{:S(2)}, u32[]{:S(2)}) collective-permute-start(bf16[16,1152]{1,0:T(8,128)(2,1)S(1)} %shard_map.141.pair_ref.refs_0_), channel_id=1, source_target_pairs={{0,5},{1,0},{2,7},{3,2},{4,1},{5,4},{6,3},{7,6},{8,13},{9,8},{10,1... | collective-permute-start | bytes 110600 | tf_op jit(solution)/shard_map/ppermute | solution.py:209
  7.6 2.3 %collective-permute-start.3 = (bf16[16,1152]{1,0:T(8,128)(2,1)S(1)}, bf16[16,1152]{1,0:T(8,128)(2,1)S(1)}, u32[]{:S(2)}, u32[]{:S(2)}) collective-permute-start(bf16[16,1152]{1,0:T(8,128)(2,1)S(1)} %shard_map.141.pair_ref.refs_0_), channel_id=1, source_target_pairs={{0,3},{1,0},{2,1},{3,2},{4,7},{5,4},{6,5},{7,6},{8,11},{9,8},{10,9... | collective-permute-start | bytes 110600 | tf_op jit(solution)/shard_map/ppermute | solution.py:209
  7.6 1.7 %collective-permute-start.4 = (bf16[16,512]{1,0:T(8,128)(2,1)S(1)}, bf16[16,512]{1,0:T(8,128)(2,1)S(1)}, u32[]{:S(2)}, u32[]{:S(2)}) collective-permute-start(bf16[16,512]{1,0:T(8,128)(2,1)S(1)} %copy-done.4), channel_id=1, source_target_pairs={{0,1},{1,0},{2,3},{3,2},{4,5},{5,4},{6,7},{7,6},{8,9},{9,8},{10,11... | collective-permute-start | bytes 49160 | tf_op jit(solution)/shard_map/ppermute | solution.py:108
  8.1 1.2 %collective-permute-start.5 = (f32[1,512]{1,0:T(1,128)S(1)}, f32[1,512]{1,0:T(1,128)S(1)}, u32[]{:S(2)}, u32[]{:S(2)}) collective-permute-start(f32[1,512]{1,0:T(1,128)S(1)} %bitcast.4), channel_id=1, source_target_pairs={{0,1},{1,0},{2,3},{3,2},{4,5},{5,4},{6,7},{7,6},{8,9},{9,8},{10,11... | collective-permute-start | bytes 6152 | tf_op jit(solution)/shard_map/ppermute | solution.py:108
  8.3 4.0 %copy-start.2 = (bf16[320,1024]{1,0:T(8,128)(2,1)S(1)}, bf16[320,1024]{1,0:T(8,128)(2,1)}, u32[]{:S(2)}) copy-start(bf16[320,1024]{1,0:T(8,128)(2,1)} %refs_1_.9) | copy-start | bytes 1966084
  8.3 4.0 %copy-start.3 = (bf16[320,1024]{1,0:T(8,128)(2,1)S(1)}, bf16[320,1024]{1,0:T(8,128)(2,1)}, u32[]{:S(2)}) copy-start(bf16[320,1024]{1,0:T(8,128)(2,1)} %refs_2_.5) | copy-start | bytes 1966084
  9.9 2.6 %collective-permute-start.6 = (bf16[3,16,1152]{2,1,0:T(8,128)(2,1)S(1)}, bf16[3,16,1152]{2,1,0:T(8,128)(2,1)S(1)}, u32[]{:S(2)}, u32[]{:S(2)}) collective-permute-start(bf16[3,16,1152]{2,1,0:T(8,128)(2,1)S(1)} %shard_map.144.refs_1_), channel_id=1, source_target_pairs={{0,1},{1,0},{2,3},{3,2},{4,5},{5,4},{6,7},{7,6},{8,9},{9,8},{10,11... | collective-permute-start | bytes 331784 | tf_op jit(solution)/shard_map/ppermute | solution.py:108
  11.5 1.7 %collective-permute-start.7 = (bf16[16,512]{1,0:T(8,128)(2,1)S(1)}, bf16[16,512]{1,0:T(8,128)(2,1)S(1)}, u32[]{:S(2)}, u32[]{:S(2)}) collective-permute-start(bf16[16,512]{1,0:T(8,128)(2,1)S(1)} %shard_map.146._), channel_id=1, source_target_pairs={{0,1},{1,0},{2,3},{3,2},{4,5},{5,4},{6,7},{7,6},{8,9},{9,8},{10,11... | collective-permute-start | bytes 49160 | tf_op jit(solution)/shard_map/ppermute | solution.py:108
  12.4 2.6 %copy-start = (bf16[512,4096]{1,0:T(8,128)(2,1)S(1)}, bf16[512,4096]{1,0:T(8,128)(2,1)}, u32[]{:S(2)}) copy-start(bf16[512,4096]{1,0:T(8,128)(2,1)} %refs_1_.13) | copy-start | bytes 12582916
  12.4 3.2 %collective-permute-start.9 = (bf16[2,320,1024]{2,1,0:T(8,128)(2,1)S(1)}, bf16[2,320,1024]{2,1,0:T(8,128)(2,1)S(1)}, u32[]{:S(2)}, u32[]{:S(2)}) collective-permute-start(bf16[2,320,1024]{2,1,0:T(8,128)(2,1)S(1)} %shard_map.148), channel_id=1, source_target_pairs={{0,1},{1,0},{2,3},{3,2},{4,5},{5,4},{6,7},{7,6},{8,9},{9,8},{10,11... | collective-permute-start | bytes 3932168 | tf_op jit(solution)/shard_map/ppermute | solution.py:108
  13.2 3.2 %collective-permute-start.8 = (bf16[16,1024]{1,0:T(8,128)(2,1)S(1)}, bf16[16,1024]{1,0:T(8,128)(2,1)S(1)}, u32[]{:S(2)}, u32[]{:S(2)}) collective-permute-start(bf16[16,1024]{1,0:T(8,128)(2,1)S(1)} %shard_map.147.query_ref._), channel_id=1, source_target_pairs={{0,7},{1,0},{2,5},{3,2},{4,3},{5,4},{6,1},{7,6},{8,15},{9,8},{10,1... | collective-permute-start | bytes 98312 | tf_op jit(solution)/shard_map/ppermute | solution.py:209
  14.8 4.4 %collective-permute-start.11 = (bf16[16,1024]{1,0:T(8,128)(2,1)S(1)}, bf16[16,1024]{1,0:T(8,128)(2,1)S(1)}, u32[]{:S(2)}, u32[]{:S(2)}) collective-permute-start(bf16[16,1024]{1,0:T(8,128)(2,1)S(1)} %shard_map.147.query_ref._), channel_id=1, source_target_pairs={{0,5},{1,0},{2,7},{3,2},{4,1},{5,4},{6,3},{7,6},{8,13},{9,8},{10,1... | collective-permute-start | bytes 98312 | tf_op jit(solution)/shard_map/ppermute | solution.py:209
  14.8 5.0 %collective-permute-start.13 = (bf16[16,1024]{1,0:T(8,128)(2,1)S(1)}, bf16[16,1024]{1,0:T(8,128)(2,1)S(1)}, u32[]{:S(2)}, u32[]{:S(2)}) collective-permute-start(bf16[16,1024]{1,0:T(8,128)(2,1)S(1)} %shard_map.147.query_ref._), channel_id=1, source_target_pairs={{0,3},{1,0},{2,1},{3,2},{4,7},{5,4},{6,5},{7,6},{8,11},{9,8},{10,9... | collective-permute-start | bytes 98312 | tf_op jit(solution)/shard_map/ppermute | solution.py:209
  15.2 8.8 %collective-permute-start.15 = (bf16[512,4096]{1,0:T(8,128)(2,1)S(1)}, bf16[512,4096]{1,0:T(8,128)(2,1)S(1)}, u32[]{:S(2)}, u32[]{:S(2)}) collective-permute-start(bf16[512,4096]{1,0:T(8,128)(2,1)S(1)} %shard_map.154), channel_id=1, source_target_pairs={{0,1},{1,0},{2,3},{3,2},{4,5},{5,4},{6,7},{7,6},{8,9},{9,8},{10,11... | collective-permute-start | bytes 12582920 | tf_op jit(solution)/shard_map/ppermute | solution.py:108
  16.4 6.1 %collective-permute-start.10 = (bf16[16,1152]{1,0:T(8,128)(2,1)S(1)}, bf16[16,1152]{1,0:T(8,128)(2,1)S(1)}, u32[]{:S(2)}, u32[]{:S(2)}) collective-permute-start(bf16[16,1152]{1,0:T(8,128)(2,1)S(1)} %shard_map.150.refs_5_), channel_id=1, source_target_pairs={{0,1},{1,6},{2,3},{3,4},{4,5},{5,2},{6,7},{7,0},{8,9},{9,14},{10,1... | collective-permute-start | bytes 110600 | tf_op jit(solution)/shard_map/ppermute | solution.py:209
  19.2 4.4 %collective-permute-start.12 = (bf16[16,1152]{1,0:T(8,128)(2,1)S(1)}, bf16[16,1152]{1,0:T(8,128)(2,1)S(1)}, u32[]{:S(2)}, u32[]{:S(2)}) collective-permute-start(bf16[16,1152]{1,0:T(8,128)(2,1)S(1)} %shard_map.151.refs_5_), channel_id=1, source_target_pairs={{0,1},{1,4},{2,3},{3,6},{4,5},{5,0},{6,7},{7,2},{8,9},{9,12},{10,1... | collective-permute-start | bytes 110600 | tf_op jit(solution)/shard_map/ppermute | solution.py:209
  19.8 3.9 %collective-permute-start.14 = (bf16[16,1152]{1,0:T(8,128)(2,1)S(1)}, bf16[16,1152]{1,0:T(8,128)(2,1)S(1)}, u32[]{:S(2)}, u32[]{:S(2)}) collective-permute-start(bf16[16,1152]{1,0:T(8,128)(2,1)S(1)} %shard_map.152), channel_id=1, source_target_pairs={{0,1},{1,2},{2,3},{3,0},{4,5},{5,6},{6,7},{7,4},{8,9},{9,10},{10,1... | collective-permute-start | bytes 110600 | tf_op jit(solution)/shard_map/ppermute | solution.py:209
  24.5 2.2 %collective-permute-start.16 = (bf16[16,1024]{1,0:T(8,128)(2,1)S(1)}, bf16[16,1024]{1,0:T(8,128)(2,1)S(1)}, u32[]{:S(2)}, u32[]{:S(2)}) collective-permute-start(bf16[16,1024]{1,0:T(8,128)(2,1)S(1)} %shard_map.155.refs_3_), channel_id=1, source_target_pairs={{0,7},{1,0},{2,5},{3,2},{4,3},{5,4},{6,1},{7,6},{8,15},{9,8},{10,1... | collective-permute-start | bytes 98312 | tf_op jit(solution)/shard_map/ppermute | solution.py:209
  25.1 2.2 %collective-permute-start.17 = (bf16[16,1024]{1,0:T(8,128)(2,1)S(1)}, bf16[16,1024]{1,0:T(8,128)(2,1)S(1)}, u32[]{:S(2)}, u32[]{:S(2)}) collective-permute-start(bf16[16,1024]{1,0:T(8,128)(2,1)S(1)} %shard_map.156.refs_3_), channel_id=1, source_target_pairs={{0,5},{1,0},{2,7},{3,2},{4,1},{5,4},{6,3},{7,6},{8,13},{9,8},{10,1... | collective-permute-start | bytes 98312 | tf_op jit(solution)/shard_map/ppermute | solution.py:209
  26.1 13.0 %copy-start.8 = (s32[64]{0:T(128)S(1)}, s32[64]{0:T(128)}, u32[]{:S(2)}) copy-start(s32[64]{0:T(128)} %param.22) | copy-start | bytes 772
  26.1 1.6 %collective-permute-start.18 = (bf16[16,1024]{1,0:T(8,128)(2,1)S(1)}, bf16[16,1024]{1,0:T(8,128)(2,1)S(1)}, u32[]{:S(2)}, u32[]{:S(2)}) collective-permute-start(bf16[16,1024]{1,0:T(8,128)(2,1)S(1)} %shard_map.157.refs_3_), channel_id=1, source_target_pairs={{0,3},{1,0},{2,1},{3,2},{4,7},{5,4},{6,5},{7,6},{8,11},{9,8},{10,9... | collective-permute-start | bytes 98312 | tf_op jit(solution)/shard_map/ppermute | solution.py:209
  26.5 1.2 %collective-permute-start.19 = (bf16[16,1024]{1,0:T(8,128)(2,1)S(1)}, bf16[16,1024]{1,0:T(8,128)(2,1)S(1)}, u32[]{:S(2)}, u32[]{:S(2)}) collective-permute-start(bf16[16,1024]{1,0:T(8,128)(2,1)S(1)} %shard_map.158), channel_id=1, source_target_pairs={{0,1},{1,0},{2,3},{3,2},{4,5},{5,4},{6,7},{7,6},{8,9},{9,8},{10,11... | collective-permute-start | bytes 98312 | tf_op jit(solution)/shard_map/ppermute | solution.py:108
  27.7 5.8 %collective-permute-start.20 = (bf16[16,1152]{1,0:T(8,128)(2,1)S(1)}, bf16[16,1152]{1,0:T(8,128)(2,1)S(1)}, u32[]{:S(2)}, u32[]{:S(2)}) collective-permute-start(bf16[16,1152]{1,0:T(8,128)(2,1)S(1)} %get-tuple-element.17.refs_3_), channel_id=1, source_target_pairs={{0,1},{1,24},{2,3},{3,26},{4,5},{5,28},{6,7},{7,30},{8,9},{9,16},{... | collective-permute-start | bytes 110600 | tf_op jit(solution)/shard_map/ppermute | solution.py:209
  29.7 3.8 %collective-permute-start.21 = (bf16[16,1152]{1,0:T(8,128)(2,1)S(1)}, bf16[16,1152]{1,0:T(8,128)(2,1)S(1)}, u32[]{:S(2)}, u32[]{:S(2)}) collective-permute-start(bf16[16,1152]{1,0:T(8,128)(2,1)S(1)} %get-tuple-element.17.refs_3_), channel_id=1, source_target_pairs={{0,1},{1,16},{2,3},{3,18},{4,5},{5,20},{6,7},{7,22},{8,9},{9,24},{... | collective-permute-start | bytes 110600 | tf_op jit(solution)/shard_map/ppermute | solution.py:209
  30.3 3.8 %collective-permute-start.22 = (bf16[16,1152]{1,0:T(8,128)(2,1)S(1)}, bf16[16,1152]{1,0:T(8,128)(2,1)S(1)}, u32[]{:S(2)}, u32[]{:S(2)}) collective-permute-start(bf16[16,1152]{1,0:T(8,128)(2,1)S(1)} %get-tuple-element.17.refs_3_), channel_id=1, source_target_pairs={{0,1},{1,8},{2,3},{3,10},{4,5},{5,12},{6,7},{7,14},{8,9},{9,0},{10... | collective-permute-start | bytes 110600 | tf_op jit(solution)/shard_map/ppermute | solution.py:209
  31.4 2.7 %collective-permute-start.23 = (bf16[16,1152]{1,0:T(8,128)(2,1)S(1)}, bf16[16,1152]{1,0:T(8,128)(2,1)S(1)}, u32[]{:S(2)}, u32[]{:S(2)}) collective-permute-start(bf16[16,1152]{1,0:T(8,128)(2,1)S(1)} %get-tuple-element.17.refs_3_), channel_id=1, source_target_pairs={{0,1},{1,0},{2,3},{3,2},{4,5},{5,4},{6,7},{7,6},{8,9},{9,8},{10,11... | collective-permute-start | bytes 110600 | tf_op jit(solution)/shard_map/ppermute | solution.py:108
  31.4 1.4 %collective-permute-start.24 = (f32[16,512]{1,0:T(8,128)S(1)}, f32[16,512]{1,0:T(8,128)S(1)}, u32[]{:S(2)}, u32[]{:S(2)}) collective-permute-start(f32[16,512]{1,0:T(8,128)S(1)} %get-tuple-element.18), channel_id=1, source_target_pairs={{0,1},{1,0},{2,3},{3,2},{4,5},{5,4},{6,7},{7,6},{8,9},{9,8},{10,11... | collective-permute-start | bytes 98312 | tf_op jit(solution)/shard_map/ppermute | solution.py:108
  34.4 2.1 %collective-permute-start.25 = (f32[48,128]{1,0:T(8,128)S(1)}, f32[48,128]{1,0:T(8,128)S(1)}, u32[]{:S(2)}, u32[]{:S(2)}) collective-permute-start(f32[48,128]{1,0:T(8,128)S(1)} %get-tuple-element.19), channel_id=1, source_target_pairs={{0,7},{1,0},{2,5},{3,2},{4,3},{5,4},{6,1},{7,6},{8,15},{9,8},{10,1... | collective-permute-start | bytes 73736 | tf_op jit(solution)/shard_map/ppermute | solution.py:209
  34.8 2.7 %collective-permute-start.26 = (f32[48,128]{1,0:T(8,128)S(1)}, f32[48,128]{1,0:T(8,128)S(1)}, u32[]{:S(2)}, u32[]{:S(2)}) collective-permute-start(f32[48,128]{1,0:T(8,128)S(1)} %get-tuple-element.19), channel_id=1, source_target_pairs={{0,5},{1,0},{2,7},{3,2},{4,1},{5,4},{6,3},{7,6},{8,13},{9,8},{10,1... | collective-permute-start | bytes 73736 | tf_op jit(solution)/shard_map/ppermute | solution.py:209
  35.9 1.8 %collective-permute-start.27 = (f32[48,128]{1,0:T(8,128)S(1)}, f32[48,128]{1,0:T(8,128)S(1)}, u32[]{:S(2)}, u32[]{:S(2)}) collective-permute-start(f32[48,128]{1,0:T(8,128)S(1)} %get-tuple-element.19), channel_id=1, source_target_pairs={{0,3},{1,0},{2,1},{3,2},{4,7},{5,4},{6,5},{7,6},{8,11},{9,8},{10,9... | collective-permute-start | bytes 73736 | tf_op jit(solution)/shard_map/ppermute | solution.py:209
  35.9 1.8 %collective-permute-start.28 = (f32[48,128]{1,0:T(8,128)S(1)}, f32[48,128]{1,0:T(8,128)S(1)}, u32[]{:S(2)}, u32[]{:S(2)}) collective-permute-start(f32[48,128]{1,0:T(8,128)S(1)} %get-tuple-element.19), channel_id=1, source_target_pairs={{0,1},{1,0},{2,3},{3,2},{4,5},{5,4},{6,7},{7,6},{8,9},{9,8},{10,11... | collective-permute-start | bytes 73736 | tf_op jit(solution)/shard_map/ppermute | solution.py:108
  36.4 2.8 %collective-permute-start.30 = (bf16[48,512]{1,0:T(8,128)(2,1)S(1)}, bf16[48,512]{1,0:T(8,128)(2,1)S(1)}, u32[]{:S(2)}, u32[]{:S(2)}) collective-permute-start(bf16[48,512]{1,0:T(8,128)(2,1)S(1)} %get-tuple-element.21), channel_id=1, source_target_pairs={{0,1},{1,0},{2,3},{3,2},{4,5},{5,4},{6,7},{7,6},{8,9},{9,8},{10,11... | collective-permute-start | bytes 147464 | tf_op jit(solution)/shard_map/ppermute | solution.py:108
  37.7 2.3 %collective-permute-start.29 = (f32[48,128]{1,0:T(8,128)S(1)}, f32[48,128]{1,0:T(8,128)S(1)}, u32[]{:S(2)}, u32[]{:S(2)}) collective-permute-start(f32[48,128]{1,0:T(8,128)S(1)} %shard_map.161.refs_0_), channel_id=1, source_target_pairs={{0,1},{1,0},{2,3},{3,2},{4,5},{5,4},{6,7},{7,6},{8,9},{9,8},{10,11... | collective-permute-start | bytes 73736 | tf_op jit(solution)/shard_map/ppermute | solution.py:108

commit v8 on v7

--- a/solution.py
+++ b/solution.py
@@ -127,16 +127,6 @@
 
 def open_window(out_ref):
     out_ref[...] = jnp.zeros_like(out_ref)
-
-
-def prepare_inputs(window_ref, hidden_ref, gain_ref, message_ref):
-    del window_ref
-    inputs = hidden_ref[...].astype(jnp.float32)
-    width = inputs.shape[1]
-    message_ref[:, :width] = (inputs * gain_ref[...]).astype(jnp.bfloat16)
-    message_ref[:, width:] = pack_statistics(
-        [jnp.sum(inputs * inputs, axis=1, keepdims=True)], core_number()
-    )
 
 
 def positions_and_ranges(
@@ -166,12 +156,12 @@
 LOG2_E = 1.4426950408889634
 
 
-def pack_statistics(values, first=0):
+def pack_statistics(values):
     rows = values[0].shape[0]
     lane = lax.broadcasted_iota(jnp.int32, (rows, 128), 1)
     rest = jnp.zeros((rows, 128), jnp.float32)
     for place, value in enumerate(values):
-        rest = jnp.where(lane == first + place, value, rest)
+        rest = jnp.where(lane == place, value, rest)
     out = rest.astype(jnp.bfloat16).astype(jnp.float32)
     for part in (1, 2):
         rest = rest - rest.astype(jnp.bfloat16).astype(jnp.float32)
@@ -179,10 +169,9 @@
     return out.astype(jnp.bfloat16)
 
 
-def read_statistic(block, first, count=1):
+def read_statistic(block, first):
     lane = lax.broadcasted_iota(jnp.int32, block.shape, 1)
-    place = (lane & 31) - first
-    mine = (place >= 0) & (place < count) & (lane < 96)
+    mine = ((lane & 31) == first) & (lane < 96)
     return jnp.sum(jnp.where(mine, block.astype(jnp.float32), 0.0), axis=1, keepdims=True)
 
 
@@ -214,24 +203,21 @@
     out_ref[1] = value_ref[...]
 
 
-def join_cores(own_ref, other_ref, pair_ref):
-    core = core_number()
-    width = own_ref.shape[1] - 128
-    refs = (own_ref, other_ref)
-    pair_ref[:, 2 * width :] = own_ref[:, width:] + other_ref[:, width:]
+def prepare_pair(_, own_ref, other_ref, own_gain_ref, other_gain_ref, pair_ref):
+    width = own_ref.shape[1]
+    squares = 0.0
+    scaled = []
+    for ref, factor_ref in ((own_ref, own_gain_ref), (other_ref, other_gain_ref)):
+        inputs = ref[...].astype(jnp.float32)
+        squares = squares + jnp.sum(inputs * inputs, axis=1, keepdims=True)
+        scaled.append((inputs * factor_ref[...]).astype(jnp.bfloat16))
+    pair_ref[:, 2 * width :] = pack_statistics([squares])
     for first in range(2):
 
-        @pl.when(core == first)
+        @pl.when(core_number() == first)
         def _():
-            pair_ref[:, :width] = refs[first][:, :width]
-            pair_ref[:, width : 2 * width] = refs[1 - first][:, :width]
-
-
-def join_blocks(*refs):
-    out_ref = refs[-1]
-    count = out_ref.shape[0]
-    for i in range(count):
-        out_ref[count - 1 - i] = refs[i][...]
+            pair_ref[:, :width] = scaled[first]
+            pair_ref[:, width : 2 * width] = scaled[1 - first]
 
 
 def project_pair(pair_ref, offset, weight_ref):
@@ -247,20 +233,43 @@
     total_ref[...] = project_pair(pair_ref, 0, weight_ref)
 
 
+def project_early(third_ref, second_ref, own_ref, weight_ref, *refs, core):
+    total_ref = refs[-1]
+
+    @pl.when(core_number() == core)
+    def _():
+        total_ref[...] = (
+            own_ref[...]
+            + project_pair(third_ref, 3, weight_ref)
+            + project_pair(second_ref, 2, weight_ref)
+        )
+
+
 def make_queries(
-    pair_ref, blocks_ref, total_ref, weight_ref, gain_ref, rope_ref, query_ref, *, core, model_width
+    third_ref,
+    second_ref,
+    first_ref,
+    pair_ref,
+    total_ref,
+    weight_ref,
+    gain_ref,
+    rope_ref,
+    *refs,
+    core,
+    model_width,
 ):
+    query_ref = refs[-1]
     width = total_ref.shape[1]
     head_dim = gain_ref.shape[1]
 
     @pl.when(core_number() == core)
     def _():
-        projected = total_ref[...]
-        squares = pair_ref[:, 2 * width :].astype(jnp.float32)
-        for i in range(blocks_ref.shape[0]):
-            projected = projected + project_pair(blocks_ref.at[i], i + 1, weight_ref)
-            squares = squares + blocks_ref[i, :, 2 * width :].astype(jnp.float32)
-        squares = read_statistic(squares, 0, 2)
+        projected = total_ref[...] + project_pair(first_ref, 1, weight_ref)
+        squares = sum(
+            ref[:, 2 * width :].astype(jnp.float32)
+            for ref in (pair_ref, first_ref, second_ref, third_ref)
+        )
+        squares = read_statistic(squares, 0)
         projected = projected * lax.rsqrt(squares / model_width + EPSILON)
         cosine = rope_ref[:, :head_dim]
         sine = rope_ref[:, head_dim:]
@@ -356,7 +365,7 @@
         out_ref[:, 2 * width :] = pack_statistics(stats)
 
 
-def attend_own(query_ref, key_ref, value_ref, other_ref, range_ref, out_ref, stats_ref):
+def attend_own(query_ref, key_ref, value_ref, other_ref, range_ref, _, out_ref, stats_ref):
     @pl.when(core_number() == 0)
     def _():
         width = query_ref.shape[1] // 2
@@ -613,11 +622,16 @@
         compiler_params=pltpu.CompilerParams(vmem_limit_bytes=1 << 20),
         cost_estimate=pl.CostEstimate(flops=1 << 34, bytes_accessed=0, transcendentals=0),
     )()
-    message = in_vmem(
-        prepare_inputs, shaped((stmts, width + 128), bf16), window, hidden_in, attn_gain[None]
-    )
+    attn_gain = attn_gain[None]
+    other_hidden_in = flip(hidden_in, "pack", 1)
     pair = in_vmem(
-        join_cores, shaped((stmts, 2 * width + 128), bf16), message, flip(message, "pack", 1)
+        prepare_pair,
+        shaped((stmts, 2 * width + 128), bf16),
+        window,
+        hidden_in,
+        other_hidden_in,
+        attn_gain,
+        flip(attn_gain, "pack", 1),
     )
     received = [send_across(pair, "pack", k, 0) for k in others]
     own_projected = in_vmem(
@@ -626,49 +640,54 @@
     rope, ranges = in_vmem(
         positions_and_ranges,
         (shaped((stmts, 2 * head_dim), f32), shaped((stmts, 256), f32)),
-        message,
+        pair,
         frequency,
         lengths,
         pack_order,
     )
-    other_hidden_in = flip(hidden_in, "pack", 1)
     other_gain = flip(final_gain, "pack", 1)
-    blocks = in_vmem(
-        join_blocks,
-        shaped((chips - 1,) + pair.shape, bf16),
-        *received[::-1],
-        other_hidden_in,
-        other_gain,
-        own_projected,
-        rope,
-    )
-    flipped_blocks = flip(blocks, "pack", 1)
-
-    def queries_on(core, blocks, flops):
+
+    def project_on(core, parts, *after):
+        first, second, third = parts
+        early = in_vmem(
+            lambda *refs: project_early(*refs, core=core),
+            shaped((stmts, width), f32),
+            third,
+            second,
+            own_projected,
+            w_query,
+            *after[:1],
+            limit=16,
+            flops=1 << 30,
+        )
         return in_vmem(
             lambda *refs: make_queries(*refs, core=core, model_width=model_width),
             shaped((stmts, width), bf16),
+            third,
+            second,
+            first,
             pair,
-            blocks,
-            own_projected,
+            early,
             w_query,
             query_gain,
             rope,
+            *after[1:],
             limit=16,
-            flops=flops,
-        )
-
-    late_queries = queries_on(1, blocks, 1 << 27)
+            flops=1 << 36 if core == 0 else 1 << 27,
+        )
+
+    late_queries = project_on(1, received, rope)
+    handed = [flip(part, "pack", 1) for part in received]
     held = in_vmem(
         copy_tokens,
         shaped((2,) + cached_keys.shape, bf16),
-        late_queries,
+        handed[0],
         cached_keys,
         cached_values,
     )
     other_held = flip(held, "pack", 1)
     second_queries = flip(late_queries, "pack", 1)
-    first_queries = queries_on(0, flipped_blocks, 1 << 36)
+    first_queries = project_on(0, handed)
     queries = in_vmem(
         join_queries, shaped((stmts, 2 * width), bf16), first_queries, second_queries
     )
@@ -685,6 +704,7 @@
         cached_values,
         other_held,
         ranges,
+        other_gain,
         flops=1 << 27,
     )
     partials = []

time: 41.1 us -> 42 us (1.022)
  waiting for transfers between devices: 11.1 us -> 11.7 us
    ppermute x13 -> x15, waiting for transfers between devices: 3.11 us -> 3.63 us  [flip(): return lax.ppermute(array, axis, [(i, i ^ offset) for i in range(size)])]
    ppermute x13 -> x15, starting transfers between devices: 6.52 us -> 6.71 us  [flip(): return lax.ppermute(array, axis, [(i, i ^ offset) for i in range(size)])]
  transfers between devices with their start and end apart: 31 -> 33, of which waited for: 16 -> 15; matrix products, arithmetic and copies ran while one was open for 0% -> 0% of each run, Pallas kernels for 9% -> 9%
where the time goes in v8:
time: 42 us; the launch traced here: 41.9 us
  starting transfers between devices  23.4 us (56%)
  waiting for transfers between devices  11.7 us (28%)
  Pallas kernels  5.47 us (13%)
  between operations  0.84 us (2%)
  local copies, waits for them, and re-layouts  0.43 us (1%)
    ppermute x18, starting transfers between devices, send_across(): return lax.ppermute(array, ('dp', 'pack'), pairs)  16.7 us
    ppermute x18, waiting for transfers between devices, send_across(): return lax.ppermute(array, ('dp', 'pack'), pairs)  8.09 us
    ppermute x15, starting transfers between devices, flip(): return lax.ppermute(array, axis, [(i, i ^ offset) for i in range(size)])  6.71 us
    pallas_call x23, Pallas kernels, in_vmem(): pl.pallas_call(body, out_shape=outputs, in_specs=[whole] * len(operands),...  4.45 us
    ppermute x15, waiting for transfers between devices, flip(): return lax.ppermute(array, axis, [(i, i ^ offset) for i in range(size)])  3.63 us
    pallas_call x1, Pallas kernels, core_roles(): pl.pallas_call(lambda *refs: losses_and_gradient(*refs, model_width=model...  1.02 us
  transfers between devices with their start and end apart: 33, of which 15 were waited for; matrix products, arithmetic and copies ran while one was open for 0% of the time, Pallas kernels for 9%

profile of v8, /device:TPU:0, one launch (start us, length us, event | category | flops | bytes accessed | tf_op | source)
XLA Modules:
  0.0 41.9 jit_solution(8789701818072712210)
XLA Ops:
  0.6 0.5 %collective-permute-start = (bf16[16,512]{1,0:T(8,128)(2,1)}, bf16[16,512]{1,0:T(8,128)(2,1)S(1)}, u32[]{:S(2)}, u32[]{:S(2)}) collective-permute-start(bf16[16,512]{1,0:T(8,128)(2,1)} %own_ref.3), channel_id=1, source_target_pairs={{0,1},{1,0},{2,3},{3,2},{4,5},{5,4},{6,7},{7,6},{8,9},{9,8},{10,11... | collective-permute-start | bytes 49160 | tf_op jit(solution)/shard_map/ppermute | solution.py:108
  1.3 1.3 %collective-permute-done.1.other_gain_ref = f32[1,512]{1,0:T(1,128)S(1)} collective-permute-done((f32[1,512]{1,0:T(1,128)}, f32[1,512]{1,0:T(1,128)S(1)}, u32[]{:S(2)}, u32[]{:S(2)}) %collective-permute-start.1) | collective-permute-done | bytes 2080 | tf_op jit(solution)/shard_map/ppermute | solution.py:108
  2.8 4.7 %collective-permute-start.2 = (bf16[16,1152]{1,0:T(8,128)(2,1)S(1)}, bf16[16,1152]{1,0:T(8,128)(2,1)S(1)}, u32[]{:S(2)}, u32[]{:S(2)}) collective-permute-start(bf16[16,1152]{1,0:T(8,128)(2,1)S(1)} %shard_map.140.pair_ref.message_ref.refs_3_), channel_id=1, source_target_pairs={{0,7},{1,0},{2,5},{3,2},{4,3},{5,4},{6,1},{7,6},{8,15},{9,8},{10,1... | collective-permute-start | bytes 110600 | tf_op jit(solution)/shard_map/ppermute | solution.py:198
  7.7 0.2 shard_map.141.refs_2_
  8.0 1.2 %collective-permute-done.2.refs_0_ = bf16[16,1152]{1,0:T(8,128)(2,1)S(1)} collective-permute-done((bf16[16,1152]{1,0:T(8,128)(2,1)S(1)}, bf16[16,1152]{1,0:T(8,128)(2,1)S(1)}, u32[]{:S(2)}, u32[]{:S(2)}) %collective-permute-start.2) | collective-permute-done | bytes 36896 | tf_op jit(solution)/shard_map/ppermute | solution.py:198
  9.1 0.3 collective-permute-start.3
  9.5 0.4 collective-permute-start.5
  9.9 1.5 %collective-permute-start.7 = (bf16[16,1152]{1,0:T(8,128)(2,1)S(1)}, bf16[16,1152]{1,0:T(8,128)(2,1)S(1)}, u32[]{:S(2)}, u32[]{:S(2)}) collective-permute-start(bf16[16,1152]{1,0:T(8,128)(2,1)S(1)} %collective-permute-done.6.refs_2_), channel_id=1, source_target_pairs={{0,1},{1,0},{2,3},{3,2},{4,5},{5,4},{6,7},{7,6},{8,9},{9,8},{10,11... | collective-permute-start | bytes 110600 | tf_op jit(solution)/shard_map/ppermute | solution.py:108
  11.4 0.9 %collective-permute-start.8 = (bf16[16,512]{1,0:T(8,128)(2,1)S(1)}, bf16[16,512]{1,0:T(8,128)(2,1)S(1)}, u32[]{:S(2)}, u32[]{:S(2)}) collective-permute-start(bf16[16,512]{1,0:T(8,128)(2,1)S(1)} %shard_map.146), channel_id=1, source_target_pairs={{0,1},{1,0},{2,3},{3,2},{4,5},{5,4},{6,7},{7,6},{8,9},{9,8},{10,11... | collective-permute-start | bytes 49160 | tf_op jit(solution)/shard_map/ppermute | solution.py:108
  12.3 0.2 copy-done.2
  12.5 0.2 copy-done.3
  12.9 0.4 shard_map.142.refs_4_
  13.3 0.4 %shard_map.144.first_ref = bf16[16,512]{1,0:T(8,128)(2,1)S(1)} custom-call(bf16[16,1152]{1,0:T(8,128)(2,1)S(1)} %collective-permute-done.3.refs_0_, bf16[16,1152]{1,0:T(8,128)(2,1)S(1)} %collective-permute-done.5.refs_1_, bf16[16,1152]{1,0:T(8,128)(2,1)S(1)} %collective-permute-done.7.refs_2_._, ...), custom_call_target="tpu_custom_call" | custom-call | flops 68719476736 | bytes 4391424 | tf_op jit(solution)/shard_map/pallas_call | solution.py:114
  13.7 1.6 %collective-permute-start.9 = (bf16[16,1024]{1,0:T(8,128)(2,1)S(1)}, bf16[16,1024]{1,0:T(8,128)(2,1)S(1)}, u32[]{:S(2)}, u32[]{:S(2)}) collective-permute-start(bf16[16,1024]{1,0:T(8,128)(2,1)S(1)} %shard_map.147.query_ref._), channel_id=1, source_target_pairs={{0,7},{1,0},{2,5},{3,2},{4,3},{5,4},{6,1},{7,6},{8,15},{9,8},{10,1... | collective-permute-start | bytes 98312 | tf_op jit(solution)/shard_map/ppermute | solution.py:198
  15.4 0.4 collective-permute-start.13
  15.7 0.3 shard_map.154
  16.0 0.5 %collective-permute-done.11._.other_gain_ref = f32[1,512]{1,0:T(1,128)S(1)} collective-permute-done((f32[1,512]{1,0:T(1,128)S(1)}, f32[1,512]{1,0:T(1,128)S(1)}, u32[]{:S(2)}, u32[]{:S(2)}) %collective-permute-start.11) | collective-permute-done | bytes 2080 | tf_op jit(solution)/shard_map/ppermute | solution.py:108
  16.7 0.5 %shard_map.149 = (f32[2,64,128]{2,1,0:T(8,128)S(1)}, f32[2,64,256]{2,1,0:T(8,128)S(1)}) custom-call(bf16[16,1024]{1,0:T(8,128)(2,1)S(1)} %shard_map.147.query_ref._, bf16[320,1024]{1,0:T(8,128)(2,1)S(1)} %copy-done.2, bf16[320,1024]{1,0:T(8,128)(2,1)S(1)} %copy-done.3, bf16[2,320,1024]{2,1,0:T(8,128)(2,1)S(1)} %collective-permute-done.10.other_ref.refs_3_, ...), custom_call_target="tpu_custom_call" | custom-call | flops 134217728 | bytes 2672640 | tf_op jit(solution)/shard_map/pallas_call | solution.py:114
  17.2 2.0 %collective-permute-start.12 = (bf16[16,1152]{1,0:T(8,128)(2,1)S(1)}, bf16[16,1152]{1,0:T(8,128)(2,1)S(1)}, u32[]{:S(2)}, u32[]{:S(2)}) collective-permute-start(bf16[16,1152]{1,0:T(8,128)(2,1)S(1)} %shard_map.150.refs_5_), channel_id=1, source_target_pairs={{0,1},{1,6},{2,3},{3,4},{4,5},{5,2},{6,7},{7,0},{8,9},{9,14},{10,1... | collective-permute-start | bytes 110600 | tf_op jit(solution)/shard_map/ppermute | solution.py:198
  19.2 1.5 %collective-permute-start.14 = (bf16[16,1152]{1,0:T(8,128)(2,1)S(1)}, bf16[16,1152]{1,0:T(8,128)(2,1)S(1)}, u32[]{:S(2)}, u32[]{:S(2)}) collective-permute-start(bf16[16,1152]{1,0:T(8,128)(2,1)S(1)} %shard_map.151.refs_5_), channel_id=1, source_target_pairs={{0,1},{1,4},{2,3},{3,6},{4,5},{5,0},{6,7},{7,2},{8,9},{9,12},{10,1... | collective-permute-start | bytes 110600 | tf_op jit(solution)/shard_map/ppermute | solution.py:198
  20.7 0.6 %collective-permute-start.16 = (bf16[16,1152]{1,0:T(8,128)(2,1)S(1)}, bf16[16,1152]{1,0:T(8,128)(2,1)S(1)}, u32[]{:S(2)}, u32[]{:S(2)}) collective-permute-start(bf16[16,1152]{1,0:T(8,128)(2,1)S(1)} %shard_map.152), channel_id=1, source_target_pairs={{0,1},{1,2},{2,3},{3,0},{4,5},{5,6},{6,7},{7,4},{8,9},{9,10},{10,1... | collective-permute-start | bytes 110600 | tf_op jit(solution)/shard_map/ppermute | solution.py:198
  21.3 2.3 %collective-permute-done.12.third_ref = bf16[16,1152]{1,0:T(8,128)(2,1)S(1)} collective-permute-done((bf16[16,1152]{1,0:T(8,128)(2,1)S(1)}, bf16[16,1152]{1,0:T(8,128)(2,1)S(1)}, u32[]{:S(2)}, u32[]{:S(2)}) %collective-permute-start.12) | collective-permute-done | bytes 36896 | tf_op jit(solution)/shard_map/ppermute | solution.py:198
  23.5 0.4 %collective-permute-done.14.second_ref = bf16[16,1152]{1,0:T(8,128)(2,1)S(1)} collective-permute-done((bf16[16,1152]{1,0:T(8,128)(2,1)S(1)}, bf16[16,1152]{1,0:T(8,128)(2,1)S(1)}, u32[]{:S(2)}, u32[]{:S(2)}) %collective-permute-start.14) | collective-permute-done | bytes 36896 | tf_op jit(solution)/shard_map/ppermute | solution.py:198
  24.0 0.3 collective-permute-done.16.first_ref
  24.2 0.3 shard_map.153.refs_0_
  24.5 0.4 shard_map.155.refs_3_
  24.9 0.7 %collective-permute-start.18 = (bf16[16,1024]{1,0:T(8,128)(2,1)S(1)}, bf16[16,1024]{1,0:T(8,128)(2,1)S(1)}, u32[]{:S(2)}, u32[]{:S(2)}) collective-permute-start(bf16[16,1024]{1,0:T(8,128)(2,1)S(1)} %shard_map.155.refs_3_), channel_id=1, source_target_pairs={{0,7},{1,0},{2,5},{3,2},{4,3},{5,4},{6,1},{7,6},{8,15},{9,8},{10,1... | collective-permute-start | bytes 98312 | tf_op jit(solution)/shard_map/ppermute | solution.py:198
  25.6 0.4 shard_map.156.refs_3_
  26.0 1.0 %collective-permute-start.19 = (bf16[16,1024]{1,0:T(8,128)(2,1)S(1)}, bf16[16,1024]{1,0:T(8,128)(2,1)S(1)}, u32[]{:S(2)}, u32[]{:S(2)}) collective-permute-start(bf16[16,1024]{1,0:T(8,128)(2,1)S(1)} %shard_map.156.refs_3_), channel_id=1, source_target_pairs={{0,5},{1,0},{2,7},{3,2},{4,1},{5,4},{6,3},{7,6},{8,13},{9,8},{10,1... | collective-permute-start | bytes 98312 | tf_op jit(solution)/shard_map/ppermute | solution.py:198
  27.0 0.4 shard_map.157.refs_3_
  27.4 0.4 shard_map.158
  27.9 0.7 %collective-permute-done.19.second_ref = bf16[16,1024]{1,0:T(8,128)(2,1)S(1)} collective-permute-done((bf16[16,1024]{1,0:T(8,128)(2,1)S(1)}, bf16[16,1024]{1,0:T(8,128)(2,1)S(1)}, u32[]{:S(2)}, u32[]{:S(2)}) %collective-permute-start.19) | collective-permute-done | bytes 32800 | tf_op jit(solution)/shard_map/ppermute | solution.py:198
  28.6 0.4 collective-permute-done.20.first_ref
  29.0 1.2 %collective-permute-start.22 = (bf16[16,1152]{1,0:T(8,128)(2,1)S(1)}, bf16[16,1152]{1,0:T(8,128)(2,1)S(1)}, u32[]{:S(2)}, u32[]{:S(2)}) collective-permute-start(bf16[16,1152]{1,0:T(8,128)(2,1)S(1)} %get-tuple-element.17.refs_3_), channel_id=1, source_target_pairs={{0,1},{1,24},{2,3},{3,26},{4,5},{5,28},{6,7},{7,30},{8,9},{9,16},{... | collective-permute-start | bytes 110600 | tf_op jit(solution)/shard_map/ppermute | solution.py:198
  30.2 1.4 %collective-permute-start.23 = (bf16[16,1152]{1,0:T(8,128)(2,1)S(1)}, bf16[16,1152]{1,0:T(8,128)(2,1)S(1)}, u32[]{:S(2)}, u32[]{:S(2)}) collective-permute-start(bf16[16,1152]{1,0:T(8,128)(2,1)S(1)} %get-tuple-element.17.refs_3_), channel_id=1, source_target_pairs={{0,1},{1,16},{2,3},{3,18},{4,5},{5,20},{6,7},{7,22},{8,9},{9,24},{... | collective-permute-start | bytes 110600 | tf_op jit(solution)/shard_map/ppermute | solution.py:198
  31.6 0.3 collective-permute-start.24
  31.9 0.4 collective-permute-start.25
  32.4 1.1 %collective-permute-done.26._.refs_6_ = f32[16,512]{1,0:T(8,128)S(1)} collective-permute-done((f32[16,512]{1,0:T(8,128)S(1)}, f32[16,512]{1,0:T(8,128)S(1)}, u32[]{:S(2)}, u32[]{:S(2)}) %collective-permute-start.26) | collective-permute-done | bytes 32800 | tf_op jit(solution)/shard_map/ppermute | solution.py:108
  33.5 0.6 %collective-permute-done.22.third_ref = bf16[16,1152]{1,0:T(8,128)(2,1)S(1)} collective-permute-done((bf16[16,1152]{1,0:T(8,128)(2,1)S(1)}, bf16[16,1152]{1,0:T(8,128)(2,1)S(1)}, u32[]{:S(2)}, u32[]{:S(2)}) %collective-permute-start.22) | collective-permute-done | bytes 36896 | tf_op jit(solution)/shard_map/ppermute | solution.py:198
  34.0 1.0 %collective-permute-done.24.first_ref = bf16[16,1152]{1,0:T(8,128)(2,1)S(1)} collective-permute-done((bf16[16,1152]{1,0:T(8,128)(2,1)S(1)}, bf16[16,1152]{1,0:T(8,128)(2,1)S(1)}, u32[]{:S(2)}, u32[]{:S(2)}) %collective-permute-start.24) | collective-permute-done | bytes 36896 | tf_op jit(solution)/shard_map/ppermute | solution.py:198
  35.0 0.2 shard_map.160
  35.2 1.4 %collective-permute-start.28 = (f32[48,128]{1,0:T(8,128)S(1)}, f32[48,128]{1,0:T(8,128)S(1)}, u32[]{:S(2)}, u32[]{:S(2)}) collective-permute-start(f32[48,128]{1,0:T(8,128)S(1)} %get-tuple-element.19), channel_id=1, source_target_pairs={{0,5},{1,0},{2,7},{3,2},{4,1},{5,4},{6,3},{7,6},{8,13},{9,8},{10,1... | collective-permute-start | bytes 73736 | tf_op jit(solution)/shard_map/ppermute | solution.py:198
  36.6 0.5 %collective-permute-start.30 = (f32[48,128]{1,0:T(8,128)S(1)}, f32[48,128]{1,0:T(8,128)S(1)}, u32[]{:S(2)}, u32[]{:S(2)}) collective-permute-start(f32[48,128]{1,0:T(8,128)S(1)} %get-tuple-element.19), channel_id=1, source_target_pairs={{0,1},{1,0},{2,3},{3,2},{4,5},{5,4},{6,7},{7,6},{8,9},{9,8},{10,11... | collective-permute-start | bytes 73736 | tf_op jit(solution)/shard_map/ppermute | solution.py:108
  37.1 1.0 %collective-permute-done.28.second_ref = f32[48,128]{1,0:T(8,128)S(1)} collective-permute-done((f32[48,128]{1,0:T(8,128)S(1)}, f32[48,128]{1,0:T(8,128)S(1)}, u32[]{:S(2)}, u32[]{:S(2)}) %collective-permute-start.28) | collective-permute-done | bytes 24608 | tf_op jit(solution)/shard_map/ppermute | solution.py:198
  38.1 0.2 collective-permute-done.29.first_ref
  38.4 1.6 %collective-permute-start.31 = (f32[48,128]{1,0:T(8,128)S(1)}, f32[48,128]{1,0:T(8,128)S(1)}, u32[]{:S(2)}, u32[]{:S(2)}) collective-permute-start(f32[48,128]{1,0:T(8,128)S(1)} %shard_map.161.refs_0_), channel_id=1, source_target_pairs={{0,1},{1,0},{2,3},{3,2},{4,5},{5,4},{6,7},{7,6},{8,9},{9,8},{10,11... | collective-permute-start | bytes 73736 | tf_op jit(solution)/shard_map/ppermute | solution.py:108
  40.1 0.7 %collective-permute-done.31.refs_1_ = f32[48,128]{1,0:T(8,128)S(1)} collective-permute-done((f32[48,128]{1,0:T(8,128)S(1)}, f32[48,128]{1,0:T(8,128)S(1)}, u32[]{:S(2)}, u32[]{:S(2)}) %collective-permute-start.31) | collective-permute-done | bytes 24608 | tf_op jit(solution)/shard_map/ppermute | solution.py:108
  40.8 1.0 %shard_map.163 = (bf16[16,512]{1,0:T(8,128)(2,1)}, f32[2]{0:T(128)}, bf16[16,512]{1,0:T(8,128)(2,1)}) custom-call(f32[48,128]{1,0:T(8,128)S(1)} %shard_map.161.refs_0_, f32[48,128]{1,0:T(8,128)S(1)} %collective-permute-done.31.refs_1_, bf16[64,512]{1,0:T(8,128)(2,1)S(1)} %get-tuple-element.20.refs_2_, bf16[16,1152]{1,0:T(8,128)(2,1)S(1)} %get-tuple-element.17.refs_3_, ...), custom_call_target="tpu_custom_call" | custom-call | tf_op jit(solution)/shard_map/pallas_call | solution.py:787
  (67 shorter events, 1.4 us)
Async XLA Ops:
  0.6 2.0 %collective-permute-start = (bf16[16,512]{1,0:T(8,128)(2,1)}, bf16[16,512]{1,0:T(8,128)(2,1)S(1)}, u32[]{:S(2)}, u32[]{:S(2)}) collective-permute-start(bf16[16,512]{1,0:T(8,128)(2,1)} %own_ref.3), channel_id=1, source_target_pairs={{0,1},{1,0},{2,3},{3,2},{4,5},{5,4},{6,7},{7,6},{8,9},{9,8},{10,11... | collective-permute-start | bytes 49160 | tf_op jit(solution)/shard_map/ppermute | solution.py:108
  1.1 1.5 %copy-start.4 = (bf16[16,512]{1,0:T(8,128)(2,1)S(1)}, bf16[16,512]{1,0:T(8,128)(2,1)}, u32[]{:S(2)}) copy-start(bf16[16,512]{1,0:T(8,128)(2,1)} %own_ref.3) | copy-start | bytes 49156
  1.2 1.5 %copy-start.6 = (f32[512]{0:T(512)S(1)}, f32[512]{0:T(512)}, u32[]{:S(2)}) copy-start(f32[512]{0:T(512)} %param.13) | copy-start | bytes 6148
  1.2 6.4 %copy-start.7 = (s32[1,16]{1,0:T(1,128)S(1)}, s32[1,16]{1,0:T(1,128)}, u32[]{:S(2)}) copy-start(s32[1,16]{1,0:T(1,128)} %lengths_ref.1) | copy-start | bytes 196
  1.2 6.4 %copy-start.8 = (s32[1,16]{1,0:T(1,128)S(1)}, s32[1,16]{1,0:T(1,128)}, u32[]{:S(2)}) copy-start(s32[1,16]{1,0:T(1,128)} %order_ref.1) | copy-start | bytes 196
  1.2 6.4 %copy-start.11 = (f32[1,128]{1,0:T(1,128)S(1)}, f32[1,128]{1,0:T(1,128)}, u32[]{:S(2)}) copy-start(f32[1,128]{1,0:T(1,128)} %constant.2.clone.frequency_ref) | copy-start | bytes 1540
  1.2 6.5 %copy-start.1 = (bf16[4096,512]{1,0:T(8,128)(2,1)S(1)}, bf16[4096,512]{1,0:T(8,128)(2,1)}, u32[]{:S(2)}) copy-start(bf16[4096,512]{1,0:T(8,128)(2,1)} %refs_5_.3) | copy-start | bytes 12582916
  1.2 1.4 %collective-permute-start.1 = (f32[1,512]{1,0:T(1,128)}, f32[1,512]{1,0:T(1,128)S(1)}, u32[]{:S(2)}, u32[]{:S(2)}) collective-permute-start(f32[1,512]{1,0:T(1,128)} %bitcast.7), channel_id=1, source_target_pairs={{0,1},{1,0},{2,3},{3,2},{4,5},{5,4},{6,7},{7,6},{8,9},{9,8},{10,11... | collective-permute-start | bytes 6152 | tf_op jit(solution)/shard_map/ppermute | solution.py:108
  2.8 6.4 %collective-permute-start.2 = (bf16[16,1152]{1,0:T(8,128)(2,1)S(1)}, bf16[16,1152]{1,0:T(8,128)(2,1)S(1)}, u32[]{:S(2)}, u32[]{:S(2)}) collective-permute-start(bf16[16,1152]{1,0:T(8,128)(2,1)S(1)} %shard_map.140.pair_ref.message_ref.refs_3_), channel_id=1, source_target_pairs={{0,7},{1,0},{2,5},{3,2},{4,3},{5,4},{6,1},{7,6},{8,15},{9,8},{10,1... | collective-permute-start | bytes 110600 | tf_op jit(solution)/shard_map/ppermute | solution.py:198
  7.5 2.0 %collective-permute-start.4 = (bf16[16,1152]{1,0:T(8,128)(2,1)S(1)}, bf16[16,1152]{1,0:T(8,128)(2,1)S(1)}, u32[]{:S(2)}, u32[]{:S(2)}) collective-permute-start(bf16[16,1152]{1,0:T(8,128)(2,1)S(1)} %shard_map.140.pair_ref.message_ref.refs_3_), channel_id=1, source_target_pairs={{0,5},{1,0},{2,7},{3,2},{4,1},{5,4},{6,3},{7,6},{8,13},{9,8},{10,1... | collective-permute-start | bytes 110600 | tf_op jit(solution)/shard_map/ppermute | solution.py:198
  7.5 2.4 %collective-permute-start.6 = (bf16[16,1152]{1,0:T(8,128)(2,1)S(1)}, bf16[16,1152]{1,0:T(8,128)(2,1)S(1)}, u32[]{:S(2)}, u32[]{:S(2)}) collective-permute-start(bf16[16,1152]{1,0:T(8,128)(2,1)S(1)} %shard_map.140.pair_ref.message_ref.refs_3_), channel_id=1, source_target_pairs={{0,3},{1,0},{2,1},{3,2},{4,7},{5,4},{6,5},{7,6},{8,11},{9,8},{10,9... | collective-permute-start | bytes 110600 | tf_op jit(solution)/shard_map/ppermute | solution.py:198
  7.7 3.7 %copy-start.9 = (f32[128]{0:T(128)S(1)}, f32[128]{0:T(128)}, u32[]{:S(2)}) copy-start(f32[128]{0:T(128)} %param.15) | copy-start | bytes 1540
  9.1 3.7 %collective-permute-start.3 = (bf16[16,1152]{1,0:T(8,128)(2,1)S(1)}, bf16[16,1152]{1,0:T(8,128)(2,1)S(1)}, u32[]{:S(2)}, u32[]{:S(2)}) collective-permute-start(bf16[16,1152]{1,0:T(8,128)(2,1)S(1)} %collective-permute-done.2.refs_0_), channel_id=1, source_target_pairs={{0,1},{1,0},{2,3},{3,2},{4,5},{5,4},{6,7},{7,6},{8,9},{9,8},{10,11... | collective-permute-start | bytes 110600 | tf_op jit(solution)/shard_map/ppermute | solution.py:108
  9.5 3.4 %collective-permute-start.5 = (bf16[16,1152]{1,0:T(8,128)(2,1)S(1)}, bf16[16,1152]{1,0:T(8,128)(2,1)S(1)}, u32[]{:S(2)}, u32[]{:S(2)}) collective-permute-start(bf16[16,1152]{1,0:T(8,128)(2,1)S(1)} %collective-permute-done.4.refs_1_), channel_id=1, source_target_pairs={{0,1},{1,0},{2,3},{3,2},{4,5},{5,4},{6,7},{7,6},{8,9},{9,8},{10,11... | collective-permute-start | bytes 110600 | tf_op jit(solution)/shard_map/ppermute | solution.py:108
  9.9 2.4 %collective-permute-start.7 = (bf16[16,1152]{1,0:T(8,128)(2,1)S(1)}, bf16[16,1152]{1,0:T(8,128)(2,1)S(1)}, u32[]{:S(2)}, u32[]{:S(2)}) collective-permute-start(bf16[16,1152]{1,0:T(8,128)(2,1)S(1)} %collective-permute-done.6.refs_2_), channel_id=1, source_target_pairs={{0,1},{1,0},{2,3},{3,2},{4,5},{5,4},{6,7},{7,6},{8,9},{9,8},{10,11... | collective-permute-start | bytes 110600 | tf_op jit(solution)/shard_map/ppermute | solution.py:108
  11.4 1.1 %copy-start.2 = (bf16[320,1024]{1,0:T(8,128)(2,1)S(1)}, bf16[320,1024]{1,0:T(8,128)(2,1)}, u32[]{:S(2)}) copy-start(bf16[320,1024]{1,0:T(8,128)(2,1)} %refs_1_.9) | copy-start | bytes 1966084
  11.4 1.3 %copy-start.3 = (bf16[320,1024]{1,0:T(8,128)(2,1)S(1)}, bf16[320,1024]{1,0:T(8,128)(2,1)}, u32[]{:S(2)}) copy-start(bf16[320,1024]{1,0:T(8,128)(2,1)} %refs_2_.5) | copy-start | bytes 1966084
  11.4 2.3 %collective-permute-start.8 = (bf16[16,512]{1,0:T(8,128)(2,1)S(1)}, bf16[16,512]{1,0:T(8,128)(2,1)S(1)}, u32[]{:S(2)}, u32[]{:S(2)}) collective-permute-start(bf16[16,512]{1,0:T(8,128)(2,1)S(1)} %shard_map.146), channel_id=1, source_target_pairs={{0,1},{1,0},{2,3},{3,2},{4,5},{5,4},{6,7},{7,6},{8,9},{9,8},{10,11... | collective-permute-start | bytes 49160 | tf_op jit(solution)/shard_map/ppermute | solution.py:108
  12.8 3.9 %collective-permute-start.10 = (bf16[2,320,1024]{2,1,0:T(8,128)(2,1)S(1)}, bf16[2,320,1024]{2,1,0:T(8,128)(2,1)S(1)}, u32[]{:S(2)}, u32[]{:S(2)}) collective-permute-start(bf16[2,320,1024]{2,1,0:T(8,128)(2,1)S(1)} %shard_map.148), channel_id=1, source_target_pairs={{0,1},{1,0},{2,3},{3,2},{4,5},{5,4},{6,7},{7,6},{8,9},{9,8},{10,11... | collective-permute-start | bytes 3932168 | tf_op jit(solution)/shard_map/ppermute | solution.py:108
  13.3 2.1 %copy-start.5 = (f32[512]{0:T(512)S(1)}, f32[512]{0:T(512)}, u32[]{:S(2)}) copy-start(f32[512]{0:T(512)} %param.19) | copy-start | bytes 6148
  13.3 2.5 %copy-start = (bf16[512,4096]{1,0:T(8,128)(2,1)S(1)}, bf16[512,4096]{1,0:T(8,128)(2,1)}, u32[]{:S(2)}) copy-start(bf16[512,4096]{1,0:T(8,128)(2,1)} %refs_1_.13) | copy-start | bytes 12582916
  13.7 3.5 %collective-permute-start.9 = (bf16[16,1024]{1,0:T(8,128)(2,1)S(1)}, bf16[16,1024]{1,0:T(8,128)(2,1)S(1)}, u32[]{:S(2)}, u32[]{:S(2)}) collective-permute-start(bf16[16,1024]{1,0:T(8,128)(2,1)S(1)} %shard_map.147.query_ref._), channel_id=1, source_target_pairs={{0,7},{1,0},{2,5},{3,2},{4,3},{5,4},{6,1},{7,6},{8,15},{9,8},{10,1... | collective-permute-start | bytes 98312 | tf_op jit(solution)/shard_map/ppermute | solution.py:198
  15.4 1.2 %collective-permute-start.11 = (f32[1,512]{1,0:T(1,128)S(1)}, f32[1,512]{1,0:T(1,128)S(1)}, u32[]{:S(2)}, u32[]{:S(2)}) collective-permute-start(f32[1,512]{1,0:T(1,128)S(1)} %bitcast.4), channel_id=1, source_target_pairs={{0,1},{1,0},{2,3},{3,2},{4,5},{5,4},{6,7},{7,6},{8,9},{9,8},{10,11... | collective-permute-start | bytes 6152 | tf_op jit(solution)/shard_map/ppermute | solution.py:108
  15.4 3.8 %collective-permute-start.13 = (bf16[16,1024]{1,0:T(8,128)(2,1)S(1)}, bf16[16,1024]{1,0:T(8,128)(2,1)S(1)}, u32[]{:S(2)}, u32[]{:S(2)}) collective-permute-start(bf16[16,1024]{1,0:T(8,128)(2,1)S(1)} %shard_map.147.query_ref._), channel_id=1, source_target_pairs={{0,5},{1,0},{2,7},{3,2},{4,1},{5,4},{6,3},{7,6},{8,13},{9,8},{10,1... | collective-permute-start | bytes 98312 | tf_op jit(solution)/shard_map/ppermute | solution.py:198
  15.7 4.9 %collective-permute-start.15 = (bf16[16,1024]{1,0:T(8,128)(2,1)S(1)}, bf16[16,1024]{1,0:T(8,128)(2,1)S(1)}, u32[]{:S(2)}, u32[]{:S(2)}) collective-permute-start(bf16[16,1024]{1,0:T(8,128)(2,1)S(1)} %shard_map.147.query_ref._), channel_id=1, source_target_pairs={{0,3},{1,0},{2,1},{3,2},{4,7},{5,4},{6,5},{7,6},{8,11},{9,8},{10,9... | collective-permute-start | bytes 98312 | tf_op jit(solution)/shard_map/ppermute | solution.py:198
  16.5 8.0 %collective-permute-start.17 = (bf16[512,4096]{1,0:T(8,128)(2,1)S(1)}, bf16[512,4096]{1,0:T(8,128)(2,1)S(1)}, u32[]{:S(2)}, u32[]{:S(2)}) collective-permute-start(bf16[512,4096]{1,0:T(8,128)(2,1)S(1)} %shard_map.154), channel_id=1, source_target_pairs={{0,1},{1,0},{2,3},{3,2},{4,5},{5,4},{6,7},{7,6},{8,9},{9,8},{10,11... | collective-permute-start | bytes 12582920 | tf_op jit(solution)/shard_map/ppermute | solution.py:108
  17.2 6.3 %collective-permute-start.12 = (bf16[16,1152]{1,0:T(8,128)(2,1)S(1)}, bf16[16,1152]{1,0:T(8,128)(2,1)S(1)}, u32[]{:S(2)}, u32[]{:S(2)}) collective-permute-start(bf16[16,1152]{1,0:T(8,128)(2,1)S(1)} %shard_map.150.refs_5_), channel_id=1, source_target_pairs={{0,1},{1,6},{2,3},{3,4},{4,5},{5,2},{6,7},{7,0},{8,9},{9,14},{10,1... | collective-permute-start | bytes 110600 | tf_op jit(solution)/shard_map/ppermute | solution.py:198
  19.2 4.8 %collective-permute-start.14 = (bf16[16,1152]{1,0:T(8,128)(2,1)S(1)}, bf16[16,1152]{1,0:T(8,128)(2,1)S(1)}, u32[]{:S(2)}, u32[]{:S(2)}) collective-permute-start(bf16[16,1152]{1,0:T(8,128)(2,1)S(1)} %shard_map.151.refs_5_), channel_id=1, source_target_pairs={{0,1},{1,4},{2,3},{3,6},{4,5},{5,0},{6,7},{7,2},{8,9},{9,12},{10,1... | collective-permute-start | bytes 110600 | tf_op jit(solution)/shard_map/ppermute | solution.py:198
  20.7 3.6 %collective-permute-start.16 = (bf16[16,1152]{1,0:T(8,128)(2,1)S(1)}, bf16[16,1152]{1,0:T(8,128)(2,1)S(1)}, u32[]{:S(2)}, u32[]{:S(2)}) collective-permute-start(bf16[16,1152]{1,0:T(8,128)(2,1)S(1)} %shard_map.152), channel_id=1, source_target_pairs={{0,1},{1,2},{2,3},{3,0},{4,5},{5,6},{6,7},{7,4},{8,9},{9,10},{10,1... | collective-permute-start | bytes 110600 | tf_op jit(solution)/shard_map/ppermute | solution.py:198
  24.9 3.0 %collective-permute-start.18 = (bf16[16,1024]{1,0:T(8,128)(2,1)S(1)}, bf16[16,1024]{1,0:T(8,128)(2,1)S(1)}, u32[]{:S(2)}, u32[]{:S(2)}) collective-permute-start(bf16[16,1024]{1,0:T(8,128)(2,1)S(1)} %shard_map.155.refs_3_), channel_id=1, source_target_pairs={{0,7},{1,0},{2,5},{3,2},{4,3},{5,4},{6,1},{7,6},{8,15},{9,8},{10,1... | collective-permute-start | bytes 98312 | tf_op jit(solution)/shard_map/ppermute | solution.py:198
  26.0 2.6 %collective-permute-start.19 = (bf16[16,1024]{1,0:T(8,128)(2,1)S(1)}, bf16[16,1024]{1,0:T(8,128)(2,1)S(1)}, u32[]{:S(2)}, u32[]{:S(2)}) collective-permute-start(bf16[16,1024]{1,0:T(8,128)(2,1)S(1)} %shard_map.156.refs_3_), channel_id=1, source_target_pairs={{0,5},{1,0},{2,7},{3,2},{4,1},{5,4},{6,3},{7,6},{8,13},{9,8},{10,1... | collective-permute-start | bytes 98312 | tf_op jit(solution)/shard_map/ppermute | solution.py:198
  27.4 12.6 %copy-start.10 = (s32[64]{0:T(128)S(1)}, s32[64]{0:T(128)}, u32[]{:S(2)}) copy-start(s32[64]{0:T(128)} %param.22) | copy-start | bytes 772
  27.4 1.6 %collective-permute-start.20 = (bf16[16,1024]{1,0:T(8,128)(2,1)S(1)}, bf16[16,1024]{1,0:T(8,128)(2,1)S(1)}, u32[]{:S(2)}, u32[]{:S(2)}) collective-permute-start(bf16[16,1024]{1,0:T(8,128)(2,1)S(1)} %shard_map.157.refs_3_), channel_id=1, source_target_pairs={{0,3},{1,0},{2,1},{3,2},{4,7},{5,4},{6,5},{7,6},{8,11},{9,8},{10,9... | collective-permute-start | bytes 98312 | tf_op jit(solution)/shard_map/ppermute | solution.py:198
  27.8 1.2 %collective-permute-start.21 = (bf16[16,1024]{1,0:T(8,128)(2,1)S(1)}, bf16[16,1024]{1,0:T(8,128)(2,1)S(1)}, u32[]{:S(2)}, u32[]{:S(2)}) collective-permute-start(bf16[16,1024]{1,0:T(8,128)(2,1)S(1)} %shard_map.158), channel_id=1, source_target_pairs={{0,1},{1,0},{2,3},{3,2},{4,5},{5,4},{6,7},{7,6},{8,9},{9,8},{10,11... | collective-permute-start | bytes 98312 | tf_op jit(solution)/shard_map/ppermute | solution.py:108
  29.0 5.0 %collective-permute-start.22 = (bf16[16,1152]{1,0:T(8,128)(2,1)S(1)}, bf16[16,1152]{1,0:T(8,128)(2,1)S(1)}, u32[]{:S(2)}, u32[]{:S(2)}) collective-permute-start(bf16[16,1152]{1,0:T(8,128)(2,1)S(1)} %get-tuple-element.17.refs_3_), channel_id=1, source_target_pairs={{0,1},{1,24},{2,3},{3,26},{4,5},{5,28},{6,7},{7,30},{8,9},{9,16},{... | collective-permute-start | bytes 110600 | tf_op jit(solution)/shard_map/ppermute | solution.py:198
  30.2 3.8 %collective-permute-start.23 = (bf16[16,1152]{1,0:T(8,128)(2,1)S(1)}, bf16[16,1152]{1,0:T(8,128)(2,1)S(1)}, u32[]{:S(2)}, u32[]{:S(2)}) collective-permute-start(bf16[16,1152]{1,0:T(8,128)(2,1)S(1)} %get-tuple-element.17.refs_3_), channel_id=1, source_target_pairs={{0,1},{1,16},{2,3},{3,18},{4,5},{5,20},{6,7},{7,22},{8,9},{9,24},{... | collective-permute-start | bytes 110600 | tf_op jit(solution)/shard_map/ppermute | solution.py:198
  31.6 3.4 %collective-permute-start.24 = (bf16[16,1152]{1,0:T(8,128)(2,1)S(1)}, bf16[16,1152]{1,0:T(8,128)(2,1)S(1)}, u32[]{:S(2)}, u32[]{:S(2)}) collective-permute-start(bf16[16,1152]{1,0:T(8,128)(2,1)S(1)} %get-tuple-element.17.refs_3_), channel_id=1, source_target_pairs={{0,1},{1,8},{2,3},{3,10},{4,5},{5,12},{6,7},{7,14},{8,9},{9,0},{10... | collective-permute-start | bytes 110600 | tf_op jit(solution)/shard_map/ppermute | solution.py:198
  31.9 3.1 %collective-permute-start.25 = (bf16[16,1152]{1,0:T(8,128)(2,1)S(1)}, bf16[16,1152]{1,0:T(8,128)(2,1)S(1)}, u32[]{:S(2)}, u32[]{:S(2)}) collective-permute-start(bf16[16,1152]{1,0:T(8,128)(2,1)S(1)} %get-tuple-element.17.refs_3_), channel_id=1, source_target_pairs={{0,1},{1,0},{2,3},{3,2},{4,5},{5,4},{6,7},{7,6},{8,9},{9,8},{10,11... | collective-permute-start | bytes 110600 | tf_op jit(solution)/shard_map/ppermute | solution.py:108
  32.2 1.2 %collective-permute-start.26 = (f32[16,512]{1,0:T(8,128)S(1)}, f32[16,512]{1,0:T(8,128)S(1)}, u32[]{:S(2)}, u32[]{:S(2)}) collective-permute-start(f32[16,512]{1,0:T(8,128)S(1)} %get-tuple-element.18), channel_id=1, source_target_pairs={{0,1},{1,0},{2,3},{3,2},{4,5},{5,4},{6,7},{7,6},{8,9},{9,8},{10,11... | collective-permute-start | bytes 98312 | tf_op jit(solution)/shard_map/ppermute | solution.py:108
  35.2 1.9 %collective-permute-start.27 = (f32[48,128]{1,0:T(8,128)S(1)}, f32[48,128]{1,0:T(8,128)S(1)}, u32[]{:S(2)}, u32[]{:S(2)}) collective-permute-start(f32[48,128]{1,0:T(8,128)S(1)} %get-tuple-element.19), channel_id=1, source_target_pairs={{0,7},{1,0},{2,5},{3,2},{4,3},{5,4},{6,1},{7,6},{8,15},{9,8},{10,1... | collective-permute-start | bytes 73736 | tf_op jit(solution)/shard_map/ppermute | solution.py:198
  35.2 2.9 %collective-permute-start.28 = (f32[48,128]{1,0:T(8,128)S(1)}, f32[48,128]{1,0:T(8,128)S(1)}, u32[]{:S(2)}, u32[]{:S(2)}) collective-permute-start(f32[48,128]{1,0:T(8,128)S(1)} %get-tuple-element.19), channel_id=1, source_target_pairs={{0,5},{1,0},{2,7},{3,2},{4,1},{5,4},{6,3},{7,6},{8,13},{9,8},{10,1... | collective-permute-start | bytes 73736 | tf_op jit(solution)/shard_map/ppermute | solution.py:198
  36.6 1.8 %collective-permute-start.29 = (f32[48,128]{1,0:T(8,128)S(1)}, f32[48,128]{1,0:T(8,128)S(1)}, u32[]{:S(2)}, u32[]{:S(2)}) collective-permute-start(f32[48,128]{1,0:T(8,128)S(1)} %get-tuple-element.19), channel_id=1, source_target_pairs={{0,3},{1,0},{2,1},{3,2},{4,7},{5,4},{6,5},{7,6},{8,11},{9,8},{10,9... | collective-permute-start | bytes 73736 | tf_op jit(solution)/shard_map/ppermute | solution.py:198
  36.6 1.8 %collective-permute-start.30 = (f32[48,128]{1,0:T(8,128)S(1)}, f32[48,128]{1,0:T(8,128)S(1)}, u32[]{:S(2)}, u32[]{:S(2)}) collective-permute-start(f32[48,128]{1,0:T(8,128)S(1)} %get-tuple-element.19), channel_id=1, source_target_pairs={{0,1},{1,0},{2,3},{3,2},{4,5},{5,4},{6,7},{7,6},{8,9},{9,8},{10,11... | collective-permute-start | bytes 73736 | tf_op jit(solution)/shard_map/ppermute | solution.py:108
  37.1 3.0 %collective-permute-start.32 = (bf16[48,512]{1,0:T(8,128)(2,1)S(1)}, bf16[48,512]{1,0:T(8,128)(2,1)S(1)}, u32[]{:S(2)}, u32[]{:S(2)}) collective-permute-start(bf16[48,512]{1,0:T(8,128)(2,1)S(1)} %get-tuple-element.21), channel_id=1, source_target_pairs={{0,1},{1,0},{2,3},{3,2},{4,5},{5,4},{6,7},{7,6},{8,9},{9,8},{10,11... | collective-permute-start | bytes 147464 | tf_op jit(solution)/shard_map/ppermute | solution.py:108
  38.4 2.5 %collective-permute-start.31 = (f32[48,128]{1,0:T(8,128)S(1)}, f32[48,128]{1,0:T(8,128)S(1)}, u32[]{:S(2)}, u32[]{:S(2)}) collective-permute-start(f32[48,128]{1,0:T(8,128)S(1)} %shard_map.161.refs_0_), channel_id=1, source_target_pairs={{0,1},{1,0},{2,3},{3,2},{4,5},{5,4},{6,7},{7,6},{8,9},{9,8},{10,11... | collective-permute-start | bytes 73736 | tf_op jit(solution)/shard_map/ppermute | solution.py:108

commit v9 on v8

--- a/solution.py
+++ b/solution.py
@@ -127,6 +127,16 @@
 
 def open_window(out_ref):
     out_ref[...] = jnp.zeros_like(out_ref)
+
+
+def prepare_inputs(window_ref, hidden_ref, gain_ref, message_ref):
+    del window_ref
+    inputs = hidden_ref[...].astype(jnp.float32)
+    width = inputs.shape[1]
+    message_ref[:, :width] = (inputs * gain_ref[...]).astype(jnp.bfloat16)
+    message_ref[:, width:] = pack_statistics(
+        [jnp.sum(inputs * inputs, axis=1, keepdims=True)], core_number()
+    )
 
 
 def positions_and_ranges(
@@ -156,12 +166,12 @@
 LOG2_E = 1.4426950408889634
 
 
-def pack_statistics(values):
+def pack_statistics(values, first=0):
     rows = values[0].shape[0]
     lane = lax.broadcasted_iota(jnp.int32, (rows, 128), 1)
     rest = jnp.zeros((rows, 128), jnp.float32)
     for place, value in enumerate(values):
-        rest = jnp.where(lane == place, value, rest)
+        rest = jnp.where(lane == first + place, value, rest)
     out = rest.astype(jnp.bfloat16).astype(jnp.float32)
     for part in (1, 2):
         rest = rest - rest.astype(jnp.bfloat16).astype(jnp.float32)
@@ -169,9 +179,10 @@
     return out.astype(jnp.bfloat16)
 
 
-def read_statistic(block, first):
+def read_statistic(block, first, count=1):
     lane = lax.broadcasted_iota(jnp.int32, block.shape, 1)
-    mine = ((lane & 31) == first) & (lane < 96)
+    place = (lane & 31) - first
+    mine = (place >= 0) & (place < count) & (lane < 96)
     return jnp.sum(jnp.where(mine, block.astype(jnp.float32), 0.0), axis=1, keepdims=True)
 
 
@@ -233,42 +244,32 @@
     total_ref[...] = project_pair(pair_ref, 0, weight_ref)
 
 
-def project_early(third_ref, second_ref, own_ref, weight_ref, *refs, core):
-    total_ref = refs[-1]
-
-    @pl.when(core_number() == core)
-    def _():
-        total_ref[...] = (
-            own_ref[...]
-            + project_pair(third_ref, 3, weight_ref)
-            + project_pair(second_ref, 2, weight_ref)
-        )
-
-
 def make_queries(
     third_ref,
     second_ref,
     first_ref,
     pair_ref,
-    total_ref,
     weight_ref,
     gain_ref,
     rope_ref,
     *refs,
-    core,
     model_width,
 ):
     query_ref = refs[-1]
-    width = total_ref.shape[1]
+    width = query_ref.shape[1]
     head_dim = gain_ref.shape[1]
 
-    @pl.when(core_number() == core)
+    @pl.when(core_number() == 1)
     def _():
-        projected = total_ref[...] + project_pair(first_ref, 1, weight_ref)
-        squares = sum(
-            ref[:, 2 * width :].astype(jnp.float32)
-            for ref in (pair_ref, first_ref, second_ref, third_ref)
-        )
+        blocks = (pair_ref, first_ref, second_ref, third_ref)
+        if len(refs) == 2:
+            projected = refs[0][...]
+        else:
+            projected = project_pair(pair_ref, 0, weight_ref)
+        squares = pair_ref[:, 2 * width :].astype(jnp.float32)
+        for offset in (3, 2, 1):
+            projected = projected + project_pair(blocks[offset], offset, weight_ref)
+            squares = squares + blocks[offset][:, 2 * width :].astype(jnp.float32)
         squares = read_statistic(squares, 0)
         projected = projected * lax.rsqrt(squares / model_width + EPSILON)
         cosine = rope_ref[:, :head_dim]
@@ -339,14 +340,14 @@
             other_ref[1, :, column],
             preferred_element_type=jnp.float32,
         )
-        out.append((highest * scale, total, numerators))
+        out.append((highest * scale + jnp.log(total), numerators / total))
     return out
 
 
 def attend_remote(query_ref, key_ref, value_ref, other_ref, range_ref, *refs, offset):
     out_ref = refs[-1]
 
-    @pl.when(core_number() == 1)
+    @pl.when(core_number() == 0)
     def _():
         rows = query_ref.shape[0]
         width = query_ref.shape[1] // 2
@@ -356,17 +357,17 @@
         heads = (2 * chip, 2 * chip + 1)
         parts = attend_heads(queries, heads, key_ref, value_ref, other_ref, masks)
         stats = []
-        for j, (highest, total, numerators) in enumerate(parts):
+        for j, (level, averages) in enumerate(parts):
             for h in range(width // 128):
                 part = slice(h * rows, (h + 1) * rows)
                 place = slice(j * width + h * 128, j * width + (h + 1) * 128)
-                out_ref[:, place] = numerators[part].astype(jnp.bfloat16)
-                stats += [highest[part], total[part]]
+                out_ref[:, place] = averages[part].astype(jnp.bfloat16)
+                stats.append(level[part])
         out_ref[:, 2 * width :] = pack_statistics(stats)
 
 
-def attend_own(query_ref, key_ref, value_ref, other_ref, range_ref, _, out_ref, stats_ref):
-    @pl.when(core_number() == 0)
+def attend_own(query_ref, key_ref, value_ref, other_ref, range_ref, out_ref, stats_ref):
+    @pl.when(core_number() == 1)
     def _():
         width = query_ref.shape[1] // 2
         masks = token_masks(range_ref, key_ref.shape[0], width // 128)
@@ -379,16 +380,15 @@
             other_ref,
             masks,
         )
-        for j, (highest, total, numerators) in enumerate(parts):
-            out_ref[j] = numerators
-            stats_ref[j, :, :128] = jnp.broadcast_to(highest, (highest.shape[0], 128))
-            stats_ref[j, :, 128:] = jnp.broadcast_to(total, (highest.shape[0], 128))
+        for j, (level, averages) in enumerate(parts):
+            out_ref[j] = averages
+            stats_ref[j] = jnp.broadcast_to(level, averages.shape)
 
 
 def merge_partials(third_ref, second_ref, first_ref, own_ref, stats_ref, *refs):
     attended_ref = refs[-1]
 
-    @pl.when(core_number() == 0)
+    @pl.when(core_number() == 1)
     def _():
         rows = attended_ref.shape[0]
         width = attended_ref.shape[1] // 2
@@ -398,22 +398,16 @@
             for h in range(width // 128):
                 part = slice(h * rows, (h + 1) * rows)
                 place = slice(j * width + h * 128, j * width + (h + 1) * 128)
-                slot = 2 * (j * (width // 128) + h)
-                maxima = [stats_ref[j, part, :1]] + [read_statistic(s, slot) for s in stats]
-                totals = [stats_ref[j, part, 128:129]]
-                totals += [read_statistic(s, slot + 1) for s in stats]
-                numerators = [own_ref[j, part, :]]
-                numerators += [ref[:, place].astype(jnp.float32) for ref in others]
-                highest = maxima[0]
-                for value in maxima[1:]:
-                    highest = jnp.maximum(highest, value)
-                denominator = 0.0
-                summed = 0.0
-                for value, total, numerator in zip(maxima, totals, numerators):
-                    factor = jnp.exp(value - highest)
-                    denominator = denominator + total * factor
-                    summed = summed + numerator * factor
-                attended_ref[:, place] = (summed / denominator).astype(jnp.bfloat16)
+                slot = j * (width // 128) + h
+                levels = [stats_ref[j, part]] + [read_statistic(s, slot) for s in stats]
+                averages = [own_ref[j, part]]
+                averages += [ref[:, place].astype(jnp.float32) for ref in others]
+                highest = levels[0]
+                for level in levels[1:]:
+                    highest = jnp.maximum(highest, level)
+                factors = [jnp.exp(level - highest) for level in levels]
+                summed = sum(factor * average for factor, average in zip(factors, averages))
+                attended_ref[:, place] = (summed / sum(factors)).astype(jnp.bfloat16)
 
 
 def copy_weights(_, weight_ref, out_ref):
@@ -423,14 +417,14 @@
 def project_out(attended_ref, weight_ref, other_weight_ref, *refs, offset):
     out_ref = refs[-1]
 
-    @pl.when(core_number() == 0)
+    @pl.when(core_number() == 1)
     def _():
         width = attended_ref.shape[1] // 2
         column = pl.ds(pl.multiple_of((chip_number() ^ offset) * 2 * width, 2 * width), 2 * width)
         total = jnp.dot(
-            attended_ref[:, :width], weight_ref[:, column], preferred_element_type=jnp.float32
+            attended_ref[:, width:], weight_ref[:, column], preferred_element_type=jnp.float32
         ) + jnp.dot(
-            attended_ref[:, width:], other_weight_ref[:, column], preferred_element_type=jnp.float32
+            attended_ref[:, :width], other_weight_ref[:, column], preferred_element_type=jnp.float32
         )
         out_ref[...] = total.astype(out_ref.dtype)
 
@@ -450,34 +444,34 @@
 ):
     width = own_ref.shape[1]
 
-    @pl.when(core_number() == 1)
+    @pl.when(core_number() == 0)
     def _():
         squares = 0.0
-        inputs = (other_ref, own_ref)
-        gains = (other_gain_ref, own_gain_ref)
+        inputs = (own_ref, other_ref)
+        gains = (own_gain_ref, other_gain_ref)
         for core in range(2):
             place = slice(core * width, (core + 1) * width)
             hidden = inputs[core][...].astype(jnp.float32)
             for ref in (kept_ref, first_ref, second_ref, third_ref):
                 hidden = hidden + ref[:, place].astype(jnp.float32)
             scaled = hidden * gains[core][...]
-            (other_scaled_ref, scaled_ref)[core][...] = scaled
+            (scaled_ref, other_scaled_ref)[core][...] = scaled
             sent_ref[:, place] = scaled.astype(jnp.bfloat16)
             squares = squares + jnp.sum(hidden * hidden, axis=1, keepdims=True)
         sent_ref[:, 2 * width :] = pack_statistics([squares])
 
 
 def gram_part(third_ref, second_ref, first_ref, own_ref, _, out_ref, near_ref, far_ref):
-    @pl.when(core_number() == 0)
+    @pl.when(core_number() == 1)
     def _():
         rows = own_ref.shape[0]
         width = far_ref.shape[1]
         refs = (own_ref, first_ref, second_ref, third_ref)
         for i, ref in enumerate(refs):
-            near_ref[i * rows : (i + 1) * rows] = ref[:, :width]
+            near_ref[i * rows : (i + 1) * rows] = ref[:, width : 2 * width]
         for i, ref in enumerate(refs[1:]):
-            far_ref[i * rows : (i + 1) * rows] = ref[:, width : 2 * width]
-        far = jnp.concatenate([ref[:, width : 2 * width] for ref in refs], axis=0)
+            far_ref[i * rows : (i + 1) * rows] = ref[:, :width]
+        far = jnp.concatenate([ref[:, :width] for ref in refs], axis=0)
         squares = read_statistic(own_ref[:, 2 * width :], 0)
         gram = 0.0
         for vectors in (near_ref[...], far):
@@ -533,11 +527,11 @@
     model_width,
 ):
     me = lax.axis_index("pack")
-    first_core = core_number() == 0
+    leads = core_number() == 1
     count, width = near_ref.shape
     rows = scaled_ref.shape[0]
     half = count // 2
-    summed = jnp.where(first_core, other_summed_ref[...], summed_ref[...])
+    summed = jnp.where(leads, other_summed_ref[...], summed_ref[...])
     gram = jnp.concatenate([summed[:half, :count], summed[:half, count:]], axis=0)
     squares = summed[half:, :1]
     shape = (count, count)
@@ -575,13 +569,13 @@
         grad_ref[...] = (gradient * grad_gain).astype(jnp.bfloat16)
         pooled_ref[...] = (scaled * pooled_scale).astype(jnp.bfloat16)
 
-    @pl.when(first_core)
+    @pl.when(leads)
     def _():
         write(near_ref[...], other_scaled_ref[...])
 
-    @pl.when(core_number() == 1)
+    @pl.when(core_number() == 0)
     def _():
-        vectors = jnp.concatenate((sent_ref[:, width : 2 * width], other_far_ref[...]), axis=0)
+        vectors = jnp.concatenate((sent_ref[:, :width], other_far_ref[...]), axis=0)
         write(vectors, scaled_ref[...])
 
 
@@ -624,6 +618,7 @@
     )()
     attn_gain = attn_gain[None]
     other_hidden_in = flip(hidden_in, "pack", 1)
+    other_w_query = flip(w_query, "pack", 1)
     pair = in_vmem(
         prepare_pair,
         shaped((stmts, 2 * width + 128), bf16),
@@ -632,6 +627,7 @@
         other_hidden_in,
         attn_gain,
         flip(attn_gain, "pack", 1),
+        flops=1 << 34,
     )
     received = [send_across(pair, "pack", k, 0) for k in others]
     own_projected = in_vmem(
@@ -645,66 +641,48 @@
         lengths,
         pack_order,
     )
-    other_gain = flip(final_gain, "pack", 1)
-
-    def project_on(core, parts, *after):
-        first, second, third = parts
-        early = in_vmem(
-            lambda *refs: project_early(*refs, core=core),
-            shaped((stmts, width), f32),
-            third,
-            second,
-            own_projected,
-            w_query,
-            *after[:1],
-            limit=16,
-            flops=1 << 30,
-        )
-        return in_vmem(
-            lambda *refs: make_queries(*refs, core=core, model_width=model_width),
-            shaped((stmts, width), bf16),
-            third,
-            second,
-            first,
-            pair,
-            early,
-            w_query,
-            query_gain,
-            rope,
-            *after[1:],
-            limit=16,
-            flops=1 << 36 if core == 0 else 1 << 27,
-        )
-
-    late_queries = project_on(1, received, rope)
-    handed = [flip(part, "pack", 1) for part in received]
     held = in_vmem(
         copy_tokens,
         shaped((2,) + cached_keys.shape, bf16),
-        handed[0],
+        own_projected,
         cached_keys,
         cached_values,
     )
     other_held = flip(held, "pack", 1)
-    second_queries = flip(late_queries, "pack", 1)
-    first_queries = project_on(0, handed)
+    other_gain = flip(final_gain, "pack", 1)
+
+    def queries_from(weights, flops, *own):
+        return in_vmem(
+            lambda *refs: make_queries(*refs, model_width=model_width),
+            shaped((stmts, width), bf16),
+            *received[::-1],
+            pair,
+            weights,
+            query_gain,
+            rope,
+            *own,
+            limit=16,
+            flops=flops,
+        )
+
+    second_queries = queries_from(w_query, 1 << 34, own_projected)
+    first_queries = queries_from(other_w_query, 1 << 27)
     queries = in_vmem(
         join_queries, shaped((stmts, 2 * width), bf16), first_queries, second_queries
     )
     other_weights = flip(
         in_vmem(copy_weights, shaped(w_out.shape, bf16), queries, w_out, limit=16), "pack", 1
     )
-    received = [send_across(queries, "pack", k, 0) for k in others]
+    received = [send_across(queries, "pack", k, 1) for k in others]
     group_rows = stmts * (width // head_dim)
     own_part, own_stats = in_vmem(
         attend_own,
-        (shaped((2, group_rows, head_dim), f32), shaped((2, group_rows, 256), f32)),
+        (shaped((2, group_rows, head_dim), f32),) * 2,
         queries,
         cached_keys,
         cached_values,
         other_held,
         ranges,
-        other_gain,
         flops=1 << 27,
     )
     partials = []
@@ -722,7 +700,7 @@
                 flops=1 << 34,
             )
         )
-    received = [send_across(part, "pack", k, 1) for k, part in zip(others, partials[::-1])]
+    received = [send_across(part, "pack", k, 0) for k, part in zip(others, partials[::-1])]
     attended = in_vmem(
         merge_partials,
         shaped((stmts, 2 * width), bf16),
@@ -747,7 +725,7 @@
     second = projected_to(2, bf16, third)
     first = projected_to(1, bf16, second)
     kept = projected_to(0, bf16, first)
-    received = [send_across(part, "pack", k, 0) for k, part in zip(others, (first, second, third))]
+    received = [send_across(part, "pack", k, 1) for k, part in zip(others, (first, second, third))]
     vector, scaled, far_scaled = in_vmem(
         finish_hidden,
         (shaped((stmts, 2 * width + 128), bf16),) + (shaped((stmts, width), f32),) * 2,
@@ -758,7 +736,7 @@
         final_gain,
         other_gain,
     )
-    received = [send_across(vector, "dp", k, 1) for k in range(1, lax.axis_size("dp"))]
+    received = [send_across(vector, "dp", k, 0) for k in range(1, lax.axis_size("dp"))]
     other_scaled = flip(far_scaled, "pack", 1)
     gram, near, far = in_vmem(
         gram_part,
@@ -771,7 +749,7 @@
         flip(vector, "pack", 1),
         other_scaled,
     )
-    received = [send_across(gram, "pack", k, 0) for k in others]
+    received = [send_across(gram, "pack", k, 1) for k in others]
     other_far = flip(far, "pack", 1)
     summed = in_vmem(
         sum_grams,

time: 42 us -> 40.1 us (0.955)
  starting transfers between devices: 23.4 us -> 21.3 us
  waiting for transfers between devices: 11.7 us -> 13.7 us
  Pallas kernels: 5.47 us -> 4.01 us
    ppermute x15 -> x12, starting transfers between devices: 6.71 us -> 3.42 us  [flip(): return lax.ppermute(array, axis, [(i, i ^ offset) for i in range(size)])]
    ppermute x18, waiting for transfers between devices: 8.09 us -> 9.73 us  [send_across(): return lax.ppermute(array, ('dp', 'pack'), pairs)]
    pallas_call x23 -> x21, Pallas kernels: 4.45 us -> 2.88 us  [in_vmem(): pl.pallas_call(body, out_shape=outputs, in_specs=[whole] * len(operands),...]
    ppermute x18, starting transfers between devices: 16.7 us -> 17.8 us  [send_across(): return lax.ppermute(array, ('dp', 'pack'), pairs)]
    ppermute x15 -> x12, waiting for transfers between devices: 3.63 us -> 4.02 us  [flip(): return lax.ppermute(array, axis, [(i, i ^ offset) for i in range(size)])]
  transfers between devices with their start and end apart: 33 -> 30, of which waited for: 15 -> 17; matrix products, arithmetic and copies ran while one was open for 0% -> 0% of each run, Pallas kernels for 9% -> 7%
where the time goes in v9:
time: 40.1 us; the launch traced here: 39.9 us
  starting transfers between devices  21.3 us (53%)
  waiting for transfers between devices  13.7 us (34%)
  Pallas kernels  4.01 us (10%)
  between operations  0.82 us (2%)
    ppermute x18, starting transfers between devices, send_across(): return lax.ppermute(array, ('dp', 'pack'), pairs)  17.8 us
    ppermute x18, waiting for transfers between devices, send_across(): return lax.ppermute(array, ('dp', 'pack'), pairs)  9.73 us
    ppermute x12, waiting for transfers between devices, flip(): return lax.ppermute(array, axis, [(i, i ^ offset) for i in range(size)])  4.02 us
    ppermute x12, starting transfers between devices, flip(): return lax.ppermute(array, axis, [(i, i ^ offset) for i in range(size)])  3.42 us
    pallas_call x21, Pallas kernels, in_vmem(): pl.pallas_call(body, out_shape=outputs, in_specs=[whole] * len(operands),...  2.88 us
    pallas_call x1, Pallas kernels, core_roles(): pl.pallas_call(lambda *refs: losses_and_gradient(*refs, model_width=model...  1.13 us
  transfers between devices with their start and end apart: 30, of which 17 were waited for; matrix products, arithmetic and copies ran while one was open for 0% of the time, Pallas kernels for 7%

profile of v9, /device:TPU:0, one launch (start us, length us, event | category | flops | bytes accessed | tf_op | source)
XLA Modules:
  0.0 39.9 jit_solution(7312831255197129538)
XLA Ops:
  0.6 0.5 %collective-permute-start = (bf16[16,512]{1,0:T(8,128)(2,1)}, bf16[16,512]{1,0:T(8,128)(2,1)S(1)}, u32[]{:S(2)}, u32[]{:S(2)}) collective-permute-start(bf16[16,512]{1,0:T(8,128)(2,1)} %own_ref.3), channel_id=1, source_target_pairs={{0,1},{1,0},{2,3},{3,2},{4,5},{5,4},{6,7},{7,6},{8,9},{9,8},{10,11... | collective-permute-start | bytes 49160 | tf_op jit(solution)/shard_map/ppermute | solution.py:108
  1.2 0.1 collective-permute-start.1
  1.2 0.4 %collective-permute-start.5 = (bf16[4096,512]{1,0:T(8,128)(2,1)}, bf16[4096,512]{1,0:T(8,128)(2,1)S(1)}, u32[]{:S(2)}, u32[]{:S(2)}) collective-permute-start(bf16[4096,512]{1,0:T(8,128)(2,1)} %refs_4_.1), channel_id=1, source_target_pairs={{0,1},{1,0},{2,3},{3,2},{4,5},{5,4},{6,7},{7,6},{8,9},{9,8},{10,11... | collective-permute-start | bytes 12582920 | tf_op jit(solution)/shard_map/ppermute | solution.py:108
  1.7 0.9 %collective-permute-done.1.other_gain_ref = f32[1,512]{1,0:T(1,128)S(1)} collective-permute-done((f32[1,512]{1,0:T(1,128)}, f32[1,512]{1,0:T(1,128)S(1)}, u32[]{:S(2)}, u32[]{:S(2)}) %collective-permute-start.1) | collective-permute-done | bytes 2080 | tf_op jit(solution)/shard_map/ppermute | solution.py:108
  2.5 0.2 shard_map.140.message_ref.refs_3_.pair_ref
  2.7 4.8 %collective-permute-start.2 = (bf16[16,1152]{1,0:T(8,128)(2,1)S(1)}, bf16[16,1152]{1,0:T(8,128)(2,1)S(1)}, u32[]{:S(2)}, u32[]{:S(2)}) collective-permute-start(bf16[16,1152]{1,0:T(8,128)(2,1)S(1)} %shard_map.140.message_ref.refs_3_.pair_ref), channel_id=1, source_target_pairs={{0,7},{1,0},{2,5},{3,2},{4,3},{5,4},{6,1},{7,6},{8,15},{9,8},{10,1... | collective-permute-start | bytes 110600 | tf_op jit(solution)/shard_map/ppermute | solution.py:209
  7.5 0.2 shard_map.143.refs_7_._
  7.8 0.1 shard_map.146
  7.9 0.6 %collective-permute-start.7 = (bf16[2,320,1024]{2,1,0:T(8,128)(2,1)S(1)}, bf16[2,320,1024]{2,1,0:T(8,128)(2,1)S(1)}, u32[]{:S(2)}, u32[]{:S(2)}) collective-permute-start(bf16[2,320,1024]{2,1,0:T(8,128)(2,1)S(1)} %shard_map.146), channel_id=1, source_target_pairs={{0,1},{1,0},{2,3},{3,2},{4,5},{5,4},{6,7},{7,6},{8,9},{9,8},{10,11... | collective-permute-start | bytes 3932168 | tf_op jit(solution)/shard_map/ppermute | solution.py:108
  8.5 0.2 shard_map.141
  8.6 0.5 %collective-permute-done.2.refs_0_ = bf16[16,1152]{1,0:T(8,128)(2,1)S(1)} collective-permute-done((bf16[16,1152]{1,0:T(8,128)(2,1)S(1)}, bf16[16,1152]{1,0:T(8,128)(2,1)S(1)}, u32[]{:S(2)}, u32[]{:S(2)}) %collective-permute-start.2) | collective-permute-done | bytes 36896 | tf_op jit(solution)/shard_map/ppermute | solution.py:209
  9.2 0.3 collective-permute-done.3.refs_1_
  9.5 0.3 collective-permute-done.4.refs_2_
  9.9 3.1 %collective-permute-start.6 = (bf16[16,1024]{1,0:T(8,128)(2,1)S(1)}, bf16[16,1024]{1,0:T(8,128)(2,1)S(1)}, u32[]{:S(2)}, u32[]{:S(2)}) collective-permute-start(bf16[16,1024]{1,0:T(8,128)(2,1)S(1)} %shard_map.145.query_ref._), channel_id=1, source_target_pairs={{0,1},{1,6},{2,3},{3,4},{4,5},{5,2},{6,7},{7,0},{8,9},{9,14},{10,1... | collective-permute-start | bytes 98312 | tf_op jit(solution)/shard_map/ppermute | solution.py:209
  13.0 0.8 %collective-permute-start.9 = (bf16[16,1024]{1,0:T(8,128)(2,1)S(1)}, bf16[16,1024]{1,0:T(8,128)(2,1)S(1)}, u32[]{:S(2)}, u32[]{:S(2)}) collective-permute-start(bf16[16,1024]{1,0:T(8,128)(2,1)S(1)} %shard_map.145.query_ref._), channel_id=1, source_target_pairs={{0,1},{1,4},{2,3},{3,6},{4,5},{5,0},{6,7},{7,2},{8,9},{9,12},{10,1... | collective-permute-start | bytes 98312 | tf_op jit(solution)/shard_map/ppermute | solution.py:209
  13.8 0.6 %collective-permute-start.11 = (bf16[16,1024]{1,0:T(8,128)(2,1)S(1)}, bf16[16,1024]{1,0:T(8,128)(2,1)S(1)}, u32[]{:S(2)}, u32[]{:S(2)}) collective-permute-start(bf16[16,1024]{1,0:T(8,128)(2,1)S(1)} %shard_map.145.query_ref._), channel_id=1, source_target_pairs={{0,1},{1,2},{2,3},{3,0},{4,5},{5,6},{6,7},{7,4},{8,9},{9,10},{10,1... | collective-permute-start | bytes 98312 | tf_op jit(solution)/shard_map/ppermute | solution.py:209
  14.4 0.3 shard_map.152
  14.7 0.1 collective-permute-start.13
  14.8 1.7 %collective-permute-done.6.refs_0_ = bf16[16,1024]{1,0:T(8,128)(2,1)S(1)} collective-permute-done((bf16[16,1024]{1,0:T(8,128)(2,1)S(1)}, bf16[16,1024]{1,0:T(8,128)(2,1)S(1)}, u32[]{:S(2)}, u32[]{:S(2)}) %collective-permute-start.6) | collective-permute-done | bytes 32800 | tf_op jit(solution)/shard_map/ppermute | solution.py:209
  16.5 0.5 %shard_map.148.refs_5_ = bf16[16,1152]{1,0:T(8,128)(2,1)S(1)} custom-call(bf16[16,1024]{1,0:T(8,128)(2,1)S(1)} %collective-permute-done.6.refs_0_, bf16[320,1024]{1,0:T(8,128)(2,1)S(1)} %copy-done.2, bf16[320,1024]{1,0:T(8,128)(2,1)S(1)} %copy-done.3, bf16[2,320,1024]{2,1,0:T(8,128)(2,1)S(1)} %collective-permute-done.7.other_ref.refs_3_, ...), custom_call_target="tpu_custom_call" | custom-call | flops 17179869184 | bytes 2736128 | tf_op jit(solution)/shard_map/pallas_call | solution.py:114
  17.1 0.2 collective-permute-start.8
  17.2 0.4 collective-permute-done.9.refs_0_
  17.6 0.5 %shard_map.149.refs_5_ = bf16[16,1152]{1,0:T(8,128)(2,1)S(1)} custom-call(bf16[16,1024]{1,0:T(8,128)(2,1)S(1)} %collective-permute-done.9.refs_0_, bf16[320,1024]{1,0:T(8,128)(2,1)S(1)} %copy-done.2, bf16[320,1024]{1,0:T(8,128)(2,1)S(1)} %copy-done.3, bf16[2,320,1024]{2,1,0:T(8,128)(2,1)S(1)} %collective-permute-done.7.other_ref.refs_3_, ...), custom_call_target="tpu_custom_call" | custom-call | flops 17179869184 | bytes 2707456 | tf_op jit(solution)/shard_map/pallas_call | solution.py:114
  18.2 0.5 %shard_map.150 = bf16[16,1152]{1,0:T(8,128)(2,1)S(1)} custom-call(bf16[16,1024]{1,0:T(8,128)(2,1)S(1)} %collective-permute-done.11.refs_0_, bf16[320,1024]{1,0:T(8,128)(2,1)S(1)} %copy-done.2, bf16[320,1024]{1,0:T(8,128)(2,1)S(1)} %copy-done.3, bf16[2,320,1024]{2,1,0:T(8,128)(2,1)S(1)} %collective-permute-done.7.other_ref.refs_3_, ...), custom_call_target="tpu_custom_call" | custom-call | flops 17179869184 | bytes 2707456 | tf_op jit(solution)/shard_map/pallas_call | solution.py:114
  18.8 3.2 %collective-permute-done.8.third_ref = bf16[16,1152]{1,0:T(8,128)(2,1)S(1)} collective-permute-done((bf16[16,1152]{1,0:T(8,128)(2,1)S(1)}, bf16[16,1152]{1,0:T(8,128)(2,1)S(1)}, u32[]{:S(2)}, u32[]{:S(2)}) %collective-permute-start.8) | collective-permute-done | bytes 36896 | tf_op jit(solution)/shard_map/ppermute | solution.py:209
  22.1 1.0 %collective-permute-start.14 = (bf16[16,1024]{1,0:T(8,128)(2,1)S(1)}, bf16[16,1024]{1,0:T(8,128)(2,1)S(1)}, u32[]{:S(2)}, u32[]{:S(2)}) collective-permute-start(bf16[16,1024]{1,0:T(8,128)(2,1)S(1)} %shard_map.153.refs_3_), channel_id=1, source_target_pairs={{0,1},{1,6},{2,3},{3,4},{4,5},{5,2},{6,7},{7,0},{8,9},{9,14},{10,1... | collective-permute-start | bytes 98312 | tf_op jit(solution)/shard_map/ppermute | solution.py:209
  23.1 1.2 %collective-permute-start.15 = (bf16[16,1024]{1,0:T(8,128)(2,1)S(1)}, bf16[16,1024]{1,0:T(8,128)(2,1)S(1)}, u32[]{:S(2)}, u32[]{:S(2)}) collective-permute-start(bf16[16,1024]{1,0:T(8,128)(2,1)S(1)} %shard_map.154.refs_3_), channel_id=1, source_target_pairs={{0,1},{1,4},{2,3},{3,6},{4,5},{5,0},{6,7},{7,2},{8,9},{9,12},{10,1... | collective-permute-start | bytes 98312 | tf_op jit(solution)/shard_map/ppermute | solution.py:209
  24.4 0.6 %collective-permute-start.16 = (bf16[16,1024]{1,0:T(8,128)(2,1)S(1)}, bf16[16,1024]{1,0:T(8,128)(2,1)S(1)}, u32[]{:S(2)}, u32[]{:S(2)}) collective-permute-start(bf16[16,1024]{1,0:T(8,128)(2,1)S(1)} %shard_map.155.refs_3_), channel_id=1, source_target_pairs={{0,1},{1,2},{2,3},{3,0},{4,5},{5,6},{6,7},{7,4},{8,9},{9,10},{10,1... | collective-permute-start | bytes 98312 | tf_op jit(solution)/shard_map/ppermute | solution.py:209
  25.0 0.4 %collective-permute-start.17 = (bf16[16,1024]{1,0:T(8,128)(2,1)S(1)}, bf16[16,1024]{1,0:T(8,128)(2,1)S(1)}, u32[]{:S(2)}, u32[]{:S(2)}) collective-permute-start(bf16[16,1024]{1,0:T(8,128)(2,1)S(1)} %shard_map.156), channel_id=1, source_target_pairs={{0,1},{1,0},{2,3},{3,2},{4,5},{5,4},{6,7},{7,6},{8,9},{9,8},{10,11... | collective-permute-start | bytes 98312 | tf_op jit(solution)/shard_map/ppermute | solution.py:108
  25.4 0.3 collective-permute-start.18
  25.7 0.9 %collective-permute-done.18.other_gain_ref = f32[1,512]{1,0:T(1,128)S(1)} collective-permute-done((f32[1,512]{1,0:T(1,128)S(1)}, f32[1,512]{1,0:T(1,128)S(1)}, u32[]{:S(2)}, u32[]{:S(2)}) %collective-permute-start.18) | collective-permute-done | bytes 2080 | tf_op jit(solution)/shard_map/ppermute | solution.py:108
  26.6 0.7 %collective-permute-done.14.third_ref = bf16[16,1024]{1,0:T(8,128)(2,1)S(1)} collective-permute-done((bf16[16,1024]{1,0:T(8,128)(2,1)S(1)}, bf16[16,1024]{1,0:T(8,128)(2,1)S(1)}, u32[]{:S(2)}, u32[]{:S(2)}) %collective-permute-start.14) | collective-permute-done | bytes 32800 | tf_op jit(solution)/shard_map/ppermute | solution.py:209
  27.3 0.4 collective-permute-done.15.second_ref
  27.6 0.3 collective-permute-done.16.first_ref
  28.0 0.2 shard_map.157
  28.1 0.8 %collective-permute-start.19 = (bf16[16,1152]{1,0:T(8,128)(2,1)S(1)}, bf16[16,1152]{1,0:T(8,128)(2,1)S(1)}, u32[]{:S(2)}, u32[]{:S(2)}) collective-permute-start(bf16[16,1152]{1,0:T(8,128)(2,1)S(1)} %get-tuple-element.17.refs_3_), channel_id=1, source_target_pairs={{0,25},{1,0},{2,27},{3,2},{4,29},{5,4},{6,31},{7,6},{8,17},{9,8},{... | collective-permute-start | bytes 110600 | tf_op jit(solution)/shard_map/ppermute | solution.py:209
  29.0 0.8 %collective-permute-start.20 = (bf16[16,1152]{1,0:T(8,128)(2,1)S(1)}, bf16[16,1152]{1,0:T(8,128)(2,1)S(1)}, u32[]{:S(2)}, u32[]{:S(2)}) collective-permute-start(bf16[16,1152]{1,0:T(8,128)(2,1)S(1)} %get-tuple-element.17.refs_3_), channel_id=1, source_target_pairs={{0,17},{1,0},{2,19},{3,2},{4,21},{5,4},{6,23},{7,6},{8,25},{9,8},{... | collective-permute-start | bytes 110600 | tf_op jit(solution)/shard_map/ppermute | solution.py:209
  29.8 0.5 %collective-permute-start.22 = (bf16[16,1152]{1,0:T(8,128)(2,1)S(1)}, bf16[16,1152]{1,0:T(8,128)(2,1)S(1)}, u32[]{:S(2)}, u32[]{:S(2)}) collective-permute-start(bf16[16,1152]{1,0:T(8,128)(2,1)S(1)} %get-tuple-element.17.refs_3_), channel_id=1, source_target_pairs={{0,1},{1,0},{2,3},{3,2},{4,5},{5,4},{6,7},{7,6},{8,9},{9,8},{10,11... | collective-permute-start | bytes 110600 | tf_op jit(solution)/shard_map/ppermute | solution.py:108
  30.3 1.2 %collective-permute-done.23._.refs_6_ = f32[16,512]{1,0:T(8,128)S(1)} collective-permute-done((f32[16,512]{1,0:T(8,128)S(1)}, f32[16,512]{1,0:T(8,128)S(1)}, u32[]{:S(2)}, u32[]{:S(2)}) %collective-permute-start.23) | collective-permute-done | bytes 32800 | tf_op jit(solution)/shard_map/ppermute | solution.py:108
  31.6 1.7 %collective-permute-start.24 = (f32[48,128]{1,0:T(8,128)S(1)}, f32[48,128]{1,0:T(8,128)S(1)}, u32[]{:S(2)}, u32[]{:S(2)}) collective-permute-start(f32[48,128]{1,0:T(8,128)S(1)} %get-tuple-element.19), channel_id=1, source_target_pairs={{0,1},{1,6},{2,3},{3,4},{4,5},{5,2},{6,7},{7,0},{8,9},{9,14},{10,1... | collective-permute-start | bytes 73736 | tf_op jit(solution)/shard_map/ppermute | solution.py:209
  33.3 0.4 %collective-permute-start.25 = (f32[48,128]{1,0:T(8,128)S(1)}, f32[48,128]{1,0:T(8,128)S(1)}, u32[]{:S(2)}, u32[]{:S(2)}) collective-permute-start(f32[48,128]{1,0:T(8,128)S(1)} %get-tuple-element.19), channel_id=1, source_target_pairs={{0,1},{1,4},{2,3},{3,6},{4,5},{5,0},{6,7},{7,2},{8,9},{9,12},{10,1... | collective-permute-start | bytes 73736 | tf_op jit(solution)/shard_map/ppermute | solution.py:209
  33.7 1.6 %collective-permute-start.26 = (f32[48,128]{1,0:T(8,128)S(1)}, f32[48,128]{1,0:T(8,128)S(1)}, u32[]{:S(2)}, u32[]{:S(2)}) collective-permute-start(f32[48,128]{1,0:T(8,128)S(1)} %get-tuple-element.19), channel_id=1, source_target_pairs={{0,1},{1,2},{2,3},{3,0},{4,5},{5,6},{6,7},{7,4},{8,9},{9,10},{10,1... | collective-permute-start | bytes 73736 | tf_op jit(solution)/shard_map/ppermute | solution.py:209
  35.3 0.5 %collective-permute-start.29 = (bf16[48,512]{1,0:T(8,128)(2,1)S(1)}, bf16[48,512]{1,0:T(8,128)(2,1)S(1)}, u32[]{:S(2)}, u32[]{:S(2)}) collective-permute-start(bf16[48,512]{1,0:T(8,128)(2,1)S(1)} %get-tuple-element.21), channel_id=1, source_target_pairs={{0,1},{1,0},{2,3},{3,2},{4,5},{5,4},{6,7},{7,6},{8,9},{9,8},{10,11... | collective-permute-start | bytes 147464 | tf_op jit(solution)/shard_map/ppermute | solution.py:108
  35.8 0.9 %collective-permute-done.24.third_ref = f32[48,128]{1,0:T(8,128)S(1)} collective-permute-done((f32[48,128]{1,0:T(8,128)S(1)}, f32[48,128]{1,0:T(8,128)S(1)}, u32[]{:S(2)}, u32[]{:S(2)}) %collective-permute-start.24) | collective-permute-done | bytes 24608 | tf_op jit(solution)/shard_map/ppermute | solution.py:209
  36.7 0.8 %collective-permute-done.25.second_ref = f32[48,128]{1,0:T(8,128)S(1)} collective-permute-done((f32[48,128]{1,0:T(8,128)S(1)}, f32[48,128]{1,0:T(8,128)S(1)}, u32[]{:S(2)}, u32[]{:S(2)}) %collective-permute-start.25) | collective-permute-done | bytes 24608 | tf_op jit(solution)/shard_map/ppermute | solution.py:209
  37.6 0.1 shard_map.160.refs_8_
  37.7 1.1 %collective-permute-done.28.refs_1_ = f32[48,128]{1,0:T(8,128)S(1)} collective-permute-done((f32[48,128]{1,0:T(8,128)S(1)}, f32[48,128]{1,0:T(8,128)S(1)}, u32[]{:S(2)}, u32[]{:S(2)}) %collective-permute-start.28) | collective-permute-done | bytes 24608 | tf_op jit(solution)/shard_map/ppermute | solution.py:108
  38.8 1.1 %shard_map.161 = (bf16[16,512]{1,0:T(8,128)(2,1)}, f32[2]{0:T(128)}, bf16[16,512]{1,0:T(8,128)(2,1)}) custom-call(f32[48,128]{1,0:T(8,128)S(1)} %shard_map.159.refs_0_, f32[48,128]{1,0:T(8,128)S(1)} %collective-permute-done.28.refs_1_, bf16[64,512]{1,0:T(8,128)(2,1)S(1)} %get-tuple-element.20.refs_2_, bf16[16,1152]{1,0:T(8,128)(2,1)S(1)} %get-tuple-element.17.refs_3_, ...), custom_call_target="tpu_custom_call" | custom-call | tf_op jit(solution)/shard_map/pallas_call | solution.py:765
  (59 shorter events, 0.4 us)
Async XLA Ops:
  0.6 1.9 %collective-permute-start = (bf16[16,512]{1,0:T(8,128)(2,1)}, bf16[16,512]{1,0:T(8,128)(2,1)S(1)}, u32[]{:S(2)}, u32[]{:S(2)}) collective-permute-start(bf16[16,512]{1,0:T(8,128)(2,1)} %own_ref.3), channel_id=1, source_target_pairs={{0,1},{1,0},{2,3},{3,2},{4,5},{5,4},{6,7},{7,6},{8,9},{9,8},{10,11... | collective-permute-start | bytes 49160 | tf_op jit(solution)/shard_map/ppermute | solution.py:108
  1.1 1.4 %copy-start.4 = (bf16[16,512]{1,0:T(8,128)(2,1)S(1)}, bf16[16,512]{1,0:T(8,128)(2,1)}, u32[]{:S(2)}) copy-start(bf16[16,512]{1,0:T(8,128)(2,1)} %own_ref.3) | copy-start | bytes 49156
  1.1 1.4 %copy-start.11 = (f32[512]{0:T(512)S(1)}, f32[512]{0:T(512)}, u32[]{:S(2)}) copy-start(f32[512]{0:T(512)} %param.13) | copy-start | bytes 6148
  1.2 1.4 %collective-permute-start.1 = (f32[1,512]{1,0:T(1,128)}, f32[1,512]{1,0:T(1,128)S(1)}, u32[]{:S(2)}, u32[]{:S(2)}) collective-permute-start(f32[1,512]{1,0:T(1,128)} %bitcast.10), channel_id=1, source_target_pairs={{0,1},{1,0},{2,3},{3,2},{4,5},{5,4},{6,7},{7,6},{8,9},{9,8},{10,11... | collective-permute-start | bytes 6152 | tf_op jit(solution)/shard_map/ppermute | solution.py:108
  1.2 8.6 %collective-permute-start.5 = (bf16[4096,512]{1,0:T(8,128)(2,1)}, bf16[4096,512]{1,0:T(8,128)(2,1)S(1)}, u32[]{:S(2)}, u32[]{:S(2)}) collective-permute-start(bf16[4096,512]{1,0:T(8,128)(2,1)} %refs_4_.1), channel_id=1, source_target_pairs={{0,1},{1,0},{2,3},{3,2},{4,5},{5,4},{6,7},{7,6},{8,9},{9,8},{10,11... | collective-permute-start | bytes 12582920 | tf_op jit(solution)/shard_map/ppermute | solution.py:108
  1.7 5.9 %copy-start.1 = (bf16[4096,512]{1,0:T(8,128)(2,1)S(1)}, bf16[4096,512]{1,0:T(8,128)(2,1)}, u32[]{:S(2)}) copy-start(bf16[4096,512]{1,0:T(8,128)(2,1)} %refs_4_.1) | copy-start | bytes 12582916
  2.7 5.1 %copy-start.2 = (bf16[320,1024]{1,0:T(8,128)(2,1)S(1)}, bf16[320,1024]{1,0:T(8,128)(2,1)}, u32[]{:S(2)}) copy-start(bf16[320,1024]{1,0:T(8,128)(2,1)} %refs_1_.9) | copy-start | bytes 1966084
  2.7 5.1 %copy-start.3 = (bf16[320,1024]{1,0:T(8,128)(2,1)S(1)}, bf16[320,1024]{1,0:T(8,128)(2,1)}, u32[]{:S(2)}) copy-start(bf16[320,1024]{1,0:T(8,128)(2,1)} %refs_2_.5) | copy-start | bytes 1966084
  2.7 5.8 %copy-start.6 = (s32[1,16]{1,0:T(1,128)S(1)}, s32[1,16]{1,0:T(1,128)}, u32[]{:S(2)}) copy-start(s32[1,16]{1,0:T(1,128)} %lengths_ref.1) | copy-start | bytes 196
  2.7 5.8 %copy-start.7 = (s32[1,16]{1,0:T(1,128)S(1)}, s32[1,16]{1,0:T(1,128)}, u32[]{:S(2)}) copy-start(s32[1,16]{1,0:T(1,128)} %order_ref.1) | copy-start | bytes 196
  2.7 5.7 %copy-start.10 = (f32[1,128]{1,0:T(1,128)S(1)}, f32[1,128]{1,0:T(1,128)}, u32[]{:S(2)}) copy-start(f32[1,128]{1,0:T(1,128)} %constant.2.clone.frequency_ref) | copy-start | bytes 1540
  2.7 7.1 %copy-start.8 = (f32[128]{0:T(128)S(1)}, f32[128]{0:T(128)}, u32[]{:S(2)}) copy-start(f32[128]{0:T(128)} %param.15) | copy-start | bytes 1540
  2.7 6.4 %collective-permute-start.2 = (bf16[16,1152]{1,0:T(8,128)(2,1)S(1)}, bf16[16,1152]{1,0:T(8,128)(2,1)S(1)}, u32[]{:S(2)}, u32[]{:S(2)}) collective-permute-start(bf16[16,1152]{1,0:T(8,128)(2,1)S(1)} %shard_map.140.message_ref.refs_3_.pair_ref), channel_id=1, source_target_pairs={{0,7},{1,0},{2,5},{3,2},{4,3},{5,4},{6,1},{7,6},{8,15},{9,8},{10,1... | collective-permute-start | bytes 110600 | tf_op jit(solution)/shard_map/ppermute | solution.py:209
  7.5 2.0 %collective-permute-start.3 = (bf16[16,1152]{1,0:T(8,128)(2,1)S(1)}, bf16[16,1152]{1,0:T(8,128)(2,1)S(1)}, u32[]{:S(2)}, u32[]{:S(2)}) collective-permute-start(bf16[16,1152]{1,0:T(8,128)(2,1)S(1)} %shard_map.140.message_ref.refs_3_.pair_ref), channel_id=1, source_target_pairs={{0,5},{1,0},{2,7},{3,2},{4,1},{5,4},{6,3},{7,6},{8,13},{9,8},{10,1... | collective-permute-start | bytes 110600 | tf_op jit(solution)/shard_map/ppermute | solution.py:209
  7.5 2.3 %collective-permute-start.4 = (bf16[16,1152]{1,0:T(8,128)(2,1)S(1)}, bf16[16,1152]{1,0:T(8,128)(2,1)S(1)}, u32[]{:S(2)}, u32[]{:S(2)}) collective-permute-start(bf16[16,1152]{1,0:T(8,128)(2,1)S(1)} %shard_map.140.message_ref.refs_3_.pair_ref), channel_id=1, source_target_pairs={{0,3},{1,0},{2,1},{3,2},{4,7},{5,4},{6,5},{7,6},{8,11},{9,8},{10,9... | collective-permute-start | bytes 110600 | tf_op jit(solution)/shard_map/ppermute | solution.py:209
  7.9 6.9 %collective-permute-start.7 = (bf16[2,320,1024]{2,1,0:T(8,128)(2,1)S(1)}, bf16[2,320,1024]{2,1,0:T(8,128)(2,1)S(1)}, u32[]{:S(2)}, u32[]{:S(2)}) collective-permute-start(bf16[2,320,1024]{2,1,0:T(8,128)(2,1)S(1)} %shard_map.146), channel_id=1, source_target_pairs={{0,1},{1,0},{2,3},{3,2},{4,5},{5,4},{6,7},{7,6},{8,9},{9,8},{10,11... | collective-permute-start | bytes 3932168 | tf_op jit(solution)/shard_map/ppermute | solution.py:108
  9.9 4.6 %copy-start = (bf16[512,4096]{1,0:T(8,128)(2,1)S(1)}, bf16[512,4096]{1,0:T(8,128)(2,1)}, u32[]{:S(2)}) copy-start(bf16[512,4096]{1,0:T(8,128)(2,1)} %refs_1_.13) | copy-start | bytes 12582916
  9.9 6.6 %collective-permute-start.6 = (bf16[16,1024]{1,0:T(8,128)(2,1)S(1)}, bf16[16,1024]{1,0:T(8,128)(2,1)S(1)}, u32[]{:S(2)}, u32[]{:S(2)}) collective-permute-start(bf16[16,1024]{1,0:T(8,128)(2,1)S(1)} %shard_map.145.query_ref._), channel_id=1, source_target_pairs={{0,1},{1,6},{2,3},{3,4},{4,5},{5,2},{6,7},{7,0},{8,9},{9,14},{10,1... | collective-permute-start | bytes 98312 | tf_op jit(solution)/shard_map/ppermute | solution.py:209
  13.0 4.6 %collective-permute-start.9 = (bf16[16,1024]{1,0:T(8,128)(2,1)S(1)}, bf16[16,1024]{1,0:T(8,128)(2,1)S(1)}, u32[]{:S(2)}, u32[]{:S(2)}) collective-permute-start(bf16[16,1024]{1,0:T(8,128)(2,1)S(1)} %shard_map.145.query_ref._), channel_id=1, source_target_pairs={{0,1},{1,4},{2,3},{3,6},{4,5},{5,0},{6,7},{7,2},{8,9},{9,12},{10,1... | collective-permute-start | bytes 98312 | tf_op jit(solution)/shard_map/ppermute | solution.py:209
  13.8 4.4 %collective-permute-start.11 = (bf16[16,1024]{1,0:T(8,128)(2,1)S(1)}, bf16[16,1024]{1,0:T(8,128)(2,1)S(1)}, u32[]{:S(2)}, u32[]{:S(2)}) collective-permute-start(bf16[16,1024]{1,0:T(8,128)(2,1)S(1)} %shard_map.145.query_ref._), channel_id=1, source_target_pairs={{0,1},{1,2},{2,3},{3,0},{4,5},{5,6},{6,7},{7,4},{8,9},{9,10},{10,1... | collective-permute-start | bytes 98312 | tf_op jit(solution)/shard_map/ppermute | solution.py:209
  14.7 7.4 %collective-permute-start.13 = (bf16[512,4096]{1,0:T(8,128)(2,1)S(1)}, bf16[512,4096]{1,0:T(8,128)(2,1)S(1)}, u32[]{:S(2)}, u32[]{:S(2)}) collective-permute-start(bf16[512,4096]{1,0:T(8,128)(2,1)S(1)} %shard_map.152), channel_id=1, source_target_pairs={{0,1},{1,0},{2,3},{3,2},{4,5},{5,4},{6,7},{7,6},{8,9},{9,8},{10,11... | collective-permute-start | bytes 12582920 | tf_op jit(solution)/shard_map/ppermute | solution.py:108
  17.1 4.9 %collective-permute-start.8 = (bf16[16,1152]{1,0:T(8,128)(2,1)S(1)}, bf16[16,1152]{1,0:T(8,128)(2,1)S(1)}, u32[]{:S(2)}, u32[]{:S(2)}) collective-permute-start(bf16[16,1152]{1,0:T(8,128)(2,1)S(1)} %shard_map.148.refs_5_), channel_id=1, source_target_pairs={{0,7},{1,0},{2,5},{3,2},{4,3},{5,4},{6,1},{7,6},{8,15},{9,8},{10,1... | collective-permute-start | bytes 110600 | tf_op jit(solution)/shard_map/ppermute | solution.py:209
  18.2 3.9 %collective-permute-start.10 = (bf16[16,1152]{1,0:T(8,128)(2,1)S(1)}, bf16[16,1152]{1,0:T(8,128)(2,1)S(1)}, u32[]{:S(2)}, u32[]{:S(2)}) collective-permute-start(bf16[16,1152]{1,0:T(8,128)(2,1)S(1)} %shard_map.149.refs_5_), channel_id=1, source_target_pairs={{0,5},{1,0},{2,7},{3,2},{4,1},{5,4},{6,3},{7,6},{8,13},{9,8},{10,1... | collective-permute-start | bytes 110600 | tf_op jit(solution)/shard_map/ppermute | solution.py:209
  18.7 3.4 %collective-permute-start.12 = (bf16[16,1152]{1,0:T(8,128)(2,1)S(1)}, bf16[16,1152]{1,0:T(8,128)(2,1)S(1)}, u32[]{:S(2)}, u32[]{:S(2)}) collective-permute-start(bf16[16,1152]{1,0:T(8,128)(2,1)S(1)} %shard_map.150), channel_id=1, source_target_pairs={{0,3},{1,0},{2,1},{3,2},{4,7},{5,4},{6,5},{7,6},{8,11},{9,8},{10,9... | collective-permute-start | bytes 110600 | tf_op jit(solution)/shard_map/ppermute | solution.py:209
  22.1 5.2 %collective-permute-start.14 = (bf16[16,1024]{1,0:T(8,128)(2,1)S(1)}, bf16[16,1024]{1,0:T(8,128)(2,1)S(1)}, u32[]{:S(2)}, u32[]{:S(2)}) collective-permute-start(bf16[16,1024]{1,0:T(8,128)(2,1)S(1)} %shard_map.153.refs_3_), channel_id=1, source_target_pairs={{0,1},{1,6},{2,3},{3,4},{4,5},{5,2},{6,7},{7,0},{8,9},{9,14},{10,1... | collective-permute-start | bytes 98312 | tf_op jit(solution)/shard_map/ppermute | solution.py:209
  23.1 4.5 %collective-permute-start.15 = (bf16[16,1024]{1,0:T(8,128)(2,1)S(1)}, bf16[16,1024]{1,0:T(8,128)(2,1)S(1)}, u32[]{:S(2)}, u32[]{:S(2)}) collective-permute-start(bf16[16,1024]{1,0:T(8,128)(2,1)S(1)} %shard_map.154.refs_3_), channel_id=1, source_target_pairs={{0,1},{1,4},{2,3},{3,6},{4,5},{5,0},{6,7},{7,2},{8,9},{9,12},{10,1... | collective-permute-start | bytes 98312 | tf_op jit(solution)/shard_map/ppermute | solution.py:209
  24.4 1.0 %copy-start.5 = (f32[512]{0:T(512)S(1)}, f32[512]{0:T(512)}, u32[]{:S(2)}) copy-start(f32[512]{0:T(512)} %param.19) | copy-start | bytes 6148
  24.4 13.2 %copy-start.9 = (s32[64]{0:T(128)S(1)}, s32[64]{0:T(128)}, u32[]{:S(2)}) copy-start(s32[64]{0:T(128)} %param.22) | copy-start | bytes 772
  24.4 3.6 %collective-permute-start.16 = (bf16[16,1024]{1,0:T(8,128)(2,1)S(1)}, bf16[16,1024]{1,0:T(8,128)(2,1)S(1)}, u32[]{:S(2)}, u32[]{:S(2)}) collective-permute-start(bf16[16,1024]{1,0:T(8,128)(2,1)S(1)} %shard_map.155.refs_3_), channel_id=1, source_target_pairs={{0,1},{1,2},{2,3},{3,0},{4,5},{5,6},{6,7},{7,4},{8,9},{9,10},{10,1... | collective-permute-start | bytes 98312 | tf_op jit(solution)/shard_map/ppermute | solution.py:209
  25.0 3.0 %collective-permute-start.17 = (bf16[16,1024]{1,0:T(8,128)(2,1)S(1)}, bf16[16,1024]{1,0:T(8,128)(2,1)S(1)}, u32[]{:S(2)}, u32[]{:S(2)}) collective-permute-start(bf16[16,1024]{1,0:T(8,128)(2,1)S(1)} %shard_map.156), channel_id=1, source_target_pairs={{0,1},{1,0},{2,3},{3,2},{4,5},{5,4},{6,7},{7,6},{8,9},{9,8},{10,11... | collective-permute-start | bytes 98312 | tf_op jit(solution)/shard_map/ppermute | solution.py:108
  25.4 1.2 %collective-permute-start.18 = (f32[1,512]{1,0:T(1,128)S(1)}, f32[1,512]{1,0:T(1,128)S(1)}, u32[]{:S(2)}, u32[]{:S(2)}) collective-permute-start(f32[1,512]{1,0:T(1,128)S(1)} %bitcast.4), channel_id=1, source_target_pairs={{0,1},{1,0},{2,3},{3,2},{4,5},{5,4},{6,7},{7,6},{8,9},{9,8},{10,11... | collective-permute-start | bytes 6152 | tf_op jit(solution)/shard_map/ppermute | solution.py:108
  28.1 3.4 %collective-permute-start.19 = (bf16[16,1152]{1,0:T(8,128)(2,1)S(1)}, bf16[16,1152]{1,0:T(8,128)(2,1)S(1)}, u32[]{:S(2)}, u32[]{:S(2)}) collective-permute-start(bf16[16,1152]{1,0:T(8,128)(2,1)S(1)} %get-tuple-element.17.refs_3_), channel_id=1, source_target_pairs={{0,25},{1,0},{2,27},{3,2},{4,29},{5,4},{6,31},{7,6},{8,17},{9,8},{... | collective-permute-start | bytes 110600 | tf_op jit(solution)/shard_map/ppermute | solution.py:209
  29.0 2.5 %collective-permute-start.20 = (bf16[16,1152]{1,0:T(8,128)(2,1)S(1)}, bf16[16,1152]{1,0:T(8,128)(2,1)S(1)}, u32[]{:S(2)}, u32[]{:S(2)}) collective-permute-start(bf16[16,1152]{1,0:T(8,128)(2,1)S(1)} %get-tuple-element.17.refs_3_), channel_id=1, source_target_pairs={{0,17},{1,0},{2,19},{3,2},{4,21},{5,4},{6,23},{7,6},{8,25},{9,8},{... | collective-permute-start | bytes 110600 | tf_op jit(solution)/shard_map/ppermute | solution.py:209
  29.8 1.7 %collective-permute-start.21 = (bf16[16,1152]{1,0:T(8,128)(2,1)S(1)}, bf16[16,1152]{1,0:T(8,128)(2,1)S(1)}, u32[]{:S(2)}, u32[]{:S(2)}) collective-permute-start(bf16[16,1152]{1,0:T(8,128)(2,1)S(1)} %get-tuple-element.17.refs_3_), channel_id=1, source_target_pairs={{0,9},{1,0},{2,11},{3,2},{4,13},{5,4},{6,15},{7,6},{8,1},{9,8},{10... | collective-permute-start | bytes 110600 | tf_op jit(solution)/shard_map/ppermute | solution.py:209
  29.8 1.7 %collective-permute-start.22 = (bf16[16,1152]{1,0:T(8,128)(2,1)S(1)}, bf16[16,1152]{1,0:T(8,128)(2,1)S(1)}, u32[]{:S(2)}, u32[]{:S(2)}) collective-permute-start(bf16[16,1152]{1,0:T(8,128)(2,1)S(1)} %get-tuple-element.17.refs_3_), channel_id=1, source_target_pairs={{0,1},{1,0},{2,3},{3,2},{4,5},{5,4},{6,7},{7,6},{8,9},{9,8},{10,11... | collective-permute-start | bytes 110600 | tf_op jit(solution)/shard_map/ppermute | solution.py:108
  30.3 1.2 %collective-permute-start.23 = (f32[16,512]{1,0:T(8,128)S(1)}, f32[16,512]{1,0:T(8,128)S(1)}, u32[]{:S(2)}, u32[]{:S(2)}) collective-permute-start(f32[16,512]{1,0:T(8,128)S(1)} %get-tuple-element.18), channel_id=1, source_target_pairs={{0,1},{1,0},{2,3},{3,2},{4,5},{5,4},{6,7},{7,6},{8,9},{9,8},{10,11... | collective-permute-start | bytes 98312 | tf_op jit(solution)/shard_map/ppermute | solution.py:108
  31.6 5.1 %collective-permute-start.24 = (f32[48,128]{1,0:T(8,128)S(1)}, f32[48,128]{1,0:T(8,128)S(1)}, u32[]{:S(2)}, u32[]{:S(2)}) collective-permute-start(f32[48,128]{1,0:T(8,128)S(1)} %get-tuple-element.19), channel_id=1, source_target_pairs={{0,1},{1,6},{2,3},{3,4},{4,5},{5,2},{6,7},{7,0},{8,9},{9,14},{10,1... | collective-permute-start | bytes 73736 | tf_op jit(solution)/shard_map/ppermute | solution.py:209
  33.3 4.2 %collective-permute-start.25 = (f32[48,128]{1,0:T(8,128)S(1)}, f32[48,128]{1,0:T(8,128)S(1)}, u32[]{:S(2)}, u32[]{:S(2)}) collective-permute-start(f32[48,128]{1,0:T(8,128)S(1)} %get-tuple-element.19), channel_id=1, source_target_pairs={{0,1},{1,4},{2,3},{3,6},{4,5},{5,0},{6,7},{7,2},{8,9},{9,12},{10,1... | collective-permute-start | bytes 73736 | tf_op jit(solution)/shard_map/ppermute | solution.py:209
  33.7 3.8 %collective-permute-start.26 = (f32[48,128]{1,0:T(8,128)S(1)}, f32[48,128]{1,0:T(8,128)S(1)}, u32[]{:S(2)}, u32[]{:S(2)}) collective-permute-start(f32[48,128]{1,0:T(8,128)S(1)} %get-tuple-element.19), channel_id=1, source_target_pairs={{0,1},{1,2},{2,3},{3,0},{4,5},{5,6},{6,7},{7,4},{8,9},{9,10},{10,1... | collective-permute-start | bytes 73736 | tf_op jit(solution)/shard_map/ppermute | solution.py:209
  35.3 2.2 %collective-permute-start.27 = (f32[48,128]{1,0:T(8,128)S(1)}, f32[48,128]{1,0:T(8,128)S(1)}, u32[]{:S(2)}, u32[]{:S(2)}) collective-permute-start(f32[48,128]{1,0:T(8,128)S(1)} %get-tuple-element.19), channel_id=1, source_target_pairs={{0,1},{1,0},{2,3},{3,2},{4,5},{5,4},{6,7},{7,6},{8,9},{9,8},{10,11... | collective-permute-start | bytes 73736 | tf_op jit(solution)/shard_map/ppermute | solution.py:108
  35.3 3.5 %collective-permute-start.29 = (bf16[48,512]{1,0:T(8,128)(2,1)S(1)}, bf16[48,512]{1,0:T(8,128)(2,1)S(1)}, u32[]{:S(2)}, u32[]{:S(2)}) collective-permute-start(bf16[48,512]{1,0:T(8,128)(2,1)S(1)} %get-tuple-element.21), channel_id=1, source_target_pairs={{0,1},{1,0},{2,3},{3,2},{4,5},{5,4},{6,7},{7,6},{8,9},{9,8},{10,11... | collective-permute-start | bytes 147464 | tf_op jit(solution)/shard_map/ppermute | solution.py:108
  37.5 1.3 %collective-permute-start.28 = (f32[48,128]{1,0:T(8,128)S(1)}, f32[48,128]{1,0:T(8,128)S(1)}, u32[]{:S(2)}, u32[]{:S(2)}) collective-permute-start(f32[48,128]{1,0:T(8,128)S(1)} %shard_map.159.refs_0_), channel_id=1, source_target_pairs={{0,1},{1,0},{2,3},{3,2},{4,5},{5,4},{6,7},{7,6},{8,9},{9,8},{10,11... | collective-permute-start | bytes 73736 | tf_op jit(solution)/shard_map/ppermute | solution.py:108

commit v10 on v9

--- a/solution.py
+++ b/solution.py
@@ -479,9 +479,10 @@
                 vectors, vectors, (((1,), (1,)), ((), ())), preferred_element_type=jnp.float32
             )
         half = gram.shape[0] // 2
-        out_ref[:half, : 2 * half] = gram[:half]
-        out_ref[:half, 2 * half :] = gram[half:]
-        out_ref[half:, :] = jnp.broadcast_to(squares, (rows, 128))
+        lane = lax.broadcasted_iota(jnp.int32, (half, 2 * half), 1)
+        squares = jnp.concatenate([squares] * (half // rows), axis=0)
+        out_ref[:, : 2 * half] = gram[:half]
+        out_ref[:, 2 * half :] = jnp.where(lane < half, squares, gram[half:])
 
 
 def sum_grams(third_ref, second_ref, first_ref, own_ref, *refs):
@@ -532,38 +533,47 @@
     rows = scaled_ref.shape[0]
     half = count // 2
     summed = jnp.where(leads, other_summed_ref[...], summed_ref[...])
-    gram = jnp.concatenate([summed[:half, :count], summed[:half, count:]], axis=0)
-    squares = summed[half:, :1]
-    shape = (count, count)
-    row = lax.broadcasted_iota(jnp.int32, shape, 0)
-    column = lax.broadcasted_iota(jnp.int32, shape, 1)
+    upper, lower = summed[:, :count], summed[:, count:]
+    squares = lower[:rows, :1]
+    row = lax.broadcasted_iota(jnp.int32, upper.shape, 0)
+    column = lax.broadcasted_iota(jnp.int32, upper.shape, 1)
     diagonal = row == column
-    on_diagonal = jnp.where(diagonal, gram, 0.0)
-    row_scale = lax.rsqrt(jnp.sum(on_diagonal, axis=1, keepdims=True))
-    column_scale = lax.rsqrt(jnp.sum(on_diagonal, axis=0, keepdims=True))
-    cosines = gram * row_scale * column_scale
+    lower_diagonal = row + half == column
+    lower = jnp.where(column >= half, lower, 0.0)
+    upper_norms = jnp.where(diagonal, upper, 0.0)
+    lower_norms = jnp.where(lower_diagonal, lower, 0.0)
+    row_scale = lax.rsqrt(jnp.sum(upper_norms, axis=1, keepdims=True))
+    lower_scale = lax.rsqrt(jnp.sum(lower_norms, axis=1, keepdims=True))
+    column_scale = lax.rsqrt(jnp.sum(upper_norms + lower_norms, axis=0, keepdims=True))
+    cosines = upper * row_scale * column_scale
     logits = cosines * (1.0 / SOFTMAX_WARMTH)
     powers = jnp.where(diagonal, 0.0, jnp.exp(logits))
+    lower_powers = jnp.exp(lower * lower_scale * column_scale * (1.0 / SOFTMAX_WARMTH))
+    lower_powers = jnp.where((column >= half) & ~lower_diagonal, lower_powers, 0.0)
+    mirrored = jnp.sum(jnp.where(column >= half, powers, 0.0), axis=1, keepdims=True)
+    column_sum = jnp.sum(
+        powers + lower_powers + jnp.where(diagonal, mirrored, 0.0), axis=0, keepdims=True
+    )
+    cosines, logits, powers = cosines[:rows], logits[:rows], powers[:rows]
     row_sum = jnp.sum(powers, axis=1, keepdims=True)
-    column_sum = jnp.sum(powers, axis=0, keepdims=True)
-    weights = (powers * (1.0 / row_sum + 1.0 / column_sum) - partner_ref[1])[:rows]
-    target = jnp.sum(partner_ref[0] * logits, axis=1, keepdims=True)
+    weights = powers * (1.0 / row_sum + 1.0 / column_sum) - partner_ref[1, :rows]
+    target = jnp.sum(partner_ref[0, :rows] * logits, axis=1, keepdims=True)
     loss = jnp.log(row_sum) - target
     own = loss_ref.shape[0]
-    index = lax.broadcasted_iota(jnp.int32, (count, 1), 0)
+    index = lax.broadcasted_iota(jnp.int32, (rows, 1), 0)
     for i in range(own):
         loss_ref[i] = jnp.sum(jnp.where(index == me * own + i, loss, 0.0))
-    inner = jnp.sum(weights * cosines[:rows], axis=1, keepdims=True)
+    inner = jnp.sum(weights * cosines, axis=1, keepdims=True)
     scaled_weights = weights * column_scale
-    upper = scaled_weights.astype(jnp.bfloat16)
-    lower = (scaled_weights - upper.astype(jnp.float32)).astype(jnp.bfloat16)
+    coarse = scaled_weights.astype(jnp.bfloat16)
+    fine = (scaled_weights - coarse.astype(jnp.float32)).astype(jnp.bfloat16)
     own_scale = row_scale[:rows]
     pooled_scale = lax.rsqrt(squares / model_width + EPSILON)
     grad_gain = gain_ref[...] * (model_width**0.5 / SOFTMAX_WARMTH)
 
     def write(vectors, scaled):
-        gradient = jnp.dot(upper, vectors, preferred_element_type=jnp.float32) + jnp.dot(
-            lower, vectors, preferred_element_type=jnp.float32
+        gradient = jnp.dot(coarse, vectors, preferred_element_type=jnp.float32) + jnp.dot(
+            fine, vectors, preferred_element_type=jnp.float32
         )
         gradient = (gradient - scaled * (own_scale * inner)) * own_scale
         grad_ref[...] = (gradient * grad_gain).astype(jnp.bfloat16)
@@ -741,7 +751,7 @@
     gram, near, far = in_vmem(
         gram_part,
         (
-            shaped((total // 2 + stmts, 128), f32),
+            shaped((total // 2, 128), f32),
             shaped((total, width), bf16),
             shaped((total - stmts, width), bf16),
         ),
@@ -756,6 +766,7 @@
         shaped(gram.shape, f32),
         *received[::-1],
         flip(gram, "pack", 1),
+        flops=1 << 30,
     )
     masks = in_vmem(
         lambda *refs: partner_masks(*refs, rows=stmts),

time: 40.1 us -> 39.9 us (level)
  no operation moved by 1% of the time
where the time goes in v10:
time: 39.9 us; the launch traced here: 39.7 us
  starting transfers between devices  21.3 us (53%)
  waiting for transfers between devices  13.6 us (34%)
  Pallas kernels  3.96 us (10%)
  between operations  0.82 us (2%)
    ppermute x18, starting transfers between devices, send_across(): return lax.ppermute(array, ('dp', 'pack'), pairs)  17.9 us
    ppermute x18, waiting for transfers between devices, send_across(): return lax.ppermute(array, ('dp', 'pack'), pairs)  9.62 us
    ppermute x12, waiting for transfers between devices, flip(): return lax.ppermute(array, axis, [(i, i ^ offset) for i in range(size)])  3.99 us
    ppermute x12, starting transfers between devices, flip(): return lax.ppermute(array, axis, [(i, i ^ offset) for i in range(size)])  3.42 us
    pallas_call x21, Pallas kernels, in_vmem(): pl.pallas_call(body, out_shape=outputs, in_specs=[whole] * len(operands),...  2.88 us
    pallas_call x1, Pallas kernels, core_roles(): pl.pallas_call(lambda *refs: losses_and_gradient(*refs, model_width=model...  1.08 us
  transfers between devices with their start and end apart: 30, of which 17 were waited for; matrix products, arithmetic and copies ran while one was open for 0% of the time, Pallas kernels for 7%

profile of v10, /device:TPU:0, one launch (start us, length us, event | category | flops | bytes accessed | tf_op | source)
XLA Modules:
  0.0 39.7 jit_solution(11761358258786384212)
XLA Ops:
  0.6 0.5 %collective-permute-start = (bf16[16,512]{1,0:T(8,128)(2,1)}, bf16[16,512]{1,0:T(8,128)(2,1)S(1)}, u32[]{:S(2)}, u32[]{:S(2)}) collective-permute-start(bf16[16,512]{1,0:T(8,128)(2,1)} %own_ref.3), channel_id=1, source_target_pairs={{0,1},{1,0},{2,3},{3,2},{4,5},{5,4},{6,7},{7,6},{8,9},{9,8},{10,11... | collective-permute-start | bytes 49160 | tf_op jit(solution)/shard_map/ppermute | solution.py:108
  1.2 0.1 collective-permute-start.1
  1.2 0.4 %collective-permute-start.5 = (bf16[4096,512]{1,0:T(8,128)(2,1)}, bf16[4096,512]{1,0:T(8,128)(2,1)S(1)}, u32[]{:S(2)}, u32[]{:S(2)}) collective-permute-start(bf16[4096,512]{1,0:T(8,128)(2,1)} %refs_4_.1), channel_id=1, source_target_pairs={{0,1},{1,0},{2,3},{3,2},{4,5},{5,4},{6,7},{7,6},{8,9},{9,8},{10,11... | collective-permute-start | bytes 12582920 | tf_op jit(solution)/shard_map/ppermute | solution.py:108
  1.7 0.9 %collective-permute-done.1.other_gain_ref = f32[1,512]{1,0:T(1,128)S(1)} collective-permute-done((f32[1,512]{1,0:T(1,128)}, f32[1,512]{1,0:T(1,128)S(1)}, u32[]{:S(2)}, u32[]{:S(2)}) %collective-permute-start.1) | collective-permute-done | bytes 2080 | tf_op jit(solution)/shard_map/ppermute | solution.py:108
  2.5 0.2 shard_map.140.message_ref.refs_3_.pair_ref
  2.7 4.8 %collective-permute-start.2 = (bf16[16,1152]{1,0:T(8,128)(2,1)S(1)}, bf16[16,1152]{1,0:T(8,128)(2,1)S(1)}, u32[]{:S(2)}, u32[]{:S(2)}) collective-permute-start(bf16[16,1152]{1,0:T(8,128)(2,1)S(1)} %shard_map.140.message_ref.refs_3_.pair_ref), channel_id=1, source_target_pairs={{0,7},{1,0},{2,5},{3,2},{4,3},{5,4},{6,1},{7,6},{8,15},{9,8},{10,1... | collective-permute-start | bytes 110600 | tf_op jit(solution)/shard_map/ppermute | solution.py:209
  7.5 0.2 shard_map.143.refs_7_._
  7.8 0.1 shard_map.146
  7.9 0.6 %collective-permute-start.7 = (bf16[2,320,1024]{2,1,0:T(8,128)(2,1)S(1)}, bf16[2,320,1024]{2,1,0:T(8,128)(2,1)S(1)}, u32[]{:S(2)}, u32[]{:S(2)}) collective-permute-start(bf16[2,320,1024]{2,1,0:T(8,128)(2,1)S(1)} %shard_map.146), channel_id=1, source_target_pairs={{0,1},{1,0},{2,3},{3,2},{4,5},{5,4},{6,7},{7,6},{8,9},{9,8},{10,11... | collective-permute-start | bytes 3932168 | tf_op jit(solution)/shard_map/ppermute | solution.py:108
  8.5 0.2 shard_map.141
  8.6 0.5 %collective-permute-done.2.refs_0_ = bf16[16,1152]{1,0:T(8,128)(2,1)S(1)} collective-permute-done((bf16[16,1152]{1,0:T(8,128)(2,1)S(1)}, bf16[16,1152]{1,0:T(8,128)(2,1)S(1)}, u32[]{:S(2)}, u32[]{:S(2)}) %collective-permute-start.2) | collective-permute-done | bytes 36896 | tf_op jit(solution)/shard_map/ppermute | solution.py:209
  9.2 0.3 collective-permute-done.3.refs_1_
  9.5 0.3 collective-permute-done.4.refs_2_
  9.9 3.1 %collective-permute-start.6 = (bf16[16,1024]{1,0:T(8,128)(2,1)S(1)}, bf16[16,1024]{1,0:T(8,128)(2,1)S(1)}, u32[]{:S(2)}, u32[]{:S(2)}) collective-permute-start(bf16[16,1024]{1,0:T(8,128)(2,1)S(1)} %shard_map.145.query_ref._), channel_id=1, source_target_pairs={{0,1},{1,6},{2,3},{3,4},{4,5},{5,2},{6,7},{7,0},{8,9},{9,14},{10,1... | collective-permute-start | bytes 98312 | tf_op jit(solution)/shard_map/ppermute | solution.py:209
  13.0 0.8 %collective-permute-start.9 = (bf16[16,1024]{1,0:T(8,128)(2,1)S(1)}, bf16[16,1024]{1,0:T(8,128)(2,1)S(1)}, u32[]{:S(2)}, u32[]{:S(2)}) collective-permute-start(bf16[16,1024]{1,0:T(8,128)(2,1)S(1)} %shard_map.145.query_ref._), channel_id=1, source_target_pairs={{0,1},{1,4},{2,3},{3,6},{4,5},{5,0},{6,7},{7,2},{8,9},{9,12},{10,1... | collective-permute-start | bytes 98312 | tf_op jit(solution)/shard_map/ppermute | solution.py:209
  13.8 0.6 %collective-permute-start.11 = (bf16[16,1024]{1,0:T(8,128)(2,1)S(1)}, bf16[16,1024]{1,0:T(8,128)(2,1)S(1)}, u32[]{:S(2)}, u32[]{:S(2)}) collective-permute-start(bf16[16,1024]{1,0:T(8,128)(2,1)S(1)} %shard_map.145.query_ref._), channel_id=1, source_target_pairs={{0,1},{1,2},{2,3},{3,0},{4,5},{5,6},{6,7},{7,4},{8,9},{9,10},{10,1... | collective-permute-start | bytes 98312 | tf_op jit(solution)/shard_map/ppermute | solution.py:209
  14.4 0.3 shard_map.152
  14.8 1.7 %collective-permute-done.6.refs_0_ = bf16[16,1024]{1,0:T(8,128)(2,1)S(1)} collective-permute-done((bf16[16,1024]{1,0:T(8,128)(2,1)S(1)}, bf16[16,1024]{1,0:T(8,128)(2,1)S(1)}, u32[]{:S(2)}, u32[]{:S(2)}) %collective-permute-start.6) | collective-permute-done | bytes 32800 | tf_op jit(solution)/shard_map/ppermute | solution.py:209
  16.5 0.5 %shard_map.148.refs_5_ = bf16[16,1152]{1,0:T(8,128)(2,1)S(1)} custom-call(bf16[16,1024]{1,0:T(8,128)(2,1)S(1)} %collective-permute-done.6.refs_0_, bf16[320,1024]{1,0:T(8,128)(2,1)S(1)} %copy-done.2, bf16[320,1024]{1,0:T(8,128)(2,1)S(1)} %copy-done.3, bf16[2,320,1024]{2,1,0:T(8,128)(2,1)S(1)} %collective-permute-done.7.other_ref.refs_3_, ...), custom_call_target="tpu_custom_call" | custom-call | flops 17179869184 | bytes 2736128 | tf_op jit(solution)/shard_map/pallas_call | solution.py:114
  17.1 0.2 collective-permute-start.8
  17.2 0.4 collective-permute-done.9.refs_0_
  17.6 0.5 %shard_map.149.refs_5_ = bf16[16,1152]{1,0:T(8,128)(2,1)S(1)} custom-call(bf16[16,1024]{1,0:T(8,128)(2,1)S(1)} %collective-permute-done.9.refs_0_, bf16[320,1024]{1,0:T(8,128)(2,1)S(1)} %copy-done.2, bf16[320,1024]{1,0:T(8,128)(2,1)S(1)} %copy-done.3, bf16[2,320,1024]{2,1,0:T(8,128)(2,1)S(1)} %collective-permute-done.7.other_ref.refs_3_, ...), custom_call_target="tpu_custom_call" | custom-call | flops 17179869184 | bytes 2707456 | tf_op jit(solution)/shard_map/pallas_call | solution.py:114
  18.2 0.5 %shard_map.150 = bf16[16,1152]{1,0:T(8,128)(2,1)S(1)} custom-call(bf16[16,1024]{1,0:T(8,128)(2,1)S(1)} %collective-permute-done.11.refs_0_, bf16[320,1024]{1,0:T(8,128)(2,1)S(1)} %copy-done.2, bf16[320,1024]{1,0:T(8,128)(2,1)S(1)} %copy-done.3, bf16[2,320,1024]{2,1,0:T(8,128)(2,1)S(1)} %collective-permute-done.7.other_ref.refs_3_, ...), custom_call_target="tpu_custom_call" | custom-call | flops 17179869184 | bytes 2707456 | tf_op jit(solution)/shard_map/pallas_call | solution.py:114
  18.8 3.2 %collective-permute-done.8.third_ref = bf16[16,1152]{1,0:T(8,128)(2,1)S(1)} collective-permute-done((bf16[16,1152]{1,0:T(8,128)(2,1)S(1)}, bf16[16,1152]{1,0:T(8,128)(2,1)S(1)}, u32[]{:S(2)}, u32[]{:S(2)}) %collective-permute-start.8) | collective-permute-done | bytes 36896 | tf_op jit(solution)/shard_map/ppermute | solution.py:209
  22.1 1.0 %collective-permute-start.14 = (bf16[16,1024]{1,0:T(8,128)(2,1)S(1)}, bf16[16,1024]{1,0:T(8,128)(2,1)S(1)}, u32[]{:S(2)}, u32[]{:S(2)}) collective-permute-start(bf16[16,1024]{1,0:T(8,128)(2,1)S(1)} %shard_map.153.refs_3_), channel_id=1, source_target_pairs={{0,1},{1,6},{2,3},{3,4},{4,5},{5,2},{6,7},{7,0},{8,9},{9,14},{10,1... | collective-permute-start | bytes 98312 | tf_op jit(solution)/shard_map/ppermute | solution.py:209
  23.1 1.2 %collective-permute-start.15 = (bf16[16,1024]{1,0:T(8,128)(2,1)S(1)}, bf16[16,1024]{1,0:T(8,128)(2,1)S(1)}, u32[]{:S(2)}, u32[]{:S(2)}) collective-permute-start(bf16[16,1024]{1,0:T(8,128)(2,1)S(1)} %shard_map.154.refs_3_), channel_id=1, source_target_pairs={{0,1},{1,4},{2,3},{3,6},{4,5},{5,0},{6,7},{7,2},{8,9},{9,12},{10,1... | collective-permute-start | bytes 98312 | tf_op jit(solution)/shard_map/ppermute | solution.py:209
  24.4 0.6 %collective-permute-start.16 = (bf16[16,1024]{1,0:T(8,128)(2,1)S(1)}, bf16[16,1024]{1,0:T(8,128)(2,1)S(1)}, u32[]{:S(2)}, u32[]{:S(2)}) collective-permute-start(bf16[16,1024]{1,0:T(8,128)(2,1)S(1)} %shard_map.155.refs_3_), channel_id=1, source_target_pairs={{0,1},{1,2},{2,3},{3,0},{4,5},{5,6},{6,7},{7,4},{8,9},{9,10},{10,1... | collective-permute-start | bytes 98312 | tf_op jit(solution)/shard_map/ppermute | solution.py:209
  25.0 0.4 collective-permute-start.17
  25.4 0.3 collective-permute-start.18
  25.7 0.9 %collective-permute-done.18.other_gain_ref = f32[1,512]{1,0:T(1,128)S(1)} collective-permute-done((f32[1,512]{1,0:T(1,128)S(1)}, f32[1,512]{1,0:T(1,128)S(1)}, u32[]{:S(2)}, u32[]{:S(2)}) %collective-permute-start.18) | collective-permute-done | bytes 2080 | tf_op jit(solution)/shard_map/ppermute | solution.py:108
  26.5 0.7 %collective-permute-done.14.third_ref = bf16[16,1024]{1,0:T(8,128)(2,1)S(1)} collective-permute-done((bf16[16,1024]{1,0:T(8,128)(2,1)S(1)}, bf16[16,1024]{1,0:T(8,128)(2,1)S(1)}, u32[]{:S(2)}, u32[]{:S(2)}) %collective-permute-start.14) | collective-permute-done | bytes 32800 | tf_op jit(solution)/shard_map/ppermute | solution.py:209
  27.3 0.4 collective-permute-done.15.second_ref
  27.6 0.3 collective-permute-done.16.first_ref
  28.0 0.2 shard_map.157
  28.1 0.8 %collective-permute-start.19 = (bf16[16,1152]{1,0:T(8,128)(2,1)S(1)}, bf16[16,1152]{1,0:T(8,128)(2,1)S(1)}, u32[]{:S(2)}, u32[]{:S(2)}) collective-permute-start(bf16[16,1152]{1,0:T(8,128)(2,1)S(1)} %get-tuple-element.17.refs_3_), channel_id=1, source_target_pairs={{0,25},{1,0},{2,27},{3,2},{4,29},{5,4},{6,31},{7,6},{8,17},{9,8},{... | collective-permute-start | bytes 110600 | tf_op jit(solution)/shard_map/ppermute | solution.py:209
  29.0 0.8 %collective-permute-start.20 = (bf16[16,1152]{1,0:T(8,128)(2,1)S(1)}, bf16[16,1152]{1,0:T(8,128)(2,1)S(1)}, u32[]{:S(2)}, u32[]{:S(2)}) collective-permute-start(bf16[16,1152]{1,0:T(8,128)(2,1)S(1)} %get-tuple-element.17.refs_3_), channel_id=1, source_target_pairs={{0,17},{1,0},{2,19},{3,2},{4,21},{5,4},{6,23},{7,6},{8,25},{9,8},{... | collective-permute-start | bytes 110600 | tf_op jit(solution)/shard_map/ppermute | solution.py:209
  29.8 0.5 %collective-permute-start.22 = (bf16[16,1152]{1,0:T(8,128)(2,1)S(1)}, bf16[16,1152]{1,0:T(8,128)(2,1)S(1)}, u32[]{:S(2)}, u32[]{:S(2)}) collective-permute-start(bf16[16,1152]{1,0:T(8,128)(2,1)S(1)} %get-tuple-element.17.refs_3_), channel_id=1, source_target_pairs={{0,1},{1,0},{2,3},{3,2},{4,5},{5,4},{6,7},{7,6},{8,9},{9,8},{10,11... | collective-permute-start | bytes 110600 | tf_op jit(solution)/shard_map/ppermute | solution.py:108
  30.3 1.2 %collective-permute-done.23._.refs_6_ = f32[16,512]{1,0:T(8,128)S(1)} collective-permute-done((f32[16,512]{1,0:T(8,128)S(1)}, f32[16,512]{1,0:T(8,128)S(1)}, u32[]{:S(2)}, u32[]{:S(2)}) %collective-permute-start.23) | collective-permute-done | bytes 32800 | tf_op jit(solution)/shard_map/ppermute | solution.py:108
  31.6 1.7 %collective-permute-start.24 = (f32[32,128]{1,0:T(8,128)S(1)}, f32[32,128]{1,0:T(8,128)S(1)}, u32[]{:S(2)}, u32[]{:S(2)}) collective-permute-start(f32[32,128]{1,0:T(8,128)S(1)} %get-tuple-element.19), channel_id=1, source_target_pairs={{0,1},{1,6},{2,3},{3,4},{4,5},{5,2},{6,7},{7,0},{8,9},{9,14},{10,1... | collective-permute-start | bytes 49160 | tf_op jit(solution)/shard_map/ppermute | solution.py:209
  33.3 0.4 %collective-permute-start.25 = (f32[32,128]{1,0:T(8,128)S(1)}, f32[32,128]{1,0:T(8,128)S(1)}, u32[]{:S(2)}, u32[]{:S(2)}) collective-permute-start(f32[32,128]{1,0:T(8,128)S(1)} %get-tuple-element.19), channel_id=1, source_target_pairs={{0,1},{1,4},{2,3},{3,6},{4,5},{5,0},{6,7},{7,2},{8,9},{9,12},{10,1... | collective-permute-start | bytes 49160 | tf_op jit(solution)/shard_map/ppermute | solution.py:209
  33.7 1.6 %collective-permute-start.26 = (f32[32,128]{1,0:T(8,128)S(1)}, f32[32,128]{1,0:T(8,128)S(1)}, u32[]{:S(2)}, u32[]{:S(2)}) collective-permute-start(f32[32,128]{1,0:T(8,128)S(1)} %get-tuple-element.19), channel_id=1, source_target_pairs={{0,1},{1,2},{2,3},{3,0},{4,5},{5,6},{6,7},{7,4},{8,9},{9,10},{10,1... | collective-permute-start | bytes 49160 | tf_op jit(solution)/shard_map/ppermute | solution.py:209
  35.3 0.5 %collective-permute-start.29 = (bf16[48,512]{1,0:T(8,128)(2,1)S(1)}, bf16[48,512]{1,0:T(8,128)(2,1)S(1)}, u32[]{:S(2)}, u32[]{:S(2)}) collective-permute-start(bf16[48,512]{1,0:T(8,128)(2,1)S(1)} %get-tuple-element.21), channel_id=1, source_target_pairs={{0,1},{1,0},{2,3},{3,2},{4,5},{5,4},{6,7},{7,6},{8,9},{9,8},{10,11... | collective-permute-start | bytes 147464 | tf_op jit(solution)/shard_map/ppermute | solution.py:108
  35.8 0.8 %collective-permute-done.24.third_ref = f32[32,128]{1,0:T(8,128)S(1)} collective-permute-done((f32[32,128]{1,0:T(8,128)S(1)}, f32[32,128]{1,0:T(8,128)S(1)}, u32[]{:S(2)}, u32[]{:S(2)}) %collective-permute-start.24) | collective-permute-done | bytes 16416 | tf_op jit(solution)/shard_map/ppermute | solution.py:209
  36.6 0.8 %collective-permute-done.25.second_ref = f32[32,128]{1,0:T(8,128)S(1)} collective-permute-done((f32[32,128]{1,0:T(8,128)S(1)}, f32[32,128]{1,0:T(8,128)S(1)}, u32[]{:S(2)}, u32[]{:S(2)}) %collective-permute-start.25) | collective-permute-done | bytes 16416 | tf_op jit(solution)/shard_map/ppermute | solution.py:209
  37.4 0.1 collective-permute-start.28
  37.5 0.1 shard_map.160.refs_8_
  37.6 1.0 %collective-permute-done.28.refs_1_ = f32[32,128]{1,0:T(8,128)S(1)} collective-permute-done((f32[32,128]{1,0:T(8,128)S(1)}, f32[32,128]{1,0:T(8,128)S(1)}, u32[]{:S(2)}, u32[]{:S(2)}) %collective-permute-start.28) | collective-permute-done | bytes 16416 | tf_op jit(solution)/shard_map/ppermute | solution.py:108
  38.6 1.1 %shard_map.161 = (bf16[16,512]{1,0:T(8,128)(2,1)}, f32[2]{0:T(128)}, bf16[16,512]{1,0:T(8,128)(2,1)}) custom-call(f32[32,128]{1,0:T(8,128)S(1)} %shard_map.159.refs_0_, f32[32,128]{1,0:T(8,128)S(1)} %collective-permute-done.28.refs_1_, bf16[64,512]{1,0:T(8,128)(2,1)S(1)} %get-tuple-element.20.refs_2_, bf16[16,1152]{1,0:T(8,128)(2,1)S(1)} %get-tuple-element.17.refs_3_, ...), custom_call_target="tpu_custom_call" | custom-call | tf_op jit(solution)/shard_map/pallas_call | solution.py:776
  (59 shorter events, 0.4 us)
Async XLA Ops:
  0.6 1.9 %collective-permute-start = (bf16[16,512]{1,0:T(8,128)(2,1)}, bf16[16,512]{1,0:T(8,128)(2,1)S(1)}, u32[]{:S(2)}, u32[]{:S(2)}) collective-permute-start(bf16[16,512]{1,0:T(8,128)(2,1)} %own_ref.3), channel_id=1, source_target_pairs={{0,1},{1,0},{2,3},{3,2},{4,5},{5,4},{6,7},{7,6},{8,9},{9,8},{10,11... | collective-permute-start | bytes 49160 | tf_op jit(solution)/shard_map/ppermute | solution.py:108
  1.1 1.4 %copy-start.4 = (bf16[16,512]{1,0:T(8,128)(2,1)S(1)}, bf16[16,512]{1,0:T(8,128)(2,1)}, u32[]{:S(2)}) copy-start(bf16[16,512]{1,0:T(8,128)(2,1)} %own_ref.3) | copy-start | bytes 49156
  1.1 1.4 %copy-start.11 = (f32[512]{0:T(512)S(1)}, f32[512]{0:T(512)}, u32[]{:S(2)}) copy-start(f32[512]{0:T(512)} %param.13) | copy-start | bytes 6148
  1.2 1.4 %collective-permute-start.1 = (f32[1,512]{1,0:T(1,128)}, f32[1,512]{1,0:T(1,128)S(1)}, u32[]{:S(2)}, u32[]{:S(2)}) collective-permute-start(f32[1,512]{1,0:T(1,128)} %bitcast.10), channel_id=1, source_target_pairs={{0,1},{1,0},{2,3},{3,2},{4,5},{5,4},{6,7},{7,6},{8,9},{9,8},{10,11... | collective-permute-start | bytes 6152 | tf_op jit(solution)/shard_map/ppermute | solution.py:108
  1.2 8.6 %collective-permute-start.5 = (bf16[4096,512]{1,0:T(8,128)(2,1)}, bf16[4096,512]{1,0:T(8,128)(2,1)S(1)}, u32[]{:S(2)}, u32[]{:S(2)}) collective-permute-start(bf16[4096,512]{1,0:T(8,128)(2,1)} %refs_4_.1), channel_id=1, source_target_pairs={{0,1},{1,0},{2,3},{3,2},{4,5},{5,4},{6,7},{7,6},{8,9},{9,8},{10,11... | collective-permute-start | bytes 12582920 | tf_op jit(solution)/shard_map/ppermute | solution.py:108
  1.7 5.9 %copy-start.1 = (bf16[4096,512]{1,0:T(8,128)(2,1)S(1)}, bf16[4096,512]{1,0:T(8,128)(2,1)}, u32[]{:S(2)}) copy-start(bf16[4096,512]{1,0:T(8,128)(2,1)} %refs_4_.1) | copy-start | bytes 12582916
  2.7 5.1 %copy-start.2 = (bf16[320,1024]{1,0:T(8,128)(2,1)S(1)}, bf16[320,1024]{1,0:T(8,128)(2,1)}, u32[]{:S(2)}) copy-start(bf16[320,1024]{1,0:T(8,128)(2,1)} %refs_1_.9) | copy-start | bytes 1966084
  2.7 5.1 %copy-start.3 = (bf16[320,1024]{1,0:T(8,128)(2,1)S(1)}, bf16[320,1024]{1,0:T(8,128)(2,1)}, u32[]{:S(2)}) copy-start(bf16[320,1024]{1,0:T(8,128)(2,1)} %refs_2_.5) | copy-start | bytes 1966084
  2.7 5.8 %copy-start.6 = (s32[1,16]{1,0:T(1,128)S(1)}, s32[1,16]{1,0:T(1,128)}, u32[]{:S(2)}) copy-start(s32[1,16]{1,0:T(1,128)} %lengths_ref.1) | copy-start | bytes 196
  2.7 5.8 %copy-start.7 = (s32[1,16]{1,0:T(1,128)S(1)}, s32[1,16]{1,0:T(1,128)}, u32[]{:S(2)}) copy-start(s32[1,16]{1,0:T(1,128)} %order_ref.1) | copy-start | bytes 196
  2.7 5.7 %copy-start.10 = (f32[1,128]{1,0:T(1,128)S(1)}, f32[1,128]{1,0:T(1,128)}, u32[]{:S(2)}) copy-start(f32[1,128]{1,0:T(1,128)} %constant.2.clone.frequency_ref) | copy-start | bytes 1540
  2.7 7.1 %copy-start.8 = (f32[128]{0:T(128)S(1)}, f32[128]{0:T(128)}, u32[]{:S(2)}) copy-start(f32[128]{0:T(128)} %param.15) | copy-start | bytes 1540
  2.7 6.4 %collective-permute-start.2 = (bf16[16,1152]{1,0:T(8,128)(2,1)S(1)}, bf16[16,1152]{1,0:T(8,128)(2,1)S(1)}, u32[]{:S(2)}, u32[]{:S(2)}) collective-permute-start(bf16[16,1152]{1,0:T(8,128)(2,1)S(1)} %shard_map.140.message_ref.refs_3_.pair_ref), channel_id=1, source_target_pairs={{0,7},{1,0},{2,5},{3,2},{4,3},{5,4},{6,1},{7,6},{8,15},{9,8},{10,1... | collective-permute-start | bytes 110600 | tf_op jit(solution)/shard_map/ppermute | solution.py:209
  7.5 2.0 %collective-permute-start.3 = (bf16[16,1152]{1,0:T(8,128)(2,1)S(1)}, bf16[16,1152]{1,0:T(8,128)(2,1)S(1)}, u32[]{:S(2)}, u32[]{:S(2)}) collective-permute-start(bf16[16,1152]{1,0:T(8,128)(2,1)S(1)} %shard_map.140.message_ref.refs_3_.pair_ref), channel_id=1, source_target_pairs={{0,5},{1,0},{2,7},{3,2},{4,1},{5,4},{6,3},{7,6},{8,13},{9,8},{10,1... | collective-permute-start | bytes 110600 | tf_op jit(solution)/shard_map/ppermute | solution.py:209
  7.5 2.3 %collective-permute-start.4 = (bf16[16,1152]{1,0:T(8,128)(2,1)S(1)}, bf16[16,1152]{1,0:T(8,128)(2,1)S(1)}, u32[]{:S(2)}, u32[]{:S(2)}) collective-permute-start(bf16[16,1152]{1,0:T(8,128)(2,1)S(1)} %shard_map.140.message_ref.refs_3_.pair_ref), channel_id=1, source_target_pairs={{0,3},{1,0},{2,1},{3,2},{4,7},{5,4},{6,5},{7,6},{8,11},{9,8},{10,9... | collective-permute-start | bytes 110600 | tf_op jit(solution)/shard_map/ppermute | solution.py:209
  7.9 6.9 %collective-permute-start.7 = (bf16[2,320,1024]{2,1,0:T(8,128)(2,1)S(1)}, bf16[2,320,1024]{2,1,0:T(8,128)(2,1)S(1)}, u32[]{:S(2)}, u32[]{:S(2)}) collective-permute-start(bf16[2,320,1024]{2,1,0:T(8,128)(2,1)S(1)} %shard_map.146), channel_id=1, source_target_pairs={{0,1},{1,0},{2,3},{3,2},{4,5},{5,4},{6,7},{7,6},{8,9},{9,8},{10,11... | collective-permute-start | bytes 3932168 | tf_op jit(solution)/shard_map/ppermute | solution.py:108
  9.9 4.6 %copy-start = (bf16[512,4096]{1,0:T(8,128)(2,1)S(1)}, bf16[512,4096]{1,0:T(8,128)(2,1)}, u32[]{:S(2)}) copy-start(bf16[512,4096]{1,0:T(8,128)(2,1)} %refs_1_.13) | copy-start | bytes 12582916
  9.9 6.6 %collective-permute-start.6 = (bf16[16,1024]{1,0:T(8,128)(2,1)S(1)}, bf16[16,1024]{1,0:T(8,128)(2,1)S(1)}, u32[]{:S(2)}, u32[]{:S(2)}) collective-permute-start(bf16[16,1024]{1,0:T(8,128)(2,1)S(1)} %shard_map.145.query_ref._), channel_id=1, source_target_pairs={{0,1},{1,6},{2,3},{3,4},{4,5},{5,2},{6,7},{7,0},{8,9},{9,14},{10,1... | collective-permute-start | bytes 98312 | tf_op jit(solution)/shard_map/ppermute | solution.py:209
  13.0 4.6 %collective-permute-start.9 = (bf16[16,1024]{1,0:T(8,128)(2,1)S(1)}, bf16[16,1024]{1,0:T(8,128)(2,1)S(1)}, u32[]{:S(2)}, u32[]{:S(2)}) collective-permute-start(bf16[16,1024]{1,0:T(8,128)(2,1)S(1)} %shard_map.145.query_ref._), channel_id=1, source_target_pairs={{0,1},{1,4},{2,3},{3,6},{4,5},{5,0},{6,7},{7,2},{8,9},{9,12},{10,1... | collective-permute-start | bytes 98312 | tf_op jit(solution)/shard_map/ppermute | solution.py:209
  13.8 4.4 %collective-permute-start.11 = (bf16[16,1024]{1,0:T(8,128)(2,1)S(1)}, bf16[16,1024]{1,0:T(8,128)(2,1)S(1)}, u32[]{:S(2)}, u32[]{:S(2)}) collective-permute-start(bf16[16,1024]{1,0:T(8,128)(2,1)S(1)} %shard_map.145.query_ref._), channel_id=1, source_target_pairs={{0,1},{1,2},{2,3},{3,0},{4,5},{5,6},{6,7},{7,4},{8,9},{9,10},{10,1... | collective-permute-start | bytes 98312 | tf_op jit(solution)/shard_map/ppermute | solution.py:209
  14.7 7.4 %collective-permute-start.13 = (bf16[512,4096]{1,0:T(8,128)(2,1)S(1)}, bf16[512,4096]{1,0:T(8,128)(2,1)S(1)}, u32[]{:S(2)}, u32[]{:S(2)}) collective-permute-start(bf16[512,4096]{1,0:T(8,128)(2,1)S(1)} %shard_map.152), channel_id=1, source_target_pairs={{0,1},{1,0},{2,3},{3,2},{4,5},{5,4},{6,7},{7,6},{8,9},{9,8},{10,11... | collective-permute-start | bytes 12582920 | tf_op jit(solution)/shard_map/ppermute | solution.py:108
  17.1 4.9 %collective-permute-start.8 = (bf16[16,1152]{1,0:T(8,128)(2,1)S(1)}, bf16[16,1152]{1,0:T(8,128)(2,1)S(1)}, u32[]{:S(2)}, u32[]{:S(2)}) collective-permute-start(bf16[16,1152]{1,0:T(8,128)(2,1)S(1)} %shard_map.148.refs_5_), channel_id=1, source_target_pairs={{0,7},{1,0},{2,5},{3,2},{4,3},{5,4},{6,1},{7,6},{8,15},{9,8},{10,1... | collective-permute-start | bytes 110600 | tf_op jit(solution)/shard_map/ppermute | solution.py:209
  18.2 3.9 %collective-permute-start.10 = (bf16[16,1152]{1,0:T(8,128)(2,1)S(1)}, bf16[16,1152]{1,0:T(8,128)(2,1)S(1)}, u32[]{:S(2)}, u32[]{:S(2)}) collective-permute-start(bf16[16,1152]{1,0:T(8,128)(2,1)S(1)} %shard_map.149.refs_5_), channel_id=1, source_target_pairs={{0,5},{1,0},{2,7},{3,2},{4,1},{5,4},{6,3},{7,6},{8,13},{9,8},{10,1... | collective-permute-start | bytes 110600 | tf_op jit(solution)/shard_map/ppermute | solution.py:209
  18.7 3.4 %collective-permute-start.12 = (bf16[16,1152]{1,0:T(8,128)(2,1)S(1)}, bf16[16,1152]{1,0:T(8,128)(2,1)S(1)}, u32[]{:S(2)}, u32[]{:S(2)}) collective-permute-start(bf16[16,1152]{1,0:T(8,128)(2,1)S(1)} %shard_map.150), channel_id=1, source_target_pairs={{0,3},{1,0},{2,1},{3,2},{4,7},{5,4},{6,5},{7,6},{8,11},{9,8},{10,9... | collective-permute-start | bytes 110600 | tf_op jit(solution)/shard_map/ppermute | solution.py:209
  22.1 5.2 %collective-permute-start.14 = (bf16[16,1024]{1,0:T(8,128)(2,1)S(1)}, bf16[16,1024]{1,0:T(8,128)(2,1)S(1)}, u32[]{:S(2)}, u32[]{:S(2)}) collective-permute-start(bf16[16,1024]{1,0:T(8,128)(2,1)S(1)} %shard_map.153.refs_3_), channel_id=1, source_target_pairs={{0,1},{1,6},{2,3},{3,4},{4,5},{5,2},{6,7},{7,0},{8,9},{9,14},{10,1... | collective-permute-start | bytes 98312 | tf_op jit(solution)/shard_map/ppermute | solution.py:209
  23.1 4.5 %collective-permute-start.15 = (bf16[16,1024]{1,0:T(8,128)(2,1)S(1)}, bf16[16,1024]{1,0:T(8,128)(2,1)S(1)}, u32[]{:S(2)}, u32[]{:S(2)}) collective-permute-start(bf16[16,1024]{1,0:T(8,128)(2,1)S(1)} %shard_map.154.refs_3_), channel_id=1, source_target_pairs={{0,1},{1,4},{2,3},{3,6},{4,5},{5,0},{6,7},{7,2},{8,9},{9,12},{10,1... | collective-permute-start | bytes 98312 | tf_op jit(solution)/shard_map/ppermute | solution.py:209
  24.4 1.0 %copy-start.5 = (f32[512]{0:T(512)S(1)}, f32[512]{0:T(512)}, u32[]{:S(2)}) copy-start(f32[512]{0:T(512)} %param.19) | copy-start | bytes 6148
  24.4 3.6 %collective-permute-start.16 = (bf16[16,1024]{1,0:T(8,128)(2,1)S(1)}, bf16[16,1024]{1,0:T(8,128)(2,1)S(1)}, u32[]{:S(2)}, u32[]{:S(2)}) collective-permute-start(bf16[16,1024]{1,0:T(8,128)(2,1)S(1)} %shard_map.155.refs_3_), channel_id=1, source_target_pairs={{0,1},{1,2},{2,3},{3,0},{4,5},{5,6},{6,7},{7,4},{8,9},{9,10},{10,1... | collective-permute-start | bytes 98312 | tf_op jit(solution)/shard_map/ppermute | solution.py:209
  25.0 12.5 %copy-start.9 = (s32[64]{0:T(128)S(1)}, s32[64]{0:T(128)}, u32[]{:S(2)}) copy-start(s32[64]{0:T(128)} %param.22) | copy-start | bytes 772
  25.0 3.0 %collective-permute-start.17 = (bf16[16,1024]{1,0:T(8,128)(2,1)S(1)}, bf16[16,1024]{1,0:T(8,128)(2,1)S(1)}, u32[]{:S(2)}, u32[]{:S(2)}) collective-permute-start(bf16[16,1024]{1,0:T(8,128)(2,1)S(1)} %shard_map.156), channel_id=1, source_target_pairs={{0,1},{1,0},{2,3},{3,2},{4,5},{5,4},{6,7},{7,6},{8,9},{9,8},{10,11... | collective-permute-start | bytes 98312 | tf_op jit(solution)/shard_map/ppermute | solution.py:108
  25.4 1.2 %collective-permute-start.18 = (f32[1,512]{1,0:T(1,128)S(1)}, f32[1,512]{1,0:T(1,128)S(1)}, u32[]{:S(2)}, u32[]{:S(2)}) collective-permute-start(f32[1,512]{1,0:T(1,128)S(1)} %bitcast.4), channel_id=1, source_target_pairs={{0,1},{1,0},{2,3},{3,2},{4,5},{5,4},{6,7},{7,6},{8,9},{9,8},{10,11... | collective-permute-start | bytes 6152 | tf_op jit(solution)/shard_map/ppermute | solution.py:108
  28.1 3.4 %collective-permute-start.19 = (bf16[16,1152]{1,0:T(8,128)(2,1)S(1)}, bf16[16,1152]{1,0:T(8,128)(2,1)S(1)}, u32[]{:S(2)}, u32[]{:S(2)}) collective-permute-start(bf16[16,1152]{1,0:T(8,128)(2,1)S(1)} %get-tuple-element.17.refs_3_), channel_id=1, source_target_pairs={{0,25},{1,0},{2,27},{3,2},{4,29},{5,4},{6,31},{7,6},{8,17},{9,8},{... | collective-permute-start | bytes 110600 | tf_op jit(solution)/shard_map/ppermute | solution.py:209
  29.0 2.5 %collective-permute-start.20 = (bf16[16,1152]{1,0:T(8,128)(2,1)S(1)}, bf16[16,1152]{1,0:T(8,128)(2,1)S(1)}, u32[]{:S(2)}, u32[]{:S(2)}) collective-permute-start(bf16[16,1152]{1,0:T(8,128)(2,1)S(1)} %get-tuple-element.17.refs_3_), channel_id=1, source_target_pairs={{0,17},{1,0},{2,19},{3,2},{4,21},{5,4},{6,23},{7,6},{8,25},{9,8},{... | collective-permute-start | bytes 110600 | tf_op jit(solution)/shard_map/ppermute | solution.py:209
  29.8 1.7 %collective-permute-start.21 = (bf16[16,1152]{1,0:T(8,128)(2,1)S(1)}, bf16[16,1152]{1,0:T(8,128)(2,1)S(1)}, u32[]{:S(2)}, u32[]{:S(2)}) collective-permute-start(bf16[16,1152]{1,0:T(8,128)(2,1)S(1)} %get-tuple-element.17.refs_3_), channel_id=1, source_target_pairs={{0,9},{1,0},{2,11},{3,2},{4,13},{5,4},{6,15},{7,6},{8,1},{9,8},{10... | collective-permute-start | bytes 110600 | tf_op jit(solution)/shard_map/ppermute | solution.py:209
  29.8 1.7 %collective-permute-start.22 = (bf16[16,1152]{1,0:T(8,128)(2,1)S(1)}, bf16[16,1152]{1,0:T(8,128)(2,1)S(1)}, u32[]{:S(2)}, u32[]{:S(2)}) collective-permute-start(bf16[16,1152]{1,0:T(8,128)(2,1)S(1)} %get-tuple-element.17.refs_3_), channel_id=1, source_target_pairs={{0,1},{1,0},{2,3},{3,2},{4,5},{5,4},{6,7},{7,6},{8,9},{9,8},{10,11... | collective-permute-start | bytes 110600 | tf_op jit(solution)/shard_map/ppermute | solution.py:108
  30.3 1.2 %collective-permute-start.23 = (f32[16,512]{1,0:T(8,128)S(1)}, f32[16,512]{1,0:T(8,128)S(1)}, u32[]{:S(2)}, u32[]{:S(2)}) collective-permute-start(f32[16,512]{1,0:T(8,128)S(1)} %get-tuple-element.18), channel_id=1, source_target_pairs={{0,1},{1,0},{2,3},{3,2},{4,5},{5,4},{6,7},{7,6},{8,9},{9,8},{10,11... | collective-permute-start | bytes 98312 | tf_op jit(solution)/shard_map/ppermute | solution.py:108
  31.6 5.0 %collective-permute-start.24 = (f32[32,128]{1,0:T(8,128)S(1)}, f32[32,128]{1,0:T(8,128)S(1)}, u32[]{:S(2)}, u32[]{:S(2)}) collective-permute-start(f32[32,128]{1,0:T(8,128)S(1)} %get-tuple-element.19), channel_id=1, source_target_pairs={{0,1},{1,6},{2,3},{3,4},{4,5},{5,2},{6,7},{7,0},{8,9},{9,14},{10,1... | collective-permute-start | bytes 49160 | tf_op jit(solution)/shard_map/ppermute | solution.py:209
  33.3 4.1 %collective-permute-start.25 = (f32[32,128]{1,0:T(8,128)S(1)}, f32[32,128]{1,0:T(8,128)S(1)}, u32[]{:S(2)}, u32[]{:S(2)}) collective-permute-start(f32[32,128]{1,0:T(8,128)S(1)} %get-tuple-element.19), channel_id=1, source_target_pairs={{0,1},{1,4},{2,3},{3,6},{4,5},{5,0},{6,7},{7,2},{8,9},{9,12},{10,1... | collective-permute-start | bytes 49160 | tf_op jit(solution)/shard_map/ppermute | solution.py:209
  33.7 3.7 %collective-permute-start.26 = (f32[32,128]{1,0:T(8,128)S(1)}, f32[32,128]{1,0:T(8,128)S(1)}, u32[]{:S(2)}, u32[]{:S(2)}) collective-permute-start(f32[32,128]{1,0:T(8,128)S(1)} %get-tuple-element.19), channel_id=1, source_target_pairs={{0,1},{1,2},{2,3},{3,0},{4,5},{5,6},{6,7},{7,4},{8,9},{9,10},{10,1... | collective-permute-start | bytes 49160 | tf_op jit(solution)/shard_map/ppermute | solution.py:209
  35.3 2.1 %collective-permute-start.27 = (f32[32,128]{1,0:T(8,128)S(1)}, f32[32,128]{1,0:T(8,128)S(1)}, u32[]{:S(2)}, u32[]{:S(2)}) collective-permute-start(f32[32,128]{1,0:T(8,128)S(1)} %get-tuple-element.19), channel_id=1, source_target_pairs={{0,1},{1,0},{2,3},{3,2},{4,5},{5,4},{6,7},{7,6},{8,9},{9,8},{10,11... | collective-permute-start | bytes 49160 | tf_op jit(solution)/shard_map/ppermute | solution.py:108
  35.3 3.3 %collective-permute-start.29 = (bf16[48,512]{1,0:T(8,128)(2,1)S(1)}, bf16[48,512]{1,0:T(8,128)(2,1)S(1)}, u32[]{:S(2)}, u32[]{:S(2)}) collective-permute-start(bf16[48,512]{1,0:T(8,128)(2,1)S(1)} %get-tuple-element.21), channel_id=1, source_target_pairs={{0,1},{1,0},{2,3},{3,2},{4,5},{5,4},{6,7},{7,6},{8,9},{9,8},{10,11... | collective-permute-start | bytes 147464 | tf_op jit(solution)/shard_map/ppermute | solution.py:108
  37.4 1.2 %collective-permute-start.28 = (f32[32,128]{1,0:T(8,128)S(1)}, f32[32,128]{1,0:T(8,128)S(1)}, u32[]{:S(2)}, u32[]{:S(2)}) collective-permute-start(f32[32,128]{1,0:T(8,128)S(1)} %shard_map.159.refs_0_), channel_id=1, source_target_pairs={{0,1},{1,0},{2,3},{3,2},{4,5},{5,4},{6,7},{7,6},{8,9},{9,8},{10,11... | collective-permute-start | bytes 49160 | tf_op jit(solution)/shard_map/ppermute | solution.py:108

commit v11 on v10

--- a/solution.py
+++ b/solution.py
@@ -214,7 +214,7 @@
     out_ref[1] = value_ref[...]
 
 
-def prepare_pair(_, own_ref, other_ref, own_gain_ref, other_gain_ref, pair_ref):
+def prepare_pair(_, own_ref, other_ref, own_gain_ref, other_gain_ref, _last, pair_ref):
     width = own_ref.shape[1]
     squares = 0.0
     scaled = []
@@ -410,8 +410,11 @@
                 attended_ref[:, place] = (summed / sum(factors)).astype(jnp.bfloat16)
 
 
-def copy_weights(_, weight_ref, out_ref):
-    out_ref[...] = weight_ref[...]
+def copy_weights(_, weight_ref, out_ref, *, offsets):
+    width = out_ref.shape[2]
+    for i, offset in enumerate(offsets):
+        column = pl.ds(pl.multiple_of((chip_number() ^ offset) * width, width), width)
+        out_ref[i] = weight_ref[:, column]
 
 
 def project_out(attended_ref, weight_ref, other_weight_ref, *refs, offset):
@@ -424,7 +427,7 @@
         total = jnp.dot(
             attended_ref[:, width:], weight_ref[:, column], preferred_element_type=jnp.float32
         ) + jnp.dot(
-            attended_ref[:, :width], other_weight_ref[:, column], preferred_element_type=jnp.float32
+            attended_ref[:, :width], other_weight_ref[1 - offset % 2], preferred_element_type=jnp.float32
         )
         out_ref[...] = total.astype(out_ref.dtype)
 
@@ -628,6 +631,7 @@
     )()
     attn_gain = attn_gain[None]
     other_hidden_in = flip(hidden_in, "pack", 1)
+    other_gain = flip(final_gain, "pack", 1)
     other_w_query = flip(w_query, "pack", 1)
     pair = in_vmem(
         prepare_pair,
@@ -637,6 +641,7 @@
         other_hidden_in,
         attn_gain,
         flip(attn_gain, "pack", 1),
+        other_gain,
         flops=1 << 34,
     )
     received = [send_across(pair, "pack", k, 0) for k in others]
@@ -659,7 +664,6 @@
         cached_values,
     )
     other_held = flip(held, "pack", 1)
-    other_gain = flip(final_gain, "pack", 1)
 
     def queries_from(weights, flops, *own):
         return in_vmem(
@@ -680,9 +684,18 @@
     queries = in_vmem(
         join_queries, shaped((stmts, 2 * width), bf16), first_queries, second_queries
     )
-    other_weights = flip(
-        in_vmem(copy_weights, shaped(w_out.shape, bf16), queries, w_out, limit=16), "pack", 1
-    )
+
+    def weights_to(offsets, after):
+        part = in_vmem(
+            lambda *refs: copy_weights(*refs, offsets=offsets),
+            shaped((2, width, 2 * width), bf16),
+            after,
+            w_out,
+            limit=16,
+        )
+        return flip(part, "pack", 1)
+
+    far_weights = weights_to((3, 2), queries)
     received = [send_across(queries, "pack", k, 1) for k in others]
     group_rows = stmts * (width // head_dim)
     own_part, own_stats = in_vmem(
@@ -711,6 +724,7 @@
             )
         )
     received = [send_across(part, "pack", k, 0) for k, part in zip(others, partials[::-1])]
+    near_weights = weights_to((1, 0), partials[-1])
     attended = in_vmem(
         merge_partials,
         shaped((stmts, 2 * width), bf16),
@@ -725,10 +739,10 @@
             shaped((stmts, 2 * width), kind),
             attended,
             w_out,
-            other_weights,
+            far_weights if offset > 1 else near_weights,
             *after,
             limit=16,
-            flops=1 << 27,
+            flops=1 << (35 if offset == 2 else 27),
         )
 
     third = projected_to(3, bf16)

time: 39.9 us -> 39.8 us (level)
  waiting for transfers between devices: 13.6 us -> 11.9 us
  starting transfers between devices: 21.3 us -> 22.9 us
    ppermute x12 -> x13, starting transfers between devices: 3.42 us -> 4.73 us  [flip(): return lax.ppermute(array, axis, [(i, i ^ offset) for i in range(size)])]
    ppermute x18, waiting for transfers between devices: 9.62 us -> 8.71 us  [send_across(): return lax.ppermute(array, ('dp', 'pack'), pairs)]
    ppermute x12 -> x13, waiting for transfers between devices: 3.99 us -> 3.17 us  [flip(): return lax.ppermute(array, axis, [(i, i ^ offset) for i in range(size)])]
    pallas_call x21 -> x22, Pallas kernels: 2.88 us -> 2.88 us  [in_vmem(): pl.pallas_call(body, out_shape=outputs, in_specs=[whole] * len(operands),...]
  transfers between devices with their start and end apart: 30 -> 31, of which waited for: 17 -> 16; matrix products, arithmetic and copies ran while one was open for 0% -> 0% of each run, Pallas kernels for 7% -> 7%
where the time goes in v11:
time: 39.8 us; the launch traced here: 39.7 us
  starting transfers between devices  22.9 us (58%)
  waiting for transfers between devices  11.9 us (30%)
  Pallas kernels  3.96 us (10%)
  between operations  0.84 us (2%)
    ppermute x18, starting transfers between devices, send_across(): return lax.ppermute(array, ('dp', 'pack'), pairs)  18.2 us
    ppermute x18, waiting for transfers between devices, send_across(): return lax.ppermute(array, ('dp', 'pack'), pairs)  8.71 us
    ppermute x13, starting transfers between devices, flip(): return lax.ppermute(array, axis, [(i, i ^ offset) for i in range(size)])  4.73 us
    ppermute x13, waiting for transfers between devices, flip(): return lax.ppermute(array, axis, [(i, i ^ offset) for i in range(size)])  3.17 us
    pallas_call x22, Pallas kernels, in_vmem(): pl.pallas_call(body, out_shape=outputs, in_specs=[whole] * len(operands),...  2.88 us
    pallas_call x1, Pallas kernels, core_roles(): pl.pallas_call(lambda *refs: losses_and_gradient(*refs, model_width=model...  1.08 us
  transfers between devices with their start and end apart: 31, of which 16 were waited for; matrix products, arithmetic and copies ran while one was open for 0% of the time, Pallas kernels for 7%

profile of v11, /device:TPU:0, one launch (start us, length us, event | category | flops | bytes accessed | tf_op | source)
XLA Modules:
  0.0 39.7 jit_solution(13825402913776808294)
XLA Ops:
  0.6 0.5 %collective-permute-start = (bf16[16,512]{1,0:T(8,128)(2,1)}, bf16[16,512]{1,0:T(8,128)(2,1)S(1)}, u32[]{:S(2)}, u32[]{:S(2)}) collective-permute-start(bf16[16,512]{1,0:T(8,128)(2,1)} %own_ref.3), channel_id=1, source_target_pairs={{0,1},{1,0},{2,3},{3,2},{4,5},{5,4},{6,7},{7,6},{8,9},{9,8},{10,11... | collective-permute-start | bytes 49160 | tf_op jit(solution)/shard_map/ppermute | solution.py:108
  1.2 0.4 %collective-permute-start.2 = (f32[1,512]{1,0:T(1,128)}, f32[1,512]{1,0:T(1,128)S(1)}, u32[]{:S(2)}, u32[]{:S(2)}) collective-permute-start(f32[1,512]{1,0:T(1,128)} %bitcast.4), channel_id=1, source_target_pairs={{0,1},{1,0},{2,3},{3,2},{4,5},{5,4},{6,7},{7,6},{8,9},{9,8},{10,11... | collective-permute-start | bytes 6152 | tf_op jit(solution)/shard_map/ppermute | solution.py:108
  1.7 0.8 %collective-permute-done.1.other_gain_ref = f32[1,512]{1,0:T(1,128)S(1)} collective-permute-done((f32[1,512]{1,0:T(1,128)}, f32[1,512]{1,0:T(1,128)S(1)}, u32[]{:S(2)}, u32[]{:S(2)}) %collective-permute-start.1) | collective-permute-done | bytes 2080 | tf_op jit(solution)/shard_map/ppermute | solution.py:108
  2.5 0.2 collective-permute-done.2._last.other_gain_ref
  2.7 0.2 shard_map.140.message_ref.refs_3_.pair_ref
  2.9 4.8 %collective-permute-start.3 = (bf16[16,1152]{1,0:T(8,128)(2,1)S(1)}, bf16[16,1152]{1,0:T(8,128)(2,1)S(1)}, u32[]{:S(2)}, u32[]{:S(2)}) collective-permute-start(bf16[16,1152]{1,0:T(8,128)(2,1)S(1)} %shard_map.140.message_ref.refs_3_.pair_ref), channel_id=1, source_target_pairs={{0,7},{1,0},{2,5},{3,2},{4,3},{5,4},{6,1},{7,6},{8,15},{9,8},{10,1... | collective-permute-start | bytes 110600 | tf_op jit(solution)/shard_map/ppermute | solution.py:209
  7.7 0.2 shard_map.143.refs_7_._
  8.0 0.1 shard_map.146
  8.1 0.6 %collective-permute-start.8 = (bf16[2,320,1024]{2,1,0:T(8,128)(2,1)S(1)}, bf16[2,320,1024]{2,1,0:T(8,128)(2,1)S(1)}, u32[]{:S(2)}, u32[]{:S(2)}) collective-permute-start(bf16[2,320,1024]{2,1,0:T(8,128)(2,1)S(1)} %shard_map.146), channel_id=1, source_target_pairs={{0,1},{1,0},{2,3},{3,2},{4,5},{5,4},{6,7},{7,6},{8,9},{9,8},{10,11... | collective-permute-start | bytes 3932168 | tf_op jit(solution)/shard_map/ppermute | solution.py:108
  8.6 0.2 shard_map.141
  8.8 0.5 %collective-permute-done.3.refs_0_ = bf16[16,1152]{1,0:T(8,128)(2,1)S(1)} collective-permute-done((bf16[16,1152]{1,0:T(8,128)(2,1)S(1)}, bf16[16,1152]{1,0:T(8,128)(2,1)S(1)}, u32[]{:S(2)}, u32[]{:S(2)}) %collective-permute-start.3) | collective-permute-done | bytes 36896 | tf_op jit(solution)/shard_map/ppermute | solution.py:209
  9.3 0.3 collective-permute-done.4.refs_1_
  9.6 0.3 collective-permute-done.5.refs_2_
  10.0 3.1 %collective-permute-start.7 = (bf16[16,1024]{1,0:T(8,128)(2,1)S(1)}, bf16[16,1024]{1,0:T(8,128)(2,1)S(1)}, u32[]{:S(2)}, u32[]{:S(2)}) collective-permute-start(bf16[16,1024]{1,0:T(8,128)(2,1)S(1)} %shard_map.145.query_ref.refs_0_), channel_id=1, source_target_pairs={{0,1},{1,6},{2,3},{3,4},{4,5},{5,2},{6,7},{7,0},{8,9},{9,14},{10,1... | collective-permute-start | bytes 98312 | tf_op jit(solution)/shard_map/ppermute | solution.py:209
  13.2 0.7 %collective-permute-start.10 = (bf16[16,1024]{1,0:T(8,128)(2,1)S(1)}, bf16[16,1024]{1,0:T(8,128)(2,1)S(1)}, u32[]{:S(2)}, u32[]{:S(2)}) collective-permute-start(bf16[16,1024]{1,0:T(8,128)(2,1)S(1)} %shard_map.145.query_ref.refs_0_), channel_id=1, source_target_pairs={{0,1},{1,4},{2,3},{3,6},{4,5},{5,0},{6,7},{7,2},{8,9},{9,12},{10,1... | collective-permute-start | bytes 98312 | tf_op jit(solution)/shard_map/ppermute | solution.py:209
  13.9 0.6 %collective-permute-start.12 = (bf16[16,1024]{1,0:T(8,128)(2,1)S(1)}, bf16[16,1024]{1,0:T(8,128)(2,1)S(1)}, u32[]{:S(2)}, u32[]{:S(2)}) collective-permute-start(bf16[16,1024]{1,0:T(8,128)(2,1)S(1)} %shard_map.145.query_ref.refs_0_), channel_id=1, source_target_pairs={{0,1},{1,2},{2,3},{3,0},{4,5},{5,6},{6,7},{7,4},{8,9},{9,10},{10,1... | collective-permute-start | bytes 98312 | tf_op jit(solution)/shard_map/ppermute | solution.py:209
  14.5 0.1 shard_map.152
  14.8 1.8 %collective-permute-done.7.refs_0_ = bf16[16,1024]{1,0:T(8,128)(2,1)S(1)} collective-permute-done((bf16[16,1024]{1,0:T(8,128)(2,1)S(1)}, bf16[16,1024]{1,0:T(8,128)(2,1)S(1)}, u32[]{:S(2)}, u32[]{:S(2)}) %collective-permute-start.7) | collective-permute-done | bytes 32800 | tf_op jit(solution)/shard_map/ppermute | solution.py:209
  16.6 0.5 %shard_map.148.refs_5_ = bf16[16,1152]{1,0:T(8,128)(2,1)S(1)} custom-call(bf16[16,1024]{1,0:T(8,128)(2,1)S(1)} %collective-permute-done.7.refs_0_, bf16[320,1024]{1,0:T(8,128)(2,1)S(1)} %copy-done.2, bf16[320,1024]{1,0:T(8,128)(2,1)S(1)} %copy-done.3, bf16[2,320,1024]{2,1,0:T(8,128)(2,1)S(1)} %collective-permute-done.8.other_ref.refs_3_, ...), custom_call_target="tpu_custom_call" | custom-call | flops 17179869184 | bytes 2736128 | tf_op jit(solution)/shard_map/pallas_call | solution.py:114
  17.1 0.1 collective-permute-start.9
  17.2 0.5 %collective-permute-done.10.refs_0_ = bf16[16,1024]{1,0:T(8,128)(2,1)S(1)} collective-permute-done((bf16[16,1024]{1,0:T(8,128)(2,1)S(1)}, bf16[16,1024]{1,0:T(8,128)(2,1)S(1)}, u32[]{:S(2)}, u32[]{:S(2)}) %collective-permute-start.10) | collective-permute-done | bytes 32800 | tf_op jit(solution)/shard_map/ppermute | solution.py:209
  17.8 0.5 %shard_map.149.refs_5_ = bf16[16,1152]{1,0:T(8,128)(2,1)S(1)} custom-call(bf16[16,1024]{1,0:T(8,128)(2,1)S(1)} %collective-permute-done.10.refs_0_, bf16[320,1024]{1,0:T(8,128)(2,1)S(1)} %copy-done.2, bf16[320,1024]{1,0:T(8,128)(2,1)S(1)} %copy-done.3, bf16[2,320,1024]{2,1,0:T(8,128)(2,1)S(1)} %collective-permute-done.8.other_ref.refs_3_, ...), custom_call_target="tpu_custom_call" | custom-call | flops 17179869184 | bytes 2707456 | tf_op jit(solution)/shard_map/pallas_call | solution.py:114
  18.3 0.5 %shard_map.150.refs_0_ = bf16[16,1152]{1,0:T(8,128)(2,1)S(1)} custom-call(bf16[16,1024]{1,0:T(8,128)(2,1)S(1)} %collective-permute-done.12.refs_0_, bf16[320,1024]{1,0:T(8,128)(2,1)S(1)} %copy-done.2, bf16[320,1024]{1,0:T(8,128)(2,1)S(1)} %copy-done.3, bf16[2,320,1024]{2,1,0:T(8,128)(2,1)S(1)} %collective-permute-done.8.other_ref.refs_3_, ...), custom_call_target="tpu_custom_call" | custom-call | flops 17179869184 | bytes 2707456 | tf_op jit(solution)/shard_map/pallas_call | solution.py:114
  18.9 0.1 shard_map.155
  19.1 0.5 %collective-permute-start.17 = (bf16[2,512,1024]{2,1,0:T(8,128)(2,1)S(1)}, bf16[2,512,1024]{2,1,0:T(8,128)(2,1)S(1)}, u32[]{:S(2)}, u32[]{:S(2)}) collective-permute-start(bf16[2,512,1024]{2,1,0:T(8,128)(2,1)S(1)} %shard_map.155), channel_id=1, source_target_pairs={{0,1},{1,0},{2,3},{3,2},{4,5},{5,4},{6,7},{7,6},{8,9},{9,8},{10,11... | collective-permute-start | bytes 6291464 | tf_op jit(solution)/shard_map/ppermute | solution.py:108
  19.6 0.3 collective-permute-done.11.second_ref
  20.0 0.6 %collective-permute-done.13.first_ref = bf16[16,1152]{1,0:T(8,128)(2,1)S(1)} collective-permute-done((bf16[16,1152]{1,0:T(8,128)(2,1)S(1)}, bf16[16,1152]{1,0:T(8,128)(2,1)S(1)}, u32[]{:S(2)}, u32[]{:S(2)}) %collective-permute-start.13) | collective-permute-done | bytes 36896 | tf_op jit(solution)/shard_map/ppermute | solution.py:209
  20.6 2.7 %collective-permute-start.15 = (bf16[16,1024]{1,0:T(8,128)(2,1)S(1)}, bf16[16,1024]{1,0:T(8,128)(2,1)S(1)}, u32[]{:S(2)}, u32[]{:S(2)}) collective-permute-start(bf16[16,1024]{1,0:T(8,128)(2,1)S(1)} %shard_map.153.refs_3_), channel_id=1, source_target_pairs={{0,1},{1,6},{2,3},{3,4},{4,5},{5,2},{6,7},{7,0},{8,9},{9,14},{10,1... | collective-permute-start | bytes 98312 | tf_op jit(solution)/shard_map/ppermute | solution.py:209
  23.2 0.4 collective-permute-start.16
  23.6 0.8 %collective-permute-start.18 = (bf16[16,1024]{1,0:T(8,128)(2,1)S(1)}, bf16[16,1024]{1,0:T(8,128)(2,1)S(1)}, u32[]{:S(2)}, u32[]{:S(2)}) collective-permute-start(bf16[16,1024]{1,0:T(8,128)(2,1)S(1)} %shard_map.156.refs_3_), channel_id=1, source_target_pairs={{0,1},{1,2},{2,3},{3,0},{4,5},{5,6},{6,7},{7,4},{8,9},{9,10},{10,1... | collective-permute-start | bytes 98312 | tf_op jit(solution)/shard_map/ppermute | solution.py:209
  24.5 1.4 %collective-permute-start.19 = (bf16[16,1024]{1,0:T(8,128)(2,1)S(1)}, bf16[16,1024]{1,0:T(8,128)(2,1)S(1)}, u32[]{:S(2)}, u32[]{:S(2)}) collective-permute-start(bf16[16,1024]{1,0:T(8,128)(2,1)S(1)} %shard_map.157), channel_id=1, source_target_pairs={{0,1},{1,0},{2,3},{3,2},{4,5},{5,4},{6,7},{7,6},{8,9},{9,8},{10,11... | collective-permute-start | bytes 98312 | tf_op jit(solution)/shard_map/ppermute | solution.py:108
  25.8 0.7 %collective-permute-done.15.third_ref = bf16[16,1024]{1,0:T(8,128)(2,1)S(1)} collective-permute-done((bf16[16,1024]{1,0:T(8,128)(2,1)S(1)}, bf16[16,1024]{1,0:T(8,128)(2,1)S(1)}, u32[]{:S(2)}, u32[]{:S(2)}) %collective-permute-start.15) | collective-permute-done | bytes 32800 | tf_op jit(solution)/shard_map/ppermute | solution.py:209
  26.5 1.0 %collective-permute-done.16.second_ref = bf16[16,1024]{1,0:T(8,128)(2,1)S(1)} collective-permute-done((bf16[16,1024]{1,0:T(8,128)(2,1)S(1)}, bf16[16,1024]{1,0:T(8,128)(2,1)S(1)}, u32[]{:S(2)}, u32[]{:S(2)}) %collective-permute-start.16) | collective-permute-done | bytes 32800 | tf_op jit(solution)/shard_map/ppermute | solution.py:209
  27.5 0.3 collective-permute-done.18.first_ref
  27.9 0.2 shard_map.158
  28.0 1.1 %collective-permute-start.20 = (bf16[16,1152]{1,0:T(8,128)(2,1)S(1)}, bf16[16,1152]{1,0:T(8,128)(2,1)S(1)}, u32[]{:S(2)}, u32[]{:S(2)}) collective-permute-start(bf16[16,1152]{1,0:T(8,128)(2,1)S(1)} %get-tuple-element.17.refs_3_), channel_id=1, source_target_pairs={{0,25},{1,0},{2,27},{3,2},{4,29},{5,4},{6,31},{7,6},{8,17},{9,8},{... | collective-permute-start | bytes 110600 | tf_op jit(solution)/shard_map/ppermute | solution.py:209
  29.1 0.6 %collective-permute-start.21 = (bf16[16,1152]{1,0:T(8,128)(2,1)S(1)}, bf16[16,1152]{1,0:T(8,128)(2,1)S(1)}, u32[]{:S(2)}, u32[]{:S(2)}) collective-permute-start(bf16[16,1152]{1,0:T(8,128)(2,1)S(1)} %get-tuple-element.17.refs_3_), channel_id=1, source_target_pairs={{0,17},{1,0},{2,19},{3,2},{4,21},{5,4},{6,23},{7,6},{8,25},{9,8},{... | collective-permute-start | bytes 110600 | tf_op jit(solution)/shard_map/ppermute | solution.py:209
  29.8 0.4 %collective-permute-start.23 = (bf16[16,1152]{1,0:T(8,128)(2,1)S(1)}, bf16[16,1152]{1,0:T(8,128)(2,1)S(1)}, u32[]{:S(2)}, u32[]{:S(2)}) collective-permute-start(bf16[16,1152]{1,0:T(8,128)(2,1)S(1)} %get-tuple-element.17.refs_3_), channel_id=1, source_target_pairs={{0,1},{1,0},{2,3},{3,2},{4,5},{5,4},{6,7},{7,6},{8,9},{9,8},{10,11... | collective-permute-start | bytes 110600 | tf_op jit(solution)/shard_map/ppermute | solution.py:108
  30.3 1.1 %collective-permute-done.24._.refs_6_ = f32[16,512]{1,0:T(8,128)S(1)} collective-permute-done((f32[16,512]{1,0:T(8,128)S(1)}, f32[16,512]{1,0:T(8,128)S(1)}, u32[]{:S(2)}, u32[]{:S(2)}) %collective-permute-start.24) | collective-permute-done | bytes 32800 | tf_op jit(solution)/shard_map/ppermute | solution.py:108
  31.5 1.8 %collective-permute-start.25 = (f32[32,128]{1,0:T(8,128)S(1)}, f32[32,128]{1,0:T(8,128)S(1)}, u32[]{:S(2)}, u32[]{:S(2)}) collective-permute-start(f32[32,128]{1,0:T(8,128)S(1)} %get-tuple-element.19), channel_id=1, source_target_pairs={{0,1},{1,6},{2,3},{3,4},{4,5},{5,2},{6,7},{7,0},{8,9},{9,14},{10,1... | collective-permute-start | bytes 49160 | tf_op jit(solution)/shard_map/ppermute | solution.py:209
  33.3 0.2 collective-permute-start.26
  33.5 1.1 %collective-permute-start.27 = (f32[32,128]{1,0:T(8,128)S(1)}, f32[32,128]{1,0:T(8,128)S(1)}, u32[]{:S(2)}, u32[]{:S(2)}) collective-permute-start(f32[32,128]{1,0:T(8,128)S(1)} %get-tuple-element.19), channel_id=1, source_target_pairs={{0,1},{1,2},{2,3},{3,0},{4,5},{5,6},{6,7},{7,4},{8,9},{9,10},{10,1... | collective-permute-start | bytes 49160 | tf_op jit(solution)/shard_map/ppermute | solution.py:209
  34.6 0.5 %collective-permute-start.30 = (bf16[48,512]{1,0:T(8,128)(2,1)S(1)}, bf16[48,512]{1,0:T(8,128)(2,1)S(1)}, u32[]{:S(2)}, u32[]{:S(2)}) collective-permute-start(bf16[48,512]{1,0:T(8,128)(2,1)S(1)} %get-tuple-element.21), channel_id=1, source_target_pairs={{0,1},{1,0},{2,3},{3,2},{4,5},{5,4},{6,7},{7,6},{8,9},{9,8},{10,11... | collective-permute-start | bytes 147464 | tf_op jit(solution)/shard_map/ppermute | solution.py:108
  35.1 1.3 %collective-permute-done.25.third_ref = f32[32,128]{1,0:T(8,128)S(1)} collective-permute-done((f32[32,128]{1,0:T(8,128)S(1)}, f32[32,128]{1,0:T(8,128)S(1)}, u32[]{:S(2)}, u32[]{:S(2)}) %collective-permute-start.25) | collective-permute-done | bytes 16416 | tf_op jit(solution)/shard_map/ppermute | solution.py:209
  36.5 0.9 %collective-permute-done.26.second_ref = f32[32,128]{1,0:T(8,128)S(1)} collective-permute-done((f32[32,128]{1,0:T(8,128)S(1)}, f32[32,128]{1,0:T(8,128)S(1)}, u32[]{:S(2)}, u32[]{:S(2)}) %collective-permute-start.26) | collective-permute-done | bytes 16416 | tf_op jit(solution)/shard_map/ppermute | solution.py:209
  37.4 0.1 shard_map.161.refs_8_
  37.5 1.0 %collective-permute-done.29.refs_1_ = f32[32,128]{1,0:T(8,128)S(1)} collective-permute-done((f32[32,128]{1,0:T(8,128)S(1)}, f32[32,128]{1,0:T(8,128)S(1)}, u32[]{:S(2)}, u32[]{:S(2)}) %collective-permute-start.29) | collective-permute-done | bytes 16416 | tf_op jit(solution)/shard_map/ppermute | solution.py:108
  38.6 1.1 %shard_map.162 = (bf16[16,512]{1,0:T(8,128)(2,1)}, f32[2]{0:T(128)}, bf16[16,512]{1,0:T(8,128)(2,1)}) custom-call(f32[32,128]{1,0:T(8,128)S(1)} %shard_map.160.refs_0_, f32[32,128]{1,0:T(8,128)S(1)} %collective-permute-done.29.refs_1_, bf16[64,512]{1,0:T(8,128)(2,1)S(1)} %get-tuple-element.20.refs_2_, bf16[16,1152]{1,0:T(8,128)(2,1)S(1)} %get-tuple-element.17.refs_3_, ...), custom_call_target="tpu_custom_call" | custom-call | tf_op jit(solution)/shard_map/pallas_call | solution.py:790
  (62 shorter events, 0.7 us)
Async XLA Ops:
  0.6 2.1 %collective-permute-start = (bf16[16,512]{1,0:T(8,128)(2,1)}, bf16[16,512]{1,0:T(8,128)(2,1)S(1)}, u32[]{:S(2)}, u32[]{:S(2)}) collective-permute-start(bf16[16,512]{1,0:T(8,128)(2,1)} %own_ref.3), channel_id=1, source_target_pairs={{0,1},{1,0},{2,3},{3,2},{4,5},{5,4},{6,7},{7,6},{8,9},{9,8},{10,11... | collective-permute-start | bytes 49160 | tf_op jit(solution)/shard_map/ppermute | solution.py:108
  1.1 1.4 %collective-permute-start.1 = (f32[1,512]{1,0:T(1,128)}, f32[1,512]{1,0:T(1,128)S(1)}, u32[]{:S(2)}, u32[]{:S(2)}) collective-permute-start(f32[1,512]{1,0:T(1,128)} %bitcast.10), channel_id=1, source_target_pairs={{0,1},{1,0},{2,3},{3,2},{4,5},{5,4},{6,7},{7,6},{8,9},{9,8},{10,11... | collective-permute-start | bytes 6152 | tf_op jit(solution)/shard_map/ppermute | solution.py:108
  1.2 1.5 %copy-start.4 = (bf16[16,512]{1,0:T(8,128)(2,1)S(1)}, bf16[16,512]{1,0:T(8,128)(2,1)}, u32[]{:S(2)}) copy-start(bf16[16,512]{1,0:T(8,128)(2,1)} %own_ref.3) | copy-start | bytes 49156
  1.2 1.5 %copy-start.11 = (f32[512]{0:T(512)S(1)}, f32[512]{0:T(512)}, u32[]{:S(2)}) copy-start(f32[512]{0:T(512)} %param.13) | copy-start | bytes 6148
  1.2 1.5 %collective-permute-start.2 = (f32[1,512]{1,0:T(1,128)}, f32[1,512]{1,0:T(1,128)S(1)}, u32[]{:S(2)}, u32[]{:S(2)}) collective-permute-start(f32[1,512]{1,0:T(1,128)} %bitcast.4), channel_id=1, source_target_pairs={{0,1},{1,0},{2,3},{3,2},{4,5},{5,4},{6,7},{7,6},{8,9},{9,8},{10,11... | collective-permute-start | bytes 6152 | tf_op jit(solution)/shard_map/ppermute | solution.py:108
  1.7 8.3 %collective-permute-start.6 = (bf16[4096,512]{1,0:T(8,128)(2,1)}, bf16[4096,512]{1,0:T(8,128)(2,1)S(1)}, u32[]{:S(2)}, u32[]{:S(2)}) collective-permute-start(bf16[4096,512]{1,0:T(8,128)(2,1)} %refs_4_.1), channel_id=1, source_target_pairs={{0,1},{1,0},{2,3},{3,2},{4,5},{5,4},{6,7},{7,6},{8,9},{9,8},{10,11... | collective-permute-start | bytes 12582920 | tf_op jit(solution)/shard_map/ppermute | solution.py:108
  2.7 5.0 %copy-start.1 = (bf16[4096,512]{1,0:T(8,128)(2,1)S(1)}, bf16[4096,512]{1,0:T(8,128)(2,1)}, u32[]{:S(2)}) copy-start(bf16[4096,512]{1,0:T(8,128)(2,1)} %refs_4_.1) | copy-start | bytes 12582916
  2.9 5.0 %copy-start.2 = (bf16[320,1024]{1,0:T(8,128)(2,1)S(1)}, bf16[320,1024]{1,0:T(8,128)(2,1)}, u32[]{:S(2)}) copy-start(bf16[320,1024]{1,0:T(8,128)(2,1)} %refs_1_.11) | copy-start | bytes 1966084
  2.9 5.0 %copy-start.3 = (bf16[320,1024]{1,0:T(8,128)(2,1)S(1)}, bf16[320,1024]{1,0:T(8,128)(2,1)}, u32[]{:S(2)}) copy-start(bf16[320,1024]{1,0:T(8,128)(2,1)} %refs_2_.5) | copy-start | bytes 1966084
  2.9 6.4 %collective-permute-start.3 = (bf16[16,1152]{1,0:T(8,128)(2,1)S(1)}, bf16[16,1152]{1,0:T(8,128)(2,1)S(1)}, u32[]{:S(2)}, u32[]{:S(2)}) collective-permute-start(bf16[16,1152]{1,0:T(8,128)(2,1)S(1)} %shard_map.140.message_ref.refs_3_.pair_ref), channel_id=1, source_target_pairs={{0,7},{1,0},{2,5},{3,2},{4,3},{5,4},{6,1},{7,6},{8,15},{9,8},{10,1... | collective-permute-start | bytes 110600 | tf_op jit(solution)/shard_map/ppermute | solution.py:209
  7.7 2.0 %collective-permute-start.4 = (bf16[16,1152]{1,0:T(8,128)(2,1)S(1)}, bf16[16,1152]{1,0:T(8,128)(2,1)S(1)}, u32[]{:S(2)}, u32[]{:S(2)}) collective-permute-start(bf16[16,1152]{1,0:T(8,128)(2,1)S(1)} %shard_map.140.message_ref.refs_3_.pair_ref), channel_id=1, source_target_pairs={{0,5},{1,0},{2,7},{3,2},{4,1},{5,4},{6,3},{7,6},{8,13},{9,8},{10,1... | collective-permute-start | bytes 110600 | tf_op jit(solution)/shard_map/ppermute | solution.py:209
  7.7 2.3 %collective-permute-start.5 = (bf16[16,1152]{1,0:T(8,128)(2,1)S(1)}, bf16[16,1152]{1,0:T(8,128)(2,1)S(1)}, u32[]{:S(2)}, u32[]{:S(2)}) collective-permute-start(bf16[16,1152]{1,0:T(8,128)(2,1)S(1)} %shard_map.140.message_ref.refs_3_.pair_ref), channel_id=1, source_target_pairs={{0,3},{1,0},{2,1},{3,2},{4,7},{5,4},{6,5},{7,6},{8,11},{9,8},{10,9... | collective-permute-start | bytes 110600 | tf_op jit(solution)/shard_map/ppermute | solution.py:209
  7.9 0.7 %copy-start.6 = (s32[1,16]{1,0:T(1,128)S(1)}, s32[1,16]{1,0:T(1,128)}, u32[]{:S(2)}) copy-start(s32[1,16]{1,0:T(1,128)} %lengths_ref.1) | copy-start | bytes 196
  7.9 0.7 %copy-start.7 = (s32[1,16]{1,0:T(1,128)S(1)}, s32[1,16]{1,0:T(1,128)}, u32[]{:S(2)}) copy-start(s32[1,16]{1,0:T(1,128)} %order_ref.1) | copy-start | bytes 196
  7.9 0.7 %copy-start.10 = (f32[1,128]{1,0:T(1,128)S(1)}, f32[1,128]{1,0:T(1,128)}, u32[]{:S(2)}) copy-start(f32[1,128]{1,0:T(1,128)} %constant.2.clone.frequency_ref) | copy-start | bytes 1540
  8.0 2.0 %copy-start.8 = (f32[128]{0:T(128)S(1)}, f32[128]{0:T(128)}, u32[]{:S(2)}) copy-start(f32[128]{0:T(128)} %param.15) | copy-start | bytes 1540
  8.1 6.7 %collective-permute-start.8 = (bf16[2,320,1024]{2,1,0:T(8,128)(2,1)S(1)}, bf16[2,320,1024]{2,1,0:T(8,128)(2,1)S(1)}, u32[]{:S(2)}, u32[]{:S(2)}) collective-permute-start(bf16[2,320,1024]{2,1,0:T(8,128)(2,1)S(1)} %shard_map.146), channel_id=1, source_target_pairs={{0,1},{1,0},{2,3},{3,2},{4,5},{5,4},{6,7},{7,6},{8,9},{9,8},{10,11... | collective-permute-start | bytes 3932168 | tf_op jit(solution)/shard_map/ppermute | solution.py:108
  10.0 4.5 %copy-start = (bf16[512,4096]{1,0:T(8,128)(2,1)S(1)}, bf16[512,4096]{1,0:T(8,128)(2,1)}, u32[]{:S(2)}) copy-start(bf16[512,4096]{1,0:T(8,128)(2,1)} %refs_1_.17) | copy-start | bytes 12582916
  10.0 6.6 %collective-permute-start.7 = (bf16[16,1024]{1,0:T(8,128)(2,1)S(1)}, bf16[16,1024]{1,0:T(8,128)(2,1)S(1)}, u32[]{:S(2)}, u32[]{:S(2)}) collective-permute-start(bf16[16,1024]{1,0:T(8,128)(2,1)S(1)} %shard_map.145.query_ref.refs_0_), channel_id=1, source_target_pairs={{0,1},{1,6},{2,3},{3,4},{4,5},{5,2},{6,7},{7,0},{8,9},{9,14},{10,1... | collective-permute-start | bytes 98312 | tf_op jit(solution)/shard_map/ppermute | solution.py:209
  13.2 4.6 %collective-permute-start.10 = (bf16[16,1024]{1,0:T(8,128)(2,1)S(1)}, bf16[16,1024]{1,0:T(8,128)(2,1)S(1)}, u32[]{:S(2)}, u32[]{:S(2)}) collective-permute-start(bf16[16,1024]{1,0:T(8,128)(2,1)S(1)} %shard_map.145.query_ref.refs_0_), channel_id=1, source_target_pairs={{0,1},{1,4},{2,3},{3,6},{4,5},{5,0},{6,7},{7,2},{8,9},{9,12},{10,1... | collective-permute-start | bytes 98312 | tf_op jit(solution)/shard_map/ppermute | solution.py:209
  13.9 4.4 %collective-permute-start.12 = (bf16[16,1024]{1,0:T(8,128)(2,1)S(1)}, bf16[16,1024]{1,0:T(8,128)(2,1)S(1)}, u32[]{:S(2)}, u32[]{:S(2)}) collective-permute-start(bf16[16,1024]{1,0:T(8,128)(2,1)S(1)} %shard_map.145.query_ref.refs_0_), channel_id=1, source_target_pairs={{0,1},{1,2},{2,3},{3,0},{4,5},{5,6},{6,7},{7,4},{8,9},{9,10},{10,1... | collective-permute-start | bytes 98312 | tf_op jit(solution)/shard_map/ppermute | solution.py:209
  14.7 5.9 %collective-permute-start.14 = (bf16[2,512,1024]{2,1,0:T(8,128)(2,1)S(1)}, bf16[2,512,1024]{2,1,0:T(8,128)(2,1)S(1)}, u32[]{:S(2)}, u32[]{:S(2)}) collective-permute-start(bf16[2,512,1024]{2,1,0:T(8,128)(2,1)S(1)} %shard_map.152), channel_id=1, source_target_pairs={{0,1},{1,0},{2,3},{3,2},{4,5},{5,4},{6,7},{7,6},{8,9},{9,8},{10,11... | collective-permute-start | bytes 6291464 | tf_op jit(solution)/shard_map/ppermute | solution.py:108
  17.1 2.5 %collective-permute-start.9 = (bf16[16,1152]{1,0:T(8,128)(2,1)S(1)}, bf16[16,1152]{1,0:T(8,128)(2,1)S(1)}, u32[]{:S(2)}, u32[]{:S(2)}) collective-permute-start(bf16[16,1152]{1,0:T(8,128)(2,1)S(1)} %shard_map.148.refs_5_), channel_id=1, source_target_pairs={{0,7},{1,0},{2,5},{3,2},{4,3},{5,4},{6,1},{7,6},{8,15},{9,8},{10,1... | collective-permute-start | bytes 110600 | tf_op jit(solution)/shard_map/ppermute | solution.py:209
  18.3 1.7 %collective-permute-start.11 = (bf16[16,1152]{1,0:T(8,128)(2,1)S(1)}, bf16[16,1152]{1,0:T(8,128)(2,1)S(1)}, u32[]{:S(2)}, u32[]{:S(2)}) collective-permute-start(bf16[16,1152]{1,0:T(8,128)(2,1)S(1)} %shard_map.149.refs_5_), channel_id=1, source_target_pairs={{0,5},{1,0},{2,7},{3,2},{4,1},{5,4},{6,3},{7,6},{8,13},{9,8},{10,1... | collective-permute-start | bytes 110600 | tf_op jit(solution)/shard_map/ppermute | solution.py:209
  18.9 1.7 %collective-permute-start.13 = (bf16[16,1152]{1,0:T(8,128)(2,1)S(1)}, bf16[16,1152]{1,0:T(8,128)(2,1)S(1)}, u32[]{:S(2)}, u32[]{:S(2)}) collective-permute-start(bf16[16,1152]{1,0:T(8,128)(2,1)S(1)} %shard_map.150.refs_0_), channel_id=1, source_target_pairs={{0,3},{1,0},{2,1},{3,2},{4,7},{5,4},{6,5},{7,6},{8,11},{9,8},{10,9... | collective-permute-start | bytes 110600 | tf_op jit(solution)/shard_map/ppermute | solution.py:209
  19.1 4.5 %collective-permute-start.17 = (bf16[2,512,1024]{2,1,0:T(8,128)(2,1)S(1)}, bf16[2,512,1024]{2,1,0:T(8,128)(2,1)S(1)}, u32[]{:S(2)}, u32[]{:S(2)}) collective-permute-start(bf16[2,512,1024]{2,1,0:T(8,128)(2,1)S(1)} %shard_map.155), channel_id=1, source_target_pairs={{0,1},{1,0},{2,3},{3,2},{4,5},{5,4},{6,7},{7,6},{8,9},{9,8},{10,11... | collective-permute-start | bytes 6291464 | tf_op jit(solution)/shard_map/ppermute | solution.py:108
  20.6 6.0 %collective-permute-start.15 = (bf16[16,1024]{1,0:T(8,128)(2,1)S(1)}, bf16[16,1024]{1,0:T(8,128)(2,1)S(1)}, u32[]{:S(2)}, u32[]{:S(2)}) collective-permute-start(bf16[16,1024]{1,0:T(8,128)(2,1)S(1)} %shard_map.153.refs_3_), channel_id=1, source_target_pairs={{0,1},{1,6},{2,3},{3,4},{4,5},{5,2},{6,7},{7,0},{8,9},{9,14},{10,1... | collective-permute-start | bytes 98312 | tf_op jit(solution)/shard_map/ppermute | solution.py:209
  23.2 4.3 %collective-permute-start.16 = (bf16[16,1024]{1,0:T(8,128)(2,1)S(1)}, bf16[16,1024]{1,0:T(8,128)(2,1)S(1)}, u32[]{:S(2)}, u32[]{:S(2)}) collective-permute-start(bf16[16,1024]{1,0:T(8,128)(2,1)S(1)} %shard_map.154.refs_3_), channel_id=1, source_target_pairs={{0,1},{1,4},{2,3},{3,6},{4,5},{5,0},{6,7},{7,2},{8,9},{9,12},{10,1... | collective-permute-start | bytes 98312 | tf_op jit(solution)/shard_map/ppermute | solution.py:209
  23.6 4.2 %copy-start.5 = (f32[512]{0:T(512)S(1)}, f32[512]{0:T(512)}, u32[]{:S(2)}) copy-start(f32[512]{0:T(512)} %param.19) | copy-start | bytes 6148
  23.6 4.2 %collective-permute-start.18 = (bf16[16,1024]{1,0:T(8,128)(2,1)S(1)}, bf16[16,1024]{1,0:T(8,128)(2,1)S(1)}, u32[]{:S(2)}, u32[]{:S(2)}) collective-permute-start(bf16[16,1024]{1,0:T(8,128)(2,1)S(1)} %shard_map.156.refs_3_), channel_id=1, source_target_pairs={{0,1},{1,2},{2,3},{3,0},{4,5},{5,6},{6,7},{7,4},{8,9},{9,10},{10,1... | collective-permute-start | bytes 98312 | tf_op jit(solution)/shard_map/ppermute | solution.py:209
  24.5 3.4 %collective-permute-start.19 = (bf16[16,1024]{1,0:T(8,128)(2,1)S(1)}, bf16[16,1024]{1,0:T(8,128)(2,1)S(1)}, u32[]{:S(2)}, u32[]{:S(2)}) collective-permute-start(bf16[16,1024]{1,0:T(8,128)(2,1)S(1)} %shard_map.157), channel_id=1, source_target_pairs={{0,1},{1,0},{2,3},{3,2},{4,5},{5,4},{6,7},{7,6},{8,9},{9,8},{10,11... | collective-permute-start | bytes 98312 | tf_op jit(solution)/shard_map/ppermute | solution.py:108
  28.0 9.4 %copy-start.9 = (s32[64]{0:T(128)S(1)}, s32[64]{0:T(128)}, u32[]{:S(2)}) copy-start(s32[64]{0:T(128)} %param.22) | copy-start | bytes 772
  28.0 3.4 %collective-permute-start.20 = (bf16[16,1152]{1,0:T(8,128)(2,1)S(1)}, bf16[16,1152]{1,0:T(8,128)(2,1)S(1)}, u32[]{:S(2)}, u32[]{:S(2)}) collective-permute-start(bf16[16,1152]{1,0:T(8,128)(2,1)S(1)} %get-tuple-element.17.refs_3_), channel_id=1, source_target_pairs={{0,25},{1,0},{2,27},{3,2},{4,29},{5,4},{6,31},{7,6},{8,17},{9,8},{... | collective-permute-start | bytes 110600 | tf_op jit(solution)/shard_map/ppermute | solution.py:209
  29.1 2.3 %collective-permute-start.21 = (bf16[16,1152]{1,0:T(8,128)(2,1)S(1)}, bf16[16,1152]{1,0:T(8,128)(2,1)S(1)}, u32[]{:S(2)}, u32[]{:S(2)}) collective-permute-start(bf16[16,1152]{1,0:T(8,128)(2,1)S(1)} %get-tuple-element.17.refs_3_), channel_id=1, source_target_pairs={{0,17},{1,0},{2,19},{3,2},{4,21},{5,4},{6,23},{7,6},{8,25},{9,8},{... | collective-permute-start | bytes 110600 | tf_op jit(solution)/shard_map/ppermute | solution.py:209
  29.7 1.7 %collective-permute-start.22 = (bf16[16,1152]{1,0:T(8,128)(2,1)S(1)}, bf16[16,1152]{1,0:T(8,128)(2,1)S(1)}, u32[]{:S(2)}, u32[]{:S(2)}) collective-permute-start(bf16[16,1152]{1,0:T(8,128)(2,1)S(1)} %get-tuple-element.17.refs_3_), channel_id=1, source_target_pairs={{0,9},{1,0},{2,11},{3,2},{4,13},{5,4},{6,15},{7,6},{8,1},{9,8},{10... | collective-permute-start | bytes 110600 | tf_op jit(solution)/shard_map/ppermute | solution.py:209
  29.8 1.7 %collective-permute-start.23 = (bf16[16,1152]{1,0:T(8,128)(2,1)S(1)}, bf16[16,1152]{1,0:T(8,128)(2,1)S(1)}, u32[]{:S(2)}, u32[]{:S(2)}) collective-permute-start(bf16[16,1152]{1,0:T(8,128)(2,1)S(1)} %get-tuple-element.17.refs_3_), channel_id=1, source_target_pairs={{0,1},{1,0},{2,3},{3,2},{4,5},{5,4},{6,7},{7,6},{8,9},{9,8},{10,11... | collective-permute-start | bytes 110600 | tf_op jit(solution)/shard_map/ppermute | solution.py:108
  30.2 1.2 %collective-permute-start.24 = (f32[16,512]{1,0:T(8,128)S(1)}, f32[16,512]{1,0:T(8,128)S(1)}, u32[]{:S(2)}, u32[]{:S(2)}) collective-permute-start(f32[16,512]{1,0:T(8,128)S(1)} %get-tuple-element.18), channel_id=1, source_target_pairs={{0,1},{1,0},{2,3},{3,2},{4,5},{5,4},{6,7},{7,6},{8,9},{9,8},{10,11... | collective-permute-start | bytes 98312 | tf_op jit(solution)/shard_map/ppermute | solution.py:108
  31.5 5.0 %collective-permute-start.25 = (f32[32,128]{1,0:T(8,128)S(1)}, f32[32,128]{1,0:T(8,128)S(1)}, u32[]{:S(2)}, u32[]{:S(2)}) collective-permute-start(f32[32,128]{1,0:T(8,128)S(1)} %get-tuple-element.19), channel_id=1, source_target_pairs={{0,1},{1,6},{2,3},{3,4},{4,5},{5,2},{6,7},{7,0},{8,9},{9,14},{10,1... | collective-permute-start | bytes 49160 | tf_op jit(solution)/shard_map/ppermute | solution.py:209
  33.3 4.1 %collective-permute-start.26 = (f32[32,128]{1,0:T(8,128)S(1)}, f32[32,128]{1,0:T(8,128)S(1)}, u32[]{:S(2)}, u32[]{:S(2)}) collective-permute-start(f32[32,128]{1,0:T(8,128)S(1)} %get-tuple-element.19), channel_id=1, source_target_pairs={{0,1},{1,4},{2,3},{3,6},{4,5},{5,0},{6,7},{7,2},{8,9},{9,12},{10,1... | collective-permute-start | bytes 49160 | tf_op jit(solution)/shard_map/ppermute | solution.py:209
  33.5 3.9 %collective-permute-start.27 = (f32[32,128]{1,0:T(8,128)S(1)}, f32[32,128]{1,0:T(8,128)S(1)}, u32[]{:S(2)}, u32[]{:S(2)}) collective-permute-start(f32[32,128]{1,0:T(8,128)S(1)} %get-tuple-element.19), channel_id=1, source_target_pairs={{0,1},{1,2},{2,3},{3,0},{4,5},{5,6},{6,7},{7,4},{8,9},{9,10},{10,1... | collective-permute-start | bytes 49160 | tf_op jit(solution)/shard_map/ppermute | solution.py:209
  34.6 2.7 %collective-permute-start.28 = (f32[32,128]{1,0:T(8,128)S(1)}, f32[32,128]{1,0:T(8,128)S(1)}, u32[]{:S(2)}, u32[]{:S(2)}) collective-permute-start(f32[32,128]{1,0:T(8,128)S(1)} %get-tuple-element.19), channel_id=1, source_target_pairs={{0,1},{1,0},{2,3},{3,2},{4,5},{5,4},{6,7},{7,6},{8,9},{9,8},{10,11... | collective-permute-start | bytes 49160 | tf_op jit(solution)/shard_map/ppermute | solution.py:108
  34.6 4.0 %collective-permute-start.30 = (bf16[48,512]{1,0:T(8,128)(2,1)S(1)}, bf16[48,512]{1,0:T(8,128)(2,1)S(1)}, u32[]{:S(2)}, u32[]{:S(2)}) collective-permute-start(bf16[48,512]{1,0:T(8,128)(2,1)S(1)} %get-tuple-element.21), channel_id=1, source_target_pairs={{0,1},{1,0},{2,3},{3,2},{4,5},{5,4},{6,7},{7,6},{8,9},{9,8},{10,11... | collective-permute-start | bytes 147464 | tf_op jit(solution)/shard_map/ppermute | solution.py:108
  37.3 1.2 %collective-permute-start.29 = (f32[32,128]{1,0:T(8,128)S(1)}, f32[32,128]{1,0:T(8,128)S(1)}, u32[]{:S(2)}, u32[]{:S(2)}) collective-permute-start(f32[32,128]{1,0:T(8,128)S(1)} %shard_map.160.refs_0_), channel_id=1, source_target_pairs={{0,1},{1,0},{2,3},{3,2},{4,5},{5,4},{6,7},{7,6},{8,9},{9,8},{10,11... | collective-permute-start | bytes 49160 | tf_op jit(solution)/shard_map/ppermute | solution.py:108

commit v12 on v11

--- a/solution.py
+++ b/solution.py
@@ -569,15 +569,12 @@
     inner = jnp.sum(weights * cosines, axis=1, keepdims=True)
     scaled_weights = weights * column_scale
     coarse = scaled_weights.astype(jnp.bfloat16)
-    fine = (scaled_weights - coarse.astype(jnp.float32)).astype(jnp.bfloat16)
     own_scale = row_scale[:rows]
     pooled_scale = lax.rsqrt(squares / model_width + EPSILON)
     grad_gain = gain_ref[...] * (model_width**0.5 / SOFTMAX_WARMTH)
 
     def write(vectors, scaled):
-        gradient = jnp.dot(coarse, vectors, preferred_element_type=jnp.float32) + jnp.dot(
-            fine, vectors, preferred_element_type=jnp.float32
-        )
+        gradient = jnp.dot(coarse, vectors, preferred_element_type=jnp.float32)
         gradient = (gradient - scaled * (own_scale * inner)) * own_scale
         grad_ref[...] = (gradient * grad_gain).astype(jnp.bfloat16)
         pooled_ref[...] = (scaled * pooled_scale).astype(jnp.bfloat16)

time: 39.8 us -> 39.8 us (level)
  no operation moved by 1% of the time
where the time goes in v12:
time: 39.8 us; the launch traced here: 39.7 us
  starting transfers between devices  22.9 us (58%)
  waiting for transfers between devices  11.9 us (30%)
  Pallas kernels  3.95 us (10%)
  between operations  0.84 us (2%)
    ppermute x18, starting transfers between devices, send_across(): return lax.ppermute(array, ('dp', 'pack'), pairs)  18.2 us
    ppermute x18, waiting for transfers between devices, send_across(): return lax.ppermute(array, ('dp', 'pack'), pairs)  8.71 us
    ppermute x13, starting transfers between devices, flip(): return lax.ppermute(array, axis, [(i, i ^ offset) for i in range(size)])  4.73 us
    ppermute x13, waiting for transfers between devices, flip(): return lax.ppermute(array, axis, [(i, i ^ offset) for i in range(size)])  3.17 us
    pallas_call x22, Pallas kernels, in_vmem(): pl.pallas_call(body, out_shape=outputs, in_specs=[whole] * len(operands),...  2.88 us
    pallas_call x1, Pallas kernels, core_roles(): pl.pallas_call(lambda *refs: losses_and_gradient(*refs, model_width=model...  1.07 us
  transfers between devices with their start and end apart: 31, of which 16 were waited for; matrix products, arithmetic and copies ran while one was open for 0% of the time, Pallas kernels for 7%

profile of v12, /device:TPU:0, one launch (start us, length us, event | category | flops | bytes accessed | tf_op | source)
XLA Modules:
  0.0 39.7 jit_solution(9943379642920751354)
XLA Ops:
  0.6 0.5 %collective-permute-start = (bf16[16,512]{1,0:T(8,128)(2,1)}, bf16[16,512]{1,0:T(8,128)(2,1)S(1)}, u32[]{:S(2)}, u32[]{:S(2)}) collective-permute-start(bf16[16,512]{1,0:T(8,128)(2,1)} %own_ref.3), channel_id=1, source_target_pairs={{0,1},{1,0},{2,3},{3,2},{4,5},{5,4},{6,7},{7,6},{8,9},{9,8},{10,11... | collective-permute-start | bytes 49160 | tf_op jit(solution)/shard_map/ppermute | solution.py:108
  1.2 0.4 %collective-permute-start.2 = (f32[1,512]{1,0:T(1,128)}, f32[1,512]{1,0:T(1,128)S(1)}, u32[]{:S(2)}, u32[]{:S(2)}) collective-permute-start(f32[1,512]{1,0:T(1,128)} %bitcast.4), channel_id=1, source_target_pairs={{0,1},{1,0},{2,3},{3,2},{4,5},{5,4},{6,7},{7,6},{8,9},{9,8},{10,11... | collective-permute-start | bytes 6152 | tf_op jit(solution)/shard_map/ppermute | solution.py:108
  1.7 0.8 %collective-permute-done.1.other_gain_ref = f32[1,512]{1,0:T(1,128)S(1)} collective-permute-done((f32[1,512]{1,0:T(1,128)}, f32[1,512]{1,0:T(1,128)S(1)}, u32[]{:S(2)}, u32[]{:S(2)}) %collective-permute-start.1) | collective-permute-done | bytes 2080 | tf_op jit(solution)/shard_map/ppermute | solution.py:108
  2.5 0.2 collective-permute-done.2._last.other_gain_ref
  2.7 0.2 shard_map.140.message_ref.refs_3_.pair_ref
  2.9 4.8 %collective-permute-start.3 = (bf16[16,1152]{1,0:T(8,128)(2,1)S(1)}, bf16[16,1152]{1,0:T(8,128)(2,1)S(1)}, u32[]{:S(2)}, u32[]{:S(2)}) collective-permute-start(bf16[16,1152]{1,0:T(8,128)(2,1)S(1)} %shard_map.140.message_ref.refs_3_.pair_ref), channel_id=1, source_target_pairs={{0,7},{1,0},{2,5},{3,2},{4,3},{5,4},{6,1},{7,6},{8,15},{9,8},{10,1... | collective-permute-start | bytes 110600 | tf_op jit(solution)/shard_map/ppermute | solution.py:209
  7.7 0.2 shard_map.143.refs_7_._
  8.0 0.1 shard_map.146
  8.1 0.6 %collective-permute-start.8 = (bf16[2,320,1024]{2,1,0:T(8,128)(2,1)S(1)}, bf16[2,320,1024]{2,1,0:T(8,128)(2,1)S(1)}, u32[]{:S(2)}, u32[]{:S(2)}) collective-permute-start(bf16[2,320,1024]{2,1,0:T(8,128)(2,1)S(1)} %shard_map.146), channel_id=1, source_target_pairs={{0,1},{1,0},{2,3},{3,2},{4,5},{5,4},{6,7},{7,6},{8,9},{9,8},{10,11... | collective-permute-start | bytes 3932168 | tf_op jit(solution)/shard_map/ppermute | solution.py:108
  8.6 0.2 shard_map.141
  8.8 0.5 %collective-permute-done.3.refs_0_ = bf16[16,1152]{1,0:T(8,128)(2,1)S(1)} collective-permute-done((bf16[16,1152]{1,0:T(8,128)(2,1)S(1)}, bf16[16,1152]{1,0:T(8,128)(2,1)S(1)}, u32[]{:S(2)}, u32[]{:S(2)}) %collective-permute-start.3) | collective-permute-done | bytes 36896 | tf_op jit(solution)/shard_map/ppermute | solution.py:209
  9.3 0.3 collective-permute-done.4.refs_1_
  9.6 0.3 collective-permute-done.5.refs_2_
  10.0 3.1 %collective-permute-start.7 = (bf16[16,1024]{1,0:T(8,128)(2,1)S(1)}, bf16[16,1024]{1,0:T(8,128)(2,1)S(1)}, u32[]{:S(2)}, u32[]{:S(2)}) collective-permute-start(bf16[16,1024]{1,0:T(8,128)(2,1)S(1)} %shard_map.145.query_ref.refs_0_), channel_id=1, source_target_pairs={{0,1},{1,6},{2,3},{3,4},{4,5},{5,2},{6,7},{7,0},{8,9},{9,14},{10,1... | collective-permute-start | bytes 98312 | tf_op jit(solution)/shard_map/ppermute | solution.py:209
  13.2 0.7 %collective-permute-start.10 = (bf16[16,1024]{1,0:T(8,128)(2,1)S(1)}, bf16[16,1024]{1,0:T(8,128)(2,1)S(1)}, u32[]{:S(2)}, u32[]{:S(2)}) collective-permute-start(bf16[16,1024]{1,0:T(8,128)(2,1)S(1)} %shard_map.145.query_ref.refs_0_), channel_id=1, source_target_pairs={{0,1},{1,4},{2,3},{3,6},{4,5},{5,0},{6,7},{7,2},{8,9},{9,12},{10,1... | collective-permute-start | bytes 98312 | tf_op jit(solution)/shard_map/ppermute | solution.py:209
  13.9 0.6 %collective-permute-start.12 = (bf16[16,1024]{1,0:T(8,128)(2,1)S(1)}, bf16[16,1024]{1,0:T(8,128)(2,1)S(1)}, u32[]{:S(2)}, u32[]{:S(2)}) collective-permute-start(bf16[16,1024]{1,0:T(8,128)(2,1)S(1)} %shard_map.145.query_ref.refs_0_), channel_id=1, source_target_pairs={{0,1},{1,2},{2,3},{3,0},{4,5},{5,6},{6,7},{7,4},{8,9},{9,10},{10,1... | collective-permute-start | bytes 98312 | tf_op jit(solution)/shard_map/ppermute | solution.py:209
  14.5 0.1 shard_map.152
  14.8 1.8 %collective-permute-done.7.refs_0_ = bf16[16,1024]{1,0:T(8,128)(2,1)S(1)} collective-permute-done((bf16[16,1024]{1,0:T(8,128)(2,1)S(1)}, bf16[16,1024]{1,0:T(8,128)(2,1)S(1)}, u32[]{:S(2)}, u32[]{:S(2)}) %collective-permute-start.7) | collective-permute-done | bytes 32800 | tf_op jit(solution)/shard_map/ppermute | solution.py:209
  16.6 0.5 %shard_map.148.refs_5_ = bf16[16,1152]{1,0:T(8,128)(2,1)S(1)} custom-call(bf16[16,1024]{1,0:T(8,128)(2,1)S(1)} %collective-permute-done.7.refs_0_, bf16[320,1024]{1,0:T(8,128)(2,1)S(1)} %copy-done.2, bf16[320,1024]{1,0:T(8,128)(2,1)S(1)} %copy-done.3, bf16[2,320,1024]{2,1,0:T(8,128)(2,1)S(1)} %collective-permute-done.8.other_ref.refs_3_, ...), custom_call_target="tpu_custom_call" | custom-call | flops 17179869184 | bytes 2736128 | tf_op jit(solution)/shard_map/pallas_call | solution.py:114
  17.1 0.1 collective-permute-start.9
  17.2 0.5 %collective-permute-done.10.refs_0_ = bf16[16,1024]{1,0:T(8,128)(2,1)S(1)} collective-permute-done((bf16[16,1024]{1,0:T(8,128)(2,1)S(1)}, bf16[16,1024]{1,0:T(8,128)(2,1)S(1)}, u32[]{:S(2)}, u32[]{:S(2)}) %collective-permute-start.10) | collective-permute-done | bytes 32800 | tf_op jit(solution)/shard_map/ppermute | solution.py:209
  17.8 0.5 %shard_map.149.refs_5_ = bf16[16,1152]{1,0:T(8,128)(2,1)S(1)} custom-call(bf16[16,1024]{1,0:T(8,128)(2,1)S(1)} %collective-permute-done.10.refs_0_, bf16[320,1024]{1,0:T(8,128)(2,1)S(1)} %copy-done.2, bf16[320,1024]{1,0:T(8,128)(2,1)S(1)} %copy-done.3, bf16[2,320,1024]{2,1,0:T(8,128)(2,1)S(1)} %collective-permute-done.8.other_ref.refs_3_, ...), custom_call_target="tpu_custom_call" | custom-call | flops 17179869184 | bytes 2707456 | tf_op jit(solution)/shard_map/pallas_call | solution.py:114
  18.3 0.5 %shard_map.150.refs_0_ = bf16[16,1152]{1,0:T(8,128)(2,1)S(1)} custom-call(bf16[16,1024]{1,0:T(8,128)(2,1)S(1)} %collective-permute-done.12.refs_0_, bf16[320,1024]{1,0:T(8,128)(2,1)S(1)} %copy-done.2, bf16[320,1024]{1,0:T(8,128)(2,1)S(1)} %copy-done.3, bf16[2,320,1024]{2,1,0:T(8,128)(2,1)S(1)} %collective-permute-done.8.other_ref.refs_3_, ...), custom_call_target="tpu_custom_call" | custom-call | flops 17179869184 | bytes 2707456 | tf_op jit(solution)/shard_map/pallas_call | solution.py:114
  18.9 0.1 shard_map.155
  19.1 0.5 %collective-permute-start.17 = (bf16[2,512,1024]{2,1,0:T(8,128)(2,1)S(1)}, bf16[2,512,1024]{2,1,0:T(8,128)(2,1)S(1)}, u32[]{:S(2)}, u32[]{:S(2)}) collective-permute-start(bf16[2,512,1024]{2,1,0:T(8,128)(2,1)S(1)} %shard_map.155), channel_id=1, source_target_pairs={{0,1},{1,0},{2,3},{3,2},{4,5},{5,4},{6,7},{7,6},{8,9},{9,8},{10,11... | collective-permute-start | bytes 6291464 | tf_op jit(solution)/shard_map/ppermute | solution.py:108
  19.6 0.3 collective-permute-done.11.second_ref
  20.0 0.6 %collective-permute-done.13.first_ref = bf16[16,1152]{1,0:T(8,128)(2,1)S(1)} collective-permute-done((bf16[16,1152]{1,0:T(8,128)(2,1)S(1)}, bf16[16,1152]{1,0:T(8,128)(2,1)S(1)}, u32[]{:S(2)}, u32[]{:S(2)}) %collective-permute-start.13) | collective-permute-done | bytes 36896 | tf_op jit(solution)/shard_map/ppermute | solution.py:209
  20.6 2.7 %collective-permute-start.15 = (bf16[16,1024]{1,0:T(8,128)(2,1)S(1)}, bf16[16,1024]{1,0:T(8,128)(2,1)S(1)}, u32[]{:S(2)}, u32[]{:S(2)}) collective-permute-start(bf16[16,1024]{1,0:T(8,128)(2,1)S(1)} %shard_map.153.refs_3_), channel_id=1, source_target_pairs={{0,1},{1,6},{2,3},{3,4},{4,5},{5,2},{6,7},{7,0},{8,9},{9,14},{10,1... | collective-permute-start | bytes 98312 | tf_op jit(solution)/shard_map/ppermute | solution.py:209
  23.2 0.4 collective-permute-start.16
  23.6 0.8 %collective-permute-start.18 = (bf16[16,1024]{1,0:T(8,128)(2,1)S(1)}, bf16[16,1024]{1,0:T(8,128)(2,1)S(1)}, u32[]{:S(2)}, u32[]{:S(2)}) collective-permute-start(bf16[16,1024]{1,0:T(8,128)(2,1)S(1)} %shard_map.156.refs_3_), channel_id=1, source_target_pairs={{0,1},{1,2},{2,3},{3,0},{4,5},{5,6},{6,7},{7,4},{8,9},{9,10},{10,1... | collective-permute-start | bytes 98312 | tf_op jit(solution)/shard_map/ppermute | solution.py:209
  24.5 1.4 %collective-permute-start.19 = (bf16[16,1024]{1,0:T(8,128)(2,1)S(1)}, bf16[16,1024]{1,0:T(8,128)(2,1)S(1)}, u32[]{:S(2)}, u32[]{:S(2)}) collective-permute-start(bf16[16,1024]{1,0:T(8,128)(2,1)S(1)} %shard_map.157), channel_id=1, source_target_pairs={{0,1},{1,0},{2,3},{3,2},{4,5},{5,4},{6,7},{7,6},{8,9},{9,8},{10,11... | collective-permute-start | bytes 98312 | tf_op jit(solution)/shard_map/ppermute | solution.py:108
  25.8 0.7 %collective-permute-done.15.third_ref = bf16[16,1024]{1,0:T(8,128)(2,1)S(1)} collective-permute-done((bf16[16,1024]{1,0:T(8,128)(2,1)S(1)}, bf16[16,1024]{1,0:T(8,128)(2,1)S(1)}, u32[]{:S(2)}, u32[]{:S(2)}) %collective-permute-start.15) | collective-permute-done | bytes 32800 | tf_op jit(solution)/shard_map/ppermute | solution.py:209
  26.5 1.0 %collective-permute-done.16.second_ref = bf16[16,1024]{1,0:T(8,128)(2,1)S(1)} collective-permute-done((bf16[16,1024]{1,0:T(8,128)(2,1)S(1)}, bf16[16,1024]{1,0:T(8,128)(2,1)S(1)}, u32[]{:S(2)}, u32[]{:S(2)}) %collective-permute-start.16) | collective-permute-done | bytes 32800 | tf_op jit(solution)/shard_map/ppermute | solution.py:209
  27.5 0.3 collective-permute-done.18.first_ref
  27.9 0.2 shard_map.158
  28.0 1.1 %collective-permute-start.20 = (bf16[16,1152]{1,0:T(8,128)(2,1)S(1)}, bf16[16,1152]{1,0:T(8,128)(2,1)S(1)}, u32[]{:S(2)}, u32[]{:S(2)}) collective-permute-start(bf16[16,1152]{1,0:T(8,128)(2,1)S(1)} %get-tuple-element.17.refs_3_), channel_id=1, source_target_pairs={{0,25},{1,0},{2,27},{3,2},{4,29},{5,4},{6,31},{7,6},{8,17},{9,8},{... | collective-permute-start | bytes 110600 | tf_op jit(solution)/shard_map/ppermute | solution.py:209
  29.1 0.6 %collective-permute-start.21 = (bf16[16,1152]{1,0:T(8,128)(2,1)S(1)}, bf16[16,1152]{1,0:T(8,128)(2,1)S(1)}, u32[]{:S(2)}, u32[]{:S(2)}) collective-permute-start(bf16[16,1152]{1,0:T(8,128)(2,1)S(1)} %get-tuple-element.17.refs_3_), channel_id=1, source_target_pairs={{0,17},{1,0},{2,19},{3,2},{4,21},{5,4},{6,23},{7,6},{8,25},{9,8},{... | collective-permute-start | bytes 110600 | tf_op jit(solution)/shard_map/ppermute | solution.py:209
  29.8 0.4 %collective-permute-start.23 = (bf16[16,1152]{1,0:T(8,128)(2,1)S(1)}, bf16[16,1152]{1,0:T(8,128)(2,1)S(1)}, u32[]{:S(2)}, u32[]{:S(2)}) collective-permute-start(bf16[16,1152]{1,0:T(8,128)(2,1)S(1)} %get-tuple-element.17.refs_3_), channel_id=1, source_target_pairs={{0,1},{1,0},{2,3},{3,2},{4,5},{5,4},{6,7},{7,6},{8,9},{9,8},{10,11... | collective-permute-start | bytes 110600 | tf_op jit(solution)/shard_map/ppermute | solution.py:108
  30.3 1.1 %collective-permute-done.24._.refs_6_ = f32[16,512]{1,0:T(8,128)S(1)} collective-permute-done((f32[16,512]{1,0:T(8,128)S(1)}, f32[16,512]{1,0:T(8,128)S(1)}, u32[]{:S(2)}, u32[]{:S(2)}) %collective-permute-start.24) | collective-permute-done | bytes 32800 | tf_op jit(solution)/shard_map/ppermute | solution.py:108
  31.5 1.8 %collective-permute-start.25 = (f32[32,128]{1,0:T(8,128)S(1)}, f32[32,128]{1,0:T(8,128)S(1)}, u32[]{:S(2)}, u32[]{:S(2)}) collective-permute-start(f32[32,128]{1,0:T(8,128)S(1)} %get-tuple-element.19), channel_id=1, source_target_pairs={{0,1},{1,6},{2,3},{3,4},{4,5},{5,2},{6,7},{7,0},{8,9},{9,14},{10,1... | collective-permute-start | bytes 49160 | tf_op jit(solution)/shard_map/ppermute | solution.py:209
  33.3 0.2 collective-permute-start.26
  33.5 1.1 %collective-permute-start.27 = (f32[32,128]{1,0:T(8,128)S(1)}, f32[32,128]{1,0:T(8,128)S(1)}, u32[]{:S(2)}, u32[]{:S(2)}) collective-permute-start(f32[32,128]{1,0:T(8,128)S(1)} %get-tuple-element.19), channel_id=1, source_target_pairs={{0,1},{1,2},{2,3},{3,0},{4,5},{5,6},{6,7},{7,4},{8,9},{9,10},{10,1... | collective-permute-start | bytes 49160 | tf_op jit(solution)/shard_map/ppermute | solution.py:209
  34.6 0.5 %collective-permute-start.30 = (bf16[48,512]{1,0:T(8,128)(2,1)S(1)}, bf16[48,512]{1,0:T(8,128)(2,1)S(1)}, u32[]{:S(2)}, u32[]{:S(2)}) collective-permute-start(bf16[48,512]{1,0:T(8,128)(2,1)S(1)} %get-tuple-element.21), channel_id=1, source_target_pairs={{0,1},{1,0},{2,3},{3,2},{4,5},{5,4},{6,7},{7,6},{8,9},{9,8},{10,11... | collective-permute-start | bytes 147464 | tf_op jit(solution)/shard_map/ppermute | solution.py:108
  35.1 1.3 %collective-permute-done.25.third_ref = f32[32,128]{1,0:T(8,128)S(1)} collective-permute-done((f32[32,128]{1,0:T(8,128)S(1)}, f32[32,128]{1,0:T(8,128)S(1)}, u32[]{:S(2)}, u32[]{:S(2)}) %collective-permute-start.25) | collective-permute-done | bytes 16416 | tf_op jit(solution)/shard_map/ppermute | solution.py:209
  36.5 0.9 %collective-permute-done.26.second_ref = f32[32,128]{1,0:T(8,128)S(1)} collective-permute-done((f32[32,128]{1,0:T(8,128)S(1)}, f32[32,128]{1,0:T(8,128)S(1)}, u32[]{:S(2)}, u32[]{:S(2)}) %collective-permute-start.26) | collective-permute-done | bytes 16416 | tf_op jit(solution)/shard_map/ppermute | solution.py:209
  37.4 0.1 shard_map.161.refs_8_
  37.5 1.0 %collective-permute-done.29.refs_1_ = f32[32,128]{1,0:T(8,128)S(1)} collective-permute-done((f32[32,128]{1,0:T(8,128)S(1)}, f32[32,128]{1,0:T(8,128)S(1)}, u32[]{:S(2)}, u32[]{:S(2)}) %collective-permute-start.29) | collective-permute-done | bytes 16416 | tf_op jit(solution)/shard_map/ppermute | solution.py:108
  38.6 1.1 %shard_map.162 = (bf16[16,512]{1,0:T(8,128)(2,1)}, f32[2]{0:T(128)}, bf16[16,512]{1,0:T(8,128)(2,1)}) custom-call(f32[32,128]{1,0:T(8,128)S(1)} %shard_map.160.refs_0_, f32[32,128]{1,0:T(8,128)S(1)} %collective-permute-done.29.refs_1_, bf16[64,512]{1,0:T(8,128)(2,1)S(1)} %get-tuple-element.20.refs_2_, bf16[16,1152]{1,0:T(8,128)(2,1)S(1)} %get-tuple-element.17.refs_3_, ...), custom_call_target="tpu_custom_call" | custom-call | tf_op jit(solution)/shard_map/pallas_call | solution.py:787
  (62 shorter events, 0.7 us)
Async XLA Ops:
  0.6 2.1 %collective-permute-start = (bf16[16,512]{1,0:T(8,128)(2,1)}, bf16[16,512]{1,0:T(8,128)(2,1)S(1)}, u32[]{:S(2)}, u32[]{:S(2)}) collective-permute-start(bf16[16,512]{1,0:T(8,128)(2,1)} %own_ref.3), channel_id=1, source_target_pairs={{0,1},{1,0},{2,3},{3,2},{4,5},{5,4},{6,7},{7,6},{8,9},{9,8},{10,11... | collective-permute-start | bytes 49160 | tf_op jit(solution)/shard_map/ppermute | solution.py:108
  1.1 1.4 %collective-permute-start.1 = (f32[1,512]{1,0:T(1,128)}, f32[1,512]{1,0:T(1,128)S(1)}, u32[]{:S(2)}, u32[]{:S(2)}) collective-permute-start(f32[1,512]{1,0:T(1,128)} %bitcast.10), channel_id=1, source_target_pairs={{0,1},{1,0},{2,3},{3,2},{4,5},{5,4},{6,7},{7,6},{8,9},{9,8},{10,11... | collective-permute-start | bytes 6152 | tf_op jit(solution)/shard_map/ppermute | solution.py:108
  1.2 1.5 %copy-start.4 = (bf16[16,512]{1,0:T(8,128)(2,1)S(1)}, bf16[16,512]{1,0:T(8,128)(2,1)}, u32[]{:S(2)}) copy-start(bf16[16,512]{1,0:T(8,128)(2,1)} %own_ref.3) | copy-start | bytes 49156
  1.2 1.5 %copy-start.11 = (f32[512]{0:T(512)S(1)}, f32[512]{0:T(512)}, u32[]{:S(2)}) copy-start(f32[512]{0:T(512)} %param.13) | copy-start | bytes 6148
  1.2 1.5 %collective-permute-start.2 = (f32[1,512]{1,0:T(1,128)}, f32[1,512]{1,0:T(1,128)S(1)}, u32[]{:S(2)}, u32[]{:S(2)}) collective-permute-start(f32[1,512]{1,0:T(1,128)} %bitcast.4), channel_id=1, source_target_pairs={{0,1},{1,0},{2,3},{3,2},{4,5},{5,4},{6,7},{7,6},{8,9},{9,8},{10,11... | collective-permute-start | bytes 6152 | tf_op jit(solution)/shard_map/ppermute | solution.py:108
  1.7 8.3 %collective-permute-start.6 = (bf16[4096,512]{1,0:T(8,128)(2,1)}, bf16[4096,512]{1,0:T(8,128)(2,1)S(1)}, u32[]{:S(2)}, u32[]{:S(2)}) collective-permute-start(bf16[4096,512]{1,0:T(8,128)(2,1)} %refs_4_.1), channel_id=1, source_target_pairs={{0,1},{1,0},{2,3},{3,2},{4,5},{5,4},{6,7},{7,6},{8,9},{9,8},{10,11... | collective-permute-start | bytes 12582920 | tf_op jit(solution)/shard_map/ppermute | solution.py:108
  2.7 5.0 %copy-start.1 = (bf16[4096,512]{1,0:T(8,128)(2,1)S(1)}, bf16[4096,512]{1,0:T(8,128)(2,1)}, u32[]{:S(2)}) copy-start(bf16[4096,512]{1,0:T(8,128)(2,1)} %refs_4_.1) | copy-start | bytes 12582916
  2.9 5.0 %copy-start.2 = (bf16[320,1024]{1,0:T(8,128)(2,1)S(1)}, bf16[320,1024]{1,0:T(8,128)(2,1)}, u32[]{:S(2)}) copy-start(bf16[320,1024]{1,0:T(8,128)(2,1)} %refs_1_.11) | copy-start | bytes 1966084
  2.9 5.0 %copy-start.3 = (bf16[320,1024]{1,0:T(8,128)(2,1)S(1)}, bf16[320,1024]{1,0:T(8,128)(2,1)}, u32[]{:S(2)}) copy-start(bf16[320,1024]{1,0:T(8,128)(2,1)} %refs_2_.5) | copy-start | bytes 1966084
  2.9 6.4 %collective-permute-start.3 = (bf16[16,1152]{1,0:T(8,128)(2,1)S(1)}, bf16[16,1152]{1,0:T(8,128)(2,1)S(1)}, u32[]{:S(2)}, u32[]{:S(2)}) collective-permute-start(bf16[16,1152]{1,0:T(8,128)(2,1)S(1)} %shard_map.140.message_ref.refs_3_.pair_ref), channel_id=1, source_target_pairs={{0,7},{1,0},{2,5},{3,2},{4,3},{5,4},{6,1},{7,6},{8,15},{9,8},{10,1... | collective-permute-start | bytes 110600 | tf_op jit(solution)/shard_map/ppermute | solution.py:209
  7.7 2.0 %collective-permute-start.4 = (bf16[16,1152]{1,0:T(8,128)(2,1)S(1)}, bf16[16,1152]{1,0:T(8,128)(2,1)S(1)}, u32[]{:S(2)}, u32[]{:S(2)}) collective-permute-start(bf16[16,1152]{1,0:T(8,128)(2,1)S(1)} %shard_map.140.message_ref.refs_3_.pair_ref), channel_id=1, source_target_pairs={{0,5},{1,0},{2,7},{3,2},{4,1},{5,4},{6,3},{7,6},{8,13},{9,8},{10,1... | collective-permute-start | bytes 110600 | tf_op jit(solution)/shard_map/ppermute | solution.py:209
  7.7 2.3 %collective-permute-start.5 = (bf16[16,1152]{1,0:T(8,128)(2,1)S(1)}, bf16[16,1152]{1,0:T(8,128)(2,1)S(1)}, u32[]{:S(2)}, u32[]{:S(2)}) collective-permute-start(bf16[16,1152]{1,0:T(8,128)(2,1)S(1)} %shard_map.140.message_ref.refs_3_.pair_ref), channel_id=1, source_target_pairs={{0,3},{1,0},{2,1},{3,2},{4,7},{5,4},{6,5},{7,6},{8,11},{9,8},{10,9... | collective-permute-start | bytes 110600 | tf_op jit(solution)/shard_map/ppermute | solution.py:209
  7.9 0.7 %copy-start.6 = (s32[1,16]{1,0:T(1,128)S(1)}, s32[1,16]{1,0:T(1,128)}, u32[]{:S(2)}) copy-start(s32[1,16]{1,0:T(1,128)} %lengths_ref.1) | copy-start | bytes 196
  7.9 0.7 %copy-start.7 = (s32[1,16]{1,0:T(1,128)S(1)}, s32[1,16]{1,0:T(1,128)}, u32[]{:S(2)}) copy-start(s32[1,16]{1,0:T(1,128)} %order_ref.1) | copy-start | bytes 196
  7.9 0.7 %copy-start.10 = (f32[1,128]{1,0:T(1,128)S(1)}, f32[1,128]{1,0:T(1,128)}, u32[]{:S(2)}) copy-start(f32[1,128]{1,0:T(1,128)} %constant.2.clone.frequency_ref) | copy-start | bytes 1540
  8.0 2.0 %copy-start.8 = (f32[128]{0:T(128)S(1)}, f32[128]{0:T(128)}, u32[]{:S(2)}) copy-start(f32[128]{0:T(128)} %param.15) | copy-start | bytes 1540
  8.1 6.7 %collective-permute-start.8 = (bf16[2,320,1024]{2,1,0:T(8,128)(2,1)S(1)}, bf16[2,320,1024]{2,1,0:T(8,128)(2,1)S(1)}, u32[]{:S(2)}, u32[]{:S(2)}) collective-permute-start(bf16[2,320,1024]{2,1,0:T(8,128)(2,1)S(1)} %shard_map.146), channel_id=1, source_target_pairs={{0,1},{1,0},{2,3},{3,2},{4,5},{5,4},{6,7},{7,6},{8,9},{9,8},{10,11... | collective-permute-start | bytes 3932168 | tf_op jit(solution)/shard_map/ppermute | solution.py:108
  10.0 4.5 %copy-start = (bf16[512,4096]{1,0:T(8,128)(2,1)S(1)}, bf16[512,4096]{1,0:T(8,128)(2,1)}, u32[]{:S(2)}) copy-start(bf16[512,4096]{1,0:T(8,128)(2,1)} %refs_1_.17) | copy-start | bytes 12582916
  10.0 6.6 %collective-permute-start.7 = (bf16[16,1024]{1,0:T(8,128)(2,1)S(1)}, bf16[16,1024]{1,0:T(8,128)(2,1)S(1)}, u32[]{:S(2)}, u32[]{:S(2)}) collective-permute-start(bf16[16,1024]{1,0:T(8,128)(2,1)S(1)} %shard_map.145.query_ref.refs_0_), channel_id=1, source_target_pairs={{0,1},{1,6},{2,3},{3,4},{4,5},{5,2},{6,7},{7,0},{8,9},{9,14},{10,1... | collective-permute-start | bytes 98312 | tf_op jit(solution)/shard_map/ppermute | solution.py:209
  13.2 4.6 %collective-permute-start.10 = (bf16[16,1024]{1,0:T(8,128)(2,1)S(1)}, bf16[16,1024]{1,0:T(8,128)(2,1)S(1)}, u32[]{:S(2)}, u32[]{:S(2)}) collective-permute-start(bf16[16,1024]{1,0:T(8,128)(2,1)S(1)} %shard_map.145.query_ref.refs_0_), channel_id=1, source_target_pairs={{0,1},{1,4},{2,3},{3,6},{4,5},{5,0},{6,7},{7,2},{8,9},{9,12},{10,1... | collective-permute-start | bytes 98312 | tf_op jit(solution)/shard_map/ppermute | solution.py:209
  13.9 4.4 %collective-permute-start.12 = (bf16[16,1024]{1,0:T(8,128)(2,1)S(1)}, bf16[16,1024]{1,0:T(8,128)(2,1)S(1)}, u32[]{:S(2)}, u32[]{:S(2)}) collective-permute-start(bf16[16,1024]{1,0:T(8,128)(2,1)S(1)} %shard_map.145.query_ref.refs_0_), channel_id=1, source_target_pairs={{0,1},{1,2},{2,3},{3,0},{4,5},{5,6},{6,7},{7,4},{8,9},{9,10},{10,1... | collective-permute-start | bytes 98312 | tf_op jit(solution)/shard_map/ppermute | solution.py:209
  14.7 5.9 %collective-permute-start.14 = (bf16[2,512,1024]{2,1,0:T(8,128)(2,1)S(1)}, bf16[2,512,1024]{2,1,0:T(8,128)(2,1)S(1)}, u32[]{:S(2)}, u32[]{:S(2)}) collective-permute-start(bf16[2,512,1024]{2,1,0:T(8,128)(2,1)S(1)} %shard_map.152), channel_id=1, source_target_pairs={{0,1},{1,0},{2,3},{3,2},{4,5},{5,4},{6,7},{7,6},{8,9},{9,8},{10,11... | collective-permute-start | bytes 6291464 | tf_op jit(solution)/shard_map/ppermute | solution.py:108
  17.1 2.5 %collective-permute-start.9 = (bf16[16,1152]{1,0:T(8,128)(2,1)S(1)}, bf16[16,1152]{1,0:T(8,128)(2,1)S(1)}, u32[]{:S(2)}, u32[]{:S(2)}) collective-permute-start(bf16[16,1152]{1,0:T(8,128)(2,1)S(1)} %shard_map.148.refs_5_), channel_id=1, source_target_pairs={{0,7},{1,0},{2,5},{3,2},{4,3},{5,4},{6,1},{7,6},{8,15},{9,8},{10,1... | collective-permute-start | bytes 110600 | tf_op jit(solution)/shard_map/ppermute | solution.py:209
  18.3 1.7 %collective-permute-start.11 = (bf16[16,1152]{1,0:T(8,128)(2,1)S(1)}, bf16[16,1152]{1,0:T(8,128)(2,1)S(1)}, u32[]{:S(2)}, u32[]{:S(2)}) collective-permute-start(bf16[16,1152]{1,0:T(8,128)(2,1)S(1)} %shard_map.149.refs_5_), channel_id=1, source_target_pairs={{0,5},{1,0},{2,7},{3,2},{4,1},{5,4},{6,3},{7,6},{8,13},{9,8},{10,1... | collective-permute-start | bytes 110600 | tf_op jit(solution)/shard_map/ppermute | solution.py:209
  18.9 1.7 %collective-permute-start.13 = (bf16[16,1152]{1,0:T(8,128)(2,1)S(1)}, bf16[16,1152]{1,0:T(8,128)(2,1)S(1)}, u32[]{:S(2)}, u32[]{:S(2)}) collective-permute-start(bf16[16,1152]{1,0:T(8,128)(2,1)S(1)} %shard_map.150.refs_0_), channel_id=1, source_target_pairs={{0,3},{1,0},{2,1},{3,2},{4,7},{5,4},{6,5},{7,6},{8,11},{9,8},{10,9... | collective-permute-start | bytes 110600 | tf_op jit(solution)/shard_map/ppermute | solution.py:209
  19.1 4.5 %collective-permute-start.17 = (bf16[2,512,1024]{2,1,0:T(8,128)(2,1)S(1)}, bf16[2,512,1024]{2,1,0:T(8,128)(2,1)S(1)}, u32[]{:S(2)}, u32[]{:S(2)}) collective-permute-start(bf16[2,512,1024]{2,1,0:T(8,128)(2,1)S(1)} %shard_map.155), channel_id=1, source_target_pairs={{0,1},{1,0},{2,3},{3,2},{4,5},{5,4},{6,7},{7,6},{8,9},{9,8},{10,11... | collective-permute-start | bytes 6291464 | tf_op jit(solution)/shard_map/ppermute | solution.py:108
  20.6 6.0 %collective-permute-start.15 = (bf16[16,1024]{1,0:T(8,128)(2,1)S(1)}, bf16[16,1024]{1,0:T(8,128)(2,1)S(1)}, u32[]{:S(2)}, u32[]{:S(2)}) collective-permute-start(bf16[16,1024]{1,0:T(8,128)(2,1)S(1)} %shard_map.153.refs_3_), channel_id=1, source_target_pairs={{0,1},{1,6},{2,3},{3,4},{4,5},{5,2},{6,7},{7,0},{8,9},{9,14},{10,1... | collective-permute-start | bytes 98312 | tf_op jit(solution)/shard_map/ppermute | solution.py:209
  23.2 4.3 %collective-permute-start.16 = (bf16[16,1024]{1,0:T(8,128)(2,1)S(1)}, bf16[16,1024]{1,0:T(8,128)(2,1)S(1)}, u32[]{:S(2)}, u32[]{:S(2)}) collective-permute-start(bf16[16,1024]{1,0:T(8,128)(2,1)S(1)} %shard_map.154.refs_3_), channel_id=1, source_target_pairs={{0,1},{1,4},{2,3},{3,6},{4,5},{5,0},{6,7},{7,2},{8,9},{9,12},{10,1... | collective-permute-start | bytes 98312 | tf_op jit(solution)/shard_map/ppermute | solution.py:209
  23.6 4.2 %copy-start.5 = (f32[512]{0:T(512)S(1)}, f32[512]{0:T(512)}, u32[]{:S(2)}) copy-start(f32[512]{0:T(512)} %param.19) | copy-start | bytes 6148
  23.6 4.2 %collective-permute-start.18 = (bf16[16,1024]{1,0:T(8,128)(2,1)S(1)}, bf16[16,1024]{1,0:T(8,128)(2,1)S(1)}, u32[]{:S(2)}, u32[]{:S(2)}) collective-permute-start(bf16[16,1024]{1,0:T(8,128)(2,1)S(1)} %shard_map.156.refs_3_), channel_id=1, source_target_pairs={{0,1},{1,2},{2,3},{3,0},{4,5},{5,6},{6,7},{7,4},{8,9},{9,10},{10,1... | collective-permute-start | bytes 98312 | tf_op jit(solution)/shard_map/ppermute | solution.py:209
  24.5 3.4 %collective-permute-start.19 = (bf16[16,1024]{1,0:T(8,128)(2,1)S(1)}, bf16[16,1024]{1,0:T(8,128)(2,1)S(1)}, u32[]{:S(2)}, u32[]{:S(2)}) collective-permute-start(bf16[16,1024]{1,0:T(8,128)(2,1)S(1)} %shard_map.157), channel_id=1, source_target_pairs={{0,1},{1,0},{2,3},{3,2},{4,5},{5,4},{6,7},{7,6},{8,9},{9,8},{10,11... | collective-permute-start | bytes 98312 | tf_op jit(solution)/shard_map/ppermute | solution.py:108
  28.0 9.4 %copy-start.9 = (s32[64]{0:T(128)S(1)}, s32[64]{0:T(128)}, u32[]{:S(2)}) copy-start(s32[64]{0:T(128)} %param.22) | copy-start | bytes 772
  28.0 3.4 %collective-permute-start.20 = (bf16[16,1152]{1,0:T(8,128)(2,1)S(1)}, bf16[16,1152]{1,0:T(8,128)(2,1)S(1)}, u32[]{:S(2)}, u32[]{:S(2)}) collective-permute-start(bf16[16,1152]{1,0:T(8,128)(2,1)S(1)} %get-tuple-element.17.refs_3_), channel_id=1, source_target_pairs={{0,25},{1,0},{2,27},{3,2},{4,29},{5,4},{6,31},{7,6},{8,17},{9,8},{... | collective-permute-start | bytes 110600 | tf_op jit(solution)/shard_map/ppermute | solution.py:209
  29.1 2.3 %collective-permute-start.21 = (bf16[16,1152]{1,0:T(8,128)(2,1)S(1)}, bf16[16,1152]{1,0:T(8,128)(2,1)S(1)}, u32[]{:S(2)}, u32[]{:S(2)}) collective-permute-start(bf16[16,1152]{1,0:T(8,128)(2,1)S(1)} %get-tuple-element.17.refs_3_), channel_id=1, source_target_pairs={{0,17},{1,0},{2,19},{3,2},{4,21},{5,4},{6,23},{7,6},{8,25},{9,8},{... | collective-permute-start | bytes 110600 | tf_op jit(solution)/shard_map/ppermute | solution.py:209
  29.7 1.7 %collective-permute-start.22 = (bf16[16,1152]{1,0:T(8,128)(2,1)S(1)}, bf16[16,1152]{1,0:T(8,128)(2,1)S(1)}, u32[]{:S(2)}, u32[]{:S(2)}) collective-permute-start(bf16[16,1152]{1,0:T(8,128)(2,1)S(1)} %get-tuple-element.17.refs_3_), channel_id=1, source_target_pairs={{0,9},{1,0},{2,11},{3,2},{4,13},{5,4},{6,15},{7,6},{8,1},{9,8},{10... | collective-permute-start | bytes 110600 | tf_op jit(solution)/shard_map/ppermute | solution.py:209
  29.8 1.7 %collective-permute-start.23 = (bf16[16,1152]{1,0:T(8,128)(2,1)S(1)}, bf16[16,1152]{1,0:T(8,128)(2,1)S(1)}, u32[]{:S(2)}, u32[]{:S(2)}) collective-permute-start(bf16[16,1152]{1,0:T(8,128)(2,1)S(1)} %get-tuple-element.17.refs_3_), channel_id=1, source_target_pairs={{0,1},{1,0},{2,3},{3,2},{4,5},{5,4},{6,7},{7,6},{8,9},{9,8},{10,11... | collective-permute-start | bytes 110600 | tf_op jit(solution)/shard_map/ppermute | solution.py:108
  30.2 1.2 %collective-permute-start.24 = (f32[16,512]{1,0:T(8,128)S(1)}, f32[16,512]{1,0:T(8,128)S(1)}, u32[]{:S(2)}, u32[]{:S(2)}) collective-permute-start(f32[16,512]{1,0:T(8,128)S(1)} %get-tuple-element.18), channel_id=1, source_target_pairs={{0,1},{1,0},{2,3},{3,2},{4,5},{5,4},{6,7},{7,6},{8,9},{9,8},{10,11... | collective-permute-start | bytes 98312 | tf_op jit(solution)/shard_map/ppermute | solution.py:108
  31.5 5.0 %collective-permute-start.25 = (f32[32,128]{1,0:T(8,128)S(1)}, f32[32,128]{1,0:T(8,128)S(1)}, u32[]{:S(2)}, u32[]{:S(2)}) collective-permute-start(f32[32,128]{1,0:T(8,128)S(1)} %get-tuple-element.19), channel_id=1, source_target_pairs={{0,1},{1,6},{2,3},{3,4},{4,5},{5,2},{6,7},{7,0},{8,9},{9,14},{10,1... | collective-permute-start | bytes 49160 | tf_op jit(solution)/shard_map/ppermute | solution.py:209
  33.3 4.1 %collective-permute-start.26 = (f32[32,128]{1,0:T(8,128)S(1)}, f32[32,128]{1,0:T(8,128)S(1)}, u32[]{:S(2)}, u32[]{:S(2)}) collective-permute-start(f32[32,128]{1,0:T(8,128)S(1)} %get-tuple-element.19), channel_id=1, source_target_pairs={{0,1},{1,4},{2,3},{3,6},{4,5},{5,0},{6,7},{7,2},{8,9},{9,12},{10,1... | collective-permute-start | bytes 49160 | tf_op jit(solution)/shard_map/ppermute | solution.py:209
  33.5 3.9 %collective-permute-start.27 = (f32[32,128]{1,0:T(8,128)S(1)}, f32[32,128]{1,0:T(8,128)S(1)}, u32[]{:S(2)}, u32[]{:S(2)}) collective-permute-start(f32[32,128]{1,0:T(8,128)S(1)} %get-tuple-element.19), channel_id=1, source_target_pairs={{0,1},{1,2},{2,3},{3,0},{4,5},{5,6},{6,7},{7,4},{8,9},{9,10},{10,1... | collective-permute-start | bytes 49160 | tf_op jit(solution)/shard_map/ppermute | solution.py:209
  34.6 2.7 %collective-permute-start.28 = (f32[32,128]{1,0:T(8,128)S(1)}, f32[32,128]{1,0:T(8,128)S(1)}, u32[]{:S(2)}, u32[]{:S(2)}) collective-permute-start(f32[32,128]{1,0:T(8,128)S(1)} %get-tuple-element.19), channel_id=1, source_target_pairs={{0,1},{1,0},{2,3},{3,2},{4,5},{5,4},{6,7},{7,6},{8,9},{9,8},{10,11... | collective-permute-start | bytes 49160 | tf_op jit(solution)/shard_map/ppermute | solution.py:108
  34.6 4.0 %collective-permute-start.30 = (bf16[48,512]{1,0:T(8,128)(2,1)S(1)}, bf16[48,512]{1,0:T(8,128)(2,1)S(1)}, u32[]{:S(2)}, u32[]{:S(2)}) collective-permute-start(bf16[48,512]{1,0:T(8,128)(2,1)S(1)} %get-tuple-element.21), channel_id=1, source_target_pairs={{0,1},{1,0},{2,3},{3,2},{4,5},{5,4},{6,7},{7,6},{8,9},{9,8},{10,11... | collective-permute-start | bytes 147464 | tf_op jit(solution)/shard_map/ppermute | solution.py:108
  37.3 1.2 %collective-permute-start.29 = (f32[32,128]{1,0:T(8,128)S(1)}, f32[32,128]{1,0:T(8,128)S(1)}, u32[]{:S(2)}, u32[]{:S(2)}) collective-permute-start(f32[32,128]{1,0:T(8,128)S(1)} %shard_map.160.refs_0_), channel_id=1, source_target_pairs={{0,1},{1,0},{2,3},{3,2},{4,5},{5,4},{6,7},{7,6},{8,9},{9,8},{10,11... | collective-permute-start | bytes 49160 | tf_op jit(solution)/shard_map/ppermute | solution.py:108
